TPU v7x, 32 devices: a whole 2x2x4 slice. The times are simulated.
32 devices in a mesh: groups: 2 (over y), seq: 4 (over z), dp: 4 (over x, core).
Axes of the slice: x: 2, y: 2, z: 4, core: 2. Of those that a mesh axis runs over, the one named last changes fastest.
Arguments:
- x_raw: bfloat16 [1024, 8192], P(('groups', 'seq'), 'dp'), parts along dimension 0, may hold values from -6 to 6
- bc_raw: bfloat16 [1024, 2048], P(('groups', 'seq'), 'dp'), parts along dimension 0, may hold values from -6 to 6
- z_gate: bfloat16 [1024, 8192], P(('groups', 'seq'), 'dp'), parts along dimension 0, may hold values from -6 to 6
- dt_raw: float32 [1024, 128], P(('groups', 'seq'), 'dp'), parts along dimension 0, may hold values from -3 to 6
- conv_x_weight: float32 [4, 8192], P(None, 'dp'), may hold values from -3 to 3
- conv_x_bias: float32 [8192], P('dp'), may hold values from -3 to 3
- conv_bc_weight: float32 [4, 2048], P(None, 'dp'), may hold values from -3 to 3
- conv_bc_bias: float32 [2048], P('dp'), may hold values from -3 to 3
- dt_bias: float32 [128], P('dp'), may hold values from -1 to 1
- a_log: float32 [128], P('dp')
- skip_d: float32 [128], P('dp'), may hold values from 0.5 to 1.5
- norm_gain: float32 [8192], P('dp'), may hold values from 0.5 to 1.5
- queries: bfloat16 [1024, 4096], P(('groups', 'seq'), 'dp'), parts along dimension 0, may hold values from -6 to 6
- keys: bfloat16 [1024, 1024], P(('groups', 'seq'), 'dp'), parts along dimension 0, may hold values from -6 to 6
- values: bfloat16 [1024, 1024], P(('groups', 'seq'), 'dp'), parts along dimension 0, may hold values from -6 to 6
- doc_lens: int32 [8], P('groups'), parts along dimension 0, may hold values from 1 to 256, 512 in all
Outputs:
- mamba_out: bfloat16 [1024, 8192], P(('groups', 'seq'), 'dp'), parts along dimension 0
- attn_out: bfloat16 [1024, 4096], P(('groups', 'seq'), 'dp'), parts along dimension 0
There are 2 independent parts, one for each index of `groups`. A program takes and returns all parts, laid end to end along the dimension named above; an argument that names none is the same for every part. Nothing has to cross between parts.
Inputs may be any that keep to these rules, and one draw needn't show every extreme that they name: doc_lens holds 4 document lengths that sum to 512; the longest is exactly 256.
All inputs are finite; a program needn't handle non-finite values.
Results may differ from a plain program's by a relative error of at most 0.018.
Values may be sent and summed in bfloat16 or wider, within the bound.
No kernel may reach another device: no remote copies, remote signals or barrier semaphores. Data moves between devices by JAX's collectives and lax.ppermute only.
A program may use at most 128 MiB of HBM per device.

v0:
```python
import jax
import jax.numpy as jnp
from jax import lax
from jax.sharding import PartitionSpec as P

HDIM = 64
STATE = 128
QHEADS = 32
KVHEADS = 8
ADIM = 128


EPSILON = 1e-05
NEGATIVE = -1e30
BARRED = -2e30
HIGHEST = lax.Precision.HIGHEST


def shifted(value, axis, steps):
    count = lax.axis_size(axis)
    first, last = (max(0, -steps), min(count, count - steps))
    return lax.ppermute(value, axis, [(source, source + steps) for source in range(first, last)])


def carried_in(array, axis, combine, identity):
    size, here = (lax.axis_size(axis), lax.axis_index(axis))
    everything = jax.tree.map(
        lambda part, kind: lax.all_gather(part.astype(kind), axis),
        array,
        (jnp.bfloat16, jnp.bfloat16),
    )
    start = jax.tree.map(
        lambda part, zero: jnp.broadcast_to(jnp.asarray(zero, part.dtype), part.shape),
        array,
        identity,
    )

    def hop(k, before):
        reached = k < here
        new = combine(
            before, jax.tree.map(lambda part, own: part[k].astype(own.dtype), everything, array)
        )
        return jax.tree.map(lambda a, b: jnp.where(reached, a, b), new, before)

    return lax.fori_loop(0, size, hop, start)


def doc_starts(doc_lens):
    ends = jnp.cumsum(doc_lens)
    return ends - doc_lens


def doc_index(positions, starts):
    inside = (starts[None, :] <= positions[:, None]).astype(jnp.int32)
    return jnp.sum(inside, axis=1) - 1


def causal_conv(padded, pad_docs, docs, weight, bias):
    count = docs.shape[0]
    total = jnp.zeros((count, bias.shape[0]), jnp.float32) + bias[None, :]
    for lag in range(weight.shape[0]):
        term = padded[lag : lag + count].astype(jnp.float32) * weight[lag][None, :]
        same = pad_docs[lag : lag + count] == docs
        total = total + jnp.where(same[:, None], term, 0.0)
    return jax.nn.silu(total).astype(jnp.bfloat16)


def ssd_terms(head_values, b_groups, c_groups, step_size, log_decay, begins):
    rows, heads, width = head_values.shape
    group_total_count = b_groups.shape[1]
    per_group = heads // group_total_count
    running = jnp.cumsum(log_decay, axis=0)
    segment = jnp.cumsum(begins.astype(jnp.int32), axis=0)
    order = jnp.arange(rows, dtype=jnp.int32)
    linked = (segment[:, None] == segment[None, :]) & (order[:, None] >= order[None, :])
    spread = running.T[:, :, None] - running.T[:, None, :]
    multiplier = jnp.where(linked[None], jnp.exp(jnp.where(linked[None], spread, 0.0)), 0.0)
    intersection = jnp.einsum(
        "ign,jgn->gij", c_groups, b_groups, preferred_element_type=jnp.float32
    )
    intersection = jnp.repeat(intersection, per_group, axis=0)
    scaled = head_values.astype(jnp.float32) * step_size[:, :, None]
    output = jnp.einsum("hij,jhp->ihp", multiplier * intersection, scaled, precision=HIGHEST)
    entry = jnp.where((segment == 0)[:, None], jnp.exp(running), 0.0)
    tail_weight = jnp.where(
        (segment == segment[-1])[:, None], jnp.exp(running[-1][None, :] - running), 0.0
    )
    weighted = (scaled * tail_weight[:, :, None]).reshape(rows, group_total_count, per_group, width)
    local_state = jnp.einsum(
        "jgqp,jgn->gqpn", weighted, b_groups.astype(jnp.float32), precision=HIGHEST
    )
    local_state = local_state.reshape(heads, width, -1)
    through = jnp.where(segment[-1] == 0, jnp.exp(running[-1]), 0.0)
    return (output, entry, local_state, through)


def apply_state(c_groups, state):
    heads, width, size = state.shape
    group_total_count = c_groups.shape[1]
    grouped = state.reshape(group_total_count, heads // group_total_count, width, size)
    result = jnp.einsum("ign,gqpn->igqp", c_groups.astype(jnp.float32), grouped, precision=HIGHEST)
    return result.reshape(c_groups.shape[0], heads, width)


def gated_norm(mixed, z_gate, norm_gain, group_total_count):
    count = mixed.shape[0]
    gated = mixed * jax.nn.silu(z_gate.astype(jnp.float32)).reshape(mixed.shape)
    grouped = gated.reshape(count, group_total_count, -1)
    multiplier = lax.rsqrt(jnp.mean(grouped * grouped, axis=-1, keepdims=True) + EPSILON)
    return ((grouped * multiplier).reshape(count, -1) * norm_gain[None, :]).astype(jnp.bfloat16)


def link_states(earlier, later):
    early_decay, early_state = earlier
    late_decay, late_state = later
    return (early_decay * late_decay, early_state * late_decay[:, None, None] + late_state)


def shards(
    x_raw,
    bc_raw,
    z_gate,
    dt_raw,
    conv_x_weight,
    conv_x_bias,
    conv_bc_weight,
    conv_bc_bias,
    dt_bias,
    a_log,
    skip_d,
    norm_gain,
    queries,
    keys,
    values,
    doc_lens,
):
    local_rows = x_raw.shape[0]
    device = lax.axis_index("seq")
    starts = doc_starts(doc_lens)
    first_row = device * local_rows
    positions = first_row + jnp.arange(local_rows, dtype=jnp.int32)
    docs = doc_index(positions, starts)
    begins = jnp.any(starts[None, :] == positions[:, None], axis=1)
    margin = conv_x_weight.shape[0] - 1
    x_width = x_raw.shape[1]
    tails = jnp.concatenate([x_raw[local_rows - margin :], bc_raw[local_rows - margin :]], axis=1)
    prior = shifted(tails, "seq", 1)
    pad_positions = first_row - margin + jnp.arange(local_rows + margin, dtype=jnp.int32)
    pad_docs = doc_index(pad_positions, starts)
    x_conv = causal_conv(
        jnp.concatenate([prior[:, :x_width], x_raw], axis=0),
        pad_docs,
        docs,
        conv_x_weight,
        conv_x_bias,
    )
    bc_conv = causal_conv(
        jnp.concatenate([prior[:, x_width:], bc_raw], axis=0),
        pad_docs,
        docs,
        conv_bc_weight,
        conv_bc_bias,
    )
    heads = dt_raw.shape[1]
    group_total_count = bc_raw.shape[1] // (2 * STATE)
    step_size = jax.nn.softplus(dt_raw + dt_bias[None, :])
    log_decay = -step_size * jnp.exp(a_log)[None, :]
    head_values = x_conv.reshape(local_rows, heads, HDIM)
    paired = bc_conv.reshape(local_rows, group_total_count, 2, STATE)
    b_groups = paired[:, :, 0]
    c_groups = paired[:, :, 1]
    output, entry, local_state, through = ssd_terms(
        head_values, b_groups, c_groups, step_size, log_decay, begins
    )
    identity = (jnp.ones_like(through), jnp.zeros_like(local_state))
    _, incoming_activation = carried_in((through, local_state), "seq", link_states, identity)
    output = output + apply_state(c_groups, incoming_activation) * entry[:, :, None]
    mixed = output + skip_d[None, :, None] * head_values.astype(jnp.float32)
    mamba_out = gated_norm(mixed, z_gate, norm_gain, group_total_count)
    kv_local = keys.shape[1] // ADIM
    share = QHEADS // KVHEADS
    scale = ADIM ** (-0.5)
    grouped_queries = queries.reshape(local_rows, kv_local, share, ADIM)
    key_piece = lax.all_gather(keys, "seq", axis=0, tiled=True)
    value_piece = lax.all_gather(values, "seq", axis=0, tiled=True)
    count = key_piece.shape[0]
    peak = jnp.full((kv_local, share, local_rows), NEGATIVE, jnp.float32)
    key_positions = jnp.arange(count, dtype=jnp.int32)
    key_docs = doc_index(key_positions, starts)
    permitted_mask = (key_positions[None, :] <= positions[:, None]) & (
        key_docs[None, :] == docs[:, None]
    )
    barrier = jnp.where(permitted_mask, 0.0, BARRED).astype(jnp.float32)
    scores = (
        jnp.einsum(
            "tkga,rka->kgtr",
            grouped_queries,
            key_piece.reshape(count, kv_local, ADIM),
            preferred_element_type=jnp.float32,
        )
        * scale
        + barrier[None, None]
    )
    fresh = jnp.maximum(peak, jnp.max(scores, axis=-1))
    expo = jnp.exp(scores - fresh[..., None])
    total = jnp.sum(expo, axis=-1)
    summed = jnp.einsum(
        "kgtr,rka->kgta",
        expo.astype(jnp.bfloat16),
        value_piece.reshape(count, kv_local, ADIM),
        preferred_element_type=jnp.float32,
    )
    accum = summed
    _, total, accum = (fresh, total, accum)
    attended = accum / total[..., None]
    attn_out = (
        attended.transpose(2, 0, 1, 3)
        .reshape(local_rows, kv_local * share * ADIM)
        .astype(jnp.bfloat16)
    )
    return (mamba_out, attn_out)


def solution(mesh):
    placed = (
        P(("groups", "seq"), "dp"),
        P(("groups", "seq"), "dp"),
        P(("groups", "seq"), "dp"),
        P(("groups", "seq"), "dp"),
        P(None, "dp"),
        P("dp"),
        P(None, "dp"),
        P("dp"),
        P("dp"),
        P("dp"),
        P("dp"),
        P("dp"),
        P(("groups", "seq"), "dp"),
        P(("groups", "seq"), "dp"),
        P(("groups", "seq"), "dp"),
        P("groups"),
    )
    return jax.shard_map(
        shards,
        mesh=mesh,
        in_specs=placed,
        out_specs=(P(("groups", "seq"), "dp"), P(("groups", "seq"), "dp")),
        check_vma=False,
    )
```

profile of v0, /device:TPU:0, one launch (start us, length us, event | category | flops | bytes accessed | tf_op | source)
XLA Modules:
  0.0 116.2 jit_solution(6453957832526377164)
XLA Ops:
  7.2 0.8 slice.86
  8.1 0.7 slice.87
  8.8 4.9 %collective-permute-start = (bf16[3,2560]{1,0:T(4,128)(2,1)S(1)}, bf16[3,2560]{1,0:T(4,128)(2,1)S(1)}, u32[]{:S(2)}, u32[]{:S(2)}) collective-permute-start(bf16[3,2560]{1,0:T(4,128)(2,1)S(1)} %pad_maximum_fusion.2), channel_id=1, source_target_pairs={{0,4},{4,8},{8,12},{1,5},{5,9},{9,13},{2,6},{6,10},{10,14},{3,7},{... | collective-permute-start | bytes 46088 | tf_op jit(solution)/shard_map/ppermute | solution.py:22
  13.8 0.8 reduce-window.10
  16.5 1.4 %fusion.41 = (f32[1,512]{1,0:T(1,128)S(1)}, f32[1,512]{1,0:T(1,128)S(1)}, f32[1,512]{1,0:T(1,128)}, f32[1,512]{1,0:T(1,128)}) fusion(f32[4,512]{1,0:T(4,128)} %param.24), kind=kLoop, calls=%fused_computation.96 | loop fusion | bytes 16384 | tf_op jit(solution)/shard_map/slice | solution.py:62
  17.9 1.5 %fusion.40 = (f32[1,2048]{1,0:T(1,128)}, f32[1,2048]{1,0:T(1,128)}, f32[1,2048]{1,0:T(1,128)}, f32[1,2048]{1,0:T(1,128)}) fusion(f32[4,2048]{1,0:T(4,128)} %param.22), kind=kLoop, calls=%fused_computation.95 | loop fusion | bytes 65536 | tf_op jit(solution)/shard_map/slice | solution.py:62
  20.1 1.2 %broadcast_compare_fusion = (pred[128]{0:T(512)(128)(4,1)}, pred[128]{0:T(512)(128)(4,1)S(1)}) fusion(s32[128]{0:T(128)S(1)} %reduce.2, s32[]{:T(128)} %bitcast.18), kind=kLoop, calls=%fused_computation.92 | loop fusion | flops 256 | bytes 772 | tf_op jit(solution)/shard_map/eq | solution.py:84
  22.0 0.8 negate_multiply_fusion
  23.3 0.7 exponential_select_fusion.1
  24.6 1.0 copy.117
  25.7 1.3 %copy.110 = bf16[128,2048]{0,1:T(8,128)(2,1)S(1)} copy(bf16[128,2048]{1,0:T(8,128)(2,1)} %param.18) | data formatting | bytes 1048576 | tf_op args[0]
  27.0 9.1 %all-gather = bf16[4,1,32]{2,1,0:T(2,128)(2,1)S(1)} all-gather(bf16[1,1,32]{2,1,0:T(2,128)(2,1)S(1)} %get-tuple-element.138), channel_id=1, replica_groups=mesh['groups'=2,'seq'=4,'dp'=4] {'seq'}, dimensions={0}, use_global_device_ids=true | all-gather | bytes 320 | tf_op jit(solution)/shard_map/all_gather | solution.py:28
  36.6 0.7 copy.114
  37.3 1.0 copy.123
  38.3 0.7 copy.126
  39.8 1.3 %multiply_convert_fusion.2 = bf16[128,512]{0,1:T(8,128)(2,1)S(1)} fusion(bf16[128,512]{0,1:T(8,128)(2,1)S(1)} %copy.117, bf16[3,512]{0,1:T(8,128)(2,1)S(1)} %copy.116, f32[512]{0:T(512)} %bitcast.124, f32[512]{0:T(512)} %bitcast.125, f32[512]{0:T(512)S(1)} %bitcast.123, f32[512]{0:T(512)S(1)} %bitcast.122, f32[512]{0:T(512)} %param.25, ...), kind=kLoop, calls=%fused_computation.46 | loop fusion | flops 1966080 | bytes 275968 | tf_op jit(solution)/shard_map/convert_element_type | solution.py:65
  41.1 3.4 %fusion.21 = f32[128,2048]{0,1:T(8,128)S(1)} fusion(f32[2048]{0:T(1024)} %bitcast.120, bf16[128,2048]{0,1:T(8,128)(2,1)S(1)} %copy.110, pred[128]{0:T(512)(128)(4,1)} %get-tuple-element.148, f32[2048]{0:T(1024)} %bitcast.121, bf16[3,2048]{0,1:T(8,128)(2,1)S(1)} %copy.109, pred[128]{0:T(512)(128)(4,1)} %get-tuple-element.149, f32[2048]{0:T(1024)} %bitcast.119, ...), kind=kLoop, calls=%fused_computation.39 | loop fusion | flops 8126464 | bytes 1626624 | tf_op jit(solution)/shard_map/convert_element_type | solution.py:82
  44.5 2.2 %convolution_convert_fusion = bf16[2,16,64,128]{3,2,1,0:T(8,128)(2,1)} fusion(f32[128,2,16,64]{0,3,2,1:T(8,128)S(1)} %bitcast.102, f32[128,2,16]{0,2,1:T(8,128)} %exponential_select_fusion.1, f32[128,2,16]{0,2,1:T(8,128)S(1)} %bitcast.116, bf16[128,2,2,128]{0,3,2,1:T(8,128)(2,1)S(1)} %bitcast.109), kind=kOutput, calls=%fused_computation.14 | convolution fusion | flops 403439616 | bytes 1671168 | tf_op jit(solution)/shard_map/jgqp,jgn->gqpn/dot_general | solution.py:89
  46.8 15.3 %all_gather.17 = bf16[512,256]{1,0:T(8,128)(2,1)S(1)} all-gather(bf16[128,256]{1,0:T(8,128)(2,1)S(1)} %copy-done.7), channel_id=1, replica_groups=mesh['groups'=2,'seq'=4,'dp'=4] {'seq'}, dimensions={0}, use_global_device_ids=true | all-gather | bytes 327680 | tf_op jit(solution)/shard_map/all_gather | solution.py:185
  62.2 16.8 %all_gather.16 = bf16[512,256]{0,1:T(8,128)(2,1)S(1)} all-gather(bf16[128,256]{0,1:T(8,128)(2,1)S(1)} %copy-done.2), channel_id=1, replica_groups=mesh['groups'=2,'seq'=4,'dp'=4] {'seq'}, dimensions={0}, use_global_device_ids=true | all-gather | bytes 327680 | tf_op jit(solution)/shard_map/all_gather | solution.py:184
  80.7 0.9 copy.131
  81.7 1.3 %convert_multiply_fusion = f32[128,2048]{0,1:T(8,128)S(1)} fusion(bf16[128,2048]{0,1:T(8,128)(2,1)} %copy.123), kind=kLoop, calls=%fused_computation.12 | loop fusion | flops 1310720 | bytes 1572864 | tf_op jit(solution)/shard_map/jit(silu)/mul | solution.py:107
  83.2 1.7 %bitcast_multiply_fusion = f32[32,128,128]{2,1,0:T(8,128)} fusion(f32[2,128,128]{2,1,0:T(8,128)S(1)} %fusion.30, f32[32,128]{1,0:T(8,128)S(1)} %copy-done.4, pred[128,128]{1,0:T(8,128)(4,1)S(1)} %fusion.33), kind=kLoop, calls=%fused_computation.4 | loop fusion | flops 2097152 | bytes 2260992 | tf_op jit(solution)/shard_map/mul | solution.py:83
  84.9 11.1 %all-gather.3.cloned.1.call-done = bf16[4,32,64,128]{3,2,1,0:T(8,128)(2,1)} async-done(((bf16[1,32,64,128]{3,2,1,0:T(8,128)(2,1)}), bf16[4,32,64,128]{3,2,1,0:T(8,128)(2,1)}) %all-gather.3.cloned.1.call-update) | async-done | bytes 2097168 | tf_op jit(solution)/shard_map/all_gather | solution.py:28
  96.0 5.3 %while.14 = (s32[]{:T(128)}, f32[32,64,128]{2,1,0:T(8,128)S(1)}, s32[]{:T(128)}, bf16[4,32]{1,0:T(4,128)(2,1)S(1)}, bf16[4,32,64,128]{3,2,1,0:T(8,128)(2,1)}, /*index=5*/s32[]{:T(128)}, s32[]{:T(128)}) while((s32[]{:T(128)}, f32[32,64,128]{2,1,0:T(8,128)S(1)}, s32[]{:T(128)}, bf16[4,32]{1,0:T(4,128)(2,1)S(1)}, ...), condition=%wide.region_7.8_spmd.clone, body=%wide.region_6.7_spmd.clone.sunk | while | flops 1310756 | bytes 2621865 | solution.py:45
  96.1 1.3 %fusion.48 = f32[32,64,128]{2,1,0:T(8,128)S(1)} fusion(f32[32,64,128]{2,1,0:T(8,128)S(1)} %get-tuple-element.196, bf16[4,32,64,128]{3,2,1,0:T(8,128)(2,1)} %get-tuple-element.206, s32[]{:T(128)} %get-tuple-element.195, f32[32]{0:T(128)S(1)} %bitcast_convert_fusion.2, pred[]{:T(512)S(6)} %compare.3, pred[]{:T(512)S(6)} %lt.22), kind=kLoop, calls=%fused_computation.1.clone.1 | loop fusion | flops 1310720 | bytes 2621574 | tf_op jit(solution)/shard_map/while/body/eval_jaxpr/jit(_where)/select_n | solution.py:43
  97.4 1.3 %fusion.48 = f32[32,64,128]{2,1,0:T(8,128)S(1)} fusion(f32[32,64,128]{2,1,0:T(8,128)S(1)} %get-tuple-element.196, bf16[4,32,64,128]{3,2,1,0:T(8,128)(2,1)} %get-tuple-element.206, s32[]{:T(128)} %get-tuple-element.195, f32[32]{0:T(128)S(1)} %bitcast_convert_fusion.2, pred[]{:T(512)S(6)} %compare.3, pred[]{:T(512)S(6)} %lt.22), kind=kLoop, calls=%fused_computation.1.clone.1 | loop fusion | flops 1310720 | bytes 2621574 | tf_op jit(solution)/shard_map/while/body/eval_jaxpr/jit(_where)/select_n | solution.py:43
  98.7 1.3 %fusion.48 = f32[32,64,128]{2,1,0:T(8,128)S(1)} fusion(f32[32,64,128]{2,1,0:T(8,128)S(1)} %get-tuple-element.196, bf16[4,32,64,128]{3,2,1,0:T(8,128)(2,1)} %get-tuple-element.206, s32[]{:T(128)} %get-tuple-element.195, f32[32]{0:T(128)S(1)} %bitcast_convert_fusion.2, pred[]{:T(512)S(6)} %compare.3, pred[]{:T(512)S(6)} %lt.22), kind=kLoop, calls=%fused_computation.1.clone.1 | loop fusion | flops 1310720 | bytes 2621574 | tf_op jit(solution)/shard_map/while/body/eval_jaxpr/jit(_where)/select_n | solution.py:43
  100.1 1.3 %fusion.48 = f32[32,64,128]{2,1,0:T(8,128)S(1)} fusion(f32[32,64,128]{2,1,0:T(8,128)S(1)} %get-tuple-element.196, bf16[4,32,64,128]{3,2,1,0:T(8,128)(2,1)} %get-tuple-element.206, s32[]{:T(128)} %get-tuple-element.195, f32[32]{0:T(128)S(1)} %bitcast_convert_fusion.2, pred[]{:T(512)S(6)} %compare.3, pred[]{:T(512)S(6)} %lt.22), kind=kLoop, calls=%fused_computation.1.clone.1 | loop fusion | flops 1310720 | bytes 2621574 | tf_op jit(solution)/shard_map/while/body/eval_jaxpr/jit(_where)/select_n | solution.py:43
  102.1 0.8 copy-done
  103.0 4.2 %multiply_reduce_fusion = (f32[128,32]{0,1:T(8,128)S(1)}, f32[128,32,64]{0,2,1:T(8,128)S(1)}) fusion(f32[128,32,64]{0,2,1:T(8,128)S(1)} %bitcast.104, f32[128,32,64]{0,2,1:T(8,128)S(1)} %bitcast.103, f32[32]{0:T(128)S(1)} %copy-done.16, f32[128,32,64]{0,2,1:T(8,128)S(1)} %bitcast_multiply_fusion.1, f32[32,128,128]{2,1,0:T(8,128)S(1)} %copy-done, ...), kind=kOutput, calls=%fused_computation.28 | convolution fusion | flops 404484096 | bytes 6324352 | tf_op jit(solution)/shard_map/hij,jhp->ihp/dot_general | solution.py:83
  108.4 0.9 multiply_convert_fusion
  (95 shorter events, 8.9 us)
Async XLA Ops:
  7.2 30.1 %copy-start.1 = (bf16[128,2048]{1,0:T(8,128)(2,1)S(1)}, bf16[128,2048]{1,0:T(8,128)(2,1)}, u32[]{:S(2)}) copy-start(bf16[128,2048]{1,0:T(8,128)(2,1)} %param.20) | copy-start | bytes 1572868
  7.2 31.1 %copy-start.8 = (bf16[128,256]{1,0:T(8,128)(2,1)S(1)}, bf16[128,256]{1,0:T(8,128)(2,1)}, u32[]{:S(2)}) copy-start(bf16[128,256]{1,0:T(8,128)(2,1)} %param.31) | copy-start | bytes 196612
  7.2 31.9 %copy-start.3 = (bf16[128,1024]{1,0:T(8,128)(2,1)S(1)}, bf16[128,1024]{1,0:T(8,128)(2,1)}, u32[]{:S(2)}) copy-start(bf16[128,1024]{1,0:T(8,128)(2,1)} %param.30) | copy-start | bytes 786436
  7.2 88.8 %all-gather.3.cloned.1.call-start = ((), (), s32[]{:S(2)}) async-start(), calls=%async_computation | async-start | bytes 2621440 | tf_op jit(solution)/shard_map/all_gather | solution.py:28
  8.8 30.4 %collective-permute-start = (bf16[3,2560]{1,0:T(4,128)(2,1)S(1)}, bf16[3,2560]{1,0:T(4,128)(2,1)S(1)}, u32[]{:S(2)}, u32[]{:S(2)}) collective-permute-start(bf16[3,2560]{1,0:T(4,128)(2,1)S(1)} %pad_maximum_fusion.2), channel_id=1, source_target_pairs={{0,4},{4,8},{8,12},{1,5},{5,9},{9,13},{2,6},{6,10},{10,14},{3,7},{... | collective-permute-start | bytes 46088 | tf_op jit(solution)/shard_map/ppermute | solution.py:22
  13.8 2.0 %copy-start.17 = (s32[128]{0:T(128)}, s32[128]{0:T(128)S(1)}, u32[]{:S(2)}) copy-start(s32[128]{0:T(128)S(1)} %iota_add_fusion.1) | copy-start | bytes 1540
  15.2 7.5 %copy-start.13 = (s32[4]{0:T(128)}, s32[4]{0:T(128)S(1)}, u32[]{:S(2)}) copy-start(s32[4]{0:T(128)S(1)} %bitcast_subtract_fusion) | copy-start | bytes 52
  15.3 8.6 %copy-start.19 = (s32[128]{0:T(128)}, s32[128]{0:T(128)S(1)}, u32[]{:S(2)}) copy-start(s32[128]{0:T(128)S(1)} %convert_reduce_fusion.2) | copy-start | bytes 1540
  16.3 6.5 %copy-start.10 = (s32[128]{0:T(128)}, s32[128]{0:T(128)S(1)}, u32[]{:S(2)}) copy-start(s32[128]{0:T(128)S(1)} %reduce.2) | copy-start | bytes 1540
  23.1 0.8 copy-start.5
  44.5 2.3 %copy-start.7 = (bf16[128,256]{1,0:T(8,128)(2,1)S(1)}, bf16[128,256]{1,0:T(8,128)(2,1)}, u32[]{:S(2)}) copy-start(bf16[128,256]{1,0:T(8,128)(2,1)} %param.32) | copy-start | bytes 196612
  44.5 17.7 %copy-start.2 = (bf16[128,256]{0,1:T(8,128)(2,1)S(1)}, bf16[128,256]{0,1:T(8,128)(2,1)}, u32[]{:S(2)}) copy-start(bf16[128,256]{0,1:T(8,128)(2,1)} %copy.126) | copy-start | bytes 196612
  44.5 34.5 %copy-start.14 = (s32[4]{0:T(128)S(1)}, s32[4]{0:T(128)}, u32[]{:S(2)}) copy-start(s32[4]{0:T(128)} %copy-done.13) | copy-start | bytes 52
  44.5 34.6 %copy-start.20 = (s32[128]{0:T(128)S(1)}, s32[128]{0:T(128)}, u32[]{:S(2)}) copy-start(s32[128]{0:T(128)} %copy-done.19) | copy-start | bytes 1540
  44.5 34.6 %copy-start.18 = (s32[128]{0:T(128)S(1)}, s32[128]{0:T(128)}, u32[]{:S(2)}) copy-start(s32[128]{0:T(128)} %copy-done.17) | copy-start | bytes 1540
  80.1 1.4 %copy-start.11 = (s32[128]{0:T(128)S(1)}, s32[128]{0:T(128)}, u32[]{:S(2)}) copy-start(s32[128]{0:T(128)} %copy-done.10) | copy-start | bytes 1540
  80.1 1.5 %copy-start.6 = (f32[128,32]{0,1:T(8,128)S(1)}, f32[128,32]{0,1:T(8,128)}, u32[]{:S(2)}) copy-start(f32[128,32]{0,1:T(8,128)} %copy-done.5) | copy-start | bytes 49156
  80.1 1.5 %copy-start.12 = (pred[128]{0:T(512)(128)(4,1)S(1)}, pred[128]{0:T(512)(128)(4,1)}, u32[]{:S(2)}) copy-start(pred[128]{0:T(512)(128)(4,1)} %get-tuple-element.151) | copy-start | bytes 388
  80.1 3.1 %copy-start.4 = (f32[32,128]{1,0:T(8,128)S(1)}, f32[32,128]{1,0:T(8,128)}, u32[]{:S(2)}) copy-start(f32[32,128]{1,0:T(8,128)} %copy.114) | copy-start | bytes 49156
  81.5 14.5 %copy-start.15 = (bf16[4,1,32]{2,0,1:T(4,128)(2,1)S(1)}, bf16[4,1,32]{2,0,1:T(4,128)(2,1)}, u32[]{:S(2)}) copy-start(bf16[4,1,32]{2,0,1:T(4,128)(2,1)} %copy.148) | copy-start | bytes 772
  101.4 1.6 %copy-start = (f32[32,128,128]{2,1,0:T(8,128)S(1)}, f32[32,128,128]{2,1,0:T(8,128)}, u32[]{:S(2)}) copy-start(f32[32,128,128]{2,1,0:T(8,128)} %bitcast_multiply_fusion) | copy-start | bytes 6291460
  101.4 1.6 %copy-start.16 = (f32[32]{0:T(128)S(1)}, f32[32]{0:T(128)}, u32[]{:S(2)}) copy-start(f32[32]{0:T(128)} %param.28) | copy-start | bytes 388
  107.7 0.7 copy-start.9
Sparse Core Ops, SparseCore 0:
  46.9 49.1 all-gather.2
where the time goes:
time: 117 us; the launch traced here: 116 us
  blocking collectives  41.2 us (35%)
  other arithmetic  20.3 us (17%)
  between operations  15.2 us (13%)
  local copies, waits for them, and re-layouts  15 us (13%)
  waiting for transfers between devices  11.2 us (10%)
  matrix products  8.25 us (7%)
  starting transfers between devices  4.97 us (4%)
    all_gather x1, blocking collectives, shards(): key_piece = lax.all_gather(keys, 'seq', axis=0, tiled=True)  16.8 us
    all_gather x1, blocking collectives, shards(): value_piece = lax.all_gather(values, 'seq', axis=0, tiled=True)  15.3 us
    all_gather x1, waiting for transfers between devices, carried_in(): lax.all_gather(part.astype(kind), axis)  11.1 us
    all_gather x1, blocking collectives, carried_in(): lax.all_gather(part.astype(kind), axis)  9.08 us
    unnamed x49, local copies, waits for them, and re-layouts  6.75 us
    select_n x4, other arithmetic, hop(): return jax.tree.map(lambda a, b: jnp.where(reached, a, b), new, before)  5.19 us
    ppermute x1, starting transfers between devices, shifted(): lax.ppermute(value, axis, [(source, source + steps) for source in range(f...  4.93 us
    dot_general x1, matrix products, ssd_terms(): jnp.einsum('hij,jhp->ihp', multiplier * intersection, scaled, precision=H...  4.22 us
  transfers between devices with their start and end apart: 2, of which 1 were waited for; matrix products, arithmetic and copies ran while one was open for 18% of the time, Pallas kernels for 0%

commit v1 on v0

v1 whole, which is shorter than its diff:
```python
import functools
import math

import jax
import jax.numpy as jnp
from jax import lax
from jax.experimental import pallas as pl
from jax.experimental.pallas import tpu as pltpu
from jax.sharding import PartitionSpec as P

HDIM = 64
STATE = 128
QHEADS = 32
KVHEADS = 8
ADIM = 128
EPSILON = 1e-05
BARRED = -2e30
HIGHEST = lax.Precision.HIGHEST
F32 = jnp.float32
BF16 = jnp.bfloat16
CHUNK = 256
VMEM_LIMIT = 48 * 1024 * 1024


def silu(value):
    return value * (0.5 * jnp.tanh(0.5 * value) + 0.5)


def softplus(value):
    return jnp.maximum(value, 0.0) + jnp.log(1.0 + jnp.exp(-jnp.abs(value)))


def doc_start(positions, lens_ref):
    begin = jnp.int32(0)
    found = jnp.zeros_like(positions)
    for doc in range(lens_ref.shape[0]):
        found = jnp.where(positions >= begin, begin, found)
        begin = begin + lens_ref[doc]
    return found


def doc_start_of(position, lens_ref):
    begin = jnp.int32(0)
    found = jnp.int32(0)
    for doc in range(lens_ref.shape[0]):
        found = jnp.where(position >= begin, begin, found)
        begin = begin + lens_ref[doc]
    return found


def widen(per_head, first, width):
    heads = per_head.shape[1]
    high = per_head.astype(BF16)
    low = (per_head - high.astype(F32)).astype(BF16)
    both = jnp.concatenate([high, low], axis=1)
    head = lax.broadcasted_iota(jnp.int32, (2 * heads, width), 0)
    head = jnp.where(head >= heads, head - heads, head)
    channel = lax.broadcasted_iota(jnp.int32, (2 * heads, width), 1) + first
    spread = (channel // HDIM == head).astype(F32).astype(BF16)
    return jnp.dot(both, spread, preferred_element_type=F32)


def steps_of(dt_ref, dt_bias_ref, a_log_ref):
    step = softplus(dt_ref[...] + dt_bias_ref[...].reshape(1, -1))
    return step, -step * jnp.exp(a_log_ref[...].reshape(1, -1))


def tails_kernel(x_ref, bc_ref, dt_ref, dt_bias_ref, a_log_ref, out_ref):
    width = x_ref.shape[1]
    rows = x_ref.shape[0]
    _, rate = steps_of(dt_ref, dt_bias_ref, a_log_ref)
    total = jnp.sum(rate, axis=0, keepdims=True)
    out_ref[:, :width] = x_ref[...].astype(F32)[rows - 4 :]
    out_ref[:, width:] = bc_ref[...].astype(F32)[rows - 4 :]
    out_ref[0:1, : total.shape[1]] = total


def conv_kernel(
    x_ref, bc_ref, tail_ref, dt_ref, wx_ref, bx_ref, wbc_ref, bbc_ref, dt_bias_ref, a_log_ref, lens_ref,
    xc_ref, bcc_ref, state_ref, step_ref, running_ref, pad_ref,
):
    rows, width = x_ref.shape
    bc_width = bc_ref.shape[1]
    taps = wx_ref.shape[0]
    first = lax.axis_index("seq") * rows
    positions = first + lax.broadcasted_iota(jnp.int32, (rows, CHUNK), 0)
    depth = positions - doc_start(positions, lens_ref)
    inside = [depth >= lag for lag in range(taps)]
    step, rate = steps_of(dt_ref, dt_bias_ref, a_log_ref)
    row = lax.broadcasted_iota(jnp.int32, (rows, rows), 0)
    column = lax.broadcasted_iota(jnp.int32, (rows, rows), 1)
    lower = (row >= column).astype(F32)
    running = jnp.dot(lower, rate, precision=HIGHEST, preferred_element_type=F32)
    step_ref[...] = step
    running_ref[...] = running
    last_begin = doc_start_of(first + rows - 1, lens_ref)
    position = first + lax.broadcasted_iota(jnp.int32, step.shape, 0)
    weight = jnp.where(
        position >= last_begin, step * jnp.exp(running[rows - 1 : rows] - running), 0.0
    )

    def conv(raw_ref, offset, start, weight_ref, bias_ref, slot):
        columns = slice(start, start + CHUNK)
        pad = pad_ref.at[slot]
        pad[4:8] = tail_ref[:, offset + start : offset + start + CHUNK]
        raw = raw_ref[:, columns].astype(F32)
        pad[8:] = raw
        total = raw * weight_ref[taps - 1 : taps, columns] + bias_ref[columns].reshape(1, -1)
        for lag in range(1, taps):
            term = pad[8 - lag : 8 - lag + rows] * weight_ref[taps - 1 - lag : taps - lag, columns]
            total = total + jnp.where(inside[lag], term, 0.0)
        return silu(total).astype(BF16)

    slots = pad_ref.shape[0]
    groups = bc_width // (2 * STATE)
    turned = []
    for group in range(groups):
        pair = conv(bc_ref, width, group * 2 * STATE, wbc_ref, bbc_ref, group % slots)
        bcc_ref[:, group * 2 * STATE : (group + 1) * 2 * STATE] = pair
        turned.append(pair[:, :STATE].astype(F32).T.astype(BF16))
    per_group = width // groups
    for start in range(0, width, CHUNK):
        xc = conv(x_ref, 0, start, wx_ref, bx_ref, (start // CHUNK) % slots)
        xc_ref[:, start : start + CHUNK] = xc
        weighted = (xc.astype(F32) * widen(weight, start, CHUNK)).astype(BF16)
        state_ref[:, start : start + CHUNK] = jnp.dot(
            turned[start // per_group], weighted, preferred_element_type=F32
        ).astype(BF16)


def local_kernel(xc_ref, bcc_ref, step_ref, running_ref, skip_ref, lens_ref, out_ref):
    rows, width = xc_ref.shape
    groups = bcc_ref.shape[1] // (2 * STATE)
    per_group = width // groups
    first = lax.axis_index("seq") * rows
    row = lax.broadcasted_iota(jnp.int32, (rows, rows), 0)
    column = lax.broadcasted_iota(jnp.int32, (rows, rows), 1)
    begin = doc_start(first + row, lens_ref)
    linked = (row >= column) & (first + column >= begin)
    running = running_ref[...]
    turned_running = running.T
    turned_step = step_ref[...].T
    skip = skip_ref[...].reshape(1, -1)
    skip = jnp.broadcast_to(skip, (8, skip.shape[1]))
    pair_width = 2 * HDIM
    lane = lax.broadcasted_iota(jnp.int32, (rows, pair_width), 1)
    for group in range(groups):
        base = group * 2 * STATE
        inputs = bcc_ref[:, base : base + STATE]
        outputs = bcc_ref[:, base + STATE : base + 2 * STATE]
        meet = lax.dot_general(
            outputs, inputs, (((1,), (1,)), ((), ())), preferred_element_type=F32
        )
        meet = jnp.where(linked, meet, 0.0)
        for start in range(group * per_group, (group + 1) * per_group, pair_width):
            parts = []
            for head in (start // HDIM, start // HDIM + 1):
                spread = running[:, head : head + 1] - turned_running[head : head + 1]
                decay = jnp.exp(jnp.minimum(spread, 0.0))
                parts.append((decay * (meet * turned_step[head : head + 1])).astype(BF16))
            mix = jnp.concatenate(parts, axis=1)
            xc = xc_ref[:, start : start + pair_width]
            zero = jnp.zeros_like(xc)
            stacked = jnp.concatenate(
                [jnp.where(lane < HDIM, xc, zero), jnp.where(lane < HDIM, zero, xc)], axis=0
            )
            value = jnp.dot(mix, stacked, preferred_element_type=F32)
            wide_skip = widen(skip, start, pair_width)[0:1]
            out_ref[:, start : start + pair_width] = value + xc.astype(F32) * wide_skip


def attend_kernel(hops, *refs):
    q_ref = refs[0]
    kv_refs = refs[1 : 2 + hops]
    lens_ref, out_ref = refs[2 + hops :]
    rows = q_ref.shape[0]
    kv_heads = kv_refs[0].shape[1] // (2 * ADIM)
    share = QHEADS // KVHEADS
    count = rows * (hops + 1)
    here = lax.axis_index("seq")
    row = here * rows + lax.broadcasted_iota(jnp.int32, (rows, count), 0)
    column = (here - hops) * rows + lax.broadcasted_iota(jnp.int32, (rows, count), 1)
    allowed = (column <= row) & (column >= doc_start(row, lens_ref))
    scale = ADIM ** (-0.5)
    for head in range(kv_heads):
        low = head * ADIM
        keys = jnp.concatenate([ref[:, low : low + ADIM] for ref in kv_refs], axis=0)
        low = (kv_heads + head) * ADIM
        values = jnp.concatenate([ref[:, low : low + ADIM] for ref in kv_refs], axis=0)
        for part in range(share):
            low = (head * share + part) * ADIM
            scores = lax.dot_general(
                q_ref[:, low : low + ADIM], keys, (((1,), (1,)), ((), ())), preferred_element_type=F32
            )
            scores = jnp.where(allowed, scores * scale, BARRED)
            expo = jnp.exp(scores - jnp.max(scores, axis=1, keepdims=True))
            total = jnp.sum(expo, axis=1, keepdims=True)
            summed = jnp.dot(expo.astype(BF16), values, preferred_element_type=F32)
            out_ref[:, low : low + ADIM] = (summed / total).astype(BF16)


def final_kernel(hops, *refs):
    mixed_ref, bcc_ref, running_ref, z_ref, gain_ref, lens_ref = refs[:6]
    state_refs = refs[6 : 6 + hops]
    total_refs = refs[6 + hops : 6 + hops + hops - 1]
    out_ref, gated_ref = refs[-2:]
    rows, width = mixed_ref.shape
    heads = running_ref.shape[1]
    groups = bcc_ref.shape[1] // (2 * STATE)
    per_group = width // groups
    here = lax.axis_index("seq")
    first = here * rows
    first_begin = doc_start_of(first, lens_ref)
    positions = first + lax.broadcasted_iota(jnp.int32, (rows, heads), 0)
    begin = doc_start(positions, lens_ref)
    entry = jnp.where(begin < first, jnp.exp(running_ref[...]), 0.0)
    decays = []
    total = jnp.zeros((1, heads), F32)
    for hop in range(2, hops + 1):
        total = total + total_refs[hop - 2][0:1, :heads]
        factor = jnp.where(first_begin < (here - hop + 1) * rows, jnp.exp(total), 0.0)
        decays.append(jnp.broadcast_to(factor, (8, heads)))
    for group in range(groups):
        base = group * 2 * STATE
        outputs = bcc_ref[:, base + STATE : base + 2 * STATE]
        squares = jnp.zeros((rows, 1), F32)
        for start in range(group * per_group, (group + 1) * per_group, CHUNK):
            columns = slice(start, start + CHUNK)
            state = state_refs[0][:, columns].astype(F32)
            for factor, ref in zip(decays, state_refs[1:]):
                state = state + widen(factor, start, CHUNK)[0:1] * ref[:, columns].astype(F32)
            carried = jnp.dot(outputs, state.astype(BF16), preferred_element_type=F32)
            mixed = mixed_ref[:, columns] + carried * widen(entry, start, CHUNK)
            gated = mixed * silu(z_ref[:, columns].astype(F32))
            gated_ref[:, columns] = gated
            squares = squares + jnp.sum(gated * gated, axis=1, keepdims=True)
        multiplier = lax.rsqrt(squares * (1.0 / per_group) + EPSILON)
        for start in range(group * per_group, (group + 1) * per_group, CHUNK):
            columns = slice(start, start + CHUNK)
            out_ref[:, columns] = (
                gated_ref[:, columns] * multiplier * gain_ref[columns].reshape(1, -1)
            ).astype(BF16)


def call(kernel, name, outs, operands, scalars=(), specs=None, scratch=(), flops=0):
    vmem = pl.BlockSpec(memory_space=pltpu.VMEM)
    smem = pl.BlockSpec(memory_space=pltpu.SMEM)
    in_specs = [vmem] * len(operands) if specs is None else list(specs)
    for at in scalars:
        in_specs[at] = smem
    moved = sum(math.prod(a.shape) * a.dtype.itemsize for a in (*operands, *outs))
    return pl.pallas_call(
        kernel,
        name=name,
        out_shape=outs,
        in_specs=in_specs,
        out_specs=[vmem] * len(outs),
        scratch_shapes=list(scratch),
        compiler_params=pltpu.CompilerParams(vmem_limit_bytes=VMEM_LIMIT),
        cost_estimate=pl.CostEstimate(flops=flops, bytes_accessed=moved, transcendentals=0),
    )(*operands)


def shifted(value, steps):
    count = lax.axis_size("seq")
    return lax.ppermute(value, "seq", [(source, source + steps) for source in range(count - steps)])


def shards(
    x_raw,
    bc_raw,
    z_gate,
    dt_raw,
    conv_x_weight,
    conv_x_bias,
    conv_bc_weight,
    conv_bc_bias,
    dt_bias,
    a_log,
    skip_d,
    norm_gain,
    queries,
    keys,
    values,
    doc_lens,
):
    rows, width = x_raw.shape
    bc_width = bc_raw.shape[1]
    heads = dt_raw.shape[1]
    count = lax.axis_size("seq")
    longest = rows * count // 2
    hops = min(count - 1, -(-(longest - 1) // rows))
    shape = jax.ShapeDtypeStruct
    whole = pl.BlockSpec(memory_space=pltpu.VMEM)
    edge = 16

    (tails,) = pl.pallas_call(
        tails_kernel,
        name="tails",
        grid=(1,),
        out_shape=[shape((4, width + bc_width), F32)],
        in_specs=[
            pl.BlockSpec((edge, width), lambda i: (rows // edge - 1, 0)),
            pl.BlockSpec((edge, bc_width), lambda i: (rows // edge - 1, 0)),
            whole,
            whole,
            whole,
        ],
        out_specs=[whole],
    )(x_raw, bc_raw, dt_raw, dt_bias, a_log)
    tail = shifted(tails, 1)
    kv = jnp.concatenate([keys, values], axis=1)
    kv_before = [shifted(kv, hop) for hop in range(1, hops + 1)]

    xc, bcc, state, step, running = call(
        conv_kernel,
        "conv_state",
        [
            shape((rows, width), BF16),
            shape((rows, bc_width), BF16),
            shape((STATE, width), BF16),
            shape((rows, heads), F32),
            shape((rows, heads), F32),
        ],
        [
            x_raw, bc_raw, tail, dt_raw, conv_x_weight, conv_x_bias, conv_bc_weight, conv_bc_bias,
            dt_bias, a_log, doc_lens,
        ],
        scalars=(10,),
        scratch=[pltpu.VMEM((4, rows + 8, CHUNK), F32)],
        flops=2 * rows * width * STATE,
    )
    states = []
    for _ in range(hops):
        states.append(shifted(states[-1] if states else state, 1))
    totals = []
    for hop in range(2, hops + 1):
        totals.append(tail[:, :STATE] if hop == 2 else shifted(totals[-1], 1))

    (mixed,) = call(
        local_kernel,
        "local_mix",
        [shape((rows, width), F32)],
        [xc, bcc, step, running, skip_d, doc_lens],
        scalars=(5,),
        flops=4 * rows * rows * width,
    )
    (attn_out,) = call(
        functools.partial(attend_kernel, hops),
        "attend",
        [shape(queries.shape, BF16)],
        [queries, *reversed(kv_before), kv, doc_lens],
        scalars=(hops + 2,),
        flops=4 * rows * rows * (hops + 1) * queries.shape[1],
    )
    (mamba_out,) = call(
        functools.partial(final_kernel, hops),
        "carry_norm",
        [shape((rows, width), BF16)],
        [mixed, bcc, running, z_gate, norm_gain, doc_lens, *states, *totals],
        scalars=(5,),
        scratch=[pltpu.VMEM((rows, width), F32)],
        flops=2 * rows * width * STATE,
    )
    return (mamba_out, attn_out)


def solution(mesh):
    split = P(("groups", "seq"), "dp")
    placed = (
        split,
        split,
        split,
        split,
        P(None, "dp"),
        P("dp"),
        P(None, "dp"),
        P("dp"),
        P("dp"),
        P("dp"),
        P("dp"),
        P("dp"),
        split,
        split,
        split,
        P("groups"),
    )
    return jax.shard_map(
        shards,
        mesh=mesh,
        in_specs=placed,
        out_specs=(split, split),
        check_vma=False,
    )
```

time: 117 us -> 55.9 us (0.48)
  the two profiles are of different devices: /device:TPU:0 before, /device:TPU:22 now
where the time goes in v1:
time: 55.9 us; the launch traced here: 55.6 us
  waiting for transfers between devices  26.4 us (47%)
  starting transfers between devices  13.9 us (25%)
  Pallas kernels  12.1 us (22%)
  local copies, waits for them, and re-layouts  2.25 us (4%)
  between operations  0.88 us (2%)
    ppermute x5, waiting for transfers between devices, shifted(): lax.ppermute(value, 'seq', [(source, source + steps) for source in range(...  26.4 us
    ppermute x5, starting transfers between devices, shifted(): lax.ppermute(value, 'seq', [(source, source + steps) for source in range(...  13.9 us
    pallas_call x4, Pallas kernels, call(): pl.pallas_call(kernel, name=name, out_shape=outs, in_specs=in_specs, out_...  10.4 us
    unnamed x34, local copies, waits for them, and re-layouts  2.24 us
    pallas_call x1, Pallas kernels, shards(): pl.pallas_call(tails_kernel, name='tails', grid=(1,), out_shape=[shape((4...  1.68 us
  transfers between devices with their start and end apart: 5, of which 4 were waited for; matrix products, arithmetic and copies ran while one was open for 0% of the time, Pallas kernels for 9%

profile of v1, /device:TPU:22, one launch (start us, length us, event | category | flops | bytes accessed | tf_op | source)
XLA Modules:
  0.0 55.6 jit_solution(15678706477892429648)
XLA Ops:
  0.6 0.0 copy-start
  0.6 1.5 %copy.18.dt_ref = f32[128,32]{1,0:T(8,128)} copy(f32[128,32]{0,1:T(8,128)} %param.19) | data formatting | bytes 32768 | tf_op args[3]
  2.2 0.0 copy-start.7
  2.2 0.0 copy-start.9
  2.2 0.0 copy-start.10
  2.2 0.0 copy-start.11
  2.2 0.0 copy-start.12
  2.2 1.7 %tails.1 = f32[4,2560]{1,0:T(4,128)} custom-call(bf16[128,2048]{1,0:T(8,128)(2,1)} %x_ref.3, bf16[128,512]{1,0:T(8,128)(2,1)} %bc_ref.3, f32[128,32]{1,0:T(8,128)} %copy.18.dt_ref, f32[32]{0:T(128)} %dt_bias_ref.3, f32[32]{0:T(128)} %a_log_ref.3), custom_call_target="tpu_custom_call" | custom-call | tf_op jit(solution)/shard_map/tails/pallas_call | solution.py:297
  3.9 3.6 %collective-permute-start = (f32[4,2560]{1,0:T(4,128)}, f32[4,2560]{1,0:T(4,128)S(1)}, u32[]{:S(2)}, u32[]{:S(2)}) collective-permute-start(f32[4,2560]{1,0:T(4,128)} %tails.1), channel_id=1, source_target_pairs={{0,4},{4,8},{8,12},{1,5},{5,9},{9,13},{2,6},{6,10},{10,14},{3,7},{... | collective-permute-start | bytes 122888 | tf_op jit(solution)/shard_map/ppermute | solution.py:266
  7.5 2.6 %collective-permute-done.tail_ref = f32[4,2560]{1,0:T(4,128)S(1)} collective-permute-done((f32[4,2560]{1,0:T(4,128)}, f32[4,2560]{1,0:T(4,128)S(1)}, u32[]{:S(2)}, u32[]{:S(2)}) %collective-permute-start) | collective-permute-done | bytes 40992 | tf_op jit(solution)/shard_map/ppermute | solution.py:266
  10.1 0.0 copy-done
  10.1 0.0 copy-done.1
  10.1 0.0 copy-done.3
  10.1 0.0 copy-done.5
  10.2 2.5 %conv_state.1 = (bf16[128,2048]{1,0:T(8,128)(2,1)S(1)}, bf16[128,512]{1,0:T(8,128)(2,1)S(1)}, bf16[128,2048]{1,0:T(8,128)(2,1)S(1)}, f32[128,32]{1,0:T(8,128)S(1)}, f32[128,32]{1,0:T(8,128)S(1)}) custom-call(bf16[128,2048]{1,0:T(8,128)(2,1)S(1)} %copy-done, bf16[128,512]{1,0:T(8,128)(2,1)S(1)} %copy-done.3, f32[4,2560]{1,0:T(4,128)S(1)} %collective-permute-done.tail_ref, ...), custom_call_target="tpu_custom_call" | custom-call | flops 67108864 | bytes 1976592 | tf_op jit(solution)/shard_map/conv_state/pallas_call | solution.py:252
  12.7 0.0 copy-start.15
  12.7 3.6 %collective-permute-start.1 = (bf16[128,2048]{1,0:T(8,128)(2,1)S(1)}, bf16[128,2048]{1,0:T(8,128)(2,1)S(1)}, u32[]{:S(2)}, u32[]{:S(2)}) collective-permute-start(bf16[128,2048]{1,0:T(8,128)(2,1)S(1)} %get-tuple-element.11), channel_id=1, source_target_pairs={{0,4},{4,8},{8,12},{1,5},{5,9},{9,13},{2,6},{6,10},{10,14},{3,7},{... | collective-permute-start | bytes 1572872 | tf_op jit(solution)/shard_map/ppermute | solution.py:266
  16.3 10.9 %collective-permute-done.1.refs_6_ = bf16[128,2048]{1,0:T(8,128)(2,1)S(1)} collective-permute-done((bf16[128,2048]{1,0:T(8,128)(2,1)S(1)}, bf16[128,2048]{1,0:T(8,128)(2,1)S(1)}, u32[]{:S(2)}, u32[]{:S(2)}) %collective-permute-start.1) | collective-permute-done | bytes 524320 | tf_op jit(solution)/shard_map/ppermute | solution.py:266
  27.2 3.5 %collective-permute-start.2 = (bf16[128,2048]{1,0:T(8,128)(2,1)S(1)}, bf16[128,2048]{1,0:T(8,128)(2,1)S(1)}, u32[]{:S(2)}, u32[]{:S(2)}) collective-permute-start(bf16[128,2048]{1,0:T(8,128)(2,1)S(1)} %collective-permute-done.1.refs_6_), channel_id=1, source_target_pairs={{0,4},{4,8},{8,12},{1,5},{5,9},{9,13},{2,6},{6,10},{10,14},{3,7},{... | collective-permute-start | bytes 1572872 | tf_op jit(solution)/shard_map/ppermute | solution.py:266
  30.8 0.0 copy-done.15
  30.8 1.3 %collective-permute-start.3 = (bf16[128,512]{1,0:T(8,128)(2,1)S(1)}, bf16[128,512]{1,0:T(8,128)(2,1)S(1)}, u32[]{:S(2)}, u32[]{:S(2)}) collective-permute-start(bf16[128,512]{1,0:T(8,128)(2,1)S(1)} %constant_dynamic-update-slice_fusion.refs_3_), channel_id=1, source_target_pairs={{0,8},{4,12},{1,9},{5,13},{2,10},{6,14},{3,11},{7,15},{16,24},{20,... | collective-permute-start | bytes 393224 | tf_op jit(solution)/shard_map/ppermute | solution.py:266
  32.1 1.9 %collective-permute-start.4 = (bf16[128,512]{1,0:T(8,128)(2,1)S(1)}, bf16[128,512]{1,0:T(8,128)(2,1)S(1)}, u32[]{:S(2)}, u32[]{:S(2)}) collective-permute-start(bf16[128,512]{1,0:T(8,128)(2,1)S(1)} %constant_dynamic-update-slice_fusion.refs_3_), channel_id=1, source_target_pairs={{0,4},{4,8},{8,12},{1,5},{5,9},{9,13},{2,6},{6,10},{10,14},{3,7},{... | collective-permute-start | bytes 393224 | tf_op jit(solution)/shard_map/ppermute | solution.py:266
  34.0 0.0 copy-start.13
  34.0 0.6 %copy-done.13 = f32[32]{0:T(128)S(1)} copy-done((f32[32]{0:T(128)S(1)}, f32[32]{0:T(128)}, u32[]{:S(2)}) %copy-start.13) | copy-done | bytes 152
  34.7 1.5 %local_mix.1.refs_0_ = f32[128,2048]{1,0:T(8,128)S(1)} custom-call(bf16[128,2048]{1,0:T(8,128)(2,1)S(1)} %get-tuple-element.7.xc_ref, bf16[128,512]{1,0:T(8,128)(2,1)S(1)} %get-tuple-element.8.bcc_ref.refs_1_, f32[128,32]{1,0:T(8,128)S(1)} %get-tuple-element.9.step_ref, f32[128,32]{1,0:T(8,128)S(1)} %get-tuple-element.10.running_ref.refs_2_, ...), custom_call_target="tpu_custom_call" | custom-call | flops 134217728 | bytes 1736848 | tf_op jit(solution)/shard_map/local_mix/pallas_call | solution.py:252
  36.2 0.0 copy-start.2
  36.2 0.0 copy-start.8
  36.2 8.7 %collective-permute-done.3.refs_1_ = bf16[128,512]{1,0:T(8,128)(2,1)S(1)} collective-permute-done((bf16[128,512]{1,0:T(8,128)(2,1)S(1)}, bf16[128,512]{1,0:T(8,128)(2,1)S(1)}, u32[]{:S(2)}, u32[]{:S(2)}) %collective-permute-start.3) | collective-permute-done | bytes 131104 | tf_op jit(solution)/shard_map/ppermute | solution.py:266
  44.9 4.2 %collective-permute-done.4.refs_2_ = bf16[128,512]{1,0:T(8,128)(2,1)S(1)} collective-permute-done((bf16[128,512]{1,0:T(8,128)(2,1)S(1)}, bf16[128,512]{1,0:T(8,128)(2,1)S(1)}, u32[]{:S(2)}, u32[]{:S(2)}) %collective-permute-start.4) | collective-permute-done | bytes 131104 | tf_op jit(solution)/shard_map/ppermute | solution.py:266
  49.2 3.5 %attend.1 = bf16[128,1024]{1,0:T(8,128)(2,1)} custom-call(bf16[128,1024]{1,0:T(8,128)(2,1)S(1)} %copy-done.4, bf16[128,512]{1,0:T(8,128)(2,1)S(1)} %collective-permute-done.3.refs_1_, bf16[128,512]{1,0:T(8,128)(2,1)S(1)} %collective-permute-done.4.refs_2_, bf16[128,512]{1,0:T(8,128)(2,1)S(1)} %constant_dynamic-update-slice_fusion.refs_3_, s32[4]{0:T(128)S(1)} %copy-done.9), custom_call_target="tpu_custom_call" | custom-call | flops 201326592 | bytes 917520 | tf_op jit(solution)/shard_map/attend/pallas_call | solution.py:252
  52.6 0.0 collective-permute-done.2.refs_7_
  52.6 2.9 %carry_norm.1 = bf16[128,2048]{1,0:T(8,128)(2,1)} custom-call(f32[128,2048]{1,0:T(8,128)S(1)} %local_mix.1.refs_0_, bf16[128,512]{1,0:T(8,128)(2,1)S(1)} %get-tuple-element.8.bcc_ref.refs_1_, f32[128,32]{1,0:T(8,128)S(1)} %get-tuple-element.10.running_ref.refs_2_, bf16[128,2048]{1,0:T(8,128)(2,1)S(1)} %copy-done.2, f32[2048]{0:T(1024)S(1)} %copy-done.8, ...), custom_call_target="tpu_custom_call" | custom-call | flops 67108864 | bytes 3303440 | tf_op jit(solution)/shard_map/carry_norm/pallas_call | solution.py:252
  (19 shorter events, 0.0 us)
Async XLA Ops:
  0.6 9.5 %copy-start = (bf16[128,2048]{1,0:T(8,128)(2,1)S(1)}, bf16[128,2048]{1,0:T(8,128)(2,1)}, u32[]{:S(2)}) copy-start(bf16[128,2048]{1,0:T(8,128)(2,1)} %x_ref.3) | copy-start | bytes 1572868
  2.1 8.0 %copy-start.1 = (f32[128,32]{1,0:T(8,128)S(1)}, f32[128,32]{1,0:T(8,128)}, u32[]{:S(2)}) copy-start(f32[128,32]{1,0:T(8,128)} %copy.18.dt_ref) | copy-start | bytes 49156
  2.1 8.0 %copy-start.3 = (bf16[128,512]{1,0:T(8,128)(2,1)S(1)}, bf16[128,512]{1,0:T(8,128)(2,1)}, u32[]{:S(2)}) copy-start(bf16[128,512]{1,0:T(8,128)(2,1)} %bc_ref.3) | copy-start | bytes 393220
  2.1 8.0 %copy-start.5 = (f32[4,2048]{1,0:T(4,128)S(1)}, f32[4,2048]{1,0:T(4,128)}, u32[]{:S(2)}) copy-start(f32[4,2048]{1,0:T(4,128)} %wx_ref.1) | copy-start | bytes 98308
  2.2 8.0 %copy-start.6 = (f32[2048]{0:T(1024)S(1)}, f32[2048]{0:T(1024)}, u32[]{:S(2)}) copy-start(f32[2048]{0:T(1024)} %bx_ref.1) | copy-start | bytes 24580
  2.2 8.0 %copy-start.7 = (f32[4,512]{1,0:T(4,128)S(1)}, f32[4,512]{1,0:T(4,128)}, u32[]{:S(2)}) copy-start(f32[4,512]{1,0:T(4,128)} %wbc_ref.1) | copy-start | bytes 24580
  2.2 8.0 %copy-start.9 = (s32[4]{0:T(128)S(1)}, s32[4]{0:T(128)}, u32[]{:S(2)}) copy-start(s32[4]{0:T(128)} %refs_4_.3) | copy-start | bytes 52
  2.2 8.0 %copy-start.10 = (f32[512]{0:T(512)S(1)}, f32[512]{0:T(512)}, u32[]{:S(2)}) copy-start(f32[512]{0:T(512)} %bbc_ref.1) | copy-start | bytes 6148
  2.2 8.0 %copy-start.11 = (f32[32]{0:T(128)S(1)}, f32[32]{0:T(128)}, u32[]{:S(2)}) copy-start(f32[32]{0:T(128)} %dt_bias_ref.3) | copy-start | bytes 388
  2.2 8.0 %copy-start.12 = (f32[32]{0:T(128)S(1)}, f32[32]{0:T(128)}, u32[]{:S(2)}) copy-start(f32[32]{0:T(128)} %a_log_ref.3) | copy-start | bytes 388
  3.9 26.8 %copy-start.14 = (bf16[128,256]{1,0:T(8,128)(2,1)S(1)}, bf16[128,256]{1,0:T(8,128)(2,1)}, u32[]{:S(2)}) copy-start(bf16[128,256]{1,0:T(8,128)(2,1)} %param.29) | copy-start | bytes 196612
  3.9 6.2 %collective-permute-start = (f32[4,2560]{1,0:T(4,128)}, f32[4,2560]{1,0:T(4,128)S(1)}, u32[]{:S(2)}, u32[]{:S(2)}) collective-permute-start(f32[4,2560]{1,0:T(4,128)} %tails.1), channel_id=1, source_target_pairs={{0,4},{4,8},{8,12},{1,5},{5,9},{9,13},{2,6},{6,10},{10,14},{3,7},{... | collective-permute-start | bytes 122888 | tf_op jit(solution)/shard_map/ppermute | solution.py:266
  12.7 18.1 %copy-start.15 = (bf16[128,256]{1,0:T(8,128)(2,1)S(1)}, bf16[128,256]{1,0:T(8,128)(2,1)}, u32[]{:S(2)}) copy-start(bf16[128,256]{1,0:T(8,128)(2,1)} %param.30) | copy-start | bytes 196612
  12.7 14.5 %collective-permute-start.1 = (bf16[128,2048]{1,0:T(8,128)(2,1)S(1)}, bf16[128,2048]{1,0:T(8,128)(2,1)S(1)}, u32[]{:S(2)}, u32[]{:S(2)}) collective-permute-start(bf16[128,2048]{1,0:T(8,128)(2,1)S(1)} %get-tuple-element.11), channel_id=1, source_target_pairs={{0,4},{4,8},{8,12},{1,5},{5,9},{9,13},{2,6},{6,10},{10,14},{3,7},{... | collective-permute-start | bytes 1572872 | tf_op jit(solution)/shard_map/ppermute | solution.py:266
  27.2 25.4 %collective-permute-start.2 = (bf16[128,2048]{1,0:T(8,128)(2,1)S(1)}, bf16[128,2048]{1,0:T(8,128)(2,1)S(1)}, u32[]{:S(2)}, u32[]{:S(2)}) collective-permute-start(bf16[128,2048]{1,0:T(8,128)(2,1)S(1)} %collective-permute-done.1.refs_6_), channel_id=1, source_target_pairs={{0,4},{4,8},{8,12},{1,5},{5,9},{9,13},{2,6},{6,10},{10,14},{3,7},{... | collective-permute-start | bytes 1572872 | tf_op jit(solution)/shard_map/ppermute | solution.py:266
  30.8 14.2 %collective-permute-start.3 = (bf16[128,512]{1,0:T(8,128)(2,1)S(1)}, bf16[128,512]{1,0:T(8,128)(2,1)S(1)}, u32[]{:S(2)}, u32[]{:S(2)}) collective-permute-start(bf16[128,512]{1,0:T(8,128)(2,1)S(1)} %constant_dynamic-update-slice_fusion.refs_3_), channel_id=1, source_target_pairs={{0,8},{4,12},{1,9},{5,13},{2,10},{6,14},{3,11},{7,15},{16,24},{20,... | collective-permute-start | bytes 393224 | tf_op jit(solution)/shard_map/ppermute | solution.py:266
  32.1 17.1 %collective-permute-start.4 = (bf16[128,512]{1,0:T(8,128)(2,1)S(1)}, bf16[128,512]{1,0:T(8,128)(2,1)S(1)}, u32[]{:S(2)}, u32[]{:S(2)}) collective-permute-start(bf16[128,512]{1,0:T(8,128)(2,1)S(1)} %constant_dynamic-update-slice_fusion.refs_3_), channel_id=1, source_target_pairs={{0,4},{4,8},{8,12},{1,5},{5,9},{9,13},{2,6},{6,10},{10,14},{3,7},{... | collective-permute-start | bytes 393224 | tf_op jit(solution)/shard_map/ppermute | solution.py:266
  34.0 0.7 %copy-start.13 = (f32[32]{0:T(128)S(1)}, f32[32]{0:T(128)}, u32[]{:S(2)}) copy-start(f32[32]{0:T(128)} %skip_ref.1) | copy-start | bytes 388
  34.7 14.5 %copy-start.4 = (bf16[128,1024]{1,0:T(8,128)(2,1)S(1)}, bf16[128,1024]{1,0:T(8,128)(2,1)}, u32[]{:S(2)}) copy-start(bf16[128,1024]{1,0:T(8,128)(2,1)} %refs_0_.1) | copy-start | bytes 786436
  36.2 16.4 %copy-start.2 = (bf16[128,2048]{1,0:T(8,128)(2,1)S(1)}, bf16[128,2048]{1,0:T(8,128)(2,1)}, u32[]{:S(2)}) copy-start(bf16[128,2048]{1,0:T(8,128)(2,1)} %refs_3_.1) | copy-start | bytes 1572868
  36.2 16.4 %copy-start.8 = (f32[2048]{0:T(1024)S(1)}, f32[2048]{0:T(1024)}, u32[]{:S(2)}) copy-start(f32[2048]{0:T(1024)} %refs_4_.2) | copy-start | bytes 24580

commit v2 on v1

v2 whole, which is shorter than its diff:
```python
import functools
import math

import jax
import jax.numpy as jnp
from jax import lax
from jax.experimental import pallas as pl
from jax.experimental.pallas import tpu as pltpu
from jax.sharding import PartitionSpec as P

HDIM = 64
STATE = 128
QHEADS = 32
KVHEADS = 8
ADIM = 128
EPSILON = 1e-05
BARRED = -2e30
HIGHEST = lax.Precision.HIGHEST
F32 = jnp.float32
BF16 = jnp.bfloat16
CHUNK = 256
EDGE = 16
MARK = 3
VMEM_LIMIT = 40 * 1024 * 1024


def silu(value):
    return value * (0.5 * jnp.tanh(0.5 * value) + 0.5)


def softplus(value):
    return jnp.maximum(value, 0.0) + jnp.log(1.0 + jnp.exp(-jnp.abs(value)))


def doc_start(positions, lens_ref):
    begin = jnp.int32(0)
    found = positions * 0
    for doc in range(lens_ref.shape[0]):
        found = jnp.where(positions >= begin, begin, found)
        begin = begin + lens_ref[doc]
    return found


def halves(value):
    high = value.astype(BF16)
    return high, (value - high.astype(F32)).astype(BF16)


def widen(per_head, first, width):
    heads = per_head.shape[1]
    both = jnp.concatenate(halves(per_head), axis=1)
    head = lax.broadcasted_iota(jnp.int32, (2 * heads, width), 0)
    head = jnp.where(head >= heads, head - heads, head)
    channel = lax.broadcasted_iota(jnp.int32, (2 * heads, width), 1) + first
    spread = (channel // HDIM == head).astype(F32).astype(BF16)
    return jnp.dot(both, spread, preferred_element_type=F32)


def rates(dt_ref, dt_bias_ref, a_log_ref):
    step = softplus(dt_ref[...].T + dt_bias_ref[...].reshape(1, -1))
    rate = -step * jnp.exp(a_log_ref[...].reshape(1, -1))
    rows = step.shape[0]
    row = lax.broadcasted_iota(jnp.int32, (rows, rows), 0)
    column = lax.broadcasted_iota(jnp.int32, (rows, rows), 1)
    lower = (row >= column).astype(F32)
    return step, jnp.dot(lower, rate, precision=HIGHEST, preferred_element_type=F32)


def insides(first, shape, taps, lens_ref):
    positions = first + lax.broadcasted_iota(jnp.int32, shape, 0)
    depth = positions - doc_start(positions, lens_ref)
    return [depth >= lag for lag in range(taps)]


def conv(pad, rows, weight, bias, inside):
    taps = weight.shape[0]
    total = pad[8 : 8 + rows] * weight[taps - 1 : taps] + bias
    for lag in range(1, taps):
        term = pad[8 - lag : 8 - lag + rows] * weight[taps - 1 - lag : taps - lag]
        total = total + jnp.where(inside[lag], term, 0.0)
    return silu(total).astype(BF16)


def state_weight(first, step, running, lens_ref):
    rows = step.shape[0]
    last_begin = doc_start(first + rows - 1, lens_ref)
    position = first + lax.broadcasted_iota(jnp.int32, step.shape, 0)
    return jnp.where(
        position >= last_begin, step * jnp.exp(running[rows - 1 : rows] - running), 0.0
    )


def message_pieces(ref, rows):
    block = ref[rows:].astype(F32)
    pieces = [block[at : at + 8] for at in range(0, block.shape[0], 8)]
    return jnp.concatenate(pieces, axis=1)


def state_kernel(group, send, *refs):
    x_ref, bc_ref, dt_ref, wx_ref, bx_ref, wbc_ref, bbc_ref, dt_bias_ref, a_log_ref, lens_ref = refs[:10]
    refs = refs[10:]
    if send:
        x_all_ref, bc_all_ref, keys_ref, values_ref = refs[:4]
        refs = refs[4:]
    xc_ref, bcc_ref, state_ref = refs[:3]
    pad_ref = refs[-1]
    rows, width = x_ref.shape
    taps = wx_ref.shape[0]
    per_group = width // HDIM
    first = lax.axis_index("seq") * rows
    inside = insides(first, (rows, CHUNK), taps, lens_ref)
    step, running = rates(dt_ref, dt_bias_ref, a_log_ref)
    weight = state_weight(first, step, running, lens_ref)
    row = lax.broadcasted_iota(jnp.int32, weight.shape, 0)
    kept = jnp.where(row >= taps - 1, weight, 0.0)[:, group * per_group : (group + 1) * per_group]
    slots = pad_ref.shape[0]

    def block(raw_ref, start, weight_ref, bias_ref, offset, slot):
        pad = pad_ref.at[slot]
        pad[0:8] = jnp.zeros((8, CHUNK), F32)
        pad[8:] = raw_ref[:, start : start + CHUNK].astype(F32)
        columns = slice(offset + start, offset + start + CHUNK)
        return conv(pad, rows, weight_ref[:, columns], bias_ref[columns].reshape(1, -1), inside)

    pair = block(bc_ref, 0, wbc_ref, bbc_ref, group * 2 * STATE, 0)
    bcc_ref[...] = pair
    turned = pair[:, :STATE].astype(F32).T.astype(BF16)
    for start in range(0, width, CHUNK):
        xc = block(x_ref, start, wx_ref, bx_ref, group * width, (start // CHUNK + 1) % slots)
        xc_ref[:, start : start + CHUNK] = xc
        weighted = (xc.astype(F32) * widen(kept, start, CHUNK)).astype(BF16)
        state_ref[:, start : start + CHUNK] = jnp.dot(
            turned, weighted, preferred_element_type=F32
        ).astype(BF16)
    if send:
        message_ref = refs[3]
        kv_width = keys_ref.shape[1]
        message_ref[:rows, :kv_width] = keys_ref[...]
        message_ref[:rows, kv_width:] = values_ref[...]
        marks = []
        for value in (weight[0:1], weight[1:2], weight[2:3], running[rows - 1 : rows]):
            marks.extend(half.astype(F32) for half in halves(value))
        marks = jnp.concatenate(marks, axis=1)
        spare = x_all_ref.shape[1] + bc_all_ref.shape[1] - marks.shape[1]
        marks = jnp.concatenate([marks, jnp.zeros((1, spare), F32)], axis=1)

        def edge(at):
            return jnp.concatenate(
                [x_all_ref[at : at + EDGE].astype(F32), bc_all_ref[at : at + EDGE].astype(F32)], axis=1
            )

        head = edge(0)[:8]
        tail = edge(rows - EDGE)[8:]
        line = lax.broadcasted_iota(jnp.int32, head.shape, 0)
        lines = jnp.where(line < MARK, head, jnp.where(line == MARK, marks, tail))
        pieces = [lines[:, at : at + 2 * kv_width] for at in range(0, lines.shape[1], 2 * kv_width)]
        if len(pieces) % 2:
            pieces.append(jnp.zeros_like(pieces[0]))
        message_ref[rows:] = jnp.concatenate(pieces, axis=0).astype(BF16)


def local_kernel(groups, *refs):
    (
        x_ref, bc_ref, message_ref, dt_ref, wx_ref, bx_ref, wbc_ref, bbc_ref,
        dt_bias_ref, a_log_ref, skip_ref, lens_ref,
    ) = refs[:12]
    xc_refs = refs[12 : 12 + groups]
    bcc_refs = refs[12 + groups : 12 + 2 * groups]
    out_ref, c_ref, pad_ref = refs[12 + 2 * groups :]
    rows, per_group = xc_refs[0].shape
    width = groups * per_group
    taps = wx_ref.shape[0]
    first = lax.axis_index("seq") * rows
    inside = insides(first, (EDGE, CHUNK), taps, lens_ref)
    lines = message_pieces(message_ref, rows)
    slots = pad_ref.shape[0]

    def top(raw_ref, start, weight_ref, bias_ref, offset, slot):
        columns = slice(start, start + CHUNK)
        pad = pad_ref.at[slot]
        pad[0:8] = lines[:, offset + start : offset + start + CHUNK]
        pad[8:] = raw_ref[:, columns].astype(F32)
        return conv(pad, EDGE, weight_ref[:, columns], bias_ref[columns].reshape(1, -1), inside)

    row = lax.broadcasted_iota(jnp.int32, (rows, rows), 0)
    column = lax.broadcasted_iota(jnp.int32, (rows, rows), 1)
    begin = doc_start(first + row, lens_ref)
    linked = (row >= column) & (first + column >= begin)
    step, running = rates(dt_ref, dt_bias_ref, a_log_ref)
    turned_running = running.T
    turned_step = step.T
    skip = skip_ref[...].reshape(1, -1)
    skip = jnp.broadcast_to(skip, (8, skip.shape[1]))
    pair_width = 2 * HDIM
    lane = lax.broadcasted_iota(jnp.int32, (rows, pair_width), 1)
    for group in range(groups):
        base = group * 2 * STATE
        pair = jnp.concatenate(
            [top(bc_ref, base, wbc_ref, bbc_ref, width, group % slots), bcc_refs[group][EDGE:]], axis=0
        )
        inputs = pair[:, :STATE]
        outputs = pair[:, STATE:]
        c_ref[:, group * STATE : (group + 1) * STATE] = outputs
        meet = lax.dot_general(
            outputs, inputs, (((1,), (1,)), ((), ())), preferred_element_type=F32
        )
        meet = jnp.where(linked, meet, 0.0)
        for chunk in range(0, per_group, CHUNK):
            at = group * per_group + chunk
            xc_all = jnp.concatenate(
                [
                    top(x_ref, at, wx_ref, bx_ref, 0, (chunk // CHUNK) % slots),
                    xc_refs[group][EDGE:, chunk : chunk + CHUNK],
                ],
                axis=0,
            )
            wide_skip = widen(skip, at, CHUNK)[0:1]
            for start in range(0, CHUNK, pair_width):
                parts = []
                for head in ((at + start) // HDIM, (at + start) // HDIM + 1):
                    spread = running[:, head : head + 1] - turned_running[head : head + 1]
                    decay = jnp.exp(jnp.minimum(spread, 0.0))
                    parts.append((decay * (meet * turned_step[head : head + 1])).astype(BF16))
                mix = jnp.concatenate(parts, axis=1)
                xc = xc_all[:, start : start + pair_width]
                zero = jnp.zeros_like(xc)
                stacked = jnp.concatenate(
                    [jnp.where(lane < HDIM, xc, zero), jnp.where(lane < HDIM, zero, xc)], axis=0
                )
                value = jnp.dot(mix, stacked, preferred_element_type=F32)
                out_ref[:, at + start : at + start + pair_width] = (
                    value + xc.astype(F32) * wide_skip[:, start : start + pair_width]
                )


def attend_kernel(hops, *refs):
    q_ref = refs[0]
    kv_refs = refs[1 : 2 + hops]
    lens_ref, out_ref = refs[2 + hops :]
    rows = q_ref.shape[0]
    kv_heads = kv_refs[0].shape[1] // (2 * ADIM)
    share = QHEADS // KVHEADS
    count = rows * (hops + 1)
    here = lax.axis_index("seq")
    row = here * rows + lax.broadcasted_iota(jnp.int32, (rows, count), 0)
    column = (here - hops) * rows + lax.broadcasted_iota(jnp.int32, (rows, count), 1)
    allowed = (column <= row) & (column >= doc_start(row, lens_ref))
    scale = ADIM ** (-0.5)
    ones = jnp.ones((count, ADIM), BF16)
    for head in range(kv_heads):
        low = head * ADIM
        keys = jnp.concatenate([ref[:rows, low : low + ADIM] for ref in kv_refs], axis=0)
        low = (kv_heads + head) * ADIM
        values = jnp.concatenate([ref[:rows, low : low + ADIM] for ref in kv_refs], axis=0)
        values = jnp.concatenate([values, ones], axis=1)
        for part in range(share):
            low = (head * share + part) * ADIM
            scores = lax.dot_general(
                q_ref[:, low : low + ADIM], keys, (((1,), (1,)), ((), ())), preferred_element_type=F32
            )
            scores = jnp.where(allowed, scores * scale, BARRED)
            expo = jnp.exp(scores - jnp.max(scores, axis=1, keepdims=True))
            summed = jnp.dot(expo.astype(BF16), values, preferred_element_type=F32)
            out_ref[:, low : low + ADIM] = (summed[:, :ADIM] / summed[:, ADIM:]).astype(BF16)


def carry_kernel(groups, hops, *refs):
    mixed_ref, c_ref, dt_ref, wx_ref, bx_ref, wbc_ref, bbc_ref, dt_bias_ref, a_log_ref, lens_ref = refs[:10]
    state_refs = refs[10 : 10 + groups]
    message_refs = refs[10 + groups : 10 + groups + hops]
    out_ref, entry_ref, pad_ref = refs[10 + groups + hops :]
    rows, width = mixed_ref.shape
    per_group = width // groups
    taps = wx_ref.shape[0]
    here = lax.axis_index("seq")
    first = here * rows
    _, running = rates(dt_ref, dt_bias_ref, a_log_ref)
    heads = running.shape[1]
    group_heads = heads // groups
    first_begin = doc_start(first, lens_ref)
    position = first + lax.broadcasted_iota(jnp.int32, running.shape, 0)
    entry = jnp.where(doc_start(position, lens_ref) < first, jnp.exp(running), 0.0)
    lines = [message_pieces(ref, rows) for ref in message_refs]

    def mark(hop, which):
        at = 2 * which * heads
        return lines[hop][MARK : MARK + 1, at : at + heads] + lines[hop][MARK : MARK + 1, at + heads : at + 2 * heads]

    line = lax.broadcasted_iota(jnp.int32, (8, heads), 0)
    total = jnp.zeros((1, heads), F32)
    weights = []
    inside = []
    for hop in range(1, hops + 1):
        factor = jnp.ones((1, heads), F32)
        if hop > 1:
            total = total + mark(hop - 2, 3)
            factor = jnp.where(first_begin < (here - hop + 1) * rows, jnp.exp(total), 0.0)
            entry_ref[hop - 2] = entry * factor
        weight = jnp.zeros((8, heads), F32)
        for at in range(taps - 1):
            weight = jnp.where(line == at, mark(hop - 1, at) * factor, weight)
        weights.append(weight)
        inside.append(insides((here - hop) * rows, (8, CHUNK), taps, lens_ref))
    slots = pad_ref.shape[0]

    def top(hop, at, weight_ref, bias_ref, start, slot):
        columns = slice(start, start + CHUNK)
        pad = pad_ref.at[slot]
        above = lines[hop + 1] if hop + 1 < hops else jnp.zeros_like(lines[0])
        pad[0:8] = above[:, at : at + CHUNK]
        pad[8:] = lines[hop][:, at : at + CHUNK]
        return conv(pad, 8, weight_ref[:, columns], bias_ref[columns].reshape(1, -1), inside[hop])

    for group in range(groups):
        outputs = c_ref[:, group * STATE : (group + 1) * STATE]
        meets = []
        for hop in range(hops):
            base = group * 2 * STATE
            inputs = top(hop, width + base, wbc_ref, bbc_ref, base, hop % slots)[:, :STATE]
            meets.append(
                lax.dot_general(outputs, inputs, (((1,), (1,)), ((), ())), preferred_element_type=F32)
            )
        meets = jnp.concatenate(meets, axis=1).astype(BF16)
        these = slice(group * group_heads, (group + 1) * group_heads)
        for chunk in range(0, per_group, CHUNK):
            at = group * per_group + chunk
            columns = slice(at, at + CHUNK)
            edges = []
            for hop in range(hops):
                xc = top(hop, at, wx_ref, bx_ref, at, hop % slots).astype(F32)
                edges.append(xc * widen(weights[hop][:, these], chunk, CHUNK))
            edges = jnp.concatenate(edges, axis=0).astype(BF16)
            carried = jnp.dot(
                outputs, state_refs[group][:, chunk : chunk + CHUNK], preferred_element_type=F32
            ) + jnp.dot(meets, edges, preferred_element_type=F32)
            out_ref[:, columns] = mixed_ref[:, columns] + carried * widen(entry[:, these], chunk, CHUNK)


def norm_kernel(group, hops, *refs):
    mixed_ref, c_ref, entry_ref, z_ref, gain_ref = refs[:5]
    state_refs = refs[5 : 5 + hops - 1]
    out_ref, gated_ref = refs[-2:]
    rows, per_group = mixed_ref.shape
    group_heads = per_group // HDIM
    these = slice(group * group_heads, (group + 1) * group_heads)
    outputs = c_ref[:, group * STATE : (group + 1) * STATE]
    squares = jnp.zeros((rows, 1), F32)
    for start in range(0, per_group, CHUNK):
        columns = slice(start, start + CHUNK)
        mixed = mixed_ref[:, columns]
        for hop, ref in enumerate(state_refs):
            carried = jnp.dot(outputs, ref[:, columns], preferred_element_type=F32)
            mixed = mixed + carried * widen(entry_ref[hop][:, these], start, CHUNK)
        gated = mixed * silu(z_ref[:, columns].astype(F32))
        gated_ref[:, columns] = gated
        squares = squares + jnp.sum(gated * gated, axis=1, keepdims=True)
    multiplier = lax.rsqrt(squares * (1.0 / per_group) + EPSILON)
    for start in range(0, per_group, CHUNK):
        columns = slice(start, start + CHUNK)
        gain = gain_ref[group * per_group + start : group * per_group + start + CHUNK]
        out_ref[:, columns] = (gated_ref[:, columns] * multiplier * gain.reshape(1, -1)).astype(BF16)


WHOLE = pl.BlockSpec(memory_space=pltpu.VMEM)
SCALARS = pl.BlockSpec(memory_space=pltpu.SMEM)
UNTOUCHED = pl.BlockSpec(memory_space=pl.ANY)


def part(rows, columns, row, column):
    return pl.BlockSpec((rows, columns), lambda step: (row, column))


def call(kernel, name, outs, operands, specs, out_specs=None, scratch=(), flops=0, aliases={}):
    moved = sum(math.prod(a.shape) * a.dtype.itemsize for a in (*operands, *outs))
    return pl.pallas_call(
        kernel,
        name=name,
        grid=(1,),
        out_shape=outs,
        in_specs=specs,
        out_specs=[WHOLE] * len(outs) if out_specs is None else out_specs,
        scratch_shapes=list(scratch),
        input_output_aliases=aliases,
        compiler_params=pltpu.CompilerParams(vmem_limit_bytes=VMEM_LIMIT),
        cost_estimate=pl.CostEstimate(flops=flops, bytes_accessed=moved, transcendentals=0),
    )(*operands)


def onward(value):
    count = lax.axis_size("seq")
    return lax.ppermute(value, "seq", [(source, source + 1) for source in range(count - 1)])


def shards(
    x_raw,
    bc_raw,
    z_gate,
    dt_raw,
    conv_x_weight,
    conv_x_bias,
    conv_bc_weight,
    conv_bc_bias,
    dt_bias,
    a_log,
    skip_d,
    norm_gain,
    queries,
    keys,
    values,
    doc_lens,
):
    rows, width = x_raw.shape
    bc_width = bc_raw.shape[1]
    heads = dt_raw.shape[1]
    groups = bc_width // (2 * STATE)
    per_group = width // groups
    count = lax.axis_size("seq")
    longest = rows * count // 2
    hops = min(count - 1, -(-(longest - 1) // rows))
    assert hops * rows >= longest
    kv_width = 2 * keys.shape[1]
    shape = jax.ShapeDtypeStruct
    dt = dt_raw.T
    convs = (conv_x_weight, conv_x_bias, conv_bc_weight, conv_bc_bias)
    pieces = -(-(width + bc_width) // kv_width)
    message_rows = rows + EDGE * -(-pieces // 2)

    xcs, bccs, states = [], [], []
    for group in range(groups):
        send = group == groups - 1
        outs = [shape((rows, per_group), BF16), shape((rows, 2 * STATE), BF16), shape((STATE, per_group), BF16)]
        operands = [x_raw, bc_raw, dt, *convs, dt_bias, a_log, doc_lens]
        specs = [part(rows, per_group, 0, group), part(rows, 2 * STATE, 0, group)] + [WHOLE] * 7 + [SCALARS]
        if send:
            outs.append(shape((message_rows, kv_width), BF16))
            operands += [x_raw, bc_raw, keys, values]
            specs += [WHOLE] * 4
        got = call(
            functools.partial(state_kernel, group, send),
            f"state_part{group}",
            outs,
            operands,
            specs,
            scratch=[pltpu.VMEM((4, rows + 8, CHUNK), F32)],
            flops=2 * rows * per_group * STATE,
        )
        xcs.append(got[0])
        bccs.append(got[1])
        states.append(got[2])
    messages = [onward(got[3])]
    for _ in range(1, hops):
        messages.append(onward(messages[-1]))
    arrived = [[onward(state)] for state in states]
    for hop in range(1, hops):
        for chain in arrived:
            chain.append(onward(chain[-1]))

    mixed, c_out = call(
        functools.partial(local_kernel, groups),
        "local_mix",
        [shape((rows, width), F32), shape((rows, groups * STATE), BF16)],
        [x_raw, bc_raw, messages[0], dt, *convs, dt_bias, a_log, skip_d, doc_lens, *xcs, *bccs],
        [part(EDGE, width, 0, 0), part(EDGE, bc_width, 0, 0)] + [WHOLE] * 9 + [SCALARS] + [WHOLE] * 2 * groups,
        scratch=[pltpu.VMEM((4, EDGE + 8, CHUNK), F32)],
        flops=4 * rows * rows * width,
    )
    (attn_out,) = call(
        functools.partial(attend_kernel, hops),
        "attend",
        [shape(queries.shape, BF16)],
        [queries, *reversed(messages), got[3], doc_lens],
        [WHOLE] * (hops + 2) + [SCALARS],
        flops=4 * rows * rows * (hops + 1) * queries.shape[1],
    )
    mixed, entry = call(
        functools.partial(carry_kernel, groups, hops),
        "carry_near",
        [shape((rows, width), F32), shape((max(hops - 1, 1), rows, heads), F32)],
        [mixed, c_out, dt, *convs, dt_bias, a_log, doc_lens, *(chain[0] for chain in arrived), *messages],
        [WHOLE] * 9 + [SCALARS] + [WHOLE] * (groups + hops),
        scratch=[pltpu.VMEM((4, 16, CHUNK), F32)],
        flops=2 * rows * width * STATE,
    )
    mamba_out = None
    for group, chain in enumerate(arrived):
        operands = [mixed, c_out, entry, z_gate, norm_gain, *chain[1:]]
        specs = [part(rows, per_group, 0, group), WHOLE, WHOLE, part(rows, per_group, 0, group)]
        specs += [WHOLE] * hops
        aliases = {}
        if mamba_out is not None:
            operands.append(mamba_out)
            specs.append(UNTOUCHED)
            aliases = {len(operands) - 1: 0}
        (mamba_out,) = call(
            functools.partial(norm_kernel, group, hops),
            f"norm_part{group}",
            [shape((rows, width), BF16)],
            operands,
            specs,
            out_specs=[part(rows, per_group, 0, group)],
            scratch=[pltpu.VMEM((rows, per_group), F32)],
            flops=2 * rows * per_group * STATE,
            aliases=aliases,
        )
    return (mamba_out, attn_out)


def solution(mesh):
    split = P(("groups", "seq"), "dp")
    placed = (
        split,
        split,
        split,
        split,
        P(None, "dp"),
        P("dp"),
        P(None, "dp"),
        P("dp"),
        P("dp"),
        P("dp"),
        P("dp"),
        P("dp"),
        split,
        split,
        split,
        P("groups"),
    )
    return jax.shard_map(
        shards,
        mesh=mesh,
        in_specs=placed,
        out_specs=(split, split),
        check_vma=False,
    )
```

time: 55.9 us -> 51.2 us (0.916)
  the two profiles are of different devices: /device:TPU:22 before, /device:TPU:0 now
where the time goes in v2:
time: 51.2 us; the launch traced here: 50.6 us
  starting transfers between devices  22.1 us (43%)
  Pallas kernels  12.7 us (25%)
  waiting for transfers between devices  8.22 us (16%)
  local copies, waits for them, and re-layouts  6.83 us (13%)
  between operations  0.82 us (2%)
    ppermute x6, starting transfers between devices, onward(): lax.ppermute(value, 'seq', [(source, source + 1) for source in range(coun...  22.1 us
    pallas_call x7, Pallas kernels, call(): pl.pallas_call(kernel, name=name, grid=(1,), out_shape=outs, in_specs=spe...  12.7 us
    ppermute x6, waiting for transfers between devices, onward(): lax.ppermute(value, 'seq', [(source, source + 1) for source in range(coun...  8.22 us
    unnamed x32, local copies, waits for them, and re-layouts  6.83 us
  transfers between devices with their start and end apart: 6, of which 2 were waited for; matrix products, arithmetic and copies ran while one was open for 0% of the time, Pallas kernels for 19%

profile of v2, /device:TPU:0, one launch (start us, length us, event | category | flops | bytes accessed | tf_op | source)
XLA Modules:
  0.0 50.6 jit_solution(2850041931991645608)
XLA Ops:
  0.7 0.6 %copy-done.13 = f32[32]{0:T(128)S(1)} copy-done((f32[32]{0:T(128)S(1)}, f32[32]{0:T(128)}, u32[]{:S(2)}) %copy-start.13) | copy-done | bytes 152
  1.3 0.0 copy-done.14
  1.3 0.0 copy-done.12
  1.3 1.0 %copy-done = bf16[128,2048]{1,0:T(8,128)(2,1)S(1)} copy-done((bf16[128,2048]{1,0:T(8,128)(2,1)S(1)}, bf16[128,2048]{1,0:T(8,128)(2,1)}, u32[]{:S(2)}) %copy-start) | copy-done | bytes 524312
  2.4 0.9 %copy-done.1 = bf16[128,512]{1,0:T(8,128)(2,1)S(1)} copy-done((bf16[128,512]{1,0:T(8,128)(2,1)S(1)}, bf16[128,512]{1,0:T(8,128)(2,1)}, u32[]{:S(2)}) %copy-start.1) | copy-done | bytes 131096
  3.3 0.8 %copy-done.3 = f32[4,2048]{1,0:T(4,128)S(1)} copy-done((f32[4,2048]{1,0:T(4,128)S(1)}, f32[4,2048]{1,0:T(4,128)}, u32[]{:S(2)}) %copy-start.3) | copy-done | bytes 32792
  4.0 0.7 %copy-done.4 = f32[128,32]{0,1:T(8,128)S(1)} copy-done((f32[128,32]{0,1:T(8,128)S(1)}, f32[128,32]{0,1:T(8,128)}, u32[]{:S(2)}) %copy-start.4) | copy-done | bytes 16408
  4.7 0.7 %copy-done.6 = f32[2048]{0:T(1024)S(1)} copy-done((f32[2048]{0:T(1024)S(1)}, f32[2048]{0:T(1024)}, u32[]{:S(2)}) %copy-start.6) | copy-done | bytes 8216
  5.4 0.7 %copy-done.7 = f32[4,512]{1,0:T(4,128)S(1)} copy-done((f32[4,512]{1,0:T(4,128)S(1)}, f32[4,512]{1,0:T(4,128)}, u32[]{:S(2)}) %copy-start.7) | copy-done | bytes 8216
  6.1 0.7 %copy-done.11 = f32[512]{0:T(512)S(1)} copy-done((f32[512]{0:T(512)S(1)}, f32[512]{0:T(512)}, u32[]{:S(2)}) %copy-start.11) | copy-done | bytes 2072
  6.8 1.8 %state_part0.1 = (bf16[128,1024]{1,0:T(8,128)(2,1)S(1)}, bf16[128,256]{1,0:T(8,128)(2,1)S(1)}, bf16[128,1024]{1,0:T(8,128)(2,1)S(1)}) custom-call(bf16[128,2048]{1,0:T(8,128)(2,1)S(1)} %copy-done, bf16[128,512]{1,0:T(8,128)(2,1)S(1)} %copy-done.1, f32[32,128]{1,0:T(8,128)S(1)} %bitcast.1, f32[4,2048]{1,0:T(4,128)S(1)} %copy-done.3, f32[2048]{0:T(1024)S(1)} %copy-done.6, ...), custom_call_target="tpu_custom_call" | custom-call | flops 33554432 | bytes 1313040 | tf_op jit(solution)/shard_map/state_part0/pallas_call | solution.py:375
  8.7 4.9 %collective-permute-start.1 = (bf16[128,1024]{1,0:T(8,128)(2,1)S(1)}, bf16[128,1024]{1,0:T(8,128)(2,1)S(1)}, u32[]{:S(2)}, u32[]{:S(2)}) collective-permute-start(bf16[128,1024]{1,0:T(8,128)(2,1)S(1)} %get-tuple-element.20), channel_id=1, source_target_pairs={{0,4},{4,8},{8,12},{1,5},{5,9},{9,13},{2,6},{6,10},{10,14},{3,7},{... | collective-permute-start | bytes 786440 | tf_op jit(solution)/shard_map/ppermute | solution.py:391
  13.6 1.8 %state_part1.1 = (bf16[128,1024]{1,0:T(8,128)(2,1)S(1)}, bf16[128,256]{1,0:T(8,128)(2,1)S(1)}, bf16[128,1024]{1,0:T(8,128)(2,1)S(1)}, bf16[176,512]{1,0:T(8,128)(2,1)S(1)}) custom-call(bf16[128,2048]{1,0:T(8,128)(2,1)S(1)} %copy-done, bf16[128,512]{1,0:T(8,128)(2,1)S(1)} %copy-done.1, f32[32,128]{1,0:T(8,128)S(1)} %bitcast.2, f32[4,2048]{1,0:T(4,128)S(1)} %copy-done.3, ...), custom_call_target="tpu_custom_call" | custom-call | flops 33554432 | bytes 2279696 | tf_op jit(solution)/shard_map/state_part1/pallas_call | solution.py:375
  15.5 3.5 %collective-permute-start.2 = (bf16[128,1024]{1,0:T(8,128)(2,1)S(1)}, bf16[128,1024]{1,0:T(8,128)(2,1)S(1)}, u32[]{:S(2)}, u32[]{:S(2)}) collective-permute-start(bf16[128,1024]{1,0:T(8,128)(2,1)S(1)} %get-tuple-element.21), channel_id=1, source_target_pairs={{0,4},{4,8},{8,12},{1,5},{5,9},{9,13},{2,6},{6,10},{10,14},{3,7},{... | collective-permute-start | bytes 786440 | tf_op jit(solution)/shard_map/ppermute | solution.py:391
  19.0 3.5 %collective-permute-start = (bf16[176,512]{1,0:T(8,128)(2,1)S(1)}, bf16[176,512]{1,0:T(8,128)(2,1)S(1)}, u32[]{:S(2)}, u32[]{:S(2)}) collective-permute-start(bf16[176,512]{1,0:T(8,128)(2,1)S(1)} %get-tuple-element.13.refs_3_), channel_id=1, source_target_pairs={{0,4},{4,8},{8,12},{1,5},{5,9},{9,13},{2,6},{6,10},{10,14},{3,7},{... | collective-permute-start | bytes 540680 | tf_op jit(solution)/shard_map/ppermute | solution.py:391
  22.5 0.0 collective-permute-done.1.refs_10_
  22.5 1.9 %collective-permute-start.5 = (bf16[128,1024]{1,0:T(8,128)(2,1)S(1)}, bf16[128,1024]{1,0:T(8,128)(2,1)S(1)}, u32[]{:S(2)}, u32[]{:S(2)}) collective-permute-start(bf16[128,1024]{1,0:T(8,128)(2,1)S(1)} %collective-permute-done.1.refs_10_), channel_id=1, source_target_pairs={{0,4},{4,8},{8,12},{1,5},{5,9},{9,13},{2,6},{6,10},{10,14},{3,7},{... | collective-permute-start | bytes 786440 | tf_op jit(solution)/shard_map/ppermute | solution.py:391
  24.4 1.3 %collective-permute-done.2.refs_11_ = bf16[128,1024]{1,0:T(8,128)(2,1)S(1)} collective-permute-done((bf16[128,1024]{1,0:T(8,128)(2,1)S(1)}, bf16[128,1024]{1,0:T(8,128)(2,1)S(1)}, u32[]{:S(2)}, u32[]{:S(2)}) %collective-permute-start.2) | collective-permute-done | bytes 262176 | tf_op jit(solution)/shard_map/ppermute | solution.py:391
  25.7 4.4 %collective-permute-start.4 = (bf16[128,1024]{1,0:T(8,128)(2,1)S(1)}, bf16[128,1024]{1,0:T(8,128)(2,1)S(1)}, u32[]{:S(2)}, u32[]{:S(2)}) collective-permute-start(bf16[128,1024]{1,0:T(8,128)(2,1)S(1)} %collective-permute-done.2.refs_11_), channel_id=1, source_target_pairs={{0,4},{4,8},{8,12},{1,5},{5,9},{9,13},{2,6},{6,10},{10,14},{3,7},{... | collective-permute-start | bytes 786440 | tf_op jit(solution)/shard_map/ppermute | solution.py:391
  30.1 0.0 collective-permute-done.refs_2_.refs_12_
  30.1 3.8 %collective-permute-start.3 = (bf16[176,512]{1,0:T(8,128)(2,1)S(1)}, bf16[176,512]{1,0:T(8,128)(2,1)S(1)}, u32[]{:S(2)}, u32[]{:S(2)}) collective-permute-start(bf16[176,512]{1,0:T(8,128)(2,1)S(1)} %collective-permute-done.refs_2_.refs_12_), channel_id=1, source_target_pairs={{0,4},{4,8},{8,12},{1,5},{5,9},{9,13},{2,6},{6,10},{10,14},{3,7},{... | collective-permute-start | bytes 540680 | tf_op jit(solution)/shard_map/ppermute | solution.py:391
  34.0 0.0 copy-start.15
  34.0 0.6 %copy-done.15 = f32[32]{0:T(128)S(1)} copy-done((f32[32]{0:T(128)S(1)}, f32[32]{0:T(128)}, u32[]{:S(2)}) %copy-start.15) | copy-done | bytes 152
  34.6 2.2 %local_mix.1 = (f32[128,2048]{1,0:T(8,128)S(1)}, bf16[128,256]{1,0:T(8,128)(2,1)S(1)}) custom-call(bf16[128,2048]{1,0:T(8,128)(2,1)S(1)} %copy-done, bf16[128,512]{1,0:T(8,128)(2,1)S(1)} %copy-done.1, bf16[176,512]{1,0:T(8,128)(2,1)S(1)} %collective-permute-done.refs_2_.refs_12_, f32[32,128]{1,0:T(8,128)S(1)} %bitcast.3, f32[4,2048]{1,0:T(4,128)S(1)} %copy-done.3, ...), custom_call_target="tpu_custom_call" | custom-call | flops 134217728 | bytes 2673040 | tf_op jit(solution)/shard_map/local_mix/pallas_call | solution.py:375
  36.8 6.9 %collective-permute-done.3.refs_13_.refs_1_ = bf16[176,512]{1,0:T(8,128)(2,1)S(1)} collective-permute-done((bf16[176,512]{1,0:T(8,128)(2,1)S(1)}, bf16[176,512]{1,0:T(8,128)(2,1)S(1)}, u32[]{:S(2)}, u32[]{:S(2)}) %collective-permute-start.3) | collective-permute-done | bytes 180256 | tf_op jit(solution)/shard_map/ppermute | solution.py:391
  43.7 2.2 %carry_near.1 = (f32[128,2048]{1,0:T(8,128)S(1)}, f32[1,128,32]{2,1,0:T(8,128)S(1)}) custom-call(f32[128,2048]{1,0:T(8,128)S(1)} %get-tuple-element.18.refs_0_, bf16[128,256]{1,0:T(8,128)(2,1)S(1)} %get-tuple-element.19.refs_1_, f32[32,128]{1,0:T(8,128)S(1)} %bitcast.4, f32[4,2048]{1,0:T(4,128)S(1)} %copy-done.3, f32[2048]{0:T(1024)S(1)} %copy-done.6, ...), custom_call_target="tpu_custom_call" | custom-call | flops 67108864 | bytes 3131664 | tf_op jit(solution)/shard_map/carry_near/pallas_call | solution.py:375
  46.0 0.0 copy-start.2
  46.0 0.0 copy-start.10
  46.0 2.3 %attend.1 = bf16[128,1024]{1,0:T(8,128)(2,1)} custom-call(bf16[128,1024]{1,0:T(8,128)(2,1)S(1)} %copy-done.5, bf16[176,512]{1,0:T(8,128)(2,1)S(1)} %collective-permute-done.3.refs_13_.refs_1_, bf16[176,512]{1,0:T(8,128)(2,1)S(1)} %collective-permute-done.refs_2_.refs_12_, bf16[176,512]{1,0:T(8,128)(2,1)S(1)} %get-tuple-element.13.refs_3_, s32[4]{0:T(128)S(1)} %copy-done.12), custom_call_target="tpu_custom_call" | custom-call | flops 201326592 | bytes 1064976 | tf_op jit(solution)/shard_map/attend/pallas_call | solution.py:375
  48.3 1.2 %norm_part0.1.refs_6_ = bf16[128,2048]{1,0:T(8,128)(2,1)} custom-call(f32[128,2048]{1,0:T(8,128)S(1)} %get-tuple-element.22.refs_0_, bf16[128,256]{1,0:T(8,128)(2,1)S(1)} %get-tuple-element.19.refs_1_, f32[1,128,32]{2,1,0:T(8,128)S(1)} %get-tuple-element.23.refs_2_, bf16[128,2048]{1,0:T(8,128)(2,1)S(1)} %copy-done.2, f32[2048]{0:T(1024)S(1)} %copy-done.10, ...), custom_call_target="tpu_custom_call" | custom-call | flops 33554432 | bytes 2449408 | tf_op jit(solution)/shard_map/norm_part0/pallas_call | solution.py:375
  49.5 0.0 collective-permute-done.4.refs_5_
  49.5 1.2 %norm_part1.1 = bf16[128,2048]{1,0:T(8,128)(2,1)} custom-call(f32[128,2048]{1,0:T(8,128)S(1)} %get-tuple-element.22.refs_0_, bf16[128,256]{1,0:T(8,128)(2,1)S(1)} %get-tuple-element.19.refs_1_, f32[1,128,32]{2,1,0:T(8,128)S(1)} %get-tuple-element.23.refs_2_, bf16[128,2048]{1,0:T(8,128)(2,1)S(1)} %copy-done.2, ...), custom_call_target="tpu_custom_call", output_to_operand_aliasing={{}: (6, {})} | custom-call | flops 33554432 | bytes 2973696 | tf_op jit(solution)/shard_map/norm_part1/pallas_call | solution.py:375
  (19 shorter events, 0.0 us)
Async XLA Ops:
  0.6 0.7 %copy-start.13 = (f32[32]{0:T(128)S(1)}, f32[32]{0:T(128)}, u32[]{:S(2)}) copy-start(f32[32]{0:T(128)} %refs_7_.7) | copy-start | bytes 388
  0.6 0.7 %copy-start.14 = (f32[32]{0:T(128)S(1)}, f32[32]{0:T(128)}, u32[]{:S(2)}) copy-start(f32[32]{0:T(128)} %refs_8_.7) | copy-start | bytes 388
  0.7 0.7 %copy-start.12 = (s32[4]{0:T(128)S(1)}, s32[4]{0:T(128)}, u32[]{:S(2)}) copy-start(s32[4]{0:T(128)} %refs_4_.13) | copy-start | bytes 52
  1.3 1.0 %copy-start = (bf16[128,2048]{1,0:T(8,128)(2,1)S(1)}, bf16[128,2048]{1,0:T(8,128)(2,1)}, u32[]{:S(2)}) copy-start(bf16[128,2048]{1,0:T(8,128)(2,1)} %refs_0_.6) | copy-start | bytes 1572868
  2.4 0.9 %copy-start.1 = (bf16[128,512]{1,0:T(8,128)(2,1)S(1)}, bf16[128,512]{1,0:T(8,128)(2,1)}, u32[]{:S(2)}) copy-start(bf16[128,512]{1,0:T(8,128)(2,1)} %refs_1_.5) | copy-start | bytes 393220
  3.3 0.8 %copy-start.3 = (f32[4,2048]{1,0:T(4,128)S(1)}, f32[4,2048]{1,0:T(4,128)}, u32[]{:S(2)}) copy-start(f32[4,2048]{1,0:T(4,128)} %refs_3_.7) | copy-start | bytes 98308
  4.0 0.7 %copy-start.4 = (f32[128,32]{0,1:T(8,128)S(1)}, f32[128,32]{0,1:T(8,128)}, u32[]{:S(2)}) copy-start(f32[128,32]{0,1:T(8,128)} %param.19) | copy-start | bytes 49156
  4.7 0.7 %copy-start.6 = (f32[2048]{0:T(1024)S(1)}, f32[2048]{0:T(1024)}, u32[]{:S(2)}) copy-start(f32[2048]{0:T(1024)} %refs_4_.10) | copy-start | bytes 24580
  5.4 0.7 %copy-start.7 = (f32[4,512]{1,0:T(4,128)S(1)}, f32[4,512]{1,0:T(4,128)}, u32[]{:S(2)}) copy-start(f32[4,512]{1,0:T(4,128)} %refs_5_.7) | copy-start | bytes 24580
  6.1 0.7 %copy-start.11 = (f32[512]{0:T(512)S(1)}, f32[512]{0:T(512)}, u32[]{:S(2)}) copy-start(f32[512]{0:T(512)} %refs_6_.7) | copy-start | bytes 6148
  6.8 6.8 %copy-start.8 = (bf16[128,256]{1,0:T(8,128)(2,1)S(1)}, bf16[128,256]{1,0:T(8,128)(2,1)}, u32[]{:S(2)}) copy-start(bf16[128,256]{1,0:T(8,128)(2,1)} %refs_12_.1) | copy-start | bytes 196612
  6.8 6.8 %copy-start.9 = (bf16[128,256]{1,0:T(8,128)(2,1)S(1)}, bf16[128,256]{1,0:T(8,128)(2,1)}, u32[]{:S(2)}) copy-start(bf16[128,256]{1,0:T(8,128)(2,1)} %refs_13_.1) | copy-start | bytes 196612
  8.7 13.8 %collective-permute-start.1 = (bf16[128,1024]{1,0:T(8,128)(2,1)S(1)}, bf16[128,1024]{1,0:T(8,128)(2,1)S(1)}, u32[]{:S(2)}, u32[]{:S(2)}) collective-permute-start(bf16[128,1024]{1,0:T(8,128)(2,1)S(1)} %get-tuple-element.20), channel_id=1, source_target_pairs={{0,4},{4,8},{8,12},{1,5},{5,9},{9,13},{2,6},{6,10},{10,14},{3,7},{... | collective-permute-start | bytes 786440 | tf_op jit(solution)/shard_map/ppermute | solution.py:391
  15.5 10.2 %collective-permute-start.2 = (bf16[128,1024]{1,0:T(8,128)(2,1)S(1)}, bf16[128,1024]{1,0:T(8,128)(2,1)S(1)}, u32[]{:S(2)}, u32[]{:S(2)}) collective-permute-start(bf16[128,1024]{1,0:T(8,128)(2,1)S(1)} %get-tuple-element.21), channel_id=1, source_target_pairs={{0,4},{4,8},{8,12},{1,5},{5,9},{9,13},{2,6},{6,10},{10,14},{3,7},{... | collective-permute-start | bytes 786440 | tf_op jit(solution)/shard_map/ppermute | solution.py:391
  19.0 11.1 %collective-permute-start = (bf16[176,512]{1,0:T(8,128)(2,1)S(1)}, bf16[176,512]{1,0:T(8,128)(2,1)S(1)}, u32[]{:S(2)}, u32[]{:S(2)}) collective-permute-start(bf16[176,512]{1,0:T(8,128)(2,1)S(1)} %get-tuple-element.13.refs_3_), channel_id=1, source_target_pairs={{0,4},{4,8},{8,12},{1,5},{5,9},{9,13},{2,6},{6,10},{10,14},{3,7},{... | collective-permute-start | bytes 540680 | tf_op jit(solution)/shard_map/ppermute | solution.py:391
  22.5 25.8 %collective-permute-start.5 = (bf16[128,1024]{1,0:T(8,128)(2,1)S(1)}, bf16[128,1024]{1,0:T(8,128)(2,1)S(1)}, u32[]{:S(2)}, u32[]{:S(2)}) collective-permute-start(bf16[128,1024]{1,0:T(8,128)(2,1)S(1)} %collective-permute-done.1.refs_10_), channel_id=1, source_target_pairs={{0,4},{4,8},{8,12},{1,5},{5,9},{9,13},{2,6},{6,10},{10,14},{3,7},{... | collective-permute-start | bytes 786440 | tf_op jit(solution)/shard_map/ppermute | solution.py:391
  25.7 23.8 %collective-permute-start.4 = (bf16[128,1024]{1,0:T(8,128)(2,1)S(1)}, bf16[128,1024]{1,0:T(8,128)(2,1)S(1)}, u32[]{:S(2)}, u32[]{:S(2)}) collective-permute-start(bf16[128,1024]{1,0:T(8,128)(2,1)S(1)} %collective-permute-done.2.refs_11_), channel_id=1, source_target_pairs={{0,4},{4,8},{8,12},{1,5},{5,9},{9,13},{2,6},{6,10},{10,14},{3,7},{... | collective-permute-start | bytes 786440 | tf_op jit(solution)/shard_map/ppermute | solution.py:391
  30.1 13.6 %collective-permute-start.3 = (bf16[176,512]{1,0:T(8,128)(2,1)S(1)}, bf16[176,512]{1,0:T(8,128)(2,1)S(1)}, u32[]{:S(2)}, u32[]{:S(2)}) collective-permute-start(bf16[176,512]{1,0:T(8,128)(2,1)S(1)} %collective-permute-done.refs_2_.refs_12_), channel_id=1, source_target_pairs={{0,4},{4,8},{8,12},{1,5},{5,9},{9,13},{2,6},{6,10},{10,14},{3,7},{... | collective-permute-start | bytes 540680 | tf_op jit(solution)/shard_map/ppermute | solution.py:391
  34.0 0.7 %copy-start.15 = (f32[32]{0:T(128)S(1)}, f32[32]{0:T(128)}, u32[]{:S(2)}) copy-start(f32[32]{0:T(128)} %refs_10_.3) | copy-start | bytes 388
  43.7 2.2 %copy-start.5 = (bf16[128,1024]{1,0:T(8,128)(2,1)S(1)}, bf16[128,1024]{1,0:T(8,128)(2,1)}, u32[]{:S(2)}) copy-start(bf16[128,1024]{1,0:T(8,128)(2,1)} %refs_0_.7) | copy-start | bytes 786436
  46.0 2.3 %copy-start.2 = (bf16[128,2048]{1,0:T(8,128)(2,1)S(1)}, bf16[128,2048]{1,0:T(8,128)(2,1)}, u32[]{:S(2)}) copy-start(bf16[128,2048]{1,0:T(8,128)(2,1)} %refs_3_.9) | copy-start | bytes 1572868
  46.0 2.3 %copy-start.10 = (f32[2048]{0:T(1024)S(1)}, f32[2048]{0:T(1024)}, u32[]{:S(2)}) copy-start(f32[2048]{0:T(1024)} %refs_4_.12) | copy-start | bytes 24580

commit v3 on v2

v3 whole, which is shorter than its diff:
```python
import functools
import math

import jax
import jax.numpy as jnp
from jax import lax
from jax.experimental import pallas as pl
from jax.experimental.pallas import tpu as pltpu
from jax.sharding import PartitionSpec as P

HDIM = 64
STATE = 128
QHEADS = 32
KVHEADS = 8
ADIM = 128
EPSILON = 1e-05
BARRED = -2e30
HIGHEST = lax.Precision.HIGHEST
F32 = jnp.float32
BF16 = jnp.bfloat16
CHUNK = 256
EDGE = 16
KERNEL_FLOPS = 2 * 10**9
VMEM_LIMIT = 40 * 1024 * 1024
VMEM_ALL = 62 * 1024 * 1024


def silu(value):
    return value * (0.5 * jnp.tanh(0.5 * value) + 0.5)


def softplus(value):
    return jnp.maximum(value, 0.0) + jnp.log(1.0 + jnp.exp(-jnp.abs(value)))


def doc_start(positions, lens_ref):
    begin = jnp.int32(0)
    found = positions * 0
    for doc in range(lens_ref.shape[0]):
        found = jnp.where(positions >= begin, begin, found)
        begin = begin + lens_ref[doc]
    return found


def halves(value):
    high = value.astype(BF16)
    return high, (value - high.astype(F32)).astype(BF16)


def widen(per_head, first, width):
    heads = per_head.shape[1]
    both = jnp.concatenate(halves(per_head), axis=1)
    head = lax.broadcasted_iota(jnp.int32, (2 * heads, width), 0)
    head = jnp.where(head >= heads, head - heads, head)
    channel = lax.broadcasted_iota(jnp.int32, (2 * heads, width), 1) + first
    spread = (channel // HDIM == head).astype(F32).astype(BF16)
    return jnp.dot(both, spread, preferred_element_type=F32)


def rates(dt_ref, dt_bias_ref, a_log_ref):
    step = softplus(dt_ref[...].T + dt_bias_ref[...].reshape(1, -1))
    rate = -step * jnp.exp(a_log_ref[...].reshape(1, -1))
    rows = step.shape[0]
    row = lax.broadcasted_iota(jnp.int32, (rows, rows), 0)
    column = lax.broadcasted_iota(jnp.int32, (rows, rows), 1)
    lower = (row >= column).astype(F32)
    return step, jnp.dot(lower, rate, precision=HIGHEST, preferred_element_type=F32)


def insides(first, shape, taps, lens_ref):
    positions = first + lax.broadcasted_iota(jnp.int32, shape, 0)
    depth = positions - doc_start(positions, lens_ref)
    return [depth >= lag for lag in range(taps)]


def conv(pad, rows, weight, bias, inside):
    taps = weight.shape[0]
    total = pad[8 : 8 + rows] * weight[taps - 1 : taps] + bias
    for lag in range(1, taps):
        term = pad[8 - lag : 8 - lag + rows] * weight[taps - 1 - lag : taps - lag]
        total = total + jnp.where(inside[lag], term, 0.0)
    return silu(total).astype(BF16)


def state_weight(first, step, running, lens_ref):
    rows = step.shape[0]
    last_begin = doc_start(first + rows - 1, lens_ref)
    position = first + lax.broadcasted_iota(jnp.int32, step.shape, 0)
    return jnp.where(
        position >= last_begin, step * jnp.exp(running[rows - 1 : rows] - running), 0.0
    )


def tail_lines(message, rows):
    block = message[rows:].astype(F32)
    return jnp.concatenate([block[at : at + 4] for at in range(0, block.shape[0], 4)], axis=1)


def reach(device, rows, lens_ref):
    return device - doc_start((device + 1) * rows - 1, lens_ref) // rows


def state_kernel(part, first_part, last_part, *refs):
    x_ref, bc_ref, dt_ref, wx_ref, bx_ref, wbc_ref, bbc_ref, dt_bias_ref, a_log_ref, lens_ref = refs[:10]
    refs = refs[10:]
    if first_part:
        x_edge_ref, bc_edge_ref = refs[:2]
        refs = refs[2:]
    if last_part:
        keys_ref, values_ref = refs[:2]
        refs = refs[2:]
    xc_ref, bcc_ref, state_ref = refs[:3]
    pad_ref = refs[-1]
    rows, width = x_ref.shape
    taps = wx_ref.shape[0]
    heads = width // HDIM
    here = lax.axis_index("seq")
    first = here * rows
    inside = insides(first, (rows, CHUNK), taps, lens_ref)
    step, running = rates(dt_ref, dt_bias_ref, a_log_ref)
    weight = state_weight(first, step, running, lens_ref)
    row = lax.broadcasted_iota(jnp.int32, weight.shape, 0)
    kept = (row >= taps - 1) | (reach(here, rows, lens_ref) == 0)
    weight = jnp.where(kept, weight, 0.0)[:, part * heads : (part + 1) * heads]
    slots = pad_ref.shape[0]

    def block(raw_ref, start, weight_ref, bias_ref, offset, slot):
        pad = pad_ref.at[slot]
        pad[0:8] = jnp.zeros((8, CHUNK), F32)
        pad[8:] = raw_ref[:, start : start + CHUNK].astype(F32)
        columns = slice(offset + start, offset + start + CHUNK)
        return conv(pad, rows, weight_ref[:, columns], bias_ref[columns].reshape(1, -1), inside)

    pair = block(bc_ref, 0, wbc_ref, bbc_ref, part * 2 * STATE, 0)
    bcc_ref[...] = pair
    turned = pair[:, :STATE].astype(F32).T.astype(BF16)
    for start in range(0, width, CHUNK):
        xc = block(x_ref, start, wx_ref, bx_ref, part * width, (start // CHUNK + 1) % slots)
        xc_ref[:, start : start + CHUNK] = xc
        weighted = (xc.astype(F32) * widen(weight, start, CHUNK)).astype(BF16)
        state_ref[:STATE, start : start + CHUNK] = jnp.dot(
            turned, weighted, preferred_element_type=F32
        ).astype(BF16)
    if first_part:
        edges = jnp.concatenate([x_edge_ref[...].astype(F32), bc_edge_ref[...].astype(F32)], axis=1)
        edges = edges[EDGE - 4 :]
        spare = -edges.shape[1] % width
        if spare:
            edges = jnp.concatenate([edges, jnp.zeros((4, spare), F32)], axis=1)
        pieces = [edges[:, at : at + width] for at in range(0, edges.shape[1], width)]
        while len(pieces) % (EDGE // 4):
            pieces.append(jnp.zeros_like(pieces[0]))
        state_ref[STATE:] = jnp.concatenate(pieces, axis=0).astype(BF16)
    if last_part:
        kv_ref = refs[3]
        kv_width = keys_ref.shape[1]
        kv_ref[:, :kv_width] = keys_ref[...]
        kv_ref[:, kv_width:] = values_ref[...]


def relay_kernel(part, offset, fresh, *refs):
    (
        x_ref, bc_ref, message_ref, got_ref, state_ref, dt_ref, wx_ref, bx_ref, wbc_ref, bbc_ref,
        dt_bias_ref, a_log_ref, lens_ref,
    ) = refs[:13]
    out_ref, pad_ref = refs[-2:]
    width = x_ref.shape[1]
    rows = dt_ref.shape[1]
    taps = wx_ref.shape[0]
    heads = width // HDIM
    here = lax.axis_index("seq")
    first = here * rows
    own = reach(here, rows, lens_ref) == 0
    inside = insides(first, (EDGE, CHUNK), taps, lens_ref)
    step, running = rates(dt_ref, dt_bias_ref, a_log_ref)
    row = lax.broadcasted_iota(jnp.int32, (EDGE, heads), 0)
    these = slice(part * heads, (part + 1) * heads)
    total = running[rows - 1 : rows, these]
    weight = step[:EDGE, these] * jnp.exp(total - running[:EDGE, these])
    weight = jnp.where((row < taps - 1) & jnp.logical_not(own), weight, 0.0)
    through = jnp.broadcast_to(jnp.exp(total), (8, heads))
    lines = tail_lines(message_ref, STATE)
    slots = pad_ref.shape[0]

    def top(raw_ref, start, line, weight_ref, bias_ref, base, slot):
        columns = slice(base + start, base + start + CHUNK)
        pad = pad_ref.at[slot]
        pad[4:8] = lines[:, line + start : line + start + CHUNK]
        pad[8:] = raw_ref[:, start : start + CHUNK].astype(F32)
        return conv(pad, EDGE, weight_ref[:, columns], bias_ref[columns].reshape(1, -1), inside)

    base = part * 2 * STATE
    inputs = top(bc_ref, 0, offset + base, wbc_ref, bbc_ref, base, 0)[:, :STATE]
    turned = inputs.astype(F32).T.astype(BF16)
    for start in range(0, width, CHUNK):
        columns = slice(start, start + CHUNK)
        xc = top(x_ref, start, part * width, wx_ref, bx_ref, part * width, (start // CHUNK + 1) % slots)
        weighted = (xc.astype(F32) * widen(weight, start, CHUNK)).astype(BF16)
        full = state_ref[:STATE, columns].astype(F32) + jnp.dot(
            turned, weighted, preferred_element_type=F32
        )
        full = full + widen(through, start, CHUNK)[0:1] * got_ref[:STATE, columns].astype(F32)
        other = refs[13] if fresh else state_ref
        out_ref[:, columns] = jnp.where(own, other[:STATE, columns].astype(F32), full).astype(BF16)


def local_kernel(groups, *refs):
    (
        x_ref, bc_ref, message_ref, dt_ref, wx_ref, bx_ref, wbc_ref, bbc_ref,
        dt_bias_ref, a_log_ref, skip_ref, lens_ref,
    ) = refs[:12]
    xc_refs = refs[12 : 12 + groups]
    bcc_refs = refs[12 + groups : 12 + 2 * groups]
    out_ref, c_ref, entry_ref, pad_ref = refs[12 + 2 * groups :]
    rows, per_group = xc_refs[0].shape
    width = groups * per_group
    taps = wx_ref.shape[0]
    first = lax.axis_index("seq") * rows
    inside = insides(first, (EDGE, CHUNK), taps, lens_ref)
    lines = tail_lines(message_ref, STATE)
    slots = pad_ref.shape[0]

    def top(raw_ref, start, weight_ref, bias_ref, offset, slot):
        columns = slice(start, start + CHUNK)
        pad = pad_ref.at[slot]
        pad[4:8] = lines[:, offset + start : offset + start + CHUNK]
        pad[8:] = raw_ref[:, columns].astype(F32)
        return conv(pad, EDGE, weight_ref[:, columns], bias_ref[columns].reshape(1, -1), inside)

    row = lax.broadcasted_iota(jnp.int32, (rows, rows), 0)
    column = lax.broadcasted_iota(jnp.int32, (rows, rows), 1)
    begin = doc_start(first + row, lens_ref)
    linked = (row >= column) & (first + column >= begin)
    step, running = rates(dt_ref, dt_bias_ref, a_log_ref)
    position = first + lax.broadcasted_iota(jnp.int32, running.shape, 0)
    entry_ref[...] = jnp.where(doc_start(position, lens_ref) < first, jnp.exp(running), 0.0)
    turned_running = running.T
    turned_step = step.T
    skip = skip_ref[...].reshape(1, -1)
    skip = jnp.broadcast_to(skip, (8, skip.shape[1]))
    pair_width = 2 * HDIM
    lane = lax.broadcasted_iota(jnp.int32, (rows, pair_width), 1)
    for group in range(groups):
        base = group * 2 * STATE
        pair = jnp.concatenate(
            [top(bc_ref, base, wbc_ref, bbc_ref, width, group % slots), bcc_refs[group][EDGE:]], axis=0
        )
        inputs = pair[:, :STATE]
        outputs = pair[:, STATE:]
        c_ref[:, group * STATE : (group + 1) * STATE] = outputs
        meet = lax.dot_general(
            outputs, inputs, (((1,), (1,)), ((), ())), preferred_element_type=F32
        )
        meet = jnp.where(linked, meet, 0.0)
        for chunk in range(0, per_group, CHUNK):
            at = group * per_group + chunk
            xc_all = jnp.concatenate(
                [
                    top(x_ref, at, wx_ref, bx_ref, 0, (chunk // CHUNK) % slots),
                    xc_refs[group][EDGE:, chunk : chunk + CHUNK],
                ],
                axis=0,
            )
            wide_skip = widen(skip, at, CHUNK)[0:1]
            for start in range(0, CHUNK, pair_width):
                parts = []
                for head in ((at + start) // HDIM, (at + start) // HDIM + 1):
                    spread = running[:, head : head + 1] - turned_running[head : head + 1]
                    decay = jnp.exp(jnp.minimum(spread, 0.0))
                    parts.append((decay * (meet * turned_step[head : head + 1])).astype(BF16))
                mix = jnp.concatenate(parts, axis=1)
                xc = xc_all[:, start : start + pair_width]
                zero = jnp.zeros_like(xc)
                stacked = jnp.concatenate(
                    [jnp.where(lane < HDIM, xc, zero), jnp.where(lane < HDIM, zero, xc)], axis=0
                )
                value = jnp.dot(mix, stacked, preferred_element_type=F32)
                out_ref[:, at + start : at + start + pair_width] = (
                    value + xc.astype(F32) * wide_skip[:, start : start + pair_width]
                )


def attend_kernel(hops, *refs):
    q_ref = refs[0]
    kv_refs = refs[1 : 2 + hops]
    lens_ref, out_ref = refs[2 + hops :]
    rows = q_ref.shape[0]
    kv_heads = kv_refs[0].shape[1] // (2 * ADIM)
    share = QHEADS // KVHEADS
    count = rows * (hops + 1)
    here = lax.axis_index("seq")
    row = here * rows + lax.broadcasted_iota(jnp.int32, (rows, count), 0)
    column = (here - hops) * rows + lax.broadcasted_iota(jnp.int32, (rows, count), 1)
    allowed = (column <= row) & (column >= doc_start(row, lens_ref))
    scale = ADIM ** (-0.5)
    ones = jnp.ones((count, ADIM), BF16)
    for head in range(kv_heads):
        low = head * ADIM
        keys = jnp.concatenate([ref[:, low : low + ADIM] for ref in kv_refs], axis=0)
        low = (kv_heads + head) * ADIM
        values = jnp.concatenate([ref[:, low : low + ADIM] for ref in kv_refs], axis=0)
        values = jnp.concatenate([values, ones], axis=1)
        for part in range(share):
            low = (head * share + part) * ADIM
            scores = lax.dot_general(
                q_ref[:, low : low + ADIM], keys, (((1,), (1,)), ((), ())), preferred_element_type=F32
            )
            scores = jnp.where(allowed, scores * scale, BARRED)
            expo = jnp.exp(scores - jnp.max(scores, axis=1, keepdims=True))
            summed = jnp.dot(expo.astype(BF16), values, preferred_element_type=F32)
            out_ref[:, low : low + ADIM] = (summed[:, :ADIM] / summed[:, ADIM:]).astype(BF16)


def norm_kernel(part, hops, *refs):
    mixed_ref, c_ref, entry_ref, z_ref, gain_ref, lens_ref = refs[:6]
    got_refs = refs[6 : 6 + hops]
    out_ref, gated_ref = refs[-2:]
    rows, width = mixed_ref.shape
    heads = width // HDIM
    entry = entry_ref[:, part * heads : (part + 1) * heads]
    outputs = c_ref[:, part * STATE : (part + 1) * STATE]
    before = reach(lax.axis_index("seq") - 1, rows, lens_ref)
    squares = jnp.zeros((rows, 1), F32)
    for start in range(0, width, CHUNK):
        columns = slice(start, start + CHUNK)
        state = got_refs[0][:STATE, columns]
        for hop in range(1, hops):
            state = jnp.where(before == hop, got_refs[hop][:STATE, columns], state)
        carried = jnp.dot(outputs, state, preferred_element_type=F32)
        mixed = mixed_ref[:, columns] + carried * widen(entry, start, CHUNK)
        gated = mixed * silu(z_ref[:, columns].astype(F32))
        gated_ref[:, columns] = gated
        squares = squares + jnp.sum(gated * gated, axis=1, keepdims=True)
    multiplier = lax.rsqrt(squares * (1.0 / width) + EPSILON)
    for start in range(0, width, CHUNK):
        columns = slice(start, start + CHUNK)
        gain = gain_ref[part * width + start : part * width + start + CHUNK]
        out_ref[:, columns] = (gated_ref[:, columns] * multiplier * gain.reshape(1, -1)).astype(BF16)


WHOLE = pl.BlockSpec(memory_space=pltpu.VMEM)
SCALARS = pl.BlockSpec(memory_space=pltpu.SMEM)
UNTOUCHED = pl.BlockSpec(memory_space=pl.ANY)


def tile(rows, columns, row, column):
    return pl.BlockSpec((rows, columns), lambda step: (row, column))


def call(kernel, name, outs, operands, specs, out_specs=None, scratch=(), flops=KERNEL_FLOPS, aliases={}, limit=VMEM_LIMIT, after=()):
    operands = [*operands, *after]
    specs = [*specs, *([UNTOUCHED] * len(after))]
    inputs = len(operands) - len(after)
    moved = sum(math.prod(a.shape) * a.dtype.itemsize for a in (*operands, *outs))
    def body(*refs):
        kernel(*refs[:inputs], *refs[inputs + len(after) :])

    return pl.pallas_call(
        body,
        name=name,
        grid=(1,),
        out_shape=outs,
        in_specs=specs,
        out_specs=[WHOLE] * len(outs) if out_specs is None else out_specs,
        scratch_shapes=list(scratch),
        input_output_aliases=aliases,
        compiler_params=pltpu.CompilerParams(vmem_limit_bytes=limit),
        cost_estimate=pl.CostEstimate(flops=flops, bytes_accessed=moved, transcendentals=0),
    )(*operands)


def onward(value, first=0):
    count = lax.axis_size("seq")
    return lax.ppermute(value, "seq", [(source, source + 1) for source in range(first, count - 1)])


def shards(
    x_raw,
    bc_raw,
    z_gate,
    dt_raw,
    conv_x_weight,
    conv_x_bias,
    conv_bc_weight,
    conv_bc_bias,
    dt_bias,
    a_log,
    skip_d,
    norm_gain,
    queries,
    keys,
    values,
    doc_lens,
):
    rows, width = x_raw.shape
    bc_width = bc_raw.shape[1]
    heads = dt_raw.shape[1]
    groups = bc_width // (2 * STATE)
    per_group = width // groups
    count = lax.axis_size("seq")
    longest = rows * count // 2
    hops = min(count - 1, -(-(longest - 1) // rows))
    assert hops * rows >= longest and (hops <= 2 or groups == 1)
    shape = jax.ShapeDtypeStruct
    dt = dt_raw.T
    params = [dt, conv_x_weight, conv_x_bias, conv_bc_weight, conv_bc_bias, dt_bias, a_log]
    pieces = -(-(width + bc_width) // per_group)
    tail_rows = EDGE * -(-4 * pieces // EDGE)
    last_edge = rows // EDGE - 1

    xcs, bccs, states = [], [], []
    for part in range(groups):
        first_part, last_part = part == 0, part == groups - 1
        outs = [
            shape((rows, per_group), BF16),
            shape((rows, 2 * STATE), BF16),
            shape((STATE + tail_rows * first_part, per_group), BF16),
        ]
        operands = [x_raw, bc_raw, *params, doc_lens]
        specs = [tile(rows, per_group, 0, part), tile(rows, 2 * STATE, 0, part)] + [WHOLE] * 7 + [SCALARS]
        if first_part:
            operands += [x_raw, bc_raw]
            specs += [tile(EDGE, width, last_edge, 0), tile(EDGE, bc_width, last_edge, 0)]
        if last_part:
            outs.append(shape((rows, 2 * keys.shape[1]), BF16))
            operands += [keys, values]
            specs += [WHOLE] * 2
        got = call(
            functools.partial(state_kernel, part, first_part, last_part),
            f"state_part{part}",
            outs,
            operands,
            specs,
            scratch=[pltpu.VMEM((4, rows + 8, CHUNK), F32)],
            limit=VMEM_ALL if first_part else VMEM_LIMIT,
        )
        xcs.append(got[0])
        bccs.append(got[1])
        states.append(got[2])
    kvs = [got[3]]
    for hop in range(hops):
        kvs.append(onward(kvs[-1], hop))

    slots = [onward(states[0])]
    mixed, c_out, entry = call(
        functools.partial(local_kernel, groups),
        "local_mix",
        [shape((rows, width), F32), shape((rows, groups * STATE), BF16), shape((rows, heads), F32)],
        [x_raw, bc_raw, slots[0], *params, skip_d, doc_lens, *xcs, *bccs],
        [tile(EDGE, width, 0, 0), tile(EDGE, bc_width, 0, 0)]
        + [WHOLE] * 9
        + [SCALARS]
        + [WHOLE] * 2 * groups,
        scratch=[pltpu.VMEM((4, EDGE + 8, CHUNK), F32)],
        after=[kvs[1]],
    )
    for slot in range(2, hops + groups):
        part = min(slot - 1, groups) - 1
        fresh = slot <= groups
        operands = [x_raw, bc_raw, slots[0], slots[-1], states[part], *params, doc_lens]
        specs = [tile(EDGE, per_group, 0, part), tile(EDGE, 2 * STATE, 0, part)] + [WHOLE] * 10 + [SCALARS]
        if fresh:
            operands.append(states[slot - 1])
            specs.append(WHOLE)
        (passed,) = call(
            functools.partial(relay_kernel, part, width, fresh),
            f"relay_slot{slot}",
            [shape((STATE, per_group), BF16)],
            operands,
            specs,
            scratch=[pltpu.VMEM((4, EDGE + 8, CHUNK), F32)],
            after=[entry] if slot == hops + groups - 1 else [],
        )
        slots.append(onward(passed, max(0, slot - groups)))

    (attn_out,) = call(
        functools.partial(attend_kernel, hops),
        "attend",
        [shape(queries.shape, BF16)],
        [queries, *reversed(kvs), doc_lens],
        [WHOLE] * (hops + 2) + [SCALARS],
    )
    mamba_out = None
    for part in range(groups):
        operands = [mixed, c_out, entry, z_gate, norm_gain, doc_lens, *slots[part : part + hops]]
        block = tile(rows, per_group, 0, part)
        specs = [block, WHOLE, WHOLE, block, WHOLE, SCALARS] + [WHOLE] * hops
        aliases = {}
        if mamba_out is not None:
            operands.append(mamba_out)
            specs.append(UNTOUCHED)
            aliases = {len(operands) - 1: 0}
        (mamba_out,) = call(
            functools.partial(norm_kernel, part, hops),
            f"norm_part{part}",
            [shape((rows, width), BF16)],
            operands,
            specs,
            out_specs=[block],
            scratch=[pltpu.VMEM((rows, per_group), F32)],
            aliases=aliases,
        )
    return (mamba_out, attn_out)


def solution(mesh):
    split = P(("groups", "seq"), "dp")
    placed = (
        split,
        split,
        split,
        split,
        P(None, "dp"),
        P("dp"),
        P(None, "dp"),
        P("dp"),
        P("dp"),
        P("dp"),
        P("dp"),
        P("dp"),
        split,
        split,
        split,
        P("groups"),
    )
    return jax.shard_map(
        shards,
        mesh=mesh,
        in_specs=placed,
        out_specs=(split, split),
        check_vma=False,
    )
```

time: 51.2 us -> 39.4 us (0.77)
  the two profiles are of different devices: /device:TPU:0 before, /device:TPU:22 now
where the time goes in v3:
time: 39.4 us; the launch traced here: 39.1 us
  Pallas kernels  16.1 us (41%)
  starting transfers between devices  14.2 us (36%)
  waiting for transfers between devices  7.11 us (18%)
  between operations  0.96 us (2%)
  local copies, waits for them, and re-layouts  0.71 us (2%)
    pallas_call x8, Pallas kernels, call(): pl.pallas_call(body, name=name, grid=(1,), out_shape=outs, in_specs=specs...  16.1 us
    ppermute x5, starting transfers between devices, onward(): lax.ppermute(value, 'seq', [(source, source + 1) for source in range(firs...  14.2 us
    ppermute x5, waiting for transfers between devices, onward(): lax.ppermute(value, 'seq', [(source, source + 1) for source in range(firs...  7.11 us
  transfers between devices with their start and end apart: 5, of which 3 were waited for; matrix products, arithmetic and copies ran while one was open for 0% of the time, Pallas kernels for 29%

profile of v3, /device:TPU:22, one launch (start us, length us, event | category | flops | bytes accessed | tf_op | source)
XLA Modules:
  0.0 39.1 jit_solution(6106749287825203765)
XLA Ops:
  0.7 3.1 %state_part0.1 = (bf16[128,1024]{1,0:T(8,128)(2,1)}, bf16[128,256]{1,0:T(8,128)(2,1)}, bf16[144,1024]{1,0:T(8,128)(2,1)}) custom-call(bf16[128,2048]{1,0:T(8,128)(2,1)} %refs_0_.10, bf16[128,512]{1,0:T(8,128)(2,1)} %refs_1_.9, f32[32,128]{1,0:T(8,128)} %bitcast.1, f32[4,2048]{1,0:T(4,128)} %refs_6_.9, f32[2048]{0:T(1024)} %refs_7_.9, f32[4,512]{1,0:T(4,128)} %refs_8_.9, ...), custom_call_target="tpu_custom_call" | custom-call | flops 2000000000 | bytes 2001168 | tf_op jit(solution)/shard_map/state_part0/pallas_call | solution.py:358
  3.9 0.0 copy-start.16
  3.9 0.0 copy-start.2
  3.9 3.6 %collective-permute-start = (bf16[144,1024]{1,0:T(8,128)(2,1)}, bf16[144,1024]{1,0:T(8,128)(2,1)S(1)}, u32[]{:S(2)}, u32[]{:S(2)}) collective-permute-start(bf16[144,1024]{1,0:T(8,128)(2,1)} %get-tuple-element.12.refs_4_), channel_id=1, source_target_pairs={{0,4},{4,8},{8,12},{1,5},{5,9},{9,13},{2,6},{6,10},{10,14},{3,7},{... | collective-permute-start | bytes 884744 | tf_op jit(solution)/shard_map/ppermute | solution.py:374
  7.5 0.0 copy-done
  7.5 0.0 copy-done.4
  7.5 0.0 copy-done.5
  7.5 0.0 copy-done.6
  7.6 0.0 copy-done.7
  7.6 0.0 copy-done.8
  7.6 0.0 copy-done.9
  7.6 0.0 copy-done.10
  7.6 1.8 %state_part1.1 = (bf16[128,1024]{1,0:T(8,128)(2,1)S(1)}, bf16[128,256]{1,0:T(8,128)(2,1)S(1)}, bf16[128,1024]{1,0:T(8,128)(2,1)S(1)}, bf16[128,512]{1,0:T(8,128)(2,1)S(1)}) custom-call(bf16[128,2048]{1,0:T(8,128)(2,1)S(1)} %copy-done, bf16[128,512]{1,0:T(8,128)(2,1)S(1)} %copy-done.4, f32[32,128]{1,0:T(8,128)S(1)} %bitcast.2, f32[4,2048]{1,0:T(4,128)S(1)} %copy-done.7, ...), custom_call_target="tpu_custom_call" | custom-call | flops 2000000000 | bytes 1575184 | tf_op jit(solution)/shard_map/state_part1/pallas_call | solution.py:358
  9.5 1.9 %collective-permute-start.1 = (bf16[128,512]{1,0:T(8,128)(2,1)S(1)}, bf16[128,512]{1,0:T(8,128)(2,1)S(1)}, u32[]{:S(2)}, u32[]{:S(2)}) collective-permute-start(bf16[128,512]{1,0:T(8,128)(2,1)S(1)} %get-tuple-element.17.refs_3_), channel_id=1, source_target_pairs={{0,4},{4,8},{8,12},{1,5},{5,9},{9,13},{2,6},{6,10},{10,14},{3,7},{... | collective-permute-start | bytes 393224 | tf_op jit(solution)/shard_map/ppermute | solution.py:374
  11.4 4.6 %collective-permute-done.refs_2_.refs_3_.refs_6_ = bf16[144,1024]{1,0:T(8,128)(2,1)S(1)} collective-permute-done((bf16[144,1024]{1,0:T(8,128)(2,1)}, bf16[144,1024]{1,0:T(8,128)(2,1)S(1)}, u32[]{:S(2)}, u32[]{:S(2)}) %collective-permute-start) | collective-permute-done | bytes 294944 | tf_op jit(solution)/shard_map/ppermute | solution.py:374
  16.0 1.6 %relay_slot2.1 = bf16[128,1024]{1,0:T(8,128)(2,1)S(1)} custom-call(bf16[128,2048]{1,0:T(8,128)(2,1)S(1)} %copy-done, bf16[128,512]{1,0:T(8,128)(2,1)S(1)} %copy-done.4, bf16[144,1024]{1,0:T(8,128)(2,1)S(1)} %collective-permute-done.refs_2_.refs_3_.refs_6_, bf16[144,1024]{1,0:T(8,128)(2,1)S(1)} %collective-permute-done.refs_2_.refs_3_.refs_6_, ...), custom_call_target="tpu_custom_call" | custom-call | flops 2000000000 | bytes 2132240 | tf_op jit(solution)/shard_map/relay_slot2/pallas_call | solution.py:358
  17.7 3.5 %collective-permute-start.2 = (bf16[128,1024]{1,0:T(8,128)(2,1)S(1)}, bf16[128,1024]{1,0:T(8,128)(2,1)S(1)}, u32[]{:S(2)}, u32[]{:S(2)}) collective-permute-start(bf16[128,1024]{1,0:T(8,128)(2,1)S(1)} %relay_slot2.1), channel_id=1, source_target_pairs={{0,4},{4,8},{8,12},{1,5},{5,9},{9,13},{2,6},{6,10},{10,14},{3,7},{... | collective-permute-start | bytes 786440 | tf_op jit(solution)/shard_map/ppermute | solution.py:374
  21.2 0.0 collective-permute-done.1.refs_16_.refs_2_
  21.2 1.9 %collective-permute-start.4 = (bf16[128,512]{1,0:T(8,128)(2,1)S(1)}, bf16[128,512]{1,0:T(8,128)(2,1)S(1)}, u32[]{:S(2)}, u32[]{:S(2)}) collective-permute-start(bf16[128,512]{1,0:T(8,128)(2,1)S(1)} %collective-permute-done.1.refs_16_.refs_2_), channel_id=1, source_target_pairs={{4,8},{8,12},{5,9},{9,13},{6,10},{10,14},{7,11},{11,15},{20,24},{2... | collective-permute-start | bytes 393224 | tf_op jit(solution)/shard_map/ppermute | solution.py:374
  23.1 0.0 copy-start.13
  23.1 0.6 %copy-done.13 = f32[32]{0:T(128)S(1)} copy-done((f32[32]{0:T(128)S(1)}, f32[32]{0:T(128)}, u32[]{:S(2)}) %copy-start.13) | copy-done | bytes 152
  23.8 2.2 %local_mix.1 = (f32[128,2048]{1,0:T(8,128)S(1)}, bf16[128,256]{1,0:T(8,128)(2,1)S(1)}, f32[128,32]{1,0:T(8,128)S(1)}) custom-call(bf16[128,2048]{1,0:T(8,128)(2,1)S(1)} %copy-done, bf16[128,512]{1,0:T(8,128)(2,1)S(1)} %copy-done.4, bf16[144,1024]{1,0:T(8,128)(2,1)S(1)} %collective-permute-done.refs_2_.refs_3_.refs_6_, f32[32,128]{1,0:T(8,128)S(1)} %bitcast.4, ...), custom_call_target="tpu_custom_call" | custom-call | flops 2000000000 | bytes 2935184 | tf_op jit(solution)/shard_map/local_mix/pallas_call | solution.py:358
  26.0 1.4 %collective-permute-done.2.refs_3_.refs_7_.refs_6_ = bf16[128,1024]{1,0:T(8,128)(2,1)S(1)} collective-permute-done((bf16[128,1024]{1,0:T(8,128)(2,1)S(1)}, bf16[128,1024]{1,0:T(8,128)(2,1)S(1)}, u32[]{:S(2)}, u32[]{:S(2)}) %collective-permute-start.2) | collective-permute-done | bytes 262176 | tf_op jit(solution)/shard_map/ppermute | solution.py:374
  27.4 1.6 %relay_slot3.1 = bf16[128,1024]{1,0:T(8,128)(2,1)S(1)} custom-call(bf16[128,2048]{1,0:T(8,128)(2,1)S(1)} %copy-done, bf16[128,512]{1,0:T(8,128)(2,1)S(1)} %copy-done.4, bf16[144,1024]{1,0:T(8,128)(2,1)S(1)} %collective-permute-done.refs_2_.refs_3_.refs_6_, bf16[128,1024]{1,0:T(8,128)(2,1)S(1)} %collective-permute-done.2.refs_3_.refs_7_.refs_6_, ...), custom_call_target="tpu_custom_call" | custom-call | flops 2000000000 | bytes 1820944 | tf_op jit(solution)/shard_map/relay_slot3/pallas_call | solution.py:358
  29.0 0.0 copy-start.1
  29.0 0.0 copy-start.11
  29.0 3.3 %collective-permute-start.3 = (bf16[128,1024]{1,0:T(8,128)(2,1)S(1)}, bf16[128,1024]{1,0:T(8,128)(2,1)S(1)}, u32[]{:S(2)}, u32[]{:S(2)}) collective-permute-start(bf16[128,1024]{1,0:T(8,128)(2,1)S(1)} %relay_slot3.1), channel_id=1, source_target_pairs={{4,8},{8,12},{5,9},{9,13},{6,10},{10,14},{7,11},{11,15},{20,24},{2... | collective-permute-start | bytes 786440 | tf_op jit(solution)/shard_map/ppermute | solution.py:374
  32.3 0.0 collective-permute-done.4.refs_1_
  32.3 2.3 %attend.1 = bf16[128,1024]{1,0:T(8,128)(2,1)} custom-call(bf16[128,1024]{1,0:T(8,128)(2,1)S(1)} %copy-done.3, bf16[128,512]{1,0:T(8,128)(2,1)S(1)} %collective-permute-done.4.refs_1_, bf16[128,512]{1,0:T(8,128)(2,1)S(1)} %collective-permute-done.1.refs_16_.refs_2_, bf16[128,512]{1,0:T(8,128)(2,1)S(1)} %get-tuple-element.17.refs_3_, s32[4]{0:T(128)S(1)} %copy-done.16), custom_call_target="tpu_custom_call" | custom-call | flops 2000000000 | bytes 917520 | tf_op jit(solution)/shard_map/attend/pallas_call | solution.py:358
  34.6 1.7 %norm_part0.1.refs_8_ = bf16[128,2048]{1,0:T(8,128)(2,1)} custom-call(f32[128,2048]{1,0:T(8,128)S(1)} %get-tuple-element.18.refs_0_, bf16[128,256]{1,0:T(8,128)(2,1)S(1)} %get-tuple-element.19.refs_1_, f32[128,32]{1,0:T(8,128)S(1)} %get-tuple-element.20.refs_13_.refs_2_, bf16[128,2048]{1,0:T(8,128)(2,1)S(1)} %copy-done.1, f32[2048]{0:T(1024)S(1)} %copy-done.11, ...), custom_call_target="tpu_custom_call" | custom-call | flops 2000000000 | bytes 2744336 | tf_op jit(solution)/shard_map/norm_part0/pallas_call | solution.py:358
  36.3 1.1 %collective-permute-done.3.refs_7_ = bf16[128,1024]{1,0:T(8,128)(2,1)S(1)} collective-permute-done((bf16[128,1024]{1,0:T(8,128)(2,1)S(1)}, bf16[128,1024]{1,0:T(8,128)(2,1)S(1)}, u32[]{:S(2)}, u32[]{:S(2)}) %collective-permute-start.3) | collective-permute-done | bytes 262176 | tf_op jit(solution)/shard_map/ppermute | solution.py:374
  37.4 1.7 %norm_part1.1 = bf16[128,2048]{1,0:T(8,128)(2,1)} custom-call(f32[128,2048]{1,0:T(8,128)S(1)} %get-tuple-element.18.refs_0_, bf16[128,256]{1,0:T(8,128)(2,1)S(1)} %get-tuple-element.19.refs_1_, f32[128,32]{1,0:T(8,128)S(1)} %get-tuple-element.20.refs_13_.refs_2_, bf16[128,2048]{1,0:T(8,128)(2,1)S(1)} %copy-done.1, ...), custom_call_target="tpu_custom_call", output_to_operand_aliasing={{}: (8, {})} | custom-call | flops 2000000000 | bytes 3235856 | tf_op jit(solution)/shard_map/norm_part1/pallas_call | solution.py:358
  (24 shorter events, 0.0 us)
Async XLA Ops:
  0.6 6.9 %copy-start = (bf16[128,2048]{1,0:T(8,128)(2,1)S(1)}, bf16[128,2048]{1,0:T(8,128)(2,1)}, u32[]{:S(2)}) copy-start(bf16[128,2048]{1,0:T(8,128)(2,1)} %refs_0_.10) | copy-start | bytes 1572868
  0.6 6.9 %copy-start.4 = (bf16[128,512]{1,0:T(8,128)(2,1)S(1)}, bf16[128,512]{1,0:T(8,128)(2,1)}, u32[]{:S(2)}) copy-start(bf16[128,512]{1,0:T(8,128)(2,1)} %refs_1_.9) | copy-start | bytes 393220
  0.7 6.9 %copy-start.5 = (bf16[128,256]{1,0:T(8,128)(2,1)S(1)}, bf16[128,256]{1,0:T(8,128)(2,1)}, u32[]{:S(2)}) copy-start(bf16[128,256]{1,0:T(8,128)(2,1)} %refs_10_.6) | copy-start | bytes 196612
  0.7 6.9 %copy-start.6 = (bf16[128,256]{1,0:T(8,128)(2,1)S(1)}, bf16[128,256]{1,0:T(8,128)(2,1)}, u32[]{:S(2)}) copy-start(bf16[128,256]{1,0:T(8,128)(2,1)} %refs_11_.6) | copy-start | bytes 196612
  0.7 6.9 %copy-start.7 = (f32[4,2048]{1,0:T(4,128)S(1)}, f32[4,2048]{1,0:T(4,128)}, u32[]{:S(2)}) copy-start(f32[4,2048]{1,0:T(4,128)} %refs_6_.9) | copy-start | bytes 98308
  0.7 6.9 %copy-start.8 = (f32[128,32]{0,1:T(8,128)S(1)}, f32[128,32]{0,1:T(8,128)}, u32[]{:S(2)}) copy-start(f32[128,32]{0,1:T(8,128)} %param.19) | copy-start | bytes 49156
  0.7 6.9 %copy-start.9 = (f32[2048]{0:T(1024)S(1)}, f32[2048]{0:T(1024)}, u32[]{:S(2)}) copy-start(f32[2048]{0:T(1024)} %refs_7_.9) | copy-start | bytes 24580
  0.7 6.9 %copy-start.10 = (f32[4,512]{1,0:T(4,128)S(1)}, f32[4,512]{1,0:T(4,128)}, u32[]{:S(2)}) copy-start(f32[4,512]{1,0:T(4,128)} %refs_8_.9) | copy-start | bytes 24580
  0.7 6.9 %copy-start.12 = (f32[512]{0:T(512)S(1)}, f32[512]{0:T(512)}, u32[]{:S(2)}) copy-start(f32[512]{0:T(512)} %refs_9_.9) | copy-start | bytes 6148
  3.9 3.7 %copy-start.14 = (f32[32]{0:T(128)S(1)}, f32[32]{0:T(128)}, u32[]{:S(2)}) copy-start(f32[32]{0:T(128)} %refs_10_.9) | copy-start | bytes 388
  3.9 3.8 %copy-start.15 = (f32[32]{0:T(128)S(1)}, f32[32]{0:T(128)}, u32[]{:S(2)}) copy-start(f32[32]{0:T(128)} %refs_11_.9) | copy-start | bytes 388
  3.9 3.8 %copy-start.16 = (s32[4]{0:T(128)S(1)}, s32[4]{0:T(128)}, u32[]{:S(2)}) copy-start(s32[4]{0:T(128)} %refs_4_.11) | copy-start | bytes 52
  3.9 12.1 %copy-start.2 = (bf16[144,1024]{1,0:T(8,128)(2,1)S(1)}, bf16[144,1024]{1,0:T(8,128)(2,1)}, u32[]{:S(2)}) copy-start(bf16[144,1024]{1,0:T(8,128)(2,1)} %get-tuple-element.12.refs_4_) | copy-start | bytes 884740
  3.9 12.1 %collective-permute-start = (bf16[144,1024]{1,0:T(8,128)(2,1)}, bf16[144,1024]{1,0:T(8,128)(2,1)S(1)}, u32[]{:S(2)}, u32[]{:S(2)}) collective-permute-start(bf16[144,1024]{1,0:T(8,128)(2,1)} %get-tuple-element.12.refs_4_), channel_id=1, source_target_pairs={{0,4},{4,8},{8,12},{1,5},{5,9},{9,13},{2,6},{6,10},{10,14},{3,7},{... | collective-permute-start | bytes 884744 | tf_op jit(solution)/shard_map/ppermute | solution.py:374
  9.5 11.7 %collective-permute-start.1 = (bf16[128,512]{1,0:T(8,128)(2,1)S(1)}, bf16[128,512]{1,0:T(8,128)(2,1)S(1)}, u32[]{:S(2)}, u32[]{:S(2)}) collective-permute-start(bf16[128,512]{1,0:T(8,128)(2,1)S(1)} %get-tuple-element.17.refs_3_), channel_id=1, source_target_pairs={{0,4},{4,8},{8,12},{1,5},{5,9},{9,13},{2,6},{6,10},{10,14},{3,7},{... | collective-permute-start | bytes 393224 | tf_op jit(solution)/shard_map/ppermute | solution.py:374
  16.0 7.1 %copy-start.17 = (bf16[128,1024]{1,0:T(8,128)(2,1)S(1)}, bf16[128,1024]{1,0:T(8,128)(2,1)}, u32[]{:S(2)}) copy-start(bf16[128,1024]{1,0:T(8,128)(2,1)} %get-tuple-element.13.refs_12_) | copy-start | bytes 786436
  16.0 7.1 %copy-start.18 = (bf16[128,256]{1,0:T(8,128)(2,1)S(1)}, bf16[128,256]{1,0:T(8,128)(2,1)}, u32[]{:S(2)}) copy-start(bf16[128,256]{1,0:T(8,128)(2,1)} %get-tuple-element.15.refs_14_) | copy-start | bytes 196612
  17.7 9.7 %collective-permute-start.2 = (bf16[128,1024]{1,0:T(8,128)(2,1)S(1)}, bf16[128,1024]{1,0:T(8,128)(2,1)S(1)}, u32[]{:S(2)}, u32[]{:S(2)}) collective-permute-start(bf16[128,1024]{1,0:T(8,128)(2,1)S(1)} %relay_slot2.1), channel_id=1, source_target_pairs={{0,4},{4,8},{8,12},{1,5},{5,9},{9,13},{2,6},{6,10},{10,14},{3,7},{... | collective-permute-start | bytes 786440 | tf_op jit(solution)/shard_map/ppermute | solution.py:374
  21.2 11.1 %collective-permute-start.4 = (bf16[128,512]{1,0:T(8,128)(2,1)S(1)}, bf16[128,512]{1,0:T(8,128)(2,1)S(1)}, u32[]{:S(2)}, u32[]{:S(2)}) collective-permute-start(bf16[128,512]{1,0:T(8,128)(2,1)S(1)} %collective-permute-done.1.refs_16_.refs_2_), channel_id=1, source_target_pairs={{4,8},{8,12},{5,9},{9,13},{6,10},{10,14},{7,11},{11,15},{20,24},{2... | collective-permute-start | bytes 393224 | tf_op jit(solution)/shard_map/ppermute | solution.py:374
  23.1 0.7 %copy-start.13 = (f32[32]{0:T(128)S(1)}, f32[32]{0:T(128)}, u32[]{:S(2)}) copy-start(f32[32]{0:T(128)} %refs_10_.7) | copy-start | bytes 388
  27.4 5.0 %copy-start.3 = (bf16[128,1024]{1,0:T(8,128)(2,1)S(1)}, bf16[128,1024]{1,0:T(8,128)(2,1)}, u32[]{:S(2)}) copy-start(bf16[128,1024]{1,0:T(8,128)(2,1)} %refs_0_.11) | copy-start | bytes 786436
  29.0 5.6 %copy-start.1 = (bf16[128,2048]{1,0:T(8,128)(2,1)S(1)}, bf16[128,2048]{1,0:T(8,128)(2,1)}, u32[]{:S(2)}) copy-start(bf16[128,2048]{1,0:T(8,128)(2,1)} %refs_3_.7) | copy-start | bytes 1572868
  29.0 5.6 %copy-start.11 = (f32[2048]{0:T(1024)S(1)}, f32[2048]{0:T(1024)}, u32[]{:S(2)}) copy-start(f32[2048]{0:T(1024)} %refs_4_.10) | copy-start | bytes 24580
  29.0 8.4 %collective-permute-start.3 = (bf16[128,1024]{1,0:T(8,128)(2,1)S(1)}, bf16[128,1024]{1,0:T(8,128)(2,1)S(1)}, u32[]{:S(2)}, u32[]{:S(2)}) collective-permute-start(bf16[128,1024]{1,0:T(8,128)(2,1)S(1)} %relay_slot3.1), channel_id=1, source_target_pairs={{4,8},{8,12},{5,9},{9,13},{6,10},{10,14},{7,11},{11,15},{20,24},{2... | collective-permute-start | bytes 786440 | tf_op jit(solution)/shard_map/ppermute | solution.py:374

commit v4 on v3

--- a/solution.py
+++ b/solution.py
@@ -63,8 +63,12 @@
     rows = step.shape[0]
     row = lax.broadcasted_iota(jnp.int32, (rows, rows), 0)
     column = lax.broadcasted_iota(jnp.int32, (rows, rows), 1)
-    lower = (row >= column).astype(F32)
-    return step, jnp.dot(lower, rate, precision=HIGHEST, preferred_element_type=F32)
+    lower = (row >= column).astype(F32).astype(BF16)
+    high = rate.astype(BF16)
+    middle, low = halves(rate - high.astype(F32))
+    parts = jnp.concatenate([high, middle, low], axis=0)
+    lowers = jnp.concatenate([lower, lower, lower], axis=1)
+    return step, jnp.dot(lowers, parts, preferred_element_type=F32)
 
 
 def insides(first, shape, taps, lens_ref):
@@ -158,82 +162,130 @@
         kv_ref[:, kv_width:] = values_ref[...]
 
 
-def relay_kernel(part, offset, fresh, *refs):
-    (
-        x_ref, bc_ref, message_ref, got_ref, state_ref, dt_ref, wx_ref, bx_ref, wbc_ref, bbc_ref,
-        dt_bias_ref, a_log_ref, lens_ref,
-    ) = refs[:13]
-    out_ref, pad_ref = refs[-2:]
+def prepare_kernel(hops, *refs):
+    x_ref, bc_ref, dt_ref, wx_ref, bx_ref, wbc_ref, bbc_ref, dt_bias_ref, a_log_ref, lens_ref = refs[:10]
+    partial_ref, weight_ref, through_ref, inside_ref, flag_ref, entry_ref, pad_ref = refs[10:]
     width = x_ref.shape[1]
-    rows = dt_ref.shape[1]
+    rows, heads = entry_ref.shape
     taps = wx_ref.shape[0]
-    heads = width // HDIM
     here = lax.axis_index("seq")
     first = here * rows
     own = reach(here, rows, lens_ref) == 0
-    inside = insides(first, (EDGE, CHUNK), taps, lens_ref)
+    inside = insides(first, (8, CHUNK), taps, lens_ref)
+    for lag in range(1, taps):
+        inside_ref[lag - 1] = inside[lag].astype(F32)
+    flag_ref[0] = jnp.broadcast_to(own.astype(F32), (8, CHUNK))
+    before = reach(here - 1, rows, lens_ref)
+    for hop in range(1, hops):
+        flag_ref[hop] = jnp.broadcast_to((before == hop).astype(F32), (8, CHUNK))
     step, running = rates(dt_ref, dt_bias_ref, a_log_ref)
-    row = lax.broadcasted_iota(jnp.int32, (EDGE, heads), 0)
-    these = slice(part * heads, (part + 1) * heads)
-    total = running[rows - 1 : rows, these]
-    weight = step[:EDGE, these] * jnp.exp(total - running[:EDGE, these])
+    position = first + lax.broadcasted_iota(jnp.int32, running.shape, 0)
+    entry_ref[...] = jnp.where(doc_start(position, lens_ref) < first, jnp.exp(running), 0.0)
+    row = lax.broadcasted_iota(jnp.int32, (8, heads), 0)
+    total = running[rows - 1 : rows]
+    weight = step[:8] * jnp.exp(total - running[:8])
     weight = jnp.where((row < taps - 1) & jnp.logical_not(own), weight, 0.0)
-    through = jnp.broadcast_to(jnp.exp(total), (8, heads))
+    through = jnp.where(own, 0.0, jnp.broadcast_to(jnp.exp(total), (8, heads)))
+    both = jnp.concatenate([weight, through], axis=0)
+    for start in range(0, width, CHUNK):
+        wide = widen(both, start, CHUNK)
+        weight_ref[:, start : start + CHUNK] = wide[:8]
+        through_ref[:, start : start + CHUNK] = wide[8:]
+    pad_ref[0:8] = jnp.zeros((8, pad_ref.shape[1]), F32)
+    pad_ref[8:, :width] = x_ref[...].astype(F32)[:8]
+    pad_ref[8:, width:] = bc_ref[...].astype(F32)[:8]
+
+    def some(columns, base, w_ref, b_ref):
+        here_columns = slice(base + columns.start, base + columns.stop)
+        total = pad_ref[8:, here_columns] * w_ref[taps - 1 : taps, columns] + b_ref[columns].reshape(1, -1)
+        for lag in range(1, taps):
+            term = pad_ref[8 - lag : 16 - lag, here_columns] * w_ref[taps - 1 - lag : taps - lag, columns]
+            total = total + jnp.where(inside[lag], term, 0.0)
+        partial_ref[:, here_columns] = total
+
+    for start in range(0, width, CHUNK):
+        some(slice(start, start + CHUNK), 0, wx_ref, bx_ref)
+    for start in range(0, bc_ref.shape[1], CHUNK):
+        some(slice(start, start + CHUNK), width, wbc_ref, bbc_ref)
+
+
+def first_rows(lines, partial_ref, inside_ref, w_ref, pad_ref, slot, at, start):
+    taps = w_ref.shape[0]
+    columns = slice(start, start + CHUNK)
+    pad = pad_ref.at[slot]
+    pad[4:8] = lines[:, at + start : at + start + CHUNK]
+    pad[8:] = jnp.zeros((8, CHUNK), F32)
+    total = partial_ref[:, at + start : at + start + CHUNK]
+    for lag in range(1, taps):
+        term = pad[8 - lag : 16 - lag] * w_ref[taps - 1 - lag : taps - lag, columns]
+        total = total + term * inside_ref[lag - 1]
+    return silu(total).astype(BF16)
+
+
+def relay_first_kernel(fresh, *refs):
+    message_ref, state_ref, partial_ref, weight_ref, through_ref, inside_ref, flag_ref, wx_ref, wbc_ref = refs[:9]
+    other_ref = refs[9] if fresh else state_ref
+    out_ref, pad_ref = refs[-2:]
+    width = out_ref.shape[1]
+    slots = pad_ref.shape[0]
     lines = tail_lines(message_ref, STATE)
-    slots = pad_ref.shape[0]
-
-    def top(raw_ref, start, line, weight_ref, bias_ref, base, slot):
-        columns = slice(base + start, base + start + CHUNK)
-        pad = pad_ref.at[slot]
-        pad[4:8] = lines[:, line + start : line + start + CHUNK]
-        pad[8:] = raw_ref[:, start : start + CHUNK].astype(F32)
-        return conv(pad, EDGE, weight_ref[:, columns], bias_ref[columns].reshape(1, -1), inside)
-
-    base = part * 2 * STATE
-    inputs = top(bc_ref, 0, offset + base, wbc_ref, bbc_ref, base, 0)[:, :STATE]
+    top = functools.partial(first_rows, lines, partial_ref, inside_ref)
+    inputs = top(wbc_ref, pad_ref, 0, wx_ref.shape[1], 0)[:, :STATE]
     turned = inputs.astype(F32).T.astype(BF16)
+    own = flag_ref[0, 0:1] > 0.5
     for start in range(0, width, CHUNK):
         columns = slice(start, start + CHUNK)
-        xc = top(x_ref, start, part * width, wx_ref, bx_ref, part * width, (start // CHUNK + 1) % slots)
-        weighted = (xc.astype(F32) * widen(weight, start, CHUNK)).astype(BF16)
+        xc = top(wx_ref, pad_ref, (start // CHUNK + 1) % slots, 0, start)
+        weighted = (xc.astype(F32) * weight_ref[:, columns]).astype(BF16)
         full = state_ref[:STATE, columns].astype(F32) + jnp.dot(
             turned, weighted, preferred_element_type=F32
         )
-        full = full + widen(through, start, CHUNK)[0:1] * got_ref[:STATE, columns].astype(F32)
-        other = refs[13] if fresh else state_ref
-        out_ref[:, columns] = jnp.where(own, other[:STATE, columns].astype(F32), full).astype(BF16)
+        full = full + through_ref[0:1, columns] * message_ref[:STATE, columns].astype(F32)
+        out_ref[:, columns] = jnp.where(own, other_ref[:STATE, columns].astype(F32), full).astype(BF16)
+
+
+def relay_kernel(part, fresh, *refs):
+    got_ref, state_ref, through_ref, flag_ref = refs[:4]
+    out_ref = refs[-1]
+    width = out_ref.shape[1]
+    own = flag_ref[0, 0:1] > 0.5
+    for start in range(0, width, CHUNK):
+        columns = slice(start, start + CHUNK)
+        through = through_ref[0:1, part * width + start : part * width + start + CHUNK]
+        full = state_ref[:, columns].astype(F32) + through * got_ref[:STATE, columns].astype(F32)
+        if fresh:
+            full = jnp.where(own, refs[4][:STATE, columns].astype(F32), full)
+        out_ref[:, columns] = full.astype(BF16)
 
 
 def local_kernel(groups, *refs):
     (
-        x_ref, bc_ref, message_ref, dt_ref, wx_ref, bx_ref, wbc_ref, bbc_ref,
-        dt_bias_ref, a_log_ref, skip_ref, lens_ref,
+        message_ref, partial_ref, weight_ref, inside_ref, wx_ref, wbc_ref, dt_ref, dt_bias_ref,
+        a_log_ref, skip_ref, lens_ref, kv_ref,
     ) = refs[:12]
     xc_refs = refs[12 : 12 + groups]
     bcc_refs = refs[12 + groups : 12 + 2 * groups]
-    out_ref, c_ref, entry_ref, pad_ref = refs[12 + 2 * groups :]
+    state_refs = refs[12 + 2 * groups : 12 + 3 * groups]
+    out_ref, c_ref, kv_out_ref = refs[12 + 3 * groups : 15 + 3 * groups]
+    full_refs = refs[15 + 3 * groups : 15 + 4 * groups]
+    pad_ref = refs[-1]
     rows, per_group = xc_refs[0].shape
     width = groups * per_group
-    taps = wx_ref.shape[0]
     first = lax.axis_index("seq") * rows
-    inside = insides(first, (EDGE, CHUNK), taps, lens_ref)
     lines = tail_lines(message_ref, STATE)
     slots = pad_ref.shape[0]
-
-    def top(raw_ref, start, weight_ref, bias_ref, offset, slot):
-        columns = slice(start, start + CHUNK)
-        pad = pad_ref.at[slot]
-        pad[4:8] = lines[:, offset + start : offset + start + CHUNK]
-        pad[8:] = raw_ref[:, columns].astype(F32)
-        return conv(pad, EDGE, weight_ref[:, columns], bias_ref[columns].reshape(1, -1), inside)
+    kv_out_ref[...] = kv_ref[...]
+
+    def top(w_ref, slot, at, start, below):
+        new = first_rows(lines, partial_ref, inside_ref, w_ref, pad_ref, slot, at, start)
+        old = below[8:EDGE].astype(F32)
+        return jnp.concatenate([jnp.concatenate([new.astype(F32), old], axis=0).astype(BF16), below[EDGE:]], axis=0)
 
     row = lax.broadcasted_iota(jnp.int32, (rows, rows), 0)
     column = lax.broadcasted_iota(jnp.int32, (rows, rows), 1)
     begin = doc_start(first + row, lens_ref)
     linked = (row >= column) & (first + column >= begin)
     step, running = rates(dt_ref, dt_bias_ref, a_log_ref)
-    position = first + lax.broadcasted_iota(jnp.int32, running.shape, 0)
-    entry_ref[...] = jnp.where(doc_start(position, lens_ref) < first, jnp.exp(running), 0.0)
     turned_running = running.T
     turned_step = step.T
     skip = skip_ref[...].reshape(1, -1)
@@ -242,25 +294,24 @@
     lane = lax.broadcasted_iota(jnp.int32, (rows, pair_width), 1)
     for group in range(groups):
         base = group * 2 * STATE
-        pair = jnp.concatenate(
-            [top(bc_ref, base, wbc_ref, bbc_ref, width, group % slots), bcc_refs[group][EDGE:]], axis=0
-        )
+        pair = top(wbc_ref, group % slots, width, base, bcc_refs[group][...])
         inputs = pair[:, :STATE]
         outputs = pair[:, STATE:]
         c_ref[:, group * STATE : (group + 1) * STATE] = outputs
+        turned = inputs[:EDGE].astype(F32).T[:, :8].astype(BF16)
         meet = lax.dot_general(
             outputs, inputs, (((1,), (1,)), ((), ())), preferred_element_type=F32
         )
         meet = jnp.where(linked, meet, 0.0)
         for chunk in range(0, per_group, CHUNK):
             at = group * per_group + chunk
-            xc_all = jnp.concatenate(
-                [
-                    top(x_ref, at, wx_ref, bx_ref, 0, (chunk // CHUNK) % slots),
-                    xc_refs[group][EDGE:, chunk : chunk + CHUNK],
-                ],
-                axis=0,
+            columns = slice(chunk, chunk + CHUNK)
+            xc_all = top(wx_ref, (chunk // CHUNK) % slots, 0, at, xc_refs[group][:, columns])
+            weighted = xc_all[:EDGE].astype(F32)[:8] * weight_ref[:, at : at + CHUNK]
+            full = state_refs[group][:STATE, columns].astype(F32) + jnp.dot(
+                turned, weighted.astype(BF16), preferred_element_type=F32
             )
+            full_refs[group][:, columns] = full.astype(BF16)
             wide_skip = widen(skip, at, CHUNK)[0:1]
             for start in range(0, CHUNK, pair_width):
                 parts = []
@@ -312,23 +363,24 @@
 
 
 def norm_kernel(part, hops, *refs):
-    mixed_ref, c_ref, entry_ref, z_ref, gain_ref, lens_ref = refs[:6]
+    mixed_ref, c_ref, entry_ref, z_ref, gain_ref, flag_ref = refs[:6]
     got_refs = refs[6 : 6 + hops]
     out_ref, gated_ref = refs[-2:]
-    rows, width = mixed_ref.shape
+    rows, width = gated_ref.shape
     heads = width // HDIM
     entry = entry_ref[:, part * heads : (part + 1) * heads]
     outputs = c_ref[:, part * STATE : (part + 1) * STATE]
-    before = reach(lax.axis_index("seq") - 1, rows, lens_ref)
     squares = jnp.zeros((rows, 1), F32)
     for start in range(0, width, CHUNK):
         columns = slice(start, start + CHUNK)
-        state = got_refs[0][:STATE, columns]
+        placed = slice(part * width + start, part * width + start + CHUNK)
+        state = got_refs[0][:STATE, columns].astype(F32)
         for hop in range(1, hops):
-            state = jnp.where(before == hop, got_refs[hop][:STATE, columns], state)
-        carried = jnp.dot(outputs, state, preferred_element_type=F32)
-        mixed = mixed_ref[:, columns] + carried * widen(entry, start, CHUNK)
-        gated = mixed * silu(z_ref[:, columns].astype(F32))
+            there = flag_ref[hop, 0:1] > 0.5
+            state = jnp.where(there, got_refs[hop][:STATE, columns].astype(F32), state)
+        carried = jnp.dot(outputs, state.astype(BF16), preferred_element_type=F32)
+        mixed = mixed_ref[:, placed] + carried * widen(entry, start, CHUNK)
+        gated = mixed * silu(z_ref[:, placed].astype(F32))
         gated_ref[:, columns] = gated
         squares = squares + jnp.sum(gated * gated, axis=1, keepdims=True)
     multiplier = lax.rsqrt(squares * (1.0 / width) + EPSILON)
@@ -347,16 +399,10 @@
     return pl.BlockSpec((rows, columns), lambda step: (row, column))
 
 
-def call(kernel, name, outs, operands, specs, out_specs=None, scratch=(), flops=KERNEL_FLOPS, aliases={}, limit=VMEM_LIMIT, after=()):
-    operands = [*operands, *after]
-    specs = [*specs, *([UNTOUCHED] * len(after))]
-    inputs = len(operands) - len(after)
+def call(kernel, name, outs, operands, specs, out_specs=None, scratch=(), flops=KERNEL_FLOPS, aliases={}, limit=VMEM_LIMIT):
     moved = sum(math.prod(a.shape) * a.dtype.itemsize for a in (*operands, *outs))
-    def body(*refs):
-        kernel(*refs[:inputs], *refs[inputs + len(after) :])
-
     return pl.pallas_call(
-        body,
+        kernel,
         name=name,
         grid=(1,),
         out_shape=outs,
@@ -437,41 +483,67 @@
         xcs.append(got[0])
         bccs.append(got[1])
         states.append(got[2])
-    kvs = [got[3]]
-    for hop in range(hops):
-        kvs.append(onward(kvs[-1], hop))
-
+    kvs = [got[3], onward(got[3])]
     slots = [onward(states[0])]
-    mixed, c_out, entry = call(
-        functools.partial(local_kernel, groups),
-        "local_mix",
-        [shape((rows, width), F32), shape((rows, groups * STATE), BF16), shape((rows, heads), F32)],
-        [x_raw, bc_raw, slots[0], *params, skip_d, doc_lens, *xcs, *bccs],
-        [tile(EDGE, width, 0, 0), tile(EDGE, bc_width, 0, 0)]
-        + [WHOLE] * 9
-        + [SCALARS]
-        + [WHOLE] * 2 * groups,
-        scratch=[pltpu.VMEM((4, EDGE + 8, CHUNK), F32)],
-        after=[kvs[1]],
+
+    partial, weight, through, inside, flags, entry = call(
+        functools.partial(prepare_kernel, hops),
+        "prepare",
+        [
+            shape((8, width + bc_width), F32),
+            shape((8, width), F32),
+            shape((8, width), F32),
+            shape((conv_x_weight.shape[0] - 1, 8, CHUNK), F32),
+            shape((hops, 8, CHUNK), F32),
+            shape((rows, heads), F32),
+        ],
+        [x_raw, bc_raw, *params, doc_lens],
+        [tile(EDGE, width, 0, 0), tile(EDGE, bc_width, 0, 0)] + [WHOLE] * 7 + [SCALARS],
+        scratch=[pltpu.VMEM((16, width + bc_width), F32)],
     )
+
+    fulls = None
     for slot in range(2, hops + groups):
         part = min(slot - 1, groups) - 1
         fresh = slot <= groups
-        operands = [x_raw, bc_raw, slots[0], slots[-1], states[part], *params, doc_lens]
-        specs = [tile(EDGE, per_group, 0, part), tile(EDGE, 2 * STATE, 0, part)] + [WHOLE] * 10 + [SCALARS]
+        if slot == 2:
+            kernel = functools.partial(relay_first_kernel, fresh)
+            operands = [slots[0], states[0], partial, weight, through, inside, flags, conv_x_weight, conv_bc_weight]
+            scratch = [pltpu.VMEM((4, 16, CHUNK), F32)]
+        else:
+            kernel = functools.partial(relay_kernel, part, fresh)
+            operands = [slots[-1], fulls[part], through, flags]
+            scratch = []
         if fresh:
             operands.append(states[slot - 1])
-            specs.append(WHOLE)
         (passed,) = call(
-            functools.partial(relay_kernel, part, width, fresh),
+            kernel,
             f"relay_slot{slot}",
             [shape((STATE, per_group), BF16)],
             operands,
-            specs,
-            scratch=[pltpu.VMEM((4, EDGE + 8, CHUNK), F32)],
-            after=[entry] if slot == hops + groups - 1 else [],
+            [WHOLE] * len(operands),
+            scratch=scratch,
         )
         slots.append(onward(passed, max(0, slot - groups)))
+        if fulls is None:
+            mixed, c_out, kv_on, *fulls = call(
+                functools.partial(local_kernel, groups),
+                "local_mix",
+                [
+                    shape((rows, width), F32),
+                    shape((rows, groups * STATE), BF16),
+                    shape(got[3].shape, BF16),
+                    *(shape((STATE, per_group), BF16) for _ in range(groups)),
+                ],
+                [
+                    slots[0], partial, weight, inside, conv_x_weight, conv_bc_weight, dt, dt_bias, a_log,
+                    skip_d, doc_lens, kvs[1], *xcs, *bccs, *states,
+                ],
+                [WHOLE] * 10 + [SCALARS] + [WHOLE] * (1 + 3 * groups),
+                scratch=[pltpu.VMEM((4, 16, CHUNK), F32)],
+            )
+    for hop in range(1, hops):
+        kvs.append(onward(kv_on if hop == 1 else kvs[-1], hop))
 
     (attn_out,) = call(
         functools.partial(attend_kernel, hops),
@@ -482,9 +554,9 @@
     )
     mamba_out = None
     for part in range(groups):
-        operands = [mixed, c_out, entry, z_gate, norm_gain, doc_lens, *slots[part : part + hops]]
+        operands = [mixed, c_out, entry, z_gate, norm_gain, flags, *slots[part : part + hops]]
         block = tile(rows, per_group, 0, part)
-        specs = [block, WHOLE, WHOLE, block, WHOLE, SCALARS] + [WHOLE] * hops
+        specs = [WHOLE] * (6 + hops)
         aliases = {}
         if mamba_out is not None:
             operands.append(mamba_out)

time: 39.4 us -> 36.2 us (0.919)
  Pallas kernels: 16.1 us -> 13.4 us
  waiting for transfers between devices: 7.11 us -> 6.33 us
    pallas_call x8 -> x9, Pallas kernels: 16.1 us -> 13.4 us  [call(): pl.pallas_call(kernel, name=name, grid=(1,), out_shape=outs, in_specs=spe...]
    ppermute x5, waiting for transfers between devices: 7.11 us -> 6.33 us  [onward(): lax.ppermute(value, 'seq', [(source, source + 1) for source in range(firs...]
  transfers between devices with their start and end apart: 5 -> 5, of which waited for: 3 -> 3; matrix products, arithmetic and copies ran while one was open for 0% -> 0% of each run, Pallas kernels for 29% -> 26%
where the time goes in v4:
time: 36.2 us; the launch traced here: 35.9 us
  starting transfers between devices  14.5 us (40%)
  Pallas kernels  13.4 us (37%)
  waiting for transfers between devices  6.33 us (17%)
  between operations  0.95 us (3%)
  local copies, waits for them, and re-layouts  0.71 us (2%)
    ppermute x5, starting transfers between devices, onward(): lax.ppermute(value, 'seq', [(source, source + 1) for source in range(firs...  14.5 us
    pallas_call x9, Pallas kernels, call(): pl.pallas_call(kernel, name=name, grid=(1,), out_shape=outs, in_specs=spe...  13.4 us
    ppermute x5, waiting for transfers between devices, onward(): lax.ppermute(value, 'seq', [(source, source + 1) for source in range(firs...  6.33 us
  transfers between devices with their start and end apart: 5, of which 3 were waited for; matrix products, arithmetic and copies ran while one was open for 0% of the time, Pallas kernels for 26%

profile of v4, /device:TPU:22, one launch (start us, length us, event | category | flops | bytes accessed | tf_op | source)
XLA Modules:
  0.0 35.9 jit_solution(13433253403918974662)
XLA Ops:
  0.6 0.0 copy-start
  0.6 0.0 copy-start.4
  0.7 0.0 copy-start.5
  0.7 0.0 copy-start.6
  0.7 0.0 copy-start.7
  0.7 0.0 copy-start.8
  0.7 3.0 %state_part0.1 = (bf16[128,1024]{1,0:T(8,128)(2,1)}, bf16[128,256]{1,0:T(8,128)(2,1)}, bf16[144,1024]{1,0:T(8,128)(2,1)}) custom-call(bf16[128,2048]{1,0:T(8,128)(2,1)} %refs_0_.6, bf16[128,512]{1,0:T(8,128)(2,1)} %refs_1_.5, f32[32,128]{1,0:T(8,128)} %bitcast.1, f32[4,2048]{1,0:T(4,128)} %refs_7_.9, f32[2048]{0:T(1024)} %refs_4_.9, f32[4,512]{1,0:T(4,128)} %refs_8_.9, ...), custom_call_target="tpu_custom_call" | custom-call | flops 2000000000 | bytes 2001168 | tf_op jit(solution)/shard_map/state_part0/pallas_call | solution.py:404
  3.8 0.0 copy-start.16
  3.8 3.6 %collective-permute-start = (bf16[144,1024]{1,0:T(8,128)(2,1)}, bf16[144,1024]{1,0:T(8,128)(2,1)S(1)}, u32[]{:S(2)}, u32[]{:S(2)}) collective-permute-start(bf16[144,1024]{1,0:T(8,128)(2,1)} %get-tuple-element.19.refs_16_.refs_1_), channel_id=1, source_target_pairs={{0,4},{4,8},{8,12},{1,5},{5,9},{9,13},{2,6},{6,10},{10,14},{3,7},{... | collective-permute-start | bytes 884744 | tf_op jit(solution)/shard_map/ppermute | solution.py:420
  7.5 1.7 %state_part1.1 = (bf16[128,1024]{1,0:T(8,128)(2,1)S(1)}, bf16[128,256]{1,0:T(8,128)(2,1)S(1)}, bf16[128,1024]{1,0:T(8,128)(2,1)S(1)}, bf16[128,512]{1,0:T(8,128)(2,1)S(1)}) custom-call(bf16[128,2048]{1,0:T(8,128)(2,1)S(1)} %copy-done, bf16[128,512]{1,0:T(8,128)(2,1)S(1)} %copy-done.4, f32[32,128]{1,0:T(8,128)S(1)} %bitcast.2, f32[4,2048]{1,0:T(4,128)S(1)} %copy-done.7, ...), custom_call_target="tpu_custom_call" | custom-call | flops 2000000000 | bytes 1575184 | tf_op jit(solution)/shard_map/state_part1/pallas_call | solution.py:404
  9.2 0.0 copy-start.2
  9.2 2.1 %collective-permute-start.1 = (bf16[128,512]{1,0:T(8,128)(2,1)S(1)}, bf16[128,512]{1,0:T(8,128)(2,1)S(1)}, u32[]{:S(2)}, u32[]{:S(2)}) collective-permute-start(bf16[128,512]{1,0:T(8,128)(2,1)S(1)} %get-tuple-element.23.refs_3_), channel_id=1, source_target_pairs={{0,4},{4,8},{8,12},{1,5},{5,9},{9,13},{2,6},{6,10},{10,14},{3,7},{... | collective-permute-start | bytes 393224 | tf_op jit(solution)/shard_map/ppermute | solution.py:420
  11.3 1.1 %prepare.1 = (f32[8,2560]{1,0:T(8,128)S(1)}, f32[8,2048]{1,0:T(8,128)S(1)}, f32[8,2048]{1,0:T(8,128)S(1)}, f32[3,8,256]{2,1,0:T(8,128)S(1)}, f32[2,8,256]{2,1,0:T(8,128)S(1)}, /*index=5*/f32[128,32]{1,0:T(8,128)S(1)}) custom-call(bf16[128,2048]{1,0:T(8,128)(2,1)S(1)} %copy-done, bf16[128,512]{1,0:T(8,128)(2,1)S(1)} %copy-done.4, f32[32,128]{1,0:T(8,128)S(1)} %bitcast.3, ...), custom_call_target="tpu_custom_call" | custom-call | flops 2000000000 | bytes 993552 | tf_op jit(solution)/shard_map/prepare/pallas_call | solution.py:404
  12.4 3.5 %collective-permute-done.refs_0_.refs_6_ = bf16[144,1024]{1,0:T(8,128)(2,1)S(1)} collective-permute-done((bf16[144,1024]{1,0:T(8,128)(2,1)}, bf16[144,1024]{1,0:T(8,128)(2,1)S(1)}, u32[]{:S(2)}, u32[]{:S(2)}) %collective-permute-start) | collective-permute-done | bytes 294944 | tf_op jit(solution)/shard_map/ppermute | solution.py:420
  15.9 0.3 relay_slot2.1
  16.2 3.5 %collective-permute-start.2 = (bf16[128,1024]{1,0:T(8,128)(2,1)S(1)}, bf16[128,1024]{1,0:T(8,128)(2,1)S(1)}, u32[]{:S(2)}, u32[]{:S(2)}) collective-permute-start(bf16[128,1024]{1,0:T(8,128)(2,1)S(1)} %relay_slot2.1), channel_id=1, source_target_pairs={{0,4},{4,8},{8,12},{1,5},{5,9},{9,13},{2,6},{6,10},{10,14},{3,7},{... | collective-permute-start | bytes 786440 | tf_op jit(solution)/shard_map/ppermute | solution.py:420
  19.7 0.0 collective-permute-done.1.refs_11_.refs_2_
  19.7 0.0 copy-start.15
  19.8 0.6 %copy-done.15 = f32[32]{0:T(128)S(1)} copy-done((f32[32]{0:T(128)S(1)}, f32[32]{0:T(128)}, u32[]{:S(2)}) %copy-start.15) | copy-done | bytes 152
  20.4 2.6 %local_mix.1 = (f32[128,2048]{1,0:T(8,128)S(1)}, bf16[128,256]{1,0:T(8,128)(2,1)S(1)}, bf16[128,512]{1,0:T(8,128)(2,1)S(1)}, bf16[128,1024]{1,0:T(8,128)(2,1)}, bf16[128,1024]{1,0:T(8,128)(2,1)S(1)}) custom-call(bf16[144,1024]{1,0:T(8,128)(2,1)S(1)} %collective-permute-done.refs_0_.refs_6_, f32[8,2560]{1,0:T(8,128)S(1)} %get-tuple-element.20.refs_1_.refs_2_, ...), custom_call_target="tpu_custom_call" | custom-call | flops 2000000000 | bytes 3637648 | tf_op jit(solution)/shard_map/local_mix/pallas_call | solution.py:404
  23.0 1.9 %collective-permute-start.4 = (bf16[128,512]{1,0:T(8,128)(2,1)S(1)}, bf16[128,512]{1,0:T(8,128)(2,1)S(1)}, u32[]{:S(2)}, u32[]{:S(2)}) collective-permute-start(bf16[128,512]{1,0:T(8,128)(2,1)S(1)} %get-tuple-element.35), channel_id=1, source_target_pairs={{4,8},{8,12},{5,9},{9,13},{6,10},{10,14},{7,11},{11,15},{20,24},{2... | collective-permute-start | bytes 393224 | tf_op jit(solution)/shard_map/ppermute | solution.py:420
  24.9 0.0 collective-permute-done.2.refs_0_.refs_7_.refs_6_
  24.9 0.0 copy-start.3
  24.9 0.1 relay_slot3.1
  25.0 0.0 copy-start.1
  25.0 0.0 copy-start.11
  25.0 3.4 %collective-permute-start.3 = (bf16[128,1024]{1,0:T(8,128)(2,1)S(1)}, bf16[128,1024]{1,0:T(8,128)(2,1)S(1)}, u32[]{:S(2)}, u32[]{:S(2)}) collective-permute-start(bf16[128,1024]{1,0:T(8,128)(2,1)S(1)} %relay_slot3.1), channel_id=1, source_target_pairs={{4,8},{8,12},{5,9},{9,13},{6,10},{10,14},{7,11},{11,15},{20,24},{2... | collective-permute-start | bytes 786440 | tf_op jit(solution)/shard_map/ppermute | solution.py:420
  28.5 2.7 %collective-permute-done.4.refs_1_ = bf16[128,512]{1,0:T(8,128)(2,1)S(1)} collective-permute-done((bf16[128,512]{1,0:T(8,128)(2,1)S(1)}, bf16[128,512]{1,0:T(8,128)(2,1)S(1)}, u32[]{:S(2)}, u32[]{:S(2)}) %collective-permute-start.4) | collective-permute-done | bytes 131104 | tf_op jit(solution)/shard_map/ppermute | solution.py:420
  31.2 2.3 %attend.1 = bf16[128,1024]{1,0:T(8,128)(2,1)} custom-call(bf16[128,1024]{1,0:T(8,128)(2,1)S(1)} %copy-done.3, bf16[128,512]{1,0:T(8,128)(2,1)S(1)} %collective-permute-done.4.refs_1_, bf16[128,512]{1,0:T(8,128)(2,1)S(1)} %collective-permute-done.1.refs_11_.refs_2_, bf16[128,512]{1,0:T(8,128)(2,1)S(1)} %get-tuple-element.23.refs_3_, s32[4]{0:T(128)S(1)} %copy-done.16), custom_call_target="tpu_custom_call" | custom-call | flops 2000000000 | bytes 917520 | tf_op jit(solution)/shard_map/attend/pallas_call | solution.py:404
  33.5 1.2 %norm_part0.1.refs_8_ = bf16[128,2048]{1,0:T(8,128)(2,1)} custom-call(f32[128,2048]{1,0:T(8,128)S(1)} %get-tuple-element.29.refs_0_, bf16[128,256]{1,0:T(8,128)(2,1)S(1)} %get-tuple-element.30.refs_1_, f32[128,32]{1,0:T(8,128)S(1)} %get-tuple-element.31.refs_2_, bf16[128,2048]{1,0:T(8,128)(2,1)S(1)} %copy-done.1, f32[2048]{0:T(1024)S(1)} %copy-done.11, ...), custom_call_target="tpu_custom_call" | custom-call | flops 2000000000 | bytes 2760704 | tf_op jit(solution)/shard_map/norm_part0/pallas_call | solution.py:404
  34.6 0.1 collective-permute-done.3.refs_7_
  34.7 1.2 %norm_part1.1 = bf16[128,2048]{1,0:T(8,128)(2,1)} custom-call(f32[128,2048]{1,0:T(8,128)S(1)} %get-tuple-element.29.refs_0_, bf16[128,256]{1,0:T(8,128)(2,1)S(1)} %get-tuple-element.30.refs_1_, f32[128,32]{1,0:T(8,128)S(1)} %get-tuple-element.31.refs_2_, bf16[128,2048]{1,0:T(8,128)(2,1)S(1)} %copy-done.1, ...), custom_call_target="tpu_custom_call", output_to_operand_aliasing={{}: (8, {})} | custom-call | flops 2000000000 | bytes 3252224 | tf_op jit(solution)/shard_map/norm_part1/pallas_call | solution.py:404
  (25 shorter events, 0.1 us)
Async XLA Ops:
  0.6 6.8 %copy-start = (bf16[128,2048]{1,0:T(8,128)(2,1)S(1)}, bf16[128,2048]{1,0:T(8,128)(2,1)}, u32[]{:S(2)}) copy-start(bf16[128,2048]{1,0:T(8,128)(2,1)} %refs_0_.6) | copy-start | bytes 1572868
  0.6 6.8 %copy-start.4 = (bf16[128,512]{1,0:T(8,128)(2,1)S(1)}, bf16[128,512]{1,0:T(8,128)(2,1)}, u32[]{:S(2)}) copy-start(bf16[128,512]{1,0:T(8,128)(2,1)} %refs_1_.5) | copy-start | bytes 393220
  0.7 6.8 %copy-start.5 = (bf16[128,256]{1,0:T(8,128)(2,1)S(1)}, bf16[128,256]{1,0:T(8,128)(2,1)}, u32[]{:S(2)}) copy-start(bf16[128,256]{1,0:T(8,128)(2,1)} %refs_10_.4) | copy-start | bytes 196612
  0.7 6.8 %copy-start.6 = (bf16[128,256]{1,0:T(8,128)(2,1)S(1)}, bf16[128,256]{1,0:T(8,128)(2,1)}, u32[]{:S(2)}) copy-start(bf16[128,256]{1,0:T(8,128)(2,1)} %refs_11_.3) | copy-start | bytes 196612
  0.7 6.8 %copy-start.7 = (f32[4,2048]{1,0:T(4,128)S(1)}, f32[4,2048]{1,0:T(4,128)}, u32[]{:S(2)}) copy-start(f32[4,2048]{1,0:T(4,128)} %refs_7_.9) | copy-start | bytes 98308
  0.7 6.8 %copy-start.8 = (f32[128,32]{0,1:T(8,128)S(1)}, f32[128,32]{0,1:T(8,128)}, u32[]{:S(2)}) copy-start(f32[128,32]{0,1:T(8,128)} %param.19) | copy-start | bytes 49156
  0.7 6.8 %copy-start.9 = (f32[2048]{0:T(1024)S(1)}, f32[2048]{0:T(1024)}, u32[]{:S(2)}) copy-start(f32[2048]{0:T(1024)} %refs_4_.9) | copy-start | bytes 24580
  0.7 6.8 %copy-start.10 = (f32[4,512]{1,0:T(4,128)S(1)}, f32[4,512]{1,0:T(4,128)}, u32[]{:S(2)}) copy-start(f32[4,512]{1,0:T(4,128)} %refs_8_.9) | copy-start | bytes 24580
  0.7 6.8 %copy-start.12 = (f32[512]{0:T(512)S(1)}, f32[512]{0:T(512)}, u32[]{:S(2)}) copy-start(f32[512]{0:T(512)} %refs_6_.5) | copy-start | bytes 6148
  3.7 3.7 %copy-start.13 = (f32[32]{0:T(128)S(1)}, f32[32]{0:T(128)}, u32[]{:S(2)}) copy-start(f32[32]{0:T(128)} %refs_7_.8) | copy-start | bytes 388
  3.7 3.7 %copy-start.14 = (f32[32]{0:T(128)S(1)}, f32[32]{0:T(128)}, u32[]{:S(2)}) copy-start(f32[32]{0:T(128)} %refs_8_.8) | copy-start | bytes 388
  3.8 3.7 %copy-start.16 = (s32[4]{0:T(128)S(1)}, s32[4]{0:T(128)}, u32[]{:S(2)}) copy-start(s32[4]{0:T(128)} %refs_4_.13) | copy-start | bytes 52
  3.8 12.1 %collective-permute-start = (bf16[144,1024]{1,0:T(8,128)(2,1)}, bf16[144,1024]{1,0:T(8,128)(2,1)S(1)}, u32[]{:S(2)}, u32[]{:S(2)}) collective-permute-start(bf16[144,1024]{1,0:T(8,128)(2,1)} %get-tuple-element.19.refs_16_.refs_1_), channel_id=1, source_target_pairs={{0,4},{4,8},{8,12},{1,5},{5,9},{9,13},{2,6},{6,10},{10,14},{3,7},{... | collective-permute-start | bytes 884744 | tf_op jit(solution)/shard_map/ppermute | solution.py:420
  9.2 6.7 %copy-start.2 = (bf16[144,1024]{1,0:T(8,128)(2,1)S(1)}, bf16[144,1024]{1,0:T(8,128)(2,1)}, u32[]{:S(2)}) copy-start(bf16[144,1024]{1,0:T(8,128)(2,1)} %get-tuple-element.19.refs_16_.refs_1_) | copy-start | bytes 884740
  9.2 10.5 %collective-permute-start.1 = (bf16[128,512]{1,0:T(8,128)(2,1)S(1)}, bf16[128,512]{1,0:T(8,128)(2,1)S(1)}, u32[]{:S(2)}, u32[]{:S(2)}) collective-permute-start(bf16[128,512]{1,0:T(8,128)(2,1)S(1)} %get-tuple-element.23.refs_3_), channel_id=1, source_target_pairs={{0,4},{4,8},{8,12},{1,5},{5,9},{9,13},{2,6},{6,10},{10,14},{3,7},{... | collective-permute-start | bytes 393224 | tf_op jit(solution)/shard_map/ppermute | solution.py:420
  15.9 3.9 %copy-start.17 = (bf16[128,1024]{1,0:T(8,128)(2,1)S(1)}, bf16[128,1024]{1,0:T(8,128)(2,1)}, u32[]{:S(2)}) copy-start(bf16[128,1024]{1,0:T(8,128)(2,1)} %get-tuple-element.24.refs_12_) | copy-start | bytes 786436
  15.9 3.9 %copy-start.18 = (bf16[128,256]{1,0:T(8,128)(2,1)S(1)}, bf16[128,256]{1,0:T(8,128)(2,1)}, u32[]{:S(2)}) copy-start(bf16[128,256]{1,0:T(8,128)(2,1)} %get-tuple-element.26.refs_14_) | copy-start | bytes 196612
  16.2 8.6 %collective-permute-start.2 = (bf16[128,1024]{1,0:T(8,128)(2,1)S(1)}, bf16[128,1024]{1,0:T(8,128)(2,1)S(1)}, u32[]{:S(2)}, u32[]{:S(2)}) collective-permute-start(bf16[128,1024]{1,0:T(8,128)(2,1)S(1)} %relay_slot2.1), channel_id=1, source_target_pairs={{0,4},{4,8},{8,12},{1,5},{5,9},{9,13},{2,6},{6,10},{10,14},{3,7},{... | collective-permute-start | bytes 786440 | tf_op jit(solution)/shard_map/ppermute | solution.py:420
  19.7 0.7 %copy-start.15 = (f32[32]{0:T(128)S(1)}, f32[32]{0:T(128)}, u32[]{:S(2)}) copy-start(f32[32]{0:T(128)} %refs_9_.7) | copy-start | bytes 388
  23.0 8.2 %collective-permute-start.4 = (bf16[128,512]{1,0:T(8,128)(2,1)S(1)}, bf16[128,512]{1,0:T(8,128)(2,1)S(1)}, u32[]{:S(2)}, u32[]{:S(2)}) collective-permute-start(bf16[128,512]{1,0:T(8,128)(2,1)S(1)} %get-tuple-element.35), channel_id=1, source_target_pairs={{4,8},{8,12},{5,9},{9,13},{6,10},{10,14},{7,11},{11,15},{20,24},{2... | collective-permute-start | bytes 393224 | tf_op jit(solution)/shard_map/ppermute | solution.py:420
  24.9 6.3 %copy-start.3 = (bf16[128,1024]{1,0:T(8,128)(2,1)S(1)}, bf16[128,1024]{1,0:T(8,128)(2,1)}, u32[]{:S(2)}) copy-start(bf16[128,1024]{1,0:T(8,128)(2,1)} %refs_0_.7) | copy-start | bytes 786436
  25.0 8.5 %copy-start.1 = (bf16[128,2048]{1,0:T(8,128)(2,1)S(1)}, bf16[128,2048]{1,0:T(8,128)(2,1)}, u32[]{:S(2)}) copy-start(bf16[128,2048]{1,0:T(8,128)(2,1)} %refs_3_.9) | copy-start | bytes 1572868
  25.0 8.4 %copy-start.11 = (f32[2048]{0:T(1024)S(1)}, f32[2048]{0:T(1024)}, u32[]{:S(2)}) copy-start(f32[2048]{0:T(1024)} %refs_4_.12) | copy-start | bytes 24580
  25.0 9.7 %collective-permute-start.3 = (bf16[128,1024]{1,0:T(8,128)(2,1)S(1)}, bf16[128,1024]{1,0:T(8,128)(2,1)S(1)}, u32[]{:S(2)}, u32[]{:S(2)}) collective-permute-start(bf16[128,1024]{1,0:T(8,128)(2,1)S(1)} %relay_slot3.1), channel_id=1, source_target_pairs={{4,8},{8,12},{5,9},{9,13},{6,10},{10,14},{7,11},{11,15},{20,24},{2... | collective-permute-start | bytes 786440 | tf_op jit(solution)/shard_map/ppermute | solution.py:420

commit v5 on v4

--- a/solution.py
+++ b/solution.py
@@ -58,8 +58,9 @@
 
 
 def rates(dt_ref, dt_bias_ref, a_log_ref):
-    step = softplus(dt_ref[...].T + dt_bias_ref[...].reshape(1, -1))
-    rate = -step * jnp.exp(a_log_ref[...].reshape(1, -1))
+    heads = dt_ref.shape[0]
+    step = softplus(dt_ref[...].T + dt_bias_ref[...].reshape(1, -1)[:, :heads])
+    rate = -step * jnp.exp(a_log_ref[...].reshape(1, -1)[:, :heads])
     rows = step.shape[0]
     row = lax.broadcasted_iota(jnp.int32, (rows, rows), 0)
     column = lax.broadcasted_iota(jnp.int32, (rows, rows), 1)
@@ -104,67 +105,124 @@
     return device - doc_start((device + 1) * rows - 1, lens_ref) // rows
 
 
-def state_kernel(part, first_part, last_part, *refs):
+def kept_weight(here, step, running, taps, lens_ref):
+    rows = step.shape[0]
+    weight = state_weight(here * rows, step, running, lens_ref)
+    row = lax.broadcasted_iota(jnp.int32, weight.shape, 0)
+    return jnp.where((row >= taps - 1) | (reach(here, rows, lens_ref) == 0), weight, 0.0)
+
+
+def conv_rows(pad, raw, weight, bias, inside):
+    pad[0:8] = jnp.zeros((8, raw.shape[1]), F32)
+    pad[8:] = raw.astype(F32)
+    return conv(pad, raw.shape[0], weight, bias.reshape(1, -1), inside)
+
+
+def first_state_kernel(*refs):
+    hbm_refs, out_hbm_ref = refs[:10], refs[10]
+    vmem_refs = refs[11:21]
+    x_edge_ref, bc_edge_ref, out_ref, b_pad_ref, pad_ref, in_sems, out_sems = refs[21:]
+    x_ref, b_ref, dt_ref, wx_ref, bx_ref, wbc_ref, bbc_ref, dt_bias_ref, a_log_ref, lens_ref = vmem_refs
+    rows, width = x_ref.shape
+    taps = wx_ref.shape[0]
+
+    def corner(ref, shape):
+        return ref.at[tuple(pl.ds(0, extent) for extent in shape)]
+
+    order = (9, 2, 7, 8, 1, 5, 6, 0, 3, 4)
+    copies = {}
+    for at in order:
+        source = corner(hbm_refs[at], vmem_refs[at].shape)
+        copies[at] = pltpu.make_async_copy(source, vmem_refs[at], in_sems.at[at])
+        copies[at].start()
+    edge_copies = []
+    for at, (source, target) in enumerate(((hbm_refs[0], x_edge_ref), (hbm_refs[1], bc_edge_ref))):
+        edge_copies.append(
+            pltpu.make_async_copy(source.at[pl.ds(rows - EDGE, EDGE)], target, in_sems.at[10 + at])
+        )
+        edge_copies[-1].start()
+
+    here = lax.axis_index("seq")
+    for at in (9, 2, 7, 8):
+        copies[at].wait()
+    inside = insides(here * rows, (rows, CHUNK), taps, lens_ref)
+    step, running = rates(dt_ref, dt_bias_ref, a_log_ref)
+    weight = kept_weight(here, step, running, taps, lens_ref)
+    for at in (1, 5, 6):
+        copies[at].wait()
+    narrow = [mask[:, :STATE] for mask in inside]
+    inputs = conv_rows(b_pad_ref, b_ref[...], wbc_ref[...], bbc_ref[...], narrow)
+    turned = inputs.astype(F32).T.astype(BF16)
+    for at in (0, 3, 4):
+        copies[at].wait()
+    slots = pad_ref.shape[0]
+    outs = []
+
+    def send(at, view):
+        copy = pltpu.make_async_copy(out_ref.at[view], out_hbm_ref.at[view], out_sems.at[at])
+        copy.start()
+        outs.append(copy)
+
+    for at, start in enumerate(range(0, width, CHUNK)):
+        columns = slice(start, start + CHUNK)
+        pad = pad_ref.at[(at + 1) % slots]
+        xc = conv_rows(pad, x_ref[:, columns], wx_ref[:, columns], bx_ref[:, columns], inside)
+        weighted = (xc.astype(F32) * widen(weight, start, CHUNK)).astype(BF16)
+        out_ref[:STATE, columns] = jnp.dot(turned, weighted, preferred_element_type=F32).astype(BF16)
+        send(at, (pl.ds(0, STATE), pl.ds(start, CHUNK)))
+    for copy in edge_copies:
+        copy.wait()
+    edges = jnp.concatenate([x_edge_ref[...].astype(F32), bc_edge_ref[...].astype(F32)], axis=1)[EDGE - 4 :]
+    spare = -edges.shape[1] % width
+    if spare:
+        edges = jnp.concatenate([edges, jnp.zeros((4, spare), F32)], axis=1)
+    pieces = [edges[:, at : at + width] for at in range(0, edges.shape[1], width)]
+    while len(pieces) % (EDGE // 4):
+        pieces.append(jnp.zeros_like(pieces[0]))
+    out_ref[STATE:] = jnp.concatenate(pieces, axis=0).astype(BF16)
+    send(width // CHUNK, (pl.ds(STATE, out_ref.shape[0] - STATE), pl.ds(0, width)))
+    for copy in outs:
+        copy.wait()
+
+
+def conv_kernel(groups, *refs):
     x_ref, bc_ref, dt_ref, wx_ref, bx_ref, wbc_ref, bbc_ref, dt_bias_ref, a_log_ref, lens_ref = refs[:10]
-    refs = refs[10:]
-    if first_part:
-        x_edge_ref, bc_edge_ref = refs[:2]
-        refs = refs[2:]
-    if last_part:
-        keys_ref, values_ref = refs[:2]
-        refs = refs[2:]
-    xc_ref, bcc_ref, state_ref = refs[:3]
+    keys_ref, values_ref, xc_ref, bcc_ref, kv_ref = refs[10:15]
+    state_refs = refs[15:-1]
     pad_ref = refs[-1]
     rows, width = x_ref.shape
+    per_group = width // groups
+    heads = per_group // HDIM
     taps = wx_ref.shape[0]
-    heads = width // HDIM
+    slots = pad_ref.shape[0]
     here = lax.axis_index("seq")
-    first = here * rows
-    inside = insides(first, (rows, CHUNK), taps, lens_ref)
+    kv_width = keys_ref.shape[1]
+    kv_ref[:, :kv_width] = keys_ref[...]
+    kv_ref[:, kv_width:] = values_ref[...]
+    inside = insides(here * rows, (rows, CHUNK), taps, lens_ref)
     step, running = rates(dt_ref, dt_bias_ref, a_log_ref)
-    weight = state_weight(first, step, running, lens_ref)
-    row = lax.broadcasted_iota(jnp.int32, weight.shape, 0)
-    kept = (row >= taps - 1) | (reach(here, rows, lens_ref) == 0)
-    weight = jnp.where(kept, weight, 0.0)[:, part * heads : (part + 1) * heads]
-    slots = pad_ref.shape[0]
-
-    def block(raw_ref, start, weight_ref, bias_ref, offset, slot):
-        pad = pad_ref.at[slot]
-        pad[0:8] = jnp.zeros((8, CHUNK), F32)
-        pad[8:] = raw_ref[:, start : start + CHUNK].astype(F32)
-        columns = slice(offset + start, offset + start + CHUNK)
-        return conv(pad, rows, weight_ref[:, columns], bias_ref[columns].reshape(1, -1), inside)
-
-    pair = block(bc_ref, 0, wbc_ref, bbc_ref, part * 2 * STATE, 0)
-    bcc_ref[...] = pair
-    turned = pair[:, :STATE].astype(F32).T.astype(BF16)
-    for start in range(0, width, CHUNK):
-        xc = block(x_ref, start, wx_ref, bx_ref, part * width, (start // CHUNK + 1) % slots)
-        xc_ref[:, start : start + CHUNK] = xc
-        weighted = (xc.astype(F32) * widen(weight, start, CHUNK)).astype(BF16)
-        state_ref[:STATE, start : start + CHUNK] = jnp.dot(
-            turned, weighted, preferred_element_type=F32
-        ).astype(BF16)
-    if first_part:
-        edges = jnp.concatenate([x_edge_ref[...].astype(F32), bc_edge_ref[...].astype(F32)], axis=1)
-        edges = edges[EDGE - 4 :]
-        spare = -edges.shape[1] % width
-        if spare:
-            edges = jnp.concatenate([edges, jnp.zeros((4, spare), F32)], axis=1)
-        pieces = [edges[:, at : at + width] for at in range(0, edges.shape[1], width)]
-        while len(pieces) % (EDGE // 4):
-            pieces.append(jnp.zeros_like(pieces[0]))
-        state_ref[STATE:] = jnp.concatenate(pieces, axis=0).astype(BF16)
-    if last_part:
-        kv_ref = refs[3]
-        kv_width = keys_ref.shape[1]
-        kv_ref[:, :kv_width] = keys_ref[...]
-        kv_ref[:, kv_width:] = values_ref[...]
+    weight = kept_weight(here, step, running, taps, lens_ref)
+    for group in range(groups):
+        base = slice(group * 2 * STATE, (group + 1) * 2 * STATE)
+        pair = conv_rows(pad_ref.at[0], bc_ref[:, base], wbc_ref[:, base], bbc_ref[base], inside)
+        bcc_ref[:, base] = pair
+        turned = pair[:, :STATE].astype(F32).T.astype(BF16)
+        part_weight = weight[:, group * heads : (group + 1) * heads]
+        for chunk in range(0, per_group, CHUNK):
+            columns = slice(group * per_group + chunk, group * per_group + chunk + CHUNK)
+            pad = pad_ref.at[(chunk // CHUNK + 1) % slots]
+            xc = conv_rows(pad, x_ref[:, columns], wx_ref[:, columns], bx_ref[columns], inside)
+            xc_ref[:, columns] = xc
+            if group:
+                weighted = (xc.astype(F32) * widen(part_weight, chunk, CHUNK)).astype(BF16)
+                state_refs[group - 1][:, chunk : chunk + CHUNK] = jnp.dot(
+                    turned, weighted, preferred_element_type=F32
+                ).astype(BF16)
 
 
 def prepare_kernel(hops, *refs):
-    x_ref, bc_ref, dt_ref, wx_ref, bx_ref, wbc_ref, bbc_ref, dt_bias_ref, a_log_ref, lens_ref = refs[:10]
-    partial_ref, weight_ref, through_ref, inside_ref, flag_ref, entry_ref, pad_ref = refs[10:]
+    x_ref, bc_ref, dt_ref, wx_ref, bx_ref, wbc_ref, bbc_ref, dt_bias_ref, a_log_ref, skip_ref, lens_ref = refs[:11]
+    partial_ref, weight_ref, through_ref, inside_ref, flag_ref, entry_ref, wide_skip_ref, pad_ref = refs[11:]
     width = x_ref.shape[1]
     rows, heads = entry_ref.shape
     taps = wx_ref.shape[0]
@@ -186,11 +244,13 @@
     weight = step[:8] * jnp.exp(total - running[:8])
     weight = jnp.where((row < taps - 1) & jnp.logical_not(own), weight, 0.0)
     through = jnp.where(own, 0.0, jnp.broadcast_to(jnp.exp(total), (8, heads)))
-    both = jnp.concatenate([weight, through], axis=0)
+    skip = jnp.broadcast_to(skip_ref[...].reshape(1, -1), (8, heads))
+    every = jnp.concatenate([weight, through, skip], axis=0)
     for start in range(0, width, CHUNK):
-        wide = widen(both, start, CHUNK)
+        wide = widen(every, start, CHUNK)
         weight_ref[:, start : start + CHUNK] = wide[:8]
-        through_ref[:, start : start + CHUNK] = wide[8:]
+        through_ref[:, start : start + CHUNK] = wide[8:16]
+        wide_skip_ref[:, start : start + CHUNK] = wide[16:]
     pad_ref[0:8] = jnp.zeros((8, pad_ref.shape[1]), F32)
     pad_ref[8:, :width] = x_ref[...].astype(F32)[:8]
     pad_ref[8:, width:] = bc_ref[...].astype(F32)[:8]
@@ -261,16 +321,14 @@
 def local_kernel(groups, *refs):
     (
         message_ref, partial_ref, weight_ref, inside_ref, wx_ref, wbc_ref, dt_ref, dt_bias_ref,
-        a_log_ref, skip_ref, lens_ref, kv_ref,
-    ) = refs[:12]
-    xc_refs = refs[12 : 12 + groups]
-    bcc_refs = refs[12 + groups : 12 + 2 * groups]
-    state_refs = refs[12 + 2 * groups : 12 + 3 * groups]
-    out_ref, c_ref, kv_out_ref = refs[12 + 3 * groups : 15 + 3 * groups]
-    full_refs = refs[15 + 3 * groups : 15 + 4 * groups]
+        a_log_ref, wide_skip_ref, lens_ref, kv_ref, xc_ref, bcc_ref,
+    ) = refs[:14]
+    state_refs = refs[14 : 14 + groups]
+    out_ref, c_ref, kv_out_ref = refs[14 + groups : 17 + groups]
+    full_refs = refs[17 + groups : 17 + 2 * groups]
     pad_ref = refs[-1]
-    rows, per_group = xc_refs[0].shape
-    width = groups * per_group
+    rows, width = xc_ref.shape
+    per_group = width // groups
     first = lax.axis_index("seq") * rows
     lines = tail_lines(message_ref, STATE)
     slots = pad_ref.shape[0]
@@ -288,13 +346,11 @@
     step, running = rates(dt_ref, dt_bias_ref, a_log_ref)
     turned_running = running.T
     turned_step = step.T
-    skip = skip_ref[...].reshape(1, -1)
-    skip = jnp.broadcast_to(skip, (8, skip.shape[1]))
     pair_width = 2 * HDIM
     lane = lax.broadcasted_iota(jnp.int32, (rows, pair_width), 1)
     for group in range(groups):
         base = group * 2 * STATE
-        pair = top(wbc_ref, group % slots, width, base, bcc_refs[group][...])
+        pair = top(wbc_ref, group % slots, width, base, bcc_ref[:, base : base + 2 * STATE])
         inputs = pair[:, :STATE]
         outputs = pair[:, STATE:]
         c_ref[:, group * STATE : (group + 1) * STATE] = outputs
@@ -306,13 +362,13 @@
         for chunk in range(0, per_group, CHUNK):
             at = group * per_group + chunk
             columns = slice(chunk, chunk + CHUNK)
-            xc_all = top(wx_ref, (chunk // CHUNK) % slots, 0, at, xc_refs[group][:, columns])
+            xc_all = top(wx_ref, (chunk // CHUNK) % slots, 0, at, xc_ref[:, at : at + CHUNK])
             weighted = xc_all[:EDGE].astype(F32)[:8] * weight_ref[:, at : at + CHUNK]
             full = state_refs[group][:STATE, columns].astype(F32) + jnp.dot(
                 turned, weighted.astype(BF16), preferred_element_type=F32
             )
             full_refs[group][:, columns] = full.astype(BF16)
-            wide_skip = widen(skip, at, CHUNK)[0:1]
+            wide_skip = wide_skip_ref[0:1, at : at + CHUNK]
             for start in range(0, CHUNK, pair_width):
                 parts = []
                 for head in ((at + start) // HDIM, (at + start) // HDIM + 1):
@@ -345,21 +401,22 @@
     allowed = (column <= row) & (column >= doc_start(row, lens_ref))
     scale = ADIM ** (-0.5)
     ones = jnp.ones((count, ADIM), BF16)
+    allowed = jnp.concatenate([allowed] * share, axis=0)
     for head in range(kv_heads):
         low = head * ADIM
         keys = jnp.concatenate([ref[:, low : low + ADIM] for ref in kv_refs], axis=0)
         low = (kv_heads + head) * ADIM
         values = jnp.concatenate([ref[:, low : low + ADIM] for ref in kv_refs], axis=0)
         values = jnp.concatenate([values, ones], axis=1)
-        for part in range(share):
-            low = (head * share + part) * ADIM
-            scores = lax.dot_general(
-                q_ref[:, low : low + ADIM], keys, (((1,), (1,)), ((), ())), preferred_element_type=F32
-            )
-            scores = jnp.where(allowed, scores * scale, BARRED)
-            expo = jnp.exp(scores - jnp.max(scores, axis=1, keepdims=True))
-            summed = jnp.dot(expo.astype(BF16), values, preferred_element_type=F32)
-            out_ref[:, low : low + ADIM] = (summed[:, :ADIM] / summed[:, ADIM:]).astype(BF16)
+        lows = [(head * share + part) * ADIM for part in range(share)]
+        asking = jnp.concatenate([q_ref[:, low : low + ADIM] for low in lows], axis=0)
+        scores = lax.dot_general(asking, keys, (((1,), (1,)), ((), ())), preferred_element_type=F32)
+        scores = jnp.where(allowed, scores * scale, BARRED)
+        expo = jnp.exp(scores - jnp.max(scores, axis=1, keepdims=True))
+        summed = jnp.dot(expo.astype(BF16), values, preferred_element_type=F32)
+        result = (summed[:, :ADIM] / summed[:, ADIM:]).astype(BF16)
+        for part, low in enumerate(lows):
+            out_ref[:, low : low + ADIM] = result[part * rows : (part + 1) * rows]
 
 
 def norm_kernel(part, hops, *refs):
@@ -452,41 +509,53 @@
     params = [dt, conv_x_weight, conv_x_bias, conv_bc_weight, conv_bc_bias, dt_bias, a_log]
     pieces = -(-(width + bc_width) // per_group)
     tail_rows = EDGE * -(-4 * pieces // EDGE)
-    last_edge = rows // EDGE - 1
-
-    xcs, bccs, states = [], [], []
-    for part in range(groups):
-        first_part, last_part = part == 0, part == groups - 1
-        outs = [
-            shape((rows, per_group), BF16),
-            shape((rows, 2 * STATE), BF16),
-            shape((STATE + tail_rows * first_part, per_group), BF16),
-        ]
-        operands = [x_raw, bc_raw, *params, doc_lens]
-        specs = [tile(rows, per_group, 0, part), tile(rows, 2 * STATE, 0, part)] + [WHOLE] * 7 + [SCALARS]
-        if first_part:
-            operands += [x_raw, bc_raw]
-            specs += [tile(EDGE, width, last_edge, 0), tile(EDGE, bc_width, last_edge, 0)]
-        if last_part:
-            outs.append(shape((rows, 2 * keys.shape[1]), BF16))
-            operands += [keys, values]
-            specs += [WHOLE] * 2
-        got = call(
-            functools.partial(state_kernel, part, first_part, last_part),
-            f"state_part{part}",
-            outs,
-            operands,
-            specs,
-            scratch=[pltpu.VMEM((4, rows + 8, CHUNK), F32)],
-            limit=VMEM_ALL if first_part else VMEM_LIMIT,
-        )
-        xcs.append(got[0])
-        bccs.append(got[1])
-        states.append(got[2])
-    kvs = [got[3], onward(got[3])]
-    slots = [onward(states[0])]
-
-    partial, weight, through, inside, flags, entry = call(
+
+    (message,) = call(
+        first_state_kernel,
+        "first_state",
+        [shape((STATE + tail_rows, per_group), BF16)],
+        [x_raw, bc_raw, *(a if a.ndim > 1 else a[None] for a in params), doc_lens],
+        [UNTOUCHED] * 10,
+        out_specs=[UNTOUCHED],
+        scratch=[
+            pltpu.VMEM((rows, per_group), BF16),
+            pltpu.VMEM((rows, STATE), BF16),
+            pltpu.VMEM((per_group // HDIM, rows), F32),
+            pltpu.VMEM((conv_x_weight.shape[0], per_group), F32),
+            pltpu.VMEM((1, per_group), F32),
+            pltpu.VMEM((conv_x_weight.shape[0], STATE), F32),
+            pltpu.VMEM((1, STATE), F32),
+            pltpu.VMEM((1, heads), F32),
+            pltpu.VMEM((1, heads), F32),
+            pltpu.SMEM(doc_lens.shape, jnp.int32),
+            pltpu.VMEM((EDGE, width), BF16),
+            pltpu.VMEM((EDGE, bc_width), BF16),
+            pltpu.VMEM((STATE + tail_rows, per_group), BF16),
+            pltpu.VMEM((rows + 8, STATE), F32),
+            pltpu.VMEM((4, rows + 8, CHUNK), F32),
+            pltpu.SemaphoreType.DMA((12,)),
+            pltpu.SemaphoreType.DMA((per_group // CHUNK + 1,)),
+        ],
+        limit=VMEM_ALL,
+    )
+    slots = [onward(message)]
+    xc, bcc, kv, *states = call(
+        functools.partial(conv_kernel, groups),
+        "conv_all",
+        [
+            shape((rows, width), BF16),
+            shape((rows, bc_width), BF16),
+            shape((rows, 2 * keys.shape[1]), BF16),
+            *(shape((STATE, per_group), BF16) for _ in range(groups - 1)),
+        ],
+        [x_raw, bc_raw, *params, doc_lens, keys, values],
+        [WHOLE] * 9 + [SCALARS] + [WHOLE] * 2,
+        scratch=[pltpu.VMEM((4, rows + 8, CHUNK), F32)],
+    )
+    states = [message, *states]
+    kvs = [kv, onward(kv)]
+
+    partial, weight, through, inside, flags, entry, wide_skip = call(
         functools.partial(prepare_kernel, hops),
         "prepare",
         [
@@ -496,9 +565,10 @@
             shape((conv_x_weight.shape[0] - 1, 8, CHUNK), F32),
             shape((hops, 8, CHUNK), F32),
             shape((rows, heads), F32),
+            shape((8, width), F32),
         ],
-        [x_raw, bc_raw, *params, doc_lens],
-        [tile(EDGE, width, 0, 0), tile(EDGE, bc_width, 0, 0)] + [WHOLE] * 7 + [SCALARS],
+        [x_raw, bc_raw, *params, skip_d, doc_lens],
+        [tile(EDGE, width, 0, 0), tile(EDGE, bc_width, 0, 0)] + [WHOLE] * 8 + [SCALARS],
         scratch=[pltpu.VMEM((16, width + bc_width), F32)],
     )
 
@@ -532,14 +602,14 @@
                 [
                     shape((rows, width), F32),
                     shape((rows, groups * STATE), BF16),
-                    shape(got[3].shape, BF16),
+                    shape(kv.shape, BF16),
                     *(shape((STATE, per_group), BF16) for _ in range(groups)),
                 ],
                 [
                     slots[0], partial, weight, inside, conv_x_weight, conv_bc_weight, dt, dt_bias, a_log,
-                    skip_d, doc_lens, kvs[1], *xcs, *bccs, *states,
+                    wide_skip, doc_lens, kvs[1], xc, bcc, *states,
                 ],
-                [WHOLE] * 10 + [SCALARS] + [WHOLE] * (1 + 3 * groups),
+                [WHOLE] * 10 + [SCALARS] + [WHOLE] * (3 + groups),
                 scratch=[pltpu.VMEM((4, 16, CHUNK), F32)],
             )
     for hop in range(1, hops):

time: 36.2 us -> 35.2 us (0.972)
  waiting for transfers between devices: 6.33 us -> 4.23 us
  starting transfers between devices: 14.5 us -> 15.9 us
  local copies, waits for them, and re-layouts: 0.71 us -> 0.08 us
  Pallas kernels: 13.4 us -> 13.8 us
    ppermute x5, waiting for transfers between devices: 6.33 us -> 4.23 us  [onward(): lax.ppermute(value, 'seq', [(source, source + 1) for source in range(firs...]
    ppermute x5, starting transfers between devices: 14.5 us -> 15.9 us  [onward(): lax.ppermute(value, 'seq', [(source, source + 1) for source in range(firs...]
    unnamed x38 -> x34, local copies, waits for them, and re-layouts: 0.71 us -> 0.08 us
    pallas_call x9, Pallas kernels: 13.4 us -> 13.8 us  [call(): pl.pallas_call(kernel, name=name, grid=(1,), out_shape=outs, in_specs=spe...]
  transfers between devices with their start and end apart: 5 -> 5, of which waited for: 3 -> 4; matrix products, arithmetic and copies ran while one was open for 0% -> 0% of each run, Pallas kernels for 26% -> 28%
where the time goes in v5:
time: 35.2 us; the launch traced here: 35 us
  starting transfers between devices  15.9 us (45%)
  Pallas kernels  13.8 us (39%)
  waiting for transfers between devices  4.23 us (12%)
  between operations  0.95 us (3%)
    ppermute x5, starting transfers between devices, onward(): lax.ppermute(value, 'seq', [(source, source + 1) for source in range(firs...  15.9 us
    pallas_call x9, Pallas kernels, call(): pl.pallas_call(kernel, name=name, grid=(1,), out_shape=outs, in_specs=spe...  13.8 us
    ppermute x5, waiting for transfers between devices, onward(): lax.ppermute(value, 'seq', [(source, source + 1) for source in range(firs...  4.23 us
  transfers between devices with their start and end apart: 5, of which 4 were waited for; matrix products, arithmetic and copies ran while one was open for 0% of the time, Pallas kernels for 28%

profile of v5, /device:TPU:22, one launch (start us, length us, event | category | flops | bytes accessed | tf_op | source)
XLA Modules:
  0.0 35.0 jit_solution(17016593341632829408)
XLA Ops:
  0.6 0.0 copy-start
  0.6 0.0 copy-start.4
  0.7 0.0 copy-start.5
  0.7 0.0 copy-start.6
  0.7 0.0 copy-start.7
  0.7 0.0 copy-start.8
  0.7 0.0 copy-start.9
  0.7 0.0 copy-start.10
  0.7 0.0 copy-start.12
  0.8 2.9 %first_state.1.refs_14_.refs_1_ = bf16[144,1024]{1,0:T(8,128)(2,1)} custom-call(bf16[128,2048]{1,0:T(8,128)(2,1)} %refs_0_.6, bf16[128,512]{1,0:T(8,128)(2,1)} %refs_1_.5, f32[32,128]{1,0:T(8,128)} %bitcast.5, f32[4,2048]{1,0:T(4,128)} %refs_7_.7, f32[1,2048]{1,0:T(1,128)} %bitcast.9, f32[4,512]{1,0:T(4,128)} %refs_8_.7, f32[1,512]{1,0:T(1,128)} %bitcast.10, ...), custom_call_target="tpu_custom_call" | custom-call | flops 2000000000 | bytes 1018128 | tf_op jit(solution)/shard_map/first_state/pallas_call | solution.py:461
  3.6 3.5 %collective-permute-start = (bf16[144,1024]{1,0:T(8,128)(2,1)}, bf16[144,1024]{1,0:T(8,128)(2,1)S(1)}, u32[]{:S(2)}, u32[]{:S(2)}) collective-permute-start(bf16[144,1024]{1,0:T(8,128)(2,1)} %first_state.1.refs_14_.refs_1_), channel_id=1, source_target_pairs={{0,4},{4,8},{8,12},{1,5},{5,9},{9,13},{2,6},{6,10},{10,14},{3,7},{... | collective-permute-start | bytes 884744 | tf_op jit(solution)/shard_map/ppermute | solution.py:477
  7.2 2.3 %conv_all.1 = (bf16[128,2048]{1,0:T(8,128)(2,1)S(1)}, bf16[128,512]{1,0:T(8,128)(2,1)S(1)}, bf16[128,512]{1,0:T(8,128)(2,1)S(1)}, bf16[128,1024]{1,0:T(8,128)(2,1)S(1)}) custom-call(bf16[128,2048]{1,0:T(8,128)(2,1)S(1)} %copy-done, bf16[128,512]{1,0:T(8,128)(2,1)S(1)} %copy-done.4, f32[32,128]{1,0:T(8,128)S(1)} %bitcast.6, f32[4,2048]{1,0:T(4,128)S(1)} %copy-done.7, ...), custom_call_target="tpu_custom_call" | custom-call | flops 2000000000 | bytes 1902864 | tf_op jit(solution)/shard_map/conv_all/pallas_call | solution.py:461
  9.5 0.0 copy-start.13
  9.5 0.0 copy-start.2
  9.6 2.1 %collective-permute-start.1 = (bf16[128,512]{1,0:T(8,128)(2,1)S(1)}, bf16[128,512]{1,0:T(8,128)(2,1)S(1)}, u32[]{:S(2)}, u32[]{:S(2)}) collective-permute-start(bf16[128,512]{1,0:T(8,128)(2,1)S(1)} %get-tuple-element.21.refs_3_), channel_id=1, source_target_pairs={{0,4},{4,8},{8,12},{1,5},{5,9},{9,13},{2,6},{6,10},{10,14},{3,7},{... | collective-permute-start | bytes 393224 | tf_op jit(solution)/shard_map/ppermute | solution.py:477
  11.6 1.1 %prepare.1 = (f32[8,2560]{1,0:T(8,128)S(1)}, f32[8,2048]{1,0:T(8,128)S(1)}, f32[8,2048]{1,0:T(8,128)S(1)}, f32[3,8,256]{2,1,0:T(8,128)S(1)}, f32[2,8,256]{2,1,0:...) custom-call(bf16[128,2048]{1,0:T(8,128)(2,1)S(1)} %copy-done, bf16[128,512]{1,0:T(8,128)(2,1)S(1)} %copy-done.4, ...), custom_call_target="tpu_custom_call" | custom-call | flops 2000000000 | bytes 1059216 | tf_op jit(solution)/shard_map/prepare/pallas_call | solution.py:461
  12.7 2.4 %collective-permute-done.refs_0_.refs_6_ = bf16[144,1024]{1,0:T(8,128)(2,1)S(1)} collective-permute-done((bf16[144,1024]{1,0:T(8,128)(2,1)}, bf16[144,1024]{1,0:T(8,128)(2,1)S(1)}, u32[]{:S(2)}, u32[]{:S(2)}) %collective-permute-start) | collective-permute-done | bytes 294944 | tf_op jit(solution)/shard_map/ppermute | solution.py:477
  15.2 0.3 relay_slot2.1
  15.5 4.0 %collective-permute-start.2 = (bf16[128,1024]{1,0:T(8,128)(2,1)S(1)}, bf16[128,1024]{1,0:T(8,128)(2,1)S(1)}, u32[]{:S(2)}, u32[]{:S(2)}) collective-permute-start(bf16[128,1024]{1,0:T(8,128)(2,1)S(1)} %relay_slot2.1), channel_id=1, source_target_pairs={{0,4},{4,8},{8,12},{1,5},{5,9},{9,13},{2,6},{6,10},{10,14},{3,7},{... | collective-permute-start | bytes 786440 | tf_op jit(solution)/shard_map/ppermute | solution.py:477
  19.5 0.0 collective-permute-done.1.refs_11_.refs_2_
  19.5 2.6 %local_mix.1 = (f32[128,2048]{1,0:T(8,128)S(1)}, bf16[128,256]{1,0:T(8,128)(2,1)S(1)}, bf16[128,512]{1,0:T(8,128)(2,1)S(1)}, bf16[128,1024]{1,0:T(8,128)(2,1)}, bf16[128,1024]{1,0:T(8,128)(2,1)S(1)}) custom-call(bf16[144,1024]{1,0:T(8,128)(2,1)S(1)} %collective-permute-done.refs_0_.refs_6_, f32[8,2560]{1,0:T(8,128)S(1)} %get-tuple-element.17.refs_1_.refs_2_, ...), custom_call_target="tpu_custom_call" | custom-call | flops 2000000000 | bytes 3703056 | tf_op jit(solution)/shard_map/local_mix/pallas_call | solution.py:461
  22.0 1.9 %collective-permute-start.4 = (bf16[128,512]{1,0:T(8,128)(2,1)S(1)}, bf16[128,512]{1,0:T(8,128)(2,1)S(1)}, u32[]{:S(2)}, u32[]{:S(2)}) collective-permute-start(bf16[128,512]{1,0:T(8,128)(2,1)S(1)} %get-tuple-element.31), channel_id=1, source_target_pairs={{4,8},{8,12},{5,9},{9,13},{6,10},{10,14},{7,11},{11,15},{20,24},{2... | collective-permute-start | bytes 393224 | tf_op jit(solution)/shard_map/ppermute | solution.py:477
  23.9 0.3 collective-permute-done.2.refs_0_.refs_7_.refs_6_
  24.2 0.1 relay_slot3.1
  24.3 0.0 copy-start.1
  24.3 0.0 copy-start.11
  24.3 4.5 %collective-permute-start.3 = (bf16[128,1024]{1,0:T(8,128)(2,1)S(1)}, bf16[128,1024]{1,0:T(8,128)(2,1)S(1)}, u32[]{:S(2)}, u32[]{:S(2)}) collective-permute-start(bf16[128,1024]{1,0:T(8,128)(2,1)S(1)} %relay_slot3.1), channel_id=1, source_target_pairs={{4,8},{8,12},{5,9},{9,13},{6,10},{10,14},{7,11},{11,15},{20,24},{2... | collective-permute-start | bytes 786440 | tf_op jit(solution)/shard_map/ppermute | solution.py:477
  28.8 1.4 %collective-permute-done.4.refs_1_ = bf16[128,512]{1,0:T(8,128)(2,1)S(1)} collective-permute-done((bf16[128,512]{1,0:T(8,128)(2,1)S(1)}, bf16[128,512]{1,0:T(8,128)(2,1)S(1)}, u32[]{:S(2)}, u32[]{:S(2)}) %collective-permute-start.4) | collective-permute-done | bytes 131104 | tf_op jit(solution)/shard_map/ppermute | solution.py:477
  30.2 2.2 %attend.1 = bf16[128,1024]{1,0:T(8,128)(2,1)} custom-call(bf16[128,1024]{1,0:T(8,128)(2,1)S(1)} %copy-done.3, bf16[128,512]{1,0:T(8,128)(2,1)S(1)} %collective-permute-done.4.refs_1_, bf16[128,512]{1,0:T(8,128)(2,1)S(1)} %collective-permute-done.1.refs_11_.refs_2_, bf16[128,512]{1,0:T(8,128)(2,1)S(1)} %get-tuple-element.21.refs_3_, s32[4]{0:T(128)S(1)} %copy-done.16), custom_call_target="tpu_custom_call" | custom-call | flops 2000000000 | bytes 917520 | tf_op jit(solution)/shard_map/attend/pallas_call | solution.py:461
  32.5 1.2 %norm_part0.1.refs_8_ = bf16[128,2048]{1,0:T(8,128)(2,1)} custom-call(f32[128,2048]{1,0:T(8,128)S(1)} %get-tuple-element.25.refs_0_, bf16[128,256]{1,0:T(8,128)(2,1)S(1)} %get-tuple-element.26.refs_1_, f32[128,32]{1,0:T(8,128)S(1)} %get-tuple-element.27.refs_2_, bf16[128,2048]{1,0:T(8,128)(2,1)S(1)} %copy-done.1, f32[2048]{0:T(1024)S(1)} %copy-done.11, ...), custom_call_target="tpu_custom_call" | custom-call | flops 2000000000 | bytes 2760704 | tf_op jit(solution)/shard_map/norm_part0/pallas_call | solution.py:461
  33.6 0.1 collective-permute-done.3.refs_7_
  33.8 1.2 %norm_part1.1 = bf16[128,2048]{1,0:T(8,128)(2,1)} custom-call(f32[128,2048]{1,0:T(8,128)S(1)} %get-tuple-element.25.refs_0_, bf16[128,256]{1,0:T(8,128)(2,1)S(1)} %get-tuple-element.26.refs_1_, f32[128,32]{1,0:T(8,128)S(1)} %get-tuple-element.27.refs_2_, bf16[128,2048]{1,0:T(8,128)(2,1)S(1)} %copy-done.1, ...), custom_call_target="tpu_custom_call", output_to_operand_aliasing={{}: (8, {})} | custom-call | flops 2000000000 | bytes 3252224 | tf_op jit(solution)/shard_map/norm_part1/pallas_call | solution.py:461
  (21 shorter events, 0.0 us)
Async XLA Ops:
  0.6 6.5 %copy-start = (bf16[128,2048]{1,0:T(8,128)(2,1)S(1)}, bf16[128,2048]{1,0:T(8,128)(2,1)}, u32[]{:S(2)}) copy-start(bf16[128,2048]{1,0:T(8,128)(2,1)} %refs_0_.6) | copy-start | bytes 1572868
  0.6 6.5 %copy-start.4 = (bf16[128,512]{1,0:T(8,128)(2,1)S(1)}, bf16[128,512]{1,0:T(8,128)(2,1)}, u32[]{:S(2)}) copy-start(bf16[128,512]{1,0:T(8,128)(2,1)} %refs_1_.5) | copy-start | bytes 393220
  0.7 6.5 %copy-start.5 = (bf16[128,256]{1,0:T(8,128)(2,1)S(1)}, bf16[128,256]{1,0:T(8,128)(2,1)}, u32[]{:S(2)}) copy-start(bf16[128,256]{1,0:T(8,128)(2,1)} %refs_10_.4) | copy-start | bytes 196612
  0.7 6.5 %copy-start.6 = (bf16[128,256]{1,0:T(8,128)(2,1)S(1)}, bf16[128,256]{1,0:T(8,128)(2,1)}, u32[]{:S(2)}) copy-start(bf16[128,256]{1,0:T(8,128)(2,1)} %refs_11_.1) | copy-start | bytes 196612
  0.7 6.5 %copy-start.7 = (f32[4,2048]{1,0:T(4,128)S(1)}, f32[4,2048]{1,0:T(4,128)}, u32[]{:S(2)}) copy-start(f32[4,2048]{1,0:T(4,128)} %refs_7_.7) | copy-start | bytes 98308
  0.7 6.5 %copy-start.8 = (f32[128,32]{0,1:T(8,128)S(1)}, f32[128,32]{0,1:T(8,128)}, u32[]{:S(2)}) copy-start(f32[128,32]{0,1:T(8,128)} %param.19) | copy-start | bytes 49156
  0.7 6.5 %copy-start.9 = (f32[2048]{0:T(1024)S(1)}, f32[2048]{0:T(1024)}, u32[]{:S(2)}) copy-start(f32[2048]{0:T(1024)} %refs_4_.7) | copy-start | bytes 24580
  0.7 6.5 %copy-start.10 = (f32[4,512]{1,0:T(4,128)S(1)}, f32[4,512]{1,0:T(4,128)}, u32[]{:S(2)}) copy-start(f32[4,512]{1,0:T(4,128)} %refs_8_.7) | copy-start | bytes 24580
  0.7 6.5 %copy-start.12 = (f32[512]{0:T(512)S(1)}, f32[512]{0:T(512)}, u32[]{:S(2)}) copy-start(f32[512]{0:T(512)} %refs_6_.3) | copy-start | bytes 6148
  0.7 6.5 %copy-start.14 = (f32[32]{0:T(128)S(1)}, f32[32]{0:T(128)}, u32[]{:S(2)}) copy-start(f32[32]{0:T(128)} %refs_7_.6) | copy-start | bytes 388
  0.7 6.5 %copy-start.15 = (f32[32]{0:T(128)S(1)}, f32[32]{0:T(128)}, u32[]{:S(2)}) copy-start(f32[32]{0:T(128)} %refs_8_.6) | copy-start | bytes 388
  0.7 6.5 %copy-start.16 = (s32[4]{0:T(128)S(1)}, s32[4]{0:T(128)}, u32[]{:S(2)}) copy-start(s32[4]{0:T(128)} %refs_4_.11) | copy-start | bytes 52
  3.6 11.5 %collective-permute-start = (bf16[144,1024]{1,0:T(8,128)(2,1)}, bf16[144,1024]{1,0:T(8,128)(2,1)S(1)}, u32[]{:S(2)}, u32[]{:S(2)}) collective-permute-start(bf16[144,1024]{1,0:T(8,128)(2,1)} %first_state.1.refs_14_.refs_1_), channel_id=1, source_target_pairs={{0,4},{4,8},{8,12},{1,5},{5,9},{9,13},{2,6},{6,10},{10,14},{3,7},{... | collective-permute-start | bytes 884744 | tf_op jit(solution)/shard_map/ppermute | solution.py:477
  9.5 2.1 %copy-start.13 = (f32[32]{0:T(128)S(1)}, f32[32]{0:T(128)}, u32[]{:S(2)}) copy-start(f32[32]{0:T(128)} %refs_9_.4) | copy-start | bytes 388
  9.5 5.6 %copy-start.2 = (bf16[144,1024]{1,0:T(8,128)(2,1)S(1)}, bf16[144,1024]{1,0:T(8,128)(2,1)}, u32[]{:S(2)}) copy-start(bf16[144,1024]{1,0:T(8,128)(2,1)} %first_state.1.refs_14_.refs_1_) | copy-start | bytes 884740
  9.6 9.9 %collective-permute-start.1 = (bf16[128,512]{1,0:T(8,128)(2,1)S(1)}, bf16[128,512]{1,0:T(8,128)(2,1)S(1)}, u32[]{:S(2)}, u32[]{:S(2)}) collective-permute-start(bf16[128,512]{1,0:T(8,128)(2,1)S(1)} %get-tuple-element.21.refs_3_), channel_id=1, source_target_pairs={{0,4},{4,8},{8,12},{1,5},{5,9},{9,13},{2,6},{6,10},{10,14},{3,7},{... | collective-permute-start | bytes 393224 | tf_op jit(solution)/shard_map/ppermute | solution.py:477
  15.5 8.7 %collective-permute-start.2 = (bf16[128,1024]{1,0:T(8,128)(2,1)S(1)}, bf16[128,1024]{1,0:T(8,128)(2,1)S(1)}, u32[]{:S(2)}, u32[]{:S(2)}) collective-permute-start(bf16[128,1024]{1,0:T(8,128)(2,1)S(1)} %relay_slot2.1), channel_id=1, source_target_pairs={{0,4},{4,8},{8,12},{1,5},{5,9},{9,13},{2,6},{6,10},{10,14},{3,7},{... | collective-permute-start | bytes 786440 | tf_op jit(solution)/shard_map/ppermute | solution.py:477
  22.0 8.2 %collective-permute-start.4 = (bf16[128,512]{1,0:T(8,128)(2,1)S(1)}, bf16[128,512]{1,0:T(8,128)(2,1)S(1)}, u32[]{:S(2)}, u32[]{:S(2)}) collective-permute-start(bf16[128,512]{1,0:T(8,128)(2,1)S(1)} %get-tuple-element.31), channel_id=1, source_target_pairs={{4,8},{8,12},{5,9},{9,13},{6,10},{10,14},{7,11},{11,15},{20,24},{2... | collective-permute-start | bytes 393224 | tf_op jit(solution)/shard_map/ppermute | solution.py:477
  24.2 6.0 %copy-start.3 = (bf16[128,1024]{1,0:T(8,128)(2,1)S(1)}, bf16[128,1024]{1,0:T(8,128)(2,1)}, u32[]{:S(2)}) copy-start(bf16[128,1024]{1,0:T(8,128)(2,1)} %refs_0_.7) | copy-start | bytes 786436
  24.3 8.2 %copy-start.1 = (bf16[128,2048]{1,0:T(8,128)(2,1)S(1)}, bf16[128,2048]{1,0:T(8,128)(2,1)}, u32[]{:S(2)}) copy-start(bf16[128,2048]{1,0:T(8,128)(2,1)} %refs_3_.9) | copy-start | bytes 1572868
  24.3 8.2 %copy-start.11 = (f32[2048]{0:T(1024)S(1)}, f32[2048]{0:T(1024)}, u32[]{:S(2)}) copy-start(f32[2048]{0:T(1024)} %refs_4_.10) | copy-start | bytes 24580
  24.3 9.5 %collective-permute-start.3 = (bf16[128,1024]{1,0:T(8,128)(2,1)S(1)}, bf16[128,1024]{1,0:T(8,128)(2,1)S(1)}, u32[]{:S(2)}, u32[]{:S(2)}) collective-permute-start(bf16[128,1024]{1,0:T(8,128)(2,1)S(1)} %relay_slot3.1), channel_id=1, source_target_pairs={{4,8},{8,12},{5,9},{9,13},{6,10},{10,14},{7,11},{11,15},{20,24},{2... | collective-permute-start | bytes 786440 | tf_op jit(solution)/shard_map/ppermute | solution.py:477

commit v6 on v5

--- a/solution.py
+++ b/solution.py
@@ -57,19 +57,22 @@
     return jnp.dot(both, spread, preferred_element_type=F32)
 
 
+def column(ref, heads):
+    return jnp.broadcast_to(ref[...].reshape(1, -1), (8, ref.size)).T[:heads, 0:1]
+
+
 def rates(dt_ref, dt_bias_ref, a_log_ref):
-    heads = dt_ref.shape[0]
-    step = softplus(dt_ref[...].T + dt_bias_ref[...].reshape(1, -1)[:, :heads])
-    rate = -step * jnp.exp(a_log_ref[...].reshape(1, -1)[:, :heads])
-    rows = step.shape[0]
+    heads, rows = dt_ref.shape
+    step = softplus(dt_ref[...] + column(dt_bias_ref, heads))
+    rate = -step * jnp.exp(column(a_log_ref, heads))
     row = lax.broadcasted_iota(jnp.int32, (rows, rows), 0)
-    column = lax.broadcasted_iota(jnp.int32, (rows, rows), 1)
-    lower = (row >= column).astype(F32).astype(BF16)
+    lane = lax.broadcasted_iota(jnp.int32, (rows, rows), 1)
+    upper = (row <= lane).astype(F32).astype(BF16)
     high = rate.astype(BF16)
     middle, low = halves(rate - high.astype(F32))
-    parts = jnp.concatenate([high, middle, low], axis=0)
-    lowers = jnp.concatenate([lower, lower, lower], axis=1)
-    return step, jnp.dot(lowers, parts, preferred_element_type=F32)
+    parts = jnp.concatenate([high, middle, low], axis=1)
+    uppers = jnp.concatenate([upper, upper, upper], axis=0)
+    return step, jnp.dot(parts, uppers, preferred_element_type=F32)
 
 
 def insides(first, shape, taps, lens_ref):
@@ -87,15 +90,6 @@
     return silu(total).astype(BF16)
 
 
-def state_weight(first, step, running, lens_ref):
-    rows = step.shape[0]
-    last_begin = doc_start(first + rows - 1, lens_ref)
-    position = first + lax.broadcasted_iota(jnp.int32, step.shape, 0)
-    return jnp.where(
-        position >= last_begin, step * jnp.exp(running[rows - 1 : rows] - running), 0.0
-    )
-
-
 def tail_lines(message, rows):
     block = message[rows:].astype(F32)
     return jnp.concatenate([block[at : at + 4] for at in range(0, block.shape[0], 4)], axis=1)
@@ -106,10 +100,12 @@
 
 
 def kept_weight(here, step, running, taps, lens_ref):
-    rows = step.shape[0]
-    weight = state_weight(here * rows, step, running, lens_ref)
-    row = lax.broadcasted_iota(jnp.int32, weight.shape, 0)
-    return jnp.where((row >= taps - 1) | (reach(here, rows, lens_ref) == 0), weight, 0.0)
+    rows = step.shape[1]
+    last_begin = doc_start((here + 1) * rows - 1, lens_ref)
+    row = lax.broadcasted_iota(jnp.int32, step.shape, 1)
+    weight = step * jnp.exp(running[:, rows - 1 : rows] - running)
+    kept = (here * rows + row >= last_begin) & ((row >= taps - 1) | (last_begin // rows >= here))
+    return jnp.where(kept, weight, 0.0).T
 
 
 def conv_rows(pad, raw, weight, bias, inside):
@@ -143,18 +139,14 @@
         edge_copies[-1].start()
 
     here = lax.axis_index("seq")
-    for at in (9, 2, 7, 8):
+    for at in order:
         copies[at].wait()
     inside = insides(here * rows, (rows, CHUNK), taps, lens_ref)
     step, running = rates(dt_ref, dt_bias_ref, a_log_ref)
     weight = kept_weight(here, step, running, taps, lens_ref)
-    for at in (1, 5, 6):
-        copies[at].wait()
     narrow = [mask[:, :STATE] for mask in inside]
     inputs = conv_rows(b_pad_ref, b_ref[...], wbc_ref[...], bbc_ref[...], narrow)
     turned = inputs.astype(F32).T.astype(BF16)
-    for at in (0, 3, 4):
-        copies[at].wait()
     slots = pad_ref.shape[0]
     outs = []
 
@@ -169,7 +161,8 @@
         xc = conv_rows(pad, x_ref[:, columns], wx_ref[:, columns], bx_ref[:, columns], inside)
         weighted = (xc.astype(F32) * widen(weight, start, CHUNK)).astype(BF16)
         out_ref[:STATE, columns] = jnp.dot(turned, weighted, preferred_element_type=F32).astype(BF16)
-        send(at, (pl.ds(0, STATE), pl.ds(start, CHUNK)))
+        if at % 2:
+            send(at // 2, (pl.ds(0, STATE), pl.ds(start - CHUNK, 2 * CHUNK)))
     for copy in edge_copies:
         copy.wait()
     edges = jnp.concatenate([x_edge_ref[...].astype(F32), bc_edge_ref[...].astype(F32)], axis=1)[EDGE - 4 :]
@@ -180,7 +173,7 @@
     while len(pieces) % (EDGE // 4):
         pieces.append(jnp.zeros_like(pieces[0]))
     out_ref[STATE:] = jnp.concatenate(pieces, axis=0).astype(BF16)
-    send(width // CHUNK, (pl.ds(STATE, out_ref.shape[0] - STATE), pl.ds(0, width)))
+    send(width // (2 * CHUNK), (pl.ds(STATE, out_ref.shape[0] - STATE), pl.ds(0, width)))
     for copy in outs:
         copy.wait()
 
@@ -222,7 +215,7 @@
 
 def prepare_kernel(hops, *refs):
     x_ref, bc_ref, dt_ref, wx_ref, bx_ref, wbc_ref, bbc_ref, dt_bias_ref, a_log_ref, skip_ref, lens_ref = refs[:11]
-    partial_ref, weight_ref, through_ref, inside_ref, flag_ref, entry_ref, wide_skip_ref, pad_ref = refs[11:]
+    partial_ref, weight_ref, through_ref, inside_ref, flag_ref, entry_ref, wide_skip_ref, begin_ref, pad_ref = refs[11:]
     width = x_ref.shape[1]
     rows, heads = entry_ref.shape
     taps = wx_ref.shape[0]
@@ -237,11 +230,13 @@
     for hop in range(1, hops):
         flag_ref[hop] = jnp.broadcast_to((before == hop).astype(F32), (8, CHUNK))
     step, running = rates(dt_ref, dt_bias_ref, a_log_ref)
-    position = first + lax.broadcasted_iota(jnp.int32, running.shape, 0)
-    entry_ref[...] = jnp.where(doc_start(position, lens_ref) < first, jnp.exp(running), 0.0)
+    begin = doc_start(first + lax.broadcasted_iota(jnp.int32, begin_ref.shape, 0), lens_ref)
+    begin_ref[...] = begin
+    turned = running.T
+    entry_ref[...] = jnp.where(begin[:, :heads] < first, jnp.exp(turned), 0.0)
     row = lax.broadcasted_iota(jnp.int32, (8, heads), 0)
-    total = running[rows - 1 : rows]
-    weight = step[:8] * jnp.exp(total - running[:8])
+    total = turned[rows - 1 : rows]
+    weight = step.T[:8] * jnp.exp(total - turned[:8])
     weight = jnp.where((row < taps - 1) & jnp.logical_not(own), weight, 0.0)
     through = jnp.where(own, 0.0, jnp.broadcast_to(jnp.exp(total), (8, heads)))
     skip = jnp.broadcast_to(skip_ref[...].reshape(1, -1), (8, heads))
@@ -321,18 +316,17 @@
 def local_kernel(groups, *refs):
     (
         message_ref, partial_ref, weight_ref, inside_ref, wx_ref, wbc_ref, dt_ref, dt_bias_ref,
-        a_log_ref, wide_skip_ref, lens_ref, kv_ref, xc_ref, bcc_ref,
-    ) = refs[:14]
-    state_refs = refs[14 : 14 + groups]
-    out_ref, c_ref, kv_out_ref = refs[14 + groups : 17 + groups]
-    full_refs = refs[17 + groups : 17 + 2 * groups]
+        a_log_ref, wide_skip_ref, begin_ref, xc_ref, bcc_ref,
+    ) = refs[:13]
+    state_refs = refs[13 : 13 + groups]
+    out_ref, c_ref = refs[13 + groups : 15 + groups]
+    full_refs = refs[15 + groups : 15 + 2 * groups]
     pad_ref = refs[-1]
     rows, width = xc_ref.shape
     per_group = width // groups
     first = lax.axis_index("seq") * rows
     lines = tail_lines(message_ref, STATE)
     slots = pad_ref.shape[0]
-    kv_out_ref[...] = kv_ref[...]
 
     def top(w_ref, slot, at, start, below):
         new = first_rows(lines, partial_ref, inside_ref, w_ref, pad_ref, slot, at, start)
@@ -340,12 +334,10 @@
         return jnp.concatenate([jnp.concatenate([new.astype(F32), old], axis=0).astype(BF16), below[EDGE:]], axis=0)
 
     row = lax.broadcasted_iota(jnp.int32, (rows, rows), 0)
-    column = lax.broadcasted_iota(jnp.int32, (rows, rows), 1)
-    begin = doc_start(first + row, lens_ref)
-    linked = (row >= column) & (first + column >= begin)
-    step, running = rates(dt_ref, dt_bias_ref, a_log_ref)
-    turned_running = running.T
-    turned_step = step.T
+    lane_row = lax.broadcasted_iota(jnp.int32, (rows, rows), 1)
+    linked = (row >= lane_row) & (first + lane_row >= begin_ref[...])
+    turned_step, turned_running = rates(dt_ref, dt_bias_ref, a_log_ref)
+    running = turned_running.T
     pair_width = 2 * HDIM
     lane = lax.broadcasted_iota(jnp.int32, (rows, pair_width), 1)
     for group in range(groups):
@@ -390,7 +382,7 @@
 def attend_kernel(hops, *refs):
     q_ref = refs[0]
     kv_refs = refs[1 : 2 + hops]
-    lens_ref, out_ref = refs[2 + hops :]
+    begin_ref, out_hbm_ref, out_ref, sems = refs[2 + hops :]
     rows = q_ref.shape[0]
     kv_heads = kv_refs[0].shape[1] // (2 * ADIM)
     share = QHEADS // KVHEADS
@@ -398,10 +390,12 @@
     here = lax.axis_index("seq")
     row = here * rows + lax.broadcasted_iota(jnp.int32, (rows, count), 0)
     column = (here - hops) * rows + lax.broadcasted_iota(jnp.int32, (rows, count), 1)
-    allowed = (column <= row) & (column >= doc_start(row, lens_ref))
+    begin = jnp.concatenate([begin_ref[...]] * (hops + 1), axis=1)
+    allowed = (column <= row) & (column >= begin)
     scale = ADIM ** (-0.5)
     ones = jnp.ones((count, ADIM), BF16)
     allowed = jnp.concatenate([allowed] * share, axis=0)
+    copies = []
     for head in range(kv_heads):
         low = head * ADIM
         keys = jnp.concatenate([ref[:, low : low + ADIM] for ref in kv_refs], axis=0)
@@ -417,12 +411,19 @@
         result = (summed[:, :ADIM] / summed[:, ADIM:]).astype(BF16)
         for part, low in enumerate(lows):
             out_ref[:, low : low + ADIM] = result[part * rows : (part + 1) * rows]
+        columns = pl.ds(head * share * ADIM, share * ADIM)
+        copies.append(
+            pltpu.make_async_copy(out_ref.at[:, columns], out_hbm_ref.at[:, columns], sems.at[head])
+        )
+        copies[-1].start()
+    for copy in copies:
+        copy.wait()
 
 
 def norm_kernel(part, hops, *refs):
     mixed_ref, c_ref, entry_ref, z_ref, gain_ref, flag_ref = refs[:6]
     got_refs = refs[6 : 6 + hops]
-    out_ref, gated_ref = refs[-2:]
+    out_hbm_ref, gated_ref, out_ref, sems = refs[-4:]
     rows, width = gated_ref.shape
     heads = width // HDIM
     entry = entry_ref[:, part * heads : (part + 1) * heads]
@@ -441,10 +442,21 @@
         gated_ref[:, columns] = gated
         squares = squares + jnp.sum(gated * gated, axis=1, keepdims=True)
     multiplier = lax.rsqrt(squares * (1.0 / width) + EPSILON)
+    copies = []
     for start in range(0, width, CHUNK):
         columns = slice(start, start + CHUNK)
         gain = gain_ref[part * width + start : part * width + start + CHUNK]
         out_ref[:, columns] = (gated_ref[:, columns] * multiplier * gain.reshape(1, -1)).astype(BF16)
+        copies.append(
+            pltpu.make_async_copy(
+                out_ref.at[:, pl.ds(start, CHUNK)],
+                out_hbm_ref.at[:, pl.ds(part * width + start, CHUNK)],
+                sems.at[start // CHUNK],
+            )
+        )
+        copies[-1].start()
+    for copy in copies:
+        copy.wait()
 
 
 WHOLE = pl.BlockSpec(memory_space=pltpu.VMEM)
@@ -534,7 +546,7 @@
             pltpu.VMEM((rows + 8, STATE), F32),
             pltpu.VMEM((4, rows + 8, CHUNK), F32),
             pltpu.SemaphoreType.DMA((12,)),
-            pltpu.SemaphoreType.DMA((per_group // CHUNK + 1,)),
+            pltpu.SemaphoreType.DMA((per_group // (2 * CHUNK) + 1,)),
         ],
         limit=VMEM_ALL,
     )
@@ -555,7 +567,7 @@
     states = [message, *states]
     kvs = [kv, onward(kv)]
 
-    partial, weight, through, inside, flags, entry, wide_skip = call(
+    partial, weight, through, inside, flags, entry, wide_skip, begin = call(
         functools.partial(prepare_kernel, hops),
         "prepare",
         [
@@ -566,6 +578,7 @@
             shape((hops, 8, CHUNK), F32),
             shape((rows, heads), F32),
             shape((8, width), F32),
+            shape((rows, rows), jnp.int32),
         ],
         [x_raw, bc_raw, *params, skip_d, doc_lens],
         [tile(EDGE, width, 0, 0), tile(EDGE, bc_width, 0, 0)] + [WHOLE] * 8 + [SCALARS],
@@ -596,36 +609,39 @@
         )
         slots.append(onward(passed, max(0, slot - groups)))
         if fulls is None:
-            mixed, c_out, kv_on, *fulls = call(
+            mixed, c_out, *fulls = call(
                 functools.partial(local_kernel, groups),
                 "local_mix",
                 [
                     shape((rows, width), F32),
                     shape((rows, groups * STATE), BF16),
-                    shape(kv.shape, BF16),
                     *(shape((STATE, per_group), BF16) for _ in range(groups)),
                 ],
                 [
                     slots[0], partial, weight, inside, conv_x_weight, conv_bc_weight, dt, dt_bias, a_log,
-                    wide_skip, doc_lens, kvs[1], xc, bcc, *states,
+                    wide_skip, begin, xc, bcc, *states,
                 ],
-                [WHOLE] * 10 + [SCALARS] + [WHOLE] * (3 + groups),
+                [WHOLE] * (13 + groups),
                 scratch=[pltpu.VMEM((4, 16, CHUNK), F32)],
             )
     for hop in range(1, hops):
-        kvs.append(onward(kv_on if hop == 1 else kvs[-1], hop))
+        kvs.append(onward(kvs[-1], hop))
 
     (attn_out,) = call(
         functools.partial(attend_kernel, hops),
         "attend",
         [shape(queries.shape, BF16)],
-        [queries, *reversed(kvs), doc_lens],
-        [WHOLE] * (hops + 2) + [SCALARS],
+        [queries, *reversed(kvs), begin],
+        [WHOLE] * (hops + 3),
+        out_specs=[UNTOUCHED],
+        scratch=[
+            pltpu.VMEM(queries.shape, BF16),
+            pltpu.SemaphoreType.DMA((keys.shape[1] // ADIM,)),
+        ],
     )
     mamba_out = None
     for part in range(groups):
         operands = [mixed, c_out, entry, z_gate, norm_gain, flags, *slots[part : part + hops]]
-        block = tile(rows, per_group, 0, part)
         specs = [WHOLE] * (6 + hops)
         aliases = {}
         if mamba_out is not None:
@@ -638,8 +654,12 @@
             [shape((rows, width), BF16)],
             operands,
             specs,
-            out_specs=[block],
-            scratch=[pltpu.VMEM((rows, per_group), F32)],
+            out_specs=[UNTOUCHED],
+            scratch=[
+                pltpu.VMEM((rows, per_group), F32),
+                pltpu.VMEM((rows, per_group), BF16),
+                pltpu.SemaphoreType.DMA((per_group // CHUNK,)),
+            ],
             aliases=aliases,
         )
     return (mamba_out, attn_out)

time: 35.2 us -> 35.4 us (level)
  waiting for transfers between devices: 4.23 us -> 5.73 us
  starting transfers between devices: 15.9 us -> 15.2 us
  Pallas kernels: 13.8 us -> 13.2 us
    ppermute x5, waiting for transfers between devices: 4.23 us -> 5.73 us  [onward(): lax.ppermute(value, 'seq', [(source, source + 1) for source in range(firs...]
    ppermute x5, starting transfers between devices: 15.9 us -> 15.2 us  [onward(): lax.ppermute(value, 'seq', [(source, source + 1) for source in range(firs...]
    pallas_call x9, Pallas kernels: 13.8 us -> 13.2 us  [call(): pl.pallas_call(kernel, name=name, grid=(1,), out_shape=outs, in_specs=spe...]
  transfers between devices with their start and end apart: 5 -> 5, of which waited for: 4 -> 3; matrix products, arithmetic and copies ran while one was open for 0% -> 0% of each run, Pallas kernels for 28% -> 26%
where the time goes in v6:
time: 35.4 us; the launch traced here: 35.2 us
  starting transfers between devices  15.2 us (43%)
  Pallas kernels  13.2 us (37%)
  waiting for transfers between devices  5.73 us (16%)
  between operations  1 us (3%)
    ppermute x5, starting transfers between devices, onward(): lax.ppermute(value, 'seq', [(source, source + 1) for source in range(firs...  15.2 us
    pallas_call x9, Pallas kernels, call(): pl.pallas_call(kernel, name=name, grid=(1,), out_shape=outs, in_specs=spe...  13.2 us
    ppermute x5, waiting for transfers between devices, onward(): lax.ppermute(value, 'seq', [(source, source + 1) for source in range(firs...  5.73 us
  transfers between devices with their start and end apart: 5, of which 3 were waited for; matrix products, arithmetic and copies ran while one was open for 0% of the time, Pallas kernels for 26%

profile of v6, /device:TPU:22, one launch (start us, length us, event | category | flops | bytes accessed | tf_op | source)
XLA Modules:
  0.0 35.2 jit_solution(5262704247855629932)
XLA Ops:
  0.6 0.0 copy-start
  0.6 0.0 copy-start.4
  0.7 0.0 copy-start.5
  0.7 0.0 copy-start.6
  0.7 0.0 copy-start.7
  0.7 0.0 copy-start.8
  0.7 0.0 copy-start.9
  0.7 0.0 copy-start.10
  0.7 0.0 copy-start.12
  0.8 3.1 %first_state.1.refs_13_.refs_1_ = bf16[144,1024]{1,0:T(8,128)(2,1)} custom-call(bf16[128,2048]{1,0:T(8,128)(2,1)} %refs_0_.6, bf16[128,512]{1,0:T(8,128)(2,1)} %refs_1_.5, f32[32,128]{1,0:T(8,128)} %bitcast.5, f32[4,2048]{1,0:T(4,128)} %refs_7_.7, f32[1,2048]{1,0:T(1,128)} %bitcast.9, f32[4,512]{1,0:T(4,128)} %refs_8_.7, f32[1,512]{1,0:T(1,128)} %bitcast.10, ...), custom_call_target="tpu_custom_call" | custom-call | flops 2000000000 | bytes 1018128 | tf_op jit(solution)/shard_map/first_state/pallas_call | solution.py:473
  3.9 3.5 %collective-permute-start = (bf16[144,1024]{1,0:T(8,128)(2,1)}, bf16[144,1024]{1,0:T(8,128)(2,1)S(1)}, u32[]{:S(2)}, u32[]{:S(2)}) collective-permute-start(bf16[144,1024]{1,0:T(8,128)(2,1)} %first_state.1.refs_13_.refs_1_), channel_id=1, source_target_pairs={{0,4},{4,8},{8,12},{1,5},{5,9},{9,13},{2,6},{6,10},{10,14},{3,7},{... | collective-permute-start | bytes 884744 | tf_op jit(solution)/shard_map/ppermute | solution.py:489
  7.5 2.4 %conv_all.1 = (bf16[128,2048]{1,0:T(8,128)(2,1)S(1)}, bf16[128,512]{1,0:T(8,128)(2,1)S(1)}, bf16[128,512]{1,0:T(8,128)(2,1)S(1)}, bf16[128,1024]{1,0:T(8,128)(2,1)S(1)}) custom-call(bf16[128,2048]{1,0:T(8,128)(2,1)S(1)} %copy-done, bf16[128,512]{1,0:T(8,128)(2,1)S(1)} %copy-done.4, f32[32,128]{1,0:T(8,128)S(1)} %bitcast.6, f32[4,2048]{1,0:T(4,128)S(1)} %copy-done.7, ...), custom_call_target="tpu_custom_call" | custom-call | flops 2000000000 | bytes 1902864 | tf_op jit(solution)/shard_map/conv_all/pallas_call | solution.py:473
  9.9 0.0 copy-start.14
  9.9 0.0 copy-start.2
  9.9 2.1 %collective-permute-start.3 = (bf16[128,512]{1,0:T(8,128)(2,1)S(1)}, bf16[128,512]{1,0:T(8,128)(2,1)S(1)}, u32[]{:S(2)}, u32[]{:S(2)}) collective-permute-start(bf16[128,512]{1,0:T(8,128)(2,1)S(1)} %get-tuple-element.31.refs_3_), channel_id=1, source_target_pairs={{0,4},{4,8},{8,12},{1,5},{5,9},{9,13},{2,6},{6,10},{10,14},{3,7},{... | collective-permute-start | bytes 393224 | tf_op jit(solution)/shard_map/ppermute | solution.py:489
  12.0 1.2 %prepare.1 = (f32[8,2560]{1,0:T(8,128)S(1)}, f32[8,2048]{1,0:T(8,128)S(1)}, f32[8,2048]{1,0:T(8,128)S(1)}, f32[3,8,256]{2,1,0:T(8,128)S(1)}, f32[2,8,256]{2,1,0:...) custom-call(bf16[128,2048]{1,0:T(8,128)(2,1)S(1)} %copy-done, ...), custom_call_target="tpu_custom_call" | custom-call | flops 2000000000 | bytes 1124752 | tf_op jit(solution)/shard_map/prepare/pallas_call | solution.py:473
  13.2 2.1 %collective-permute-done.refs_0_.refs_6_ = bf16[144,1024]{1,0:T(8,128)(2,1)S(1)} collective-permute-done((bf16[144,1024]{1,0:T(8,128)(2,1)}, bf16[144,1024]{1,0:T(8,128)(2,1)S(1)}, u32[]{:S(2)}, u32[]{:S(2)}) %collective-permute-start) | collective-permute-done | bytes 294944 | tf_op jit(solution)/shard_map/ppermute | solution.py:489
  15.3 0.3 relay_slot2.1
  15.6 4.1 %collective-permute-start.1 = (bf16[128,1024]{1,0:T(8,128)(2,1)S(1)}, bf16[128,1024]{1,0:T(8,128)(2,1)S(1)}, u32[]{:S(2)}, u32[]{:S(2)}) collective-permute-start(bf16[128,1024]{1,0:T(8,128)(2,1)S(1)} %relay_slot2.1), channel_id=1, source_target_pairs={{0,4},{4,8},{8,12},{1,5},{5,9},{9,13},{2,6},{6,10},{10,14},{3,7},{... | collective-permute-start | bytes 786440 | tf_op jit(solution)/shard_map/ppermute | solution.py:489
  19.7 0.0 collective-permute-done.3.refs_2_
  19.7 1.9 %collective-permute-start.4 = (bf16[128,512]{1,0:T(8,128)(2,1)S(1)}, bf16[128,512]{1,0:T(8,128)(2,1)S(1)}, u32[]{:S(2)}, u32[]{:S(2)}) collective-permute-start(bf16[128,512]{1,0:T(8,128)(2,1)S(1)} %collective-permute-done.3.refs_2_), channel_id=1, source_target_pairs={{4,8},{8,12},{5,9},{9,13},{6,10},{10,14},{7,11},{11,15},{20,24},{2... | collective-permute-start | bytes 393224 | tf_op jit(solution)/shard_map/ppermute | solution.py:489
  21.6 2.1 %local_mix.1 = (f32[128,2048]{1,0:T(8,128)S(1)}, bf16[128,256]{1,0:T(8,128)(2,1)S(1)}, bf16[128,1024]{1,0:T(8,128)(2,1)}, bf16[128,1024]{1,0:T(8,128)(2,1)S(1)}) custom-call(bf16[144,1024]{1,0:T(8,128)(2,1)S(1)} %collective-permute-done.refs_0_.refs_6_, f32[8,2560]{1,0:T(8,128)S(1)} %get-tuple-element.17.refs_1_.refs_2_, ...), custom_call_target="tpu_custom_call" | custom-call | flops 2000000000 | bytes 3506432 | tf_op jit(solution)/shard_map/local_mix/pallas_call | solution.py:473
  23.7 1.8 %collective-permute-done.1.refs_0_.refs_7_.refs_6_ = bf16[128,1024]{1,0:T(8,128)(2,1)S(1)} collective-permute-done((bf16[128,1024]{1,0:T(8,128)(2,1)S(1)}, bf16[128,1024]{1,0:T(8,128)(2,1)S(1)}, u32[]{:S(2)}, u32[]{:S(2)}) %collective-permute-start.1) | collective-permute-done | bytes 262176 | tf_op jit(solution)/shard_map/ppermute | solution.py:489
  25.5 0.1 relay_slot3.1
  25.6 0.0 copy-start.1
  25.6 0.0 copy-start.11
  25.6 3.6 %collective-permute-start.2 = (bf16[128,1024]{1,0:T(8,128)(2,1)S(1)}, bf16[128,1024]{1,0:T(8,128)(2,1)S(1)}, u32[]{:S(2)}, u32[]{:S(2)}) collective-permute-start(bf16[128,1024]{1,0:T(8,128)(2,1)S(1)} %relay_slot3.1), channel_id=1, source_target_pairs={{4,8},{8,12},{5,9},{9,13},{6,10},{10,14},{7,11},{11,15},{20,24},{2... | collective-permute-start | bytes 786440 | tf_op jit(solution)/shard_map/ppermute | solution.py:489
  29.3 0.0 collective-permute-done.4.refs_1_
  29.3 1.7 %attend.1 = bf16[128,1024]{1,0:T(8,128)(2,1)} custom-call(bf16[128,1024]{1,0:T(8,128)(2,1)S(1)} %copy-done.3, bf16[128,512]{1,0:T(8,128)(2,1)S(1)} %collective-permute-done.4.refs_1_, bf16[128,512]{1,0:T(8,128)(2,1)S(1)} %collective-permute-done.3.refs_2_, bf16[128,512]{1,0:T(8,128)(2,1)S(1)} %get-tuple-element.31.refs_3_, ...), custom_call_target="tpu_custom_call" | custom-call | flops 2000000000 | bytes 983040 | tf_op jit(solution)/shard_map/attend/pallas_call | solution.py:473
  31.0 1.2 %norm_part0.1.refs_8_ = bf16[128,2048]{1,0:T(8,128)(2,1)} custom-call(f32[128,2048]{1,0:T(8,128)S(1)} %get-tuple-element.25.refs_0_, bf16[128,256]{1,0:T(8,128)(2,1)S(1)} %get-tuple-element.26.refs_1_, f32[128,32]{1,0:T(8,128)S(1)} %get-tuple-element.27.refs_2_, bf16[128,2048]{1,0:T(8,128)(2,1)S(1)} %copy-done.1, f32[2048]{0:T(1024)S(1)} %copy-done.11, ...), custom_call_target="tpu_custom_call" | custom-call | flops 2000000000 | bytes 2760704 | tf_op jit(solution)/shard_map/norm_part0/pallas_call | solution.py:473
  32.2 1.8 %collective-permute-done.2.refs_7_ = bf16[128,1024]{1,0:T(8,128)(2,1)S(1)} collective-permute-done((bf16[128,1024]{1,0:T(8,128)(2,1)S(1)}, bf16[128,1024]{1,0:T(8,128)(2,1)S(1)}, u32[]{:S(2)}, u32[]{:S(2)}) %collective-permute-start.2) | collective-permute-done | bytes 262176 | tf_op jit(solution)/shard_map/ppermute | solution.py:489
  34.0 1.2 %norm_part1.1 = bf16[128,2048]{1,0:T(8,128)(2,1)} custom-call(f32[128,2048]{1,0:T(8,128)S(1)} %get-tuple-element.25.refs_0_, bf16[128,256]{1,0:T(8,128)(2,1)S(1)} %get-tuple-element.26.refs_1_, f32[128,32]{1,0:T(8,128)S(1)} %get-tuple-element.27.refs_2_, bf16[128,2048]{1,0:T(8,128)(2,1)S(1)} %copy-done.1, ...), custom_call_target="tpu_custom_call", output_to_operand_aliasing={{}: (8, {})} | custom-call | flops 2000000000 | bytes 3252224 | tf_op jit(solution)/shard_map/norm_part1/pallas_call | solution.py:473
  (21 shorter events, 0.0 us)
Async XLA Ops:
  0.6 6.7 %copy-start = (bf16[128,2048]{1,0:T(8,128)(2,1)S(1)}, bf16[128,2048]{1,0:T(8,128)(2,1)}, u32[]{:S(2)}) copy-start(bf16[128,2048]{1,0:T(8,128)(2,1)} %refs_0_.6) | copy-start | bytes 1572868
  0.6 6.7 %copy-start.4 = (bf16[128,512]{1,0:T(8,128)(2,1)S(1)}, bf16[128,512]{1,0:T(8,128)(2,1)}, u32[]{:S(2)}) copy-start(bf16[128,512]{1,0:T(8,128)(2,1)} %refs_1_.5) | copy-start | bytes 393220
  0.7 6.7 %copy-start.5 = (bf16[128,256]{1,0:T(8,128)(2,1)S(1)}, bf16[128,256]{1,0:T(8,128)(2,1)}, u32[]{:S(2)}) copy-start(bf16[128,256]{1,0:T(8,128)(2,1)} %refs_10_.3) | copy-start | bytes 196612
  0.7 6.7 %copy-start.6 = (bf16[128,256]{1,0:T(8,128)(2,1)S(1)}, bf16[128,256]{1,0:T(8,128)(2,1)}, u32[]{:S(2)}) copy-start(bf16[128,256]{1,0:T(8,128)(2,1)} %refs_11_.1) | copy-start | bytes 196612
  0.7 6.7 %copy-start.7 = (f32[4,2048]{1,0:T(4,128)S(1)}, f32[4,2048]{1,0:T(4,128)}, u32[]{:S(2)}) copy-start(f32[4,2048]{1,0:T(4,128)} %refs_7_.7) | copy-start | bytes 98308
  0.7 6.7 %copy-start.8 = (f32[128,32]{0,1:T(8,128)S(1)}, f32[128,32]{0,1:T(8,128)}, u32[]{:S(2)}) copy-start(f32[128,32]{0,1:T(8,128)} %param.19) | copy-start | bytes 49156
  0.7 6.7 %copy-start.9 = (f32[2048]{0:T(1024)S(1)}, f32[2048]{0:T(1024)}, u32[]{:S(2)}) copy-start(f32[2048]{0:T(1024)} %refs_4_.6) | copy-start | bytes 24580
  0.7 6.7 %copy-start.10 = (f32[4,512]{1,0:T(4,128)S(1)}, f32[4,512]{1,0:T(4,128)}, u32[]{:S(2)}) copy-start(f32[4,512]{1,0:T(4,128)} %refs_8_.7) | copy-start | bytes 24580
  0.7 6.7 %copy-start.12 = (f32[512]{0:T(512)S(1)}, f32[512]{0:T(512)}, u32[]{:S(2)}) copy-start(f32[512]{0:T(512)} %refs_6_.3) | copy-start | bytes 6148
  0.7 6.7 %copy-start.13 = (s32[4]{0:T(128)S(1)}, s32[4]{0:T(128)}, u32[]{:S(2)}) copy-start(s32[4]{0:T(128)} %refs_9_.5) | copy-start | bytes 52
  0.7 6.7 %copy-start.15 = (f32[32]{0:T(128)S(1)}, f32[32]{0:T(128)}, u32[]{:S(2)}) copy-start(f32[32]{0:T(128)} %refs_7_.6) | copy-start | bytes 388
  0.7 6.7 %copy-start.16 = (f32[32]{0:T(128)S(1)}, f32[32]{0:T(128)}, u32[]{:S(2)}) copy-start(f32[32]{0:T(128)} %refs_8_.6) | copy-start | bytes 388
  3.9 11.4 %collective-permute-start = (bf16[144,1024]{1,0:T(8,128)(2,1)}, bf16[144,1024]{1,0:T(8,128)(2,1)S(1)}, u32[]{:S(2)}, u32[]{:S(2)}) collective-permute-start(bf16[144,1024]{1,0:T(8,128)(2,1)} %first_state.1.refs_13_.refs_1_), channel_id=1, source_target_pairs={{0,4},{4,8},{8,12},{1,5},{5,9},{9,13},{2,6},{6,10},{10,14},{3,7},{... | collective-permute-start | bytes 884744 | tf_op jit(solution)/shard_map/ppermute | solution.py:489
  9.9 2.1 %copy-start.14 = (f32[32]{0:T(128)S(1)}, f32[32]{0:T(128)}, u32[]{:S(2)}) copy-start(f32[32]{0:T(128)} %refs_9_.4) | copy-start | bytes 388
  9.9 5.3 %copy-start.2 = (bf16[144,1024]{1,0:T(8,128)(2,1)S(1)}, bf16[144,1024]{1,0:T(8,128)(2,1)}, u32[]{:S(2)}) copy-start(bf16[144,1024]{1,0:T(8,128)(2,1)} %first_state.1.refs_13_.refs_1_) | copy-start | bytes 884740
  9.9 9.8 %collective-permute-start.3 = (bf16[128,512]{1,0:T(8,128)(2,1)S(1)}, bf16[128,512]{1,0:T(8,128)(2,1)S(1)}, u32[]{:S(2)}, u32[]{:S(2)}) collective-permute-start(bf16[128,512]{1,0:T(8,128)(2,1)S(1)} %get-tuple-element.31.refs_3_), channel_id=1, source_target_pairs={{0,4},{4,8},{8,12},{1,5},{5,9},{9,13},{2,6},{6,10},{10,14},{3,7},{... | collective-permute-start | bytes 393224 | tf_op jit(solution)/shard_map/ppermute | solution.py:489
  15.6 9.9 %collective-permute-start.1 = (bf16[128,1024]{1,0:T(8,128)(2,1)S(1)}, bf16[128,1024]{1,0:T(8,128)(2,1)S(1)}, u32[]{:S(2)}, u32[]{:S(2)}) collective-permute-start(bf16[128,1024]{1,0:T(8,128)(2,1)S(1)} %relay_slot2.1), channel_id=1, source_target_pairs={{0,4},{4,8},{8,12},{1,5},{5,9},{9,13},{2,6},{6,10},{10,14},{3,7},{... | collective-permute-start | bytes 786440 | tf_op jit(solution)/shard_map/ppermute | solution.py:489
  19.7 9.6 %collective-permute-start.4 = (bf16[128,512]{1,0:T(8,128)(2,1)S(1)}, bf16[128,512]{1,0:T(8,128)(2,1)S(1)}, u32[]{:S(2)}, u32[]{:S(2)}) collective-permute-start(bf16[128,512]{1,0:T(8,128)(2,1)S(1)} %collective-permute-done.3.refs_2_), channel_id=1, source_target_pairs={{4,8},{8,12},{5,9},{9,13},{6,10},{10,14},{7,11},{11,15},{20,24},{2... | collective-permute-start | bytes 393224 | tf_op jit(solution)/shard_map/ppermute | solution.py:489
  25.5 3.7 %copy-start.3 = (bf16[128,1024]{1,0:T(8,128)(2,1)S(1)}, bf16[128,1024]{1,0:T(8,128)(2,1)}, u32[]{:S(2)}) copy-start(bf16[128,1024]{1,0:T(8,128)(2,1)} %refs_0_.7) | copy-start | bytes 786436
  25.6 5.4 %copy-start.1 = (bf16[128,2048]{1,0:T(8,128)(2,1)S(1)}, bf16[128,2048]{1,0:T(8,128)(2,1)}, u32[]{:S(2)}) copy-start(bf16[128,2048]{1,0:T(8,128)(2,1)} %refs_3_.9) | copy-start | bytes 1572868
  25.6 5.4 %copy-start.11 = (f32[2048]{0:T(1024)S(1)}, f32[2048]{0:T(1024)}, u32[]{:S(2)}) copy-start(f32[2048]{0:T(1024)} %refs_4_.9) | copy-start | bytes 24580
  25.6 8.4 %collective-permute-start.2 = (bf16[128,1024]{1,0:T(8,128)(2,1)S(1)}, bf16[128,1024]{1,0:T(8,128)(2,1)S(1)}, u32[]{:S(2)}, u32[]{:S(2)}) collective-permute-start(bf16[128,1024]{1,0:T(8,128)(2,1)S(1)} %relay_slot3.1), channel_id=1, source_target_pairs={{4,8},{8,12},{5,9},{9,13},{6,10},{10,14},{7,11},{11,15},{20,24},{2... | collective-permute-start | bytes 786440 | tf_op jit(solution)/shard_map/ppermute | solution.py:489

commit v7 on v6

--- a/solution.py
+++ b/solution.py
@@ -57,22 +57,19 @@
     return jnp.dot(both, spread, preferred_element_type=F32)
 
 
-def column(ref, heads):
-    return jnp.broadcast_to(ref[...].reshape(1, -1), (8, ref.size)).T[:heads, 0:1]
-
-
 def rates(dt_ref, dt_bias_ref, a_log_ref):
-    heads, rows = dt_ref.shape
-    step = softplus(dt_ref[...] + column(dt_bias_ref, heads))
-    rate = -step * jnp.exp(column(a_log_ref, heads))
+    heads = dt_ref.shape[0]
+    step = softplus(dt_ref[...].T + dt_bias_ref[...].reshape(1, -1)[:, :heads])
+    rate = -step * jnp.exp(a_log_ref[...].reshape(1, -1)[:, :heads])
+    rows = step.shape[0]
     row = lax.broadcasted_iota(jnp.int32, (rows, rows), 0)
-    lane = lax.broadcasted_iota(jnp.int32, (rows, rows), 1)
-    upper = (row <= lane).astype(F32).astype(BF16)
+    column = lax.broadcasted_iota(jnp.int32, (rows, rows), 1)
+    lower = (row >= column).astype(F32).astype(BF16)
     high = rate.astype(BF16)
     middle, low = halves(rate - high.astype(F32))
-    parts = jnp.concatenate([high, middle, low], axis=1)
-    uppers = jnp.concatenate([upper, upper, upper], axis=0)
-    return step, jnp.dot(parts, uppers, preferred_element_type=F32)
+    parts = jnp.concatenate([high, middle, low], axis=0)
+    lowers = jnp.concatenate([lower, lower, lower], axis=1)
+    return step, jnp.dot(lowers, parts, preferred_element_type=F32)
 
 
 def insides(first, shape, taps, lens_ref):
@@ -100,12 +97,12 @@
 
 
 def kept_weight(here, step, running, taps, lens_ref):
-    rows = step.shape[1]
+    rows = step.shape[0]
     last_begin = doc_start((here + 1) * rows - 1, lens_ref)
-    row = lax.broadcasted_iota(jnp.int32, step.shape, 1)
-    weight = step * jnp.exp(running[:, rows - 1 : rows] - running)
+    row = lax.broadcasted_iota(jnp.int32, step.shape, 0)
+    weight = step * jnp.exp(running[rows - 1 : rows] - running)
     kept = (here * rows + row >= last_begin) & ((row >= taps - 1) | (last_begin // rows >= here))
-    return jnp.where(kept, weight, 0.0).T
+    return jnp.where(kept, weight, 0.0)
 
 
 def conv_rows(pad, raw, weight, bias, inside):
@@ -139,14 +136,18 @@
         edge_copies[-1].start()
 
     here = lax.axis_index("seq")
-    for at in order:
+    for at in (9, 2, 7, 8):
         copies[at].wait()
     inside = insides(here * rows, (rows, CHUNK), taps, lens_ref)
     step, running = rates(dt_ref, dt_bias_ref, a_log_ref)
     weight = kept_weight(here, step, running, taps, lens_ref)
     narrow = [mask[:, :STATE] for mask in inside]
+    for at in (1, 5, 6):
+        copies[at].wait()
     inputs = conv_rows(b_pad_ref, b_ref[...], wbc_ref[...], bbc_ref[...], narrow)
     turned = inputs.astype(F32).T.astype(BF16)
+    for at in (0, 3, 4):
+        copies[at].wait()
     slots = pad_ref.shape[0]
     outs = []
 
@@ -232,11 +233,10 @@
     step, running = rates(dt_ref, dt_bias_ref, a_log_ref)
     begin = doc_start(first + lax.broadcasted_iota(jnp.int32, begin_ref.shape, 0), lens_ref)
     begin_ref[...] = begin
-    turned = running.T
-    entry_ref[...] = jnp.where(begin[:, :heads] < first, jnp.exp(turned), 0.0)
+    entry_ref[...] = jnp.where(begin[:, :heads] < first, jnp.exp(running), 0.0)
     row = lax.broadcasted_iota(jnp.int32, (8, heads), 0)
-    total = turned[rows - 1 : rows]
-    weight = step.T[:8] * jnp.exp(total - turned[:8])
+    total = running[rows - 1 : rows]
+    weight = step[:8] * jnp.exp(total - running[:8])
     weight = jnp.where((row < taps - 1) & jnp.logical_not(own), weight, 0.0)
     through = jnp.where(own, 0.0, jnp.broadcast_to(jnp.exp(total), (8, heads)))
     skip = jnp.broadcast_to(skip_ref[...].reshape(1, -1), (8, heads))
@@ -316,11 +316,12 @@
 def local_kernel(groups, *refs):
     (
         message_ref, partial_ref, weight_ref, inside_ref, wx_ref, wbc_ref, dt_ref, dt_bias_ref,
-        a_log_ref, wide_skip_ref, begin_ref, xc_ref, bcc_ref,
-    ) = refs[:13]
-    state_refs = refs[13 : 13 + groups]
-    out_ref, c_ref = refs[13 + groups : 15 + groups]
-    full_refs = refs[15 + groups : 15 + 2 * groups]
+        a_log_ref, wide_skip_ref, begin_ref, kv_ref, xc_ref, bcc_ref,
+    ) = refs[:14]
+    state_refs = refs[14 : 14 + groups]
+    out_ref, c_ref, kv_out_ref = refs[14 + groups : 17 + groups]
+    full_refs = refs[17 + groups : 17 + 2 * groups]
+    kv_out_ref[...] = kv_ref[...]
     pad_ref = refs[-1]
     rows, width = xc_ref.shape
     per_group = width // groups
@@ -336,8 +337,9 @@
     row = lax.broadcasted_iota(jnp.int32, (rows, rows), 0)
     lane_row = lax.broadcasted_iota(jnp.int32, (rows, rows), 1)
     linked = (row >= lane_row) & (first + lane_row >= begin_ref[...])
-    turned_step, turned_running = rates(dt_ref, dt_bias_ref, a_log_ref)
-    running = turned_running.T
+    step, running = rates(dt_ref, dt_bias_ref, a_log_ref)
+    turned_running = running.T
+    turned_step = step.T
     pair_width = 2 * HDIM
     lane = lax.broadcasted_iota(jnp.int32, (rows, pair_width), 1)
     for group in range(groups):
@@ -428,19 +430,21 @@
     heads = width // HDIM
     entry = entry_ref[:, part * heads : (part + 1) * heads]
     outputs = c_ref[:, part * STATE : (part + 1) * STATE]
-    squares = jnp.zeros((rows, 1), F32)
+    squares = jnp.zeros((rows, 128), F32)
     for start in range(0, width, CHUNK):
         columns = slice(start, start + CHUNK)
         placed = slice(part * width + start, part * width + start + CHUNK)
-        state = got_refs[0][:STATE, columns].astype(F32)
+        state = got_refs[0][:STATE, columns]
         for hop in range(1, hops):
             there = flag_ref[hop, 0:1] > 0.5
-            state = jnp.where(there, got_refs[hop][:STATE, columns].astype(F32), state)
+            state = jnp.where(there, got_refs[hop][:STATE, columns].astype(F32), state.astype(F32))
         carried = jnp.dot(outputs, state.astype(BF16), preferred_element_type=F32)
         mixed = mixed_ref[:, placed] + carried * widen(entry, start, CHUNK)
         gated = mixed * silu(z_ref[:, placed].astype(F32))
         gated_ref[:, columns] = gated
-        squares = squares + jnp.sum(gated * gated, axis=1, keepdims=True)
+        for lane in range(0, CHUNK, 128):
+            squares = squares + gated[:, lane : lane + 128] * gated[:, lane : lane + 128]
+    squares = jnp.sum(squares, axis=1, keepdims=True)
     multiplier = lax.rsqrt(squares * (1.0 / width) + EPSILON)
     copies = []
     for start in range(0, width, CHUNK):
@@ -607,25 +611,26 @@
             [WHOLE] * len(operands),
             scratch=scratch,
         )
-        slots.append(onward(passed, max(0, slot - groups)))
+        slots.append(onward(passed))
         if fulls is None:
-            mixed, c_out, *fulls = call(
+            mixed, c_out, kv_on, *fulls = call(
                 functools.partial(local_kernel, groups),
                 "local_mix",
                 [
                     shape((rows, width), F32),
                     shape((rows, groups * STATE), BF16),
+                    shape(kv.shape, BF16),
                     *(shape((STATE, per_group), BF16) for _ in range(groups)),
                 ],
                 [
                     slots[0], partial, weight, inside, conv_x_weight, conv_bc_weight, dt, dt_bias, a_log,
-                    wide_skip, begin, xc, bcc, *states,
+                    wide_skip, begin, kvs[1], xc, bcc, *states,
                 ],
-                [WHOLE] * (13 + groups),
+                [WHOLE] * (14 + groups),
                 scratch=[pltpu.VMEM((4, 16, CHUNK), F32)],
             )
     for hop in range(1, hops):
-        kvs.append(onward(kvs[-1], hop))
+        kvs.append(onward(kv_on if hop == 1 else kvs[-1], hop))
 
     (attn_out,) = call(
         functools.partial(attend_kernel, hops),
@@ -641,15 +646,16 @@
     )
     mamba_out = None
     for part in range(groups):
-        operands = [mixed, c_out, entry, z_gate, norm_gain, flags, *slots[part : part + hops]]
-        specs = [WHOLE] * (6 + hops)
+        got = slots[-1:] if part == groups - 1 else slots[part : part + hops]
+        operands = [mixed, c_out, entry, z_gate, norm_gain, flags, *got]
+        specs = [WHOLE] * (6 + len(got))
         aliases = {}
         if mamba_out is not None:
             operands.append(mamba_out)
             specs.append(UNTOUCHED)
             aliases = {len(operands) - 1: 0}
         (mamba_out,) = call(
-            functools.partial(norm_kernel, part, hops),
+            functools.partial(norm_kernel, part, len(got)),
             f"norm_part{part}",
             [shape((rows, width), BF16)],
             operands,

time: 35.4 us -> 35.6 us (level)
  the two profiles are of different devices: /device:TPU:22 before, /device:TPU:24 now
where the time goes in v7:
time: 35.6 us; the launch traced here: 35.3 us
  waiting for transfers between devices  14.9 us (42%)
  Pallas kernels  12.7 us (36%)
  starting transfers between devices  6.71 us (19%)
  between operations  0.97 us (3%)
    ppermute x5, waiting for transfers between devices, onward(): lax.ppermute(value, 'seq', [(source, source + 1) for source in range(firs...  14.9 us
    pallas_call x9, Pallas kernels, call(): pl.pallas_call(kernel, name=name, grid=(1,), out_shape=outs, in_specs=spe...  12.7 us
    ppermute x5, starting transfers between devices, onward(): lax.ppermute(value, 'seq', [(source, source + 1) for source in range(firs...  6.71 us
  transfers between devices with their start and end apart: 5, of which 4 were waited for; matrix products, arithmetic and copies ran while one was open for 0% of the time, Pallas kernels for 25%

profile of v7, /device:TPU:24, one launch (start us, length us, event | category | flops | bytes accessed | tf_op | source)
XLA Modules:
  0.0 35.3 jit_solution(7546162197045852584)
XLA Ops:
  0.6 0.0 copy-start
  0.6 0.0 copy-start.4
  0.7 0.0 copy-start.5
  0.7 0.0 copy-start.6
  0.7 0.0 copy-start.7
  0.7 0.0 copy-start.8
  0.7 0.0 copy-start.9
  0.7 0.0 copy-start.10
  0.8 2.9 %first_state.1.refs_14_.refs_1_ = bf16[144,1024]{1,0:T(8,128)(2,1)} custom-call(bf16[128,2048]{1,0:T(8,128)(2,1)} %refs_0_.6, bf16[128,512]{1,0:T(8,128)(2,1)} %refs_1_.5, f32[32,128]{1,0:T(8,128)} %bitcast.5, f32[4,2048]{1,0:T(4,128)} %refs_7_.7, f32[1,2048]{1,0:T(1,128)} %bitcast.9, f32[4,512]{1,0:T(4,128)} %refs_8_.7, f32[1,512]{1,0:T(1,128)} %bitcast.10, ...), custom_call_target="tpu_custom_call" | custom-call | flops 2000000000 | bytes 1018128 | tf_op jit(solution)/shard_map/first_state/pallas_call | solution.py:477
  3.6 1.3 %collective-permute-start = (bf16[144,1024]{1,0:T(8,128)(2,1)}, bf16[144,1024]{1,0:T(8,128)(2,1)S(1)}, u32[]{:S(2)}, u32[]{:S(2)}) collective-permute-start(bf16[144,1024]{1,0:T(8,128)(2,1)} %first_state.1.refs_14_.refs_1_), channel_id=1, source_target_pairs={{0,4},{4,8},{8,12},{1,5},{5,9},{9,13},{2,6},{6,10},{10,14},{3,7},{... | collective-permute-start | bytes 884744 | tf_op jit(solution)/shard_map/ppermute | solution.py:493
  5.1 2.3 %conv_all.1 = (bf16[128,2048]{1,0:T(8,128)(2,1)S(1)}, bf16[128,512]{1,0:T(8,128)(2,1)S(1)}, bf16[128,512]{1,0:T(8,128)(2,1)S(1)}, bf16[128,1024]{1,0:T(8,128)(2,1)S(1)}) custom-call(bf16[128,2048]{1,0:T(8,128)(2,1)S(1)} %copy-done, bf16[128,512]{1,0:T(8,128)(2,1)S(1)} %copy-done.4, f32[32,128]{1,0:T(8,128)S(1)} %bitcast.6, f32[4,2048]{1,0:T(4,128)S(1)} %copy-done.7, ...), custom_call_target="tpu_custom_call" | custom-call | flops 2000000000 | bytes 1902864 | tf_op jit(solution)/shard_map/conv_all/pallas_call | solution.py:477
  7.3 0.0 copy-start.14
  7.4 0.0 copy-start.2
  7.4 1.4 %collective-permute-start.1 = (bf16[128,512]{1,0:T(8,128)(2,1)S(1)}, bf16[128,512]{1,0:T(8,128)(2,1)S(1)}, u32[]{:S(2)}, u32[]{:S(2)}) collective-permute-start(bf16[128,512]{1,0:T(8,128)(2,1)S(1)} %get-tuple-element.23.refs_3_), channel_id=1, source_target_pairs={{0,4},{4,8},{8,12},{1,5},{5,9},{9,13},{2,6},{6,10},{10,14},{3,7},{... | collective-permute-start | bytes 393224 | tf_op jit(solution)/shard_map/ppermute | solution.py:493
  8.8 1.1 %prepare.1 = (f32[8,2560]{1,0:T(8,128)S(1)}, f32[8,2048]{1,0:T(8,128)S(1)}, f32[8,2048]{1,0:T(8,128)S(1)}, f32[3,8,256]{2,1,0:T(8,128)S(1)}, f32[2,8,256]{2,1,0:...) custom-call(bf16[128,2048]{1,0:T(8,128)(2,1)S(1)} %copy-done, ...), custom_call_target="tpu_custom_call" | custom-call | flops 2000000000 | bytes 1124752 | tf_op jit(solution)/shard_map/prepare/pallas_call | solution.py:477
  9.9 5.7 %collective-permute-done.refs_0_.refs_6_ = bf16[144,1024]{1,0:T(8,128)(2,1)S(1)} collective-permute-done((bf16[144,1024]{1,0:T(8,128)(2,1)}, bf16[144,1024]{1,0:T(8,128)(2,1)S(1)}, u32[]{:S(2)}, u32[]{:S(2)}) %collective-permute-start) | collective-permute-done | bytes 294944 | tf_op jit(solution)/shard_map/ppermute | solution.py:493
  15.6 0.3 relay_slot2.1
  16.0 1.3 %collective-permute-start.2 = (bf16[128,1024]{1,0:T(8,128)(2,1)S(1)}, bf16[128,1024]{1,0:T(8,128)(2,1)S(1)}, u32[]{:S(2)}, u32[]{:S(2)}) collective-permute-start(bf16[128,1024]{1,0:T(8,128)(2,1)S(1)} %relay_slot2.1), channel_id=1, source_target_pairs={{0,4},{4,8},{8,12},{1,5},{5,9},{9,13},{2,6},{6,10},{10,14},{3,7},{... | collective-permute-start | bytes 786440 | tf_op jit(solution)/shard_map/ppermute | solution.py:493
  17.3 0.0 collective-permute-done.1.refs_11_.refs_2_
  17.3 2.0 %local_mix.1 = (f32[128,2048]{1,0:T(8,128)S(1)}, bf16[128,256]{1,0:T(8,128)(2,1)S(1)}, bf16[128,512]{1,0:T(8,128)(2,1)S(1)}, bf16[128,1024]{1,0:T(8,128)(2,1)}, bf16[128,1024]{1,0:T(8,128)(2,1)S(1)}) custom-call(bf16[144,1024]{1,0:T(8,128)(2,1)S(1)} %collective-permute-done.refs_0_.refs_6_, f32[8,2560]{1,0:T(8,128)S(1)} %get-tuple-element.18.refs_1_.refs_2_, ...), custom_call_target="tpu_custom_call" | custom-call | flops 2000000000 | bytes 3768576 | tf_op jit(solution)/shard_map/local_mix/pallas_call | solution.py:477
  19.3 1.3 %collective-permute-start.4 = (bf16[128,512]{1,0:T(8,128)(2,1)S(1)}, bf16[128,512]{1,0:T(8,128)(2,1)S(1)}, u32[]{:S(2)}, u32[]{:S(2)}) collective-permute-start(bf16[128,512]{1,0:T(8,128)(2,1)S(1)} %get-tuple-element.33), channel_id=1, source_target_pairs={{4,8},{8,12},{5,9},{9,13},{6,10},{10,14},{7,11},{11,15},{20,24},{2... | collective-permute-start | bytes 393224 | tf_op jit(solution)/shard_map/ppermute | solution.py:493
  20.6 5.1 %collective-permute-done.2.refs_0_.refs_7_ = bf16[128,1024]{1,0:T(8,128)(2,1)S(1)} collective-permute-done((bf16[128,1024]{1,0:T(8,128)(2,1)S(1)}, bf16[128,1024]{1,0:T(8,128)(2,1)S(1)}, u32[]{:S(2)}, u32[]{:S(2)}) %collective-permute-start.2) | collective-permute-done | bytes 262176 | tf_op jit(solution)/shard_map/ppermute | solution.py:493
  25.6 0.1 relay_slot3.1
  25.7 0.0 copy-start.1
  25.7 0.0 copy-start.11
  25.8 1.4 %collective-permute-start.3 = (bf16[128,1024]{1,0:T(8,128)(2,1)S(1)}, bf16[128,1024]{1,0:T(8,128)(2,1)S(1)}, u32[]{:S(2)}, u32[]{:S(2)}) collective-permute-start(bf16[128,1024]{1,0:T(8,128)(2,1)S(1)} %relay_slot3.1), channel_id=1, source_target_pairs={{0,4},{4,8},{8,12},{1,5},{5,9},{9,13},{2,6},{6,10},{10,14},{3,7},{... | collective-permute-start | bytes 786440 | tf_op jit(solution)/shard_map/ppermute | solution.py:493
  27.2 1.2 %collective-permute-done.4.refs_1_ = bf16[128,512]{1,0:T(8,128)(2,1)S(1)} collective-permute-done((bf16[128,512]{1,0:T(8,128)(2,1)S(1)}, bf16[128,512]{1,0:T(8,128)(2,1)S(1)}, u32[]{:S(2)}, u32[]{:S(2)}) %collective-permute-start.4) | collective-permute-done | bytes 131104 | tf_op jit(solution)/shard_map/ppermute | solution.py:493
  28.4 0.0 copy-done.3
  28.4 1.7 %attend.1 = bf16[128,1024]{1,0:T(8,128)(2,1)} custom-call(bf16[128,1024]{1,0:T(8,128)(2,1)S(1)} %copy-done.3, bf16[128,512]{1,0:T(8,128)(2,1)S(1)} %collective-permute-done.4.refs_1_, bf16[128,512]{1,0:T(8,128)(2,1)S(1)} %collective-permute-done.1.refs_11_.refs_2_, bf16[128,512]{1,0:T(8,128)(2,1)S(1)} %get-tuple-element.23.refs_3_, ...), custom_call_target="tpu_custom_call" | custom-call | flops 2000000000 | bytes 983040 | tf_op jit(solution)/shard_map/attend/pallas_call | solution.py:477
  30.1 1.2 %norm_part0.1.refs_7_ = bf16[128,2048]{1,0:T(8,128)(2,1)} custom-call(f32[128,2048]{1,0:T(8,128)S(1)} %get-tuple-element.27.refs_0_, bf16[128,256]{1,0:T(8,128)(2,1)S(1)} %get-tuple-element.28.refs_1_, f32[128,32]{1,0:T(8,128)S(1)} %get-tuple-element.29.refs_2_, bf16[128,2048]{1,0:T(8,128)(2,1)S(1)} %copy-done.1, f32[2048]{0:T(1024)S(1)} %copy-done.11, ...), custom_call_target="tpu_custom_call" | custom-call | flops 2000000000 | bytes 2760704 | tf_op jit(solution)/shard_map/norm_part0/pallas_call | solution.py:477
  31.3 2.8 %collective-permute-done.3.refs_6_ = bf16[128,1024]{1,0:T(8,128)(2,1)S(1)} collective-permute-done((bf16[128,1024]{1,0:T(8,128)(2,1)S(1)}, bf16[128,1024]{1,0:T(8,128)(2,1)S(1)}, u32[]{:S(2)}, u32[]{:S(2)}) %collective-permute-start.3) | collective-permute-done | bytes 262176 | tf_op jit(solution)/shard_map/ppermute | solution.py:493
  34.2 1.2 %norm_part1.1 = bf16[128,2048]{1,0:T(8,128)(2,1)} custom-call(f32[128,2048]{1,0:T(8,128)S(1)} %get-tuple-element.27.refs_0_, bf16[128,256]{1,0:T(8,128)(2,1)S(1)} %get-tuple-element.28.refs_1_, f32[128,32]{1,0:T(8,128)S(1)} %get-tuple-element.29.refs_2_, bf16[128,2048]{1,0:T(8,128)(2,1)S(1)} %copy-done.1, ...), custom_call_target="tpu_custom_call", output_to_operand_aliasing={{}: (7, {})} | custom-call | flops 2000000000 | bytes 2990080 | tf_op jit(solution)/shard_map/norm_part1/pallas_call | solution.py:477
  (21 shorter events, 0.0 us)
Async XLA Ops:
  0.6 4.3 %copy-start = (bf16[128,2048]{1,0:T(8,128)(2,1)S(1)}, bf16[128,2048]{1,0:T(8,128)(2,1)}, u32[]{:S(2)}) copy-start(bf16[128,2048]{1,0:T(8,128)(2,1)} %refs_0_.6) | copy-start | bytes 1572868
  0.6 4.3 %copy-start.4 = (bf16[128,512]{1,0:T(8,128)(2,1)S(1)}, bf16[128,512]{1,0:T(8,128)(2,1)}, u32[]{:S(2)}) copy-start(bf16[128,512]{1,0:T(8,128)(2,1)} %refs_1_.5) | copy-start | bytes 393220
  0.7 4.3 %copy-start.5 = (bf16[128,256]{1,0:T(8,128)(2,1)S(1)}, bf16[128,256]{1,0:T(8,128)(2,1)}, u32[]{:S(2)}) copy-start(bf16[128,256]{1,0:T(8,128)(2,1)} %refs_10_.3) | copy-start | bytes 196612
  0.7 4.3 %copy-start.6 = (bf16[128,256]{1,0:T(8,128)(2,1)S(1)}, bf16[128,256]{1,0:T(8,128)(2,1)}, u32[]{:S(2)}) copy-start(bf16[128,256]{1,0:T(8,128)(2,1)} %refs_11_.1) | copy-start | bytes 196612
  0.7 4.3 %copy-start.7 = (f32[4,2048]{1,0:T(4,128)S(1)}, f32[4,2048]{1,0:T(4,128)}, u32[]{:S(2)}) copy-start(f32[4,2048]{1,0:T(4,128)} %refs_7_.7) | copy-start | bytes 98308
  0.7 4.3 %copy-start.8 = (f32[128,32]{0,1:T(8,128)S(1)}, f32[128,32]{0,1:T(8,128)}, u32[]{:S(2)}) copy-start(f32[128,32]{0,1:T(8,128)} %param.19) | copy-start | bytes 49156
  0.7 4.3 %copy-start.9 = (f32[2048]{0:T(1024)S(1)}, f32[2048]{0:T(1024)}, u32[]{:S(2)}) copy-start(f32[2048]{0:T(1024)} %refs_4_.6) | copy-start | bytes 24580
  0.7 4.3 %copy-start.10 = (f32[4,512]{1,0:T(4,128)S(1)}, f32[4,512]{1,0:T(4,128)}, u32[]{:S(2)}) copy-start(f32[4,512]{1,0:T(4,128)} %refs_8_.7) | copy-start | bytes 24580
  0.7 4.3 %copy-start.12 = (f32[512]{0:T(512)S(1)}, f32[512]{0:T(512)}, u32[]{:S(2)}) copy-start(f32[512]{0:T(512)} %refs_6_.3) | copy-start | bytes 6148
  0.7 4.3 %copy-start.13 = (s32[4]{0:T(128)S(1)}, s32[4]{0:T(128)}, u32[]{:S(2)}) copy-start(s32[4]{0:T(128)} %refs_9_.5) | copy-start | bytes 52
  0.7 4.3 %copy-start.15 = (f32[32]{0:T(128)S(1)}, f32[32]{0:T(128)}, u32[]{:S(2)}) copy-start(f32[32]{0:T(128)} %refs_7_.6) | copy-start | bytes 388
  0.7 4.3 %copy-start.16 = (f32[32]{0:T(128)S(1)}, f32[32]{0:T(128)}, u32[]{:S(2)}) copy-start(f32[32]{0:T(128)} %refs_8_.6) | copy-start | bytes 388
  3.6 12.0 %collective-permute-start = (bf16[144,1024]{1,0:T(8,128)(2,1)}, bf16[144,1024]{1,0:T(8,128)(2,1)S(1)}, u32[]{:S(2)}, u32[]{:S(2)}) collective-permute-start(bf16[144,1024]{1,0:T(8,128)(2,1)} %first_state.1.refs_14_.refs_1_), channel_id=1, source_target_pairs={{0,4},{4,8},{8,12},{1,5},{5,9},{9,13},{2,6},{6,10},{10,14},{3,7},{... | collective-permute-start | bytes 884744 | tf_op jit(solution)/shard_map/ppermute | solution.py:493
  7.3 1.5 %copy-start.14 = (f32[32]{0:T(128)S(1)}, f32[32]{0:T(128)}, u32[]{:S(2)}) copy-start(f32[32]{0:T(128)} %refs_9_.4) | copy-start | bytes 388
  7.4 8.3 %copy-start.2 = (bf16[144,1024]{1,0:T(8,128)(2,1)S(1)}, bf16[144,1024]{1,0:T(8,128)(2,1)}, u32[]{:S(2)}) copy-start(bf16[144,1024]{1,0:T(8,128)(2,1)} %first_state.1.refs_14_.refs_1_) | copy-start | bytes 884740
  7.4 9.9 %collective-permute-start.1 = (bf16[128,512]{1,0:T(8,128)(2,1)S(1)}, bf16[128,512]{1,0:T(8,128)(2,1)S(1)}, u32[]{:S(2)}, u32[]{:S(2)}) collective-permute-start(bf16[128,512]{1,0:T(8,128)(2,1)S(1)} %get-tuple-element.23.refs_3_), channel_id=1, source_target_pairs={{0,4},{4,8},{8,12},{1,5},{5,9},{9,13},{2,6},{6,10},{10,14},{3,7},{... | collective-permute-start | bytes 393224 | tf_op jit(solution)/shard_map/ppermute | solution.py:493
  16.0 9.7 %collective-permute-start.2 = (bf16[128,1024]{1,0:T(8,128)(2,1)S(1)}, bf16[128,1024]{1,0:T(8,128)(2,1)S(1)}, u32[]{:S(2)}, u32[]{:S(2)}) collective-permute-start(bf16[128,1024]{1,0:T(8,128)(2,1)S(1)} %relay_slot2.1), channel_id=1, source_target_pairs={{0,4},{4,8},{8,12},{1,5},{5,9},{9,13},{2,6},{6,10},{10,14},{3,7},{... | collective-permute-start | bytes 786440 | tf_op jit(solution)/shard_map/ppermute | solution.py:493
  19.3 9.1 %collective-permute-start.4 = (bf16[128,512]{1,0:T(8,128)(2,1)S(1)}, bf16[128,512]{1,0:T(8,128)(2,1)S(1)}, u32[]{:S(2)}, u32[]{:S(2)}) collective-permute-start(bf16[128,512]{1,0:T(8,128)(2,1)S(1)} %get-tuple-element.33), channel_id=1, source_target_pairs={{4,8},{8,12},{5,9},{9,13},{6,10},{10,14},{7,11},{11,15},{20,24},{2... | collective-permute-start | bytes 393224 | tf_op jit(solution)/shard_map/ppermute | solution.py:493
  25.6 2.8 %copy-start.3 = (bf16[128,1024]{1,0:T(8,128)(2,1)S(1)}, bf16[128,1024]{1,0:T(8,128)(2,1)}, u32[]{:S(2)}) copy-start(bf16[128,1024]{1,0:T(8,128)(2,1)} %refs_0_.7) | copy-start | bytes 786436
  25.7 4.4 %copy-start.1 = (bf16[128,2048]{1,0:T(8,128)(2,1)S(1)}, bf16[128,2048]{1,0:T(8,128)(2,1)}, u32[]{:S(2)}) copy-start(bf16[128,2048]{1,0:T(8,128)(2,1)} %refs_3_.9) | copy-start | bytes 1572868
  25.7 4.4 %copy-start.11 = (f32[2048]{0:T(1024)S(1)}, f32[2048]{0:T(1024)}, u32[]{:S(2)}) copy-start(f32[2048]{0:T(1024)} %refs_4_.9) | copy-start | bytes 24580
  25.8 8.4 %collective-permute-start.3 = (bf16[128,1024]{1,0:T(8,128)(2,1)S(1)}, bf16[128,1024]{1,0:T(8,128)(2,1)S(1)}, u32[]{:S(2)}, u32[]{:S(2)}) collective-permute-start(bf16[128,1024]{1,0:T(8,128)(2,1)S(1)} %relay_slot3.1), channel_id=1, source_target_pairs={{0,4},{4,8},{8,12},{1,5},{5,9},{9,13},{2,6},{6,10},{10,14},{3,7},{... | collective-permute-start | bytes 786440 | tf_op jit(solution)/shard_map/ppermute | solution.py:493

commit v8 on v7

--- a/solution.py
+++ b/solution.py
@@ -179,29 +179,33 @@
         copy.wait()
 
 
-def conv_kernel(groups, *refs):
-    x_ref, bc_ref, dt_ref, wx_ref, bx_ref, wbc_ref, bbc_ref, dt_bias_ref, a_log_ref, lens_ref = refs[:10]
-    keys_ref, values_ref, xc_ref, bcc_ref, kv_ref = refs[10:15]
-    state_refs = refs[15:-1]
-    pad_ref = refs[-1]
+def prepare_kernel(hops, groups, *refs):
+    x_ref, bc_ref, dt_ref, wx_ref, bx_ref, wbc_ref, bbc_ref, dt_bias_ref, a_log_ref, skip_ref, lens_ref = refs[:11]
+    keys_ref, values_ref = refs[11:13]
+    xc_ref, bcc_ref, kv_ref, partial_ref, weight_ref, through_ref, inside_ref, flag_ref, entry_ref = refs[13:22]
+    wide_skip_ref, begin_ref = refs[22:24]
+    state_refs = refs[24:-2]
+    top_ref, pad_ref = refs[-2:]
     rows, width = x_ref.shape
     per_group = width // groups
-    heads = per_group // HDIM
     taps = wx_ref.shape[0]
     slots = pad_ref.shape[0]
     here = lax.axis_index("seq")
+    first = here * rows
     kv_width = keys_ref.shape[1]
     kv_ref[:, :kv_width] = keys_ref[...]
     kv_ref[:, kv_width:] = values_ref[...]
-    inside = insides(here * rows, (rows, CHUNK), taps, lens_ref)
+    inside = insides(first, (rows, CHUNK), taps, lens_ref)
     step, running = rates(dt_ref, dt_bias_ref, a_log_ref)
-    weight = kept_weight(here, step, running, taps, lens_ref)
+    heads = step.shape[1]
+    group_heads = heads // groups
+    kept = kept_weight(here, step, running, taps, lens_ref)
     for group in range(groups):
         base = slice(group * 2 * STATE, (group + 1) * 2 * STATE)
         pair = conv_rows(pad_ref.at[0], bc_ref[:, base], wbc_ref[:, base], bbc_ref[base], inside)
         bcc_ref[:, base] = pair
         turned = pair[:, :STATE].astype(F32).T.astype(BF16)
-        part_weight = weight[:, group * heads : (group + 1) * heads]
+        part_weight = kept[:, group * group_heads : (group + 1) * group_heads]
         for chunk in range(0, per_group, CHUNK):
             columns = slice(group * per_group + chunk, group * per_group + chunk + CHUNK)
             pad = pad_ref.at[(chunk // CHUNK + 1) % slots]
@@ -213,24 +217,14 @@
                     turned, weighted, preferred_element_type=F32
                 ).astype(BF16)
 
-
-def prepare_kernel(hops, *refs):
-    x_ref, bc_ref, dt_ref, wx_ref, bx_ref, wbc_ref, bbc_ref, dt_bias_ref, a_log_ref, skip_ref, lens_ref = refs[:11]
-    partial_ref, weight_ref, through_ref, inside_ref, flag_ref, entry_ref, wide_skip_ref, begin_ref, pad_ref = refs[11:]
-    width = x_ref.shape[1]
-    rows, heads = entry_ref.shape
-    taps = wx_ref.shape[0]
-    here = lax.axis_index("seq")
-    first = here * rows
     own = reach(here, rows, lens_ref) == 0
-    inside = insides(first, (8, CHUNK), taps, lens_ref)
+    inside = [mask[:8] for mask in inside]
     for lag in range(1, taps):
         inside_ref[lag - 1] = inside[lag].astype(F32)
     flag_ref[0] = jnp.broadcast_to(own.astype(F32), (8, CHUNK))
     before = reach(here - 1, rows, lens_ref)
     for hop in range(1, hops):
         flag_ref[hop] = jnp.broadcast_to((before == hop).astype(F32), (8, CHUNK))
-    step, running = rates(dt_ref, dt_bias_ref, a_log_ref)
     begin = doc_start(first + lax.broadcasted_iota(jnp.int32, begin_ref.shape, 0), lens_ref)
     begin_ref[...] = begin
     entry_ref[...] = jnp.where(begin[:, :heads] < first, jnp.exp(running), 0.0)
@@ -246,15 +240,15 @@
         weight_ref[:, start : start + CHUNK] = wide[:8]
         through_ref[:, start : start + CHUNK] = wide[8:16]
         wide_skip_ref[:, start : start + CHUNK] = wide[16:]
-    pad_ref[0:8] = jnp.zeros((8, pad_ref.shape[1]), F32)
-    pad_ref[8:, :width] = x_ref[...].astype(F32)[:8]
-    pad_ref[8:, width:] = bc_ref[...].astype(F32)[:8]
+    top_ref[0:8] = jnp.zeros((8, top_ref.shape[1]), F32)
+    top_ref[8:, :width] = x_ref[:EDGE].astype(F32)[:8]
+    top_ref[8:, width:] = bc_ref[:EDGE].astype(F32)[:8]
 
     def some(columns, base, w_ref, b_ref):
         here_columns = slice(base + columns.start, base + columns.stop)
-        total = pad_ref[8:, here_columns] * w_ref[taps - 1 : taps, columns] + b_ref[columns].reshape(1, -1)
+        total = top_ref[8:, here_columns] * w_ref[taps - 1 : taps, columns] + b_ref[columns].reshape(1, -1)
         for lag in range(1, taps):
-            term = pad_ref[8 - lag : 16 - lag, here_columns] * w_ref[taps - 1 - lag : taps - lag, columns]
+            term = top_ref[8 - lag : 16 - lag, here_columns] * w_ref[taps - 1 - lag : taps - lag, columns]
             total = total + jnp.where(inside[lag], term, 0.0)
         partial_ref[:, here_columns] = total
 
@@ -316,15 +310,16 @@
 def local_kernel(groups, *refs):
     (
         message_ref, partial_ref, weight_ref, inside_ref, wx_ref, wbc_ref, dt_ref, dt_bias_ref,
-        a_log_ref, wide_skip_ref, begin_ref, kv_ref, xc_ref, bcc_ref,
-    ) = refs[:14]
-    state_refs = refs[14 : 14 + groups]
-    out_ref, c_ref, kv_out_ref = refs[14 + groups : 17 + groups]
-    full_refs = refs[17 + groups : 17 + 2 * groups]
+        a_log_ref, wide_skip_ref, begin_ref, kv_ref, entry_ref, z_ref, xc_ref, bcc_ref,
+    ) = refs[:16]
+    state_refs = refs[16 : 16 + groups]
+    out_ref, decay_ref, c_ref, kv_out_ref = refs[16 + groups : 20 + groups]
+    full_refs = refs[20 + groups : 20 + 2 * groups]
     kv_out_ref[...] = kv_ref[...]
     pad_ref = refs[-1]
     rows, width = xc_ref.shape
     per_group = width // groups
+    heads = per_group // HDIM
     first = lax.axis_index("seq") * rows
     lines = tail_lines(message_ref, STATE)
     slots = pad_ref.shape[0]
@@ -363,6 +358,9 @@
             )
             full_refs[group][:, columns] = full.astype(BF16)
             wide_skip = wide_skip_ref[0:1, at : at + CHUNK]
+            gate = silu(z_ref[:, at : at + CHUNK].astype(F32))
+            entry = entry_ref[:, group * heads : (group + 1) * heads]
+            decay_ref[:, at : at + CHUNK] = widen(entry, chunk, CHUNK) * gate
             for start in range(0, CHUNK, pair_width):
                 parts = []
                 for head in ((at + start) // HDIM, (at + start) // HDIM + 1):
@@ -376,9 +374,8 @@
                     [jnp.where(lane < HDIM, xc, zero), jnp.where(lane < HDIM, zero, xc)], axis=0
                 )
                 value = jnp.dot(mix, stacked, preferred_element_type=F32)
-                out_ref[:, at + start : at + start + pair_width] = (
-                    value + xc.astype(F32) * wide_skip[:, start : start + pair_width]
-                )
+                value = value + xc.astype(F32) * wide_skip[:, start : start + pair_width]
+                out_ref[:, at + start : at + start + pair_width] = value * gate[:, start : start + pair_width]
 
 
 def attend_kernel(hops, *refs):
@@ -423,12 +420,10 @@
 
 
 def norm_kernel(part, hops, *refs):
-    mixed_ref, c_ref, entry_ref, z_ref, gain_ref, flag_ref = refs[:6]
-    got_refs = refs[6 : 6 + hops]
+    local_ref, decay_ref, c_ref, gain_ref, flag_ref = refs[:5]
+    got_refs = refs[5 : 5 + hops]
     out_hbm_ref, gated_ref, out_ref, sems = refs[-4:]
     rows, width = gated_ref.shape
-    heads = width // HDIM
-    entry = entry_ref[:, part * heads : (part + 1) * heads]
     outputs = c_ref[:, part * STATE : (part + 1) * STATE]
     squares = jnp.zeros((rows, 128), F32)
     for start in range(0, width, CHUNK):
@@ -439,8 +434,7 @@
             there = flag_ref[hop, 0:1] > 0.5
             state = jnp.where(there, got_refs[hop][:STATE, columns].astype(F32), state.astype(F32))
         carried = jnp.dot(outputs, state.astype(BF16), preferred_element_type=F32)
-        mixed = mixed_ref[:, placed] + carried * widen(entry, start, CHUNK)
-        gated = mixed * silu(z_ref[:, placed].astype(F32))
+        gated = local_ref[:, placed] + carried * decay_ref[:, placed]
         gated_ref[:, columns] = gated
         for lane in range(0, CHUNK, 128):
             squares = squares + gated[:, lane : lane + 128] * gated[:, lane : lane + 128]
@@ -555,26 +549,13 @@
         limit=VMEM_ALL,
     )
     slots = [onward(message)]
-    xc, bcc, kv, *states = call(
-        functools.partial(conv_kernel, groups),
-        "conv_all",
+    prepared = call(
+        functools.partial(prepare_kernel, hops, groups),
+        "prepare",
         [
             shape((rows, width), BF16),
             shape((rows, bc_width), BF16),
             shape((rows, 2 * keys.shape[1]), BF16),
-            *(shape((STATE, per_group), BF16) for _ in range(groups - 1)),
-        ],
-        [x_raw, bc_raw, *params, doc_lens, keys, values],
-        [WHOLE] * 9 + [SCALARS] + [WHOLE] * 2,
-        scratch=[pltpu.VMEM((4, rows + 8, CHUNK), F32)],
-    )
-    states = [message, *states]
-    kvs = [kv, onward(kv)]
-
-    partial, weight, through, inside, flags, entry, wide_skip, begin = call(
-        functools.partial(prepare_kernel, hops),
-        "prepare",
-        [
             shape((8, width + bc_width), F32),
             shape((8, width), F32),
             shape((8, width), F32),
@@ -583,12 +564,18 @@
             shape((rows, heads), F32),
             shape((8, width), F32),
             shape((rows, rows), jnp.int32),
+            *(shape((STATE, per_group), BF16) for _ in range(groups - 1)),
         ],
-        [x_raw, bc_raw, *params, skip_d, doc_lens],
-        [tile(EDGE, width, 0, 0), tile(EDGE, bc_width, 0, 0)] + [WHOLE] * 8 + [SCALARS],
-        scratch=[pltpu.VMEM((16, width + bc_width), F32)],
+        [x_raw, bc_raw, *params, skip_d, doc_lens, keys, values],
+        [WHOLE] * 10 + [SCALARS] + [WHOLE] * 2,
+        scratch=[
+            pltpu.VMEM((16, width + bc_width), F32),
+            pltpu.VMEM((4, rows + 8, CHUNK), F32),
+        ],
     )
-
+    xc, bcc, kv, partial, weight, through, inside, flags, entry, wide_skip, begin, *states = prepared
+    states = [message, *states]
+    kvs = [kv, onward(kv)]
     fulls = None
     for slot in range(2, hops + groups):
         part = min(slot - 1, groups) - 1
@@ -613,10 +600,11 @@
         )
         slots.append(onward(passed))
         if fulls is None:
-            mixed, c_out, kv_on, *fulls = call(
+            gated, decay, c_out, kv_on, *fulls = call(
                 functools.partial(local_kernel, groups),
                 "local_mix",
                 [
+                    shape((rows, width), F32),
                     shape((rows, width), F32),
                     shape((rows, groups * STATE), BF16),
                     shape(kv.shape, BF16),
@@ -624,9 +612,9 @@
                 ],
                 [
                     slots[0], partial, weight, inside, conv_x_weight, conv_bc_weight, dt, dt_bias, a_log,
-                    wide_skip, begin, kvs[1], xc, bcc, *states,
+                    wide_skip, begin, kvs[1], entry, z_gate, xc, bcc, *states,
                 ],
-                [WHOLE] * (14 + groups),
+                [WHOLE] * (16 + groups),
                 scratch=[pltpu.VMEM((4, 16, CHUNK), F32)],
             )
     for hop in range(1, hops):
@@ -647,8 +635,8 @@
     mamba_out = None
     for part in range(groups):
         got = slots[-1:] if part == groups - 1 else slots[part : part + hops]
-        operands = [mixed, c_out, entry, z_gate, norm_gain, flags, *got]
-        specs = [WHOLE] * (6 + len(got))
+        operands = [gated, decay, c_out, norm_gain, flags, *got]
+        specs = [WHOLE] * (5 + len(got))
         aliases = {}
         if mamba_out is not None:
             operands.append(mamba_out)

time: 35.6 us -> 35.5 us (level)
  the two profiles are of different devices: /device:TPU:24 before, /device:TPU:0 now
where the time goes in v8:
time: 35.5 us; the launch traced here: 35.3 us
  starting transfers between devices  19.2 us (54%)
  Pallas kernels  11.6 us (33%)
  waiting for transfers between devices  3.43 us (10%)
  between operations  0.98 us (3%)
    ppermute x5, starting transfers between devices, onward(): lax.ppermute(value, 'seq', [(source, source + 1) for source in range(firs...  19.2 us
    pallas_call x8, Pallas kernels, call(): pl.pallas_call(kernel, name=name, grid=(1,), out_shape=outs, in_specs=spe...  11.6 us
    ppermute x5, waiting for transfers between devices, onward(): lax.ppermute(value, 'seq', [(source, source + 1) for source in range(firs...  3.43 us
  transfers between devices with their start and end apart: 5, of which 3 were waited for; matrix products, arithmetic and copies ran while one was open for 0% of the time, Pallas kernels for 22%

profile of v8, /device:TPU:0, one launch (start us, length us, event | category | flops | bytes accessed | tf_op | source)
XLA Modules:
  0.0 35.3 jit_solution(10501992691713344569)
XLA Ops:
  0.6 0.0 copy-start
  0.6 0.0 copy-start.4
  0.7 0.0 copy-start.5
  0.7 0.0 copy-start.6
  0.7 0.0 copy-start.7
  0.7 0.0 copy-start.8
  0.7 0.0 copy-start.9
  0.7 0.0 copy-start.10
  0.7 0.0 copy-start.12
  0.7 0.0 copy-start.13
  0.7 0.0 copy-start.14
  0.7 0.0 copy-start.15
  0.8 2.9 %first_state.1.refs_16_.refs_1_ = bf16[144,1024]{1,0:T(8,128)(2,1)} custom-call(bf16[128,2048]{1,0:T(8,128)(2,1)} %refs_0_.4, bf16[128,512]{1,0:T(8,128)(2,1)} %refs_1_.3, f32[32,128]{1,0:T(8,128)} %bitcast.5, f32[4,2048]{1,0:T(4,128)} %refs_7_.5, f32[1,2048]{1,0:T(1,128)} %bitcast.8, f32[4,512]{1,0:T(4,128)} %refs_8_.5, f32[1,512]{1,0:T(1,128)} %bitcast.9, ...), custom_call_target="tpu_custom_call" | custom-call | flops 2000000000 | bytes 1018128 | tf_op jit(solution)/shard_map/first_state/pallas_call | solution.py:471
  3.6 0.0 copy-start.2
  3.7 5.1 %collective-permute-start = (bf16[144,1024]{1,0:T(8,128)(2,1)}, bf16[144,1024]{1,0:T(8,128)(2,1)S(1)}, u32[]{:S(2)}, u32[]{:S(2)}) collective-permute-start(bf16[144,1024]{1,0:T(8,128)(2,1)} %first_state.1.refs_16_.refs_1_), channel_id=1, source_target_pairs={{0,4},{4,8},{8,12},{1,5},{5,9},{9,13},{2,6},{6,10},{10,14},{3,7},{... | collective-permute-start | bytes 884744 | tf_op jit(solution)/shard_map/ppermute | solution.py:487
  8.9 2.4 %prepare.1 = (bf16[128,2048]{1,0:T(8,128)(2,1)S(1)}, bf16[128,512]{1,0:T(8,128)(2,1)S(1)}, bf16[128,512]{1,0:T(8,128)(2,1)S(1)}, f32[8,2560]{1,0:T(8,128)S(1)}, ...) custom-call(bf16[128,2048]{1,0:T(8,128)(2,1)S(1)} %copy-done, ...), custom_call_target="tpu_custom_call" | custom-call | flops 2000000000 | bytes 2304400 | tf_op jit(solution)/shard_map/prepare/pallas_call | solution.py:471
  11.3 3.5 %collective-permute-start.1 = (bf16[128,512]{1,0:T(8,128)(2,1)S(1)}, bf16[128,512]{1,0:T(8,128)(2,1)S(1)}, u32[]{:S(2)}, u32[]{:S(2)}) collective-permute-start(bf16[128,512]{1,0:T(8,128)(2,1)S(1)} %get-tuple-element.24.refs_3_), channel_id=1, source_target_pairs={{0,4},{4,8},{8,12},{1,5},{5,9},{9,13},{2,6},{6,10},{10,14},{3,7},{... | collective-permute-start | bytes 393224 | tf_op jit(solution)/shard_map/ppermute | solution.py:487
  14.7 1.3 %collective-permute-done.refs_0_.refs_5_ = bf16[144,1024]{1,0:T(8,128)(2,1)S(1)} collective-permute-done((bf16[144,1024]{1,0:T(8,128)(2,1)}, bf16[144,1024]{1,0:T(8,128)(2,1)S(1)}, u32[]{:S(2)}, u32[]{:S(2)}) %collective-permute-start) | collective-permute-done | bytes 294944 | tf_op jit(solution)/shard_map/ppermute | solution.py:487
  16.0 0.3 relay_slot2.1
  16.3 4.3 %collective-permute-start.2 = (bf16[128,1024]{1,0:T(8,128)(2,1)S(1)}, bf16[128,1024]{1,0:T(8,128)(2,1)S(1)}, u32[]{:S(2)}, u32[]{:S(2)}) collective-permute-start(bf16[128,1024]{1,0:T(8,128)(2,1)S(1)} %relay_slot2.1), channel_id=1, source_target_pairs={{0,4},{4,8},{8,12},{1,5},{5,9},{9,13},{2,6},{6,10},{10,14},{3,7},{... | collective-permute-start | bytes 786440 | tf_op jit(solution)/shard_map/ppermute | solution.py:487
  20.6 0.0 collective-permute-done.1.refs_11_.refs_2_
  20.7 2.2 %local_mix.1 = (f32[128,2048]{1,0:T(8,128)S(1)}, f32[128,2048]{1,0:T(8,128)S(1)}, bf16[128,256]{1,0:T(8,128)(2,1)S(1)}, bf16[128,512]{1,0:T(8,128)(2,1)S(1)}, bf...) custom-call(bf16[144,1024]{1,0:T(8,128)(2,1)S(1)} %collective-permute-done.refs_0_.refs_5_, ...), custom_call_target="tpu_custom_call" | custom-call | flops 2000000000 | bytes 5357824 | tf_op jit(solution)/shard_map/local_mix/pallas_call | solution.py:471
  22.8 0.7 %collective-permute-start.4 = (bf16[128,512]{1,0:T(8,128)(2,1)S(1)}, bf16[128,512]{1,0:T(8,128)(2,1)S(1)}, u32[]{:S(2)}, u32[]{:S(2)}) collective-permute-start(bf16[128,512]{1,0:T(8,128)(2,1)S(1)} %get-tuple-element.35), channel_id=1, source_target_pairs={{4,8},{8,12},{5,9},{9,13},{6,10},{10,14},{7,11},{11,15},{20,24},{2... | collective-permute-start | bytes 393224 | tf_op jit(solution)/shard_map/ppermute | solution.py:487
  23.5 1.1 %collective-permute-done.2.refs_0_.refs_6_ = bf16[128,1024]{1,0:T(8,128)(2,1)S(1)} collective-permute-done((bf16[128,1024]{1,0:T(8,128)(2,1)S(1)}, bf16[128,1024]{1,0:T(8,128)(2,1)S(1)}, u32[]{:S(2)}, u32[]{:S(2)}) %collective-permute-start.2) | collective-permute-done | bytes 262176 | tf_op jit(solution)/shard_map/ppermute | solution.py:487
  24.6 0.1 relay_slot3.1
  24.7 0.0 copy-start.11
  24.7 5.7 %collective-permute-start.3 = (bf16[128,1024]{1,0:T(8,128)(2,1)S(1)}, bf16[128,1024]{1,0:T(8,128)(2,1)S(1)}, u32[]{:S(2)}, u32[]{:S(2)}) collective-permute-start(bf16[128,1024]{1,0:T(8,128)(2,1)S(1)} %relay_slot3.1), channel_id=1, source_target_pairs={{0,4},{4,8},{8,12},{1,5},{5,9},{9,13},{2,6},{6,10},{10,14},{3,7},{... | collective-permute-start | bytes 786440 | tf_op jit(solution)/shard_map/ppermute | solution.py:487
  30.4 0.0 collective-permute-done.4.refs_1_
  30.4 1.7 %attend.1 = bf16[128,1024]{1,0:T(8,128)(2,1)} custom-call(bf16[128,1024]{1,0:T(8,128)(2,1)S(1)} %copy-done.3, bf16[128,512]{1,0:T(8,128)(2,1)S(1)} %collective-permute-done.4.refs_1_, bf16[128,512]{1,0:T(8,128)(2,1)S(1)} %collective-permute-done.1.refs_11_.refs_2_, bf16[128,512]{1,0:T(8,128)(2,1)S(1)} %get-tuple-element.24.refs_3_, ...), custom_call_target="tpu_custom_call" | custom-call | flops 2000000000 | bytes 983040 | tf_op jit(solution)/shard_map/attend/pallas_call | solution.py:471
  32.1 1.1 %norm_part0.1.refs_6_ = bf16[128,2048]{1,0:T(8,128)(2,1)} custom-call(f32[128,2048]{1,0:T(8,128)S(1)} %get-tuple-element.29.refs_0_, f32[128,2048]{1,0:T(8,128)S(1)} %get-tuple-element.30.refs_1_, bf16[128,256]{1,0:T(8,128)(2,1)S(1)} %get-tuple-element.31.refs_2_, f32[2048]{0:T(1024)S(1)} %copy-done.11, ...), custom_call_target="tpu_custom_call" | custom-call | flops 2000000000 | bytes 3268608 | tf_op jit(solution)/shard_map/norm_part0/pallas_call | solution.py:471
  33.1 1.1 %collective-permute-done.3.refs_5_ = bf16[128,1024]{1,0:T(8,128)(2,1)S(1)} collective-permute-done((bf16[128,1024]{1,0:T(8,128)(2,1)S(1)}, bf16[128,1024]{1,0:T(8,128)(2,1)S(1)}, u32[]{:S(2)}, u32[]{:S(2)}) %collective-permute-start.3) | collective-permute-done | bytes 262176 | tf_op jit(solution)/shard_map/ppermute | solution.py:487
  34.2 1.0 %norm_part1.1 = bf16[128,2048]{1,0:T(8,128)(2,1)} custom-call(f32[128,2048]{1,0:T(8,128)S(1)} %get-tuple-element.29.refs_0_, f32[128,2048]{1,0:T(8,128)S(1)} %get-tuple-element.30.refs_1_, bf16[128,256]{1,0:T(8,128)(2,1)S(1)} %get-tuple-element.31.refs_2_, f32[2048]{0:T(1024)S(1)} %copy-done.11, ...), custom_call_target="tpu_custom_call", output_to_operand_aliasing={{}: (6, {})} | custom-call | flops 2000000000 | bytes 3497984 | tf_op jit(solution)/shard_map/norm_part1/pallas_call | solution.py:471
  (20 shorter events, 0.0 us)
Async XLA Ops:
  0.6 8.1 %copy-start = (bf16[128,2048]{1,0:T(8,128)(2,1)S(1)}, bf16[128,2048]{1,0:T(8,128)(2,1)}, u32[]{:S(2)}) copy-start(bf16[128,2048]{1,0:T(8,128)(2,1)} %refs_0_.4) | copy-start | bytes 1572868
  0.6 8.1 %copy-start.4 = (bf16[128,512]{1,0:T(8,128)(2,1)S(1)}, bf16[128,512]{1,0:T(8,128)(2,1)}, u32[]{:S(2)}) copy-start(bf16[128,512]{1,0:T(8,128)(2,1)} %refs_1_.3) | copy-start | bytes 393220
  0.7 8.1 %copy-start.5 = (bf16[128,256]{1,0:T(8,128)(2,1)S(1)}, bf16[128,256]{1,0:T(8,128)(2,1)}, u32[]{:S(2)}) copy-start(bf16[128,256]{1,0:T(8,128)(2,1)} %refs_11_.1) | copy-start | bytes 196612
  0.7 8.1 %copy-start.6 = (bf16[128,256]{1,0:T(8,128)(2,1)S(1)}, bf16[128,256]{1,0:T(8,128)(2,1)}, u32[]{:S(2)}) copy-start(bf16[128,256]{1,0:T(8,128)(2,1)} %refs_12_.1) | copy-start | bytes 196612
  0.7 8.1 %copy-start.7 = (f32[4,2048]{1,0:T(4,128)S(1)}, f32[4,2048]{1,0:T(4,128)}, u32[]{:S(2)}) copy-start(f32[4,2048]{1,0:T(4,128)} %refs_7_.5) | copy-start | bytes 98308
  0.7 8.1 %copy-start.8 = (f32[128,32]{0,1:T(8,128)S(1)}, f32[128,32]{0,1:T(8,128)}, u32[]{:S(2)}) copy-start(f32[128,32]{0,1:T(8,128)} %param.19) | copy-start | bytes 49156
  0.7 8.1 %copy-start.9 = (f32[2048]{0:T(1024)S(1)}, f32[2048]{0:T(1024)}, u32[]{:S(2)}) copy-start(f32[2048]{0:T(1024)} %refs_4_.2) | copy-start | bytes 24580
  0.7 8.1 %copy-start.10 = (f32[4,512]{1,0:T(4,128)S(1)}, f32[4,512]{1,0:T(4,128)}, u32[]{:S(2)}) copy-start(f32[4,512]{1,0:T(4,128)} %refs_8_.5) | copy-start | bytes 24580
  0.7 8.1 %copy-start.12 = (f32[512]{0:T(512)S(1)}, f32[512]{0:T(512)}, u32[]{:S(2)}) copy-start(f32[512]{0:T(512)} %refs_6_.1) | copy-start | bytes 6148
  0.7 8.1 %copy-start.13 = (s32[4]{0:T(128)S(1)}, s32[4]{0:T(128)}, u32[]{:S(2)}) copy-start(s32[4]{0:T(128)} %refs_10_.1) | copy-start | bytes 52
  0.7 8.1 %copy-start.14 = (f32[32]{0:T(128)S(1)}, f32[32]{0:T(128)}, u32[]{:S(2)}) copy-start(f32[32]{0:T(128)} %refs_9_.3) | copy-start | bytes 388
  0.7 8.1 %copy-start.15 = (f32[32]{0:T(128)S(1)}, f32[32]{0:T(128)}, u32[]{:S(2)}) copy-start(f32[32]{0:T(128)} %refs_7_.4) | copy-start | bytes 388
  0.8 8.1 %copy-start.16 = (f32[32]{0:T(128)S(1)}, f32[32]{0:T(128)}, u32[]{:S(2)}) copy-start(f32[32]{0:T(128)} %refs_8_.4) | copy-start | bytes 388
  3.6 12.4 %copy-start.2 = (bf16[144,1024]{1,0:T(8,128)(2,1)S(1)}, bf16[144,1024]{1,0:T(8,128)(2,1)}, u32[]{:S(2)}) copy-start(bf16[144,1024]{1,0:T(8,128)(2,1)} %first_state.1.refs_16_.refs_1_) | copy-start | bytes 884740
  3.7 12.4 %collective-permute-start = (bf16[144,1024]{1,0:T(8,128)(2,1)}, bf16[144,1024]{1,0:T(8,128)(2,1)S(1)}, u32[]{:S(2)}, u32[]{:S(2)}) collective-permute-start(bf16[144,1024]{1,0:T(8,128)(2,1)} %first_state.1.refs_16_.refs_1_), channel_id=1, source_target_pairs={{0,4},{4,8},{8,12},{1,5},{5,9},{9,13},{2,6},{6,10},{10,14},{3,7},{... | collective-permute-start | bytes 884744 | tf_op jit(solution)/shard_map/ppermute | solution.py:487
  11.3 9.4 %collective-permute-start.1 = (bf16[128,512]{1,0:T(8,128)(2,1)S(1)}, bf16[128,512]{1,0:T(8,128)(2,1)S(1)}, u32[]{:S(2)}, u32[]{:S(2)}) collective-permute-start(bf16[128,512]{1,0:T(8,128)(2,1)S(1)} %get-tuple-element.24.refs_3_), channel_id=1, source_target_pairs={{0,4},{4,8},{8,12},{1,5},{5,9},{9,13},{2,6},{6,10},{10,14},{3,7},{... | collective-permute-start | bytes 393224 | tf_op jit(solution)/shard_map/ppermute | solution.py:487
  16.0 4.6 %copy-start.1 = (bf16[128,2048]{1,0:T(8,128)(2,1)S(1)}, bf16[128,2048]{1,0:T(8,128)(2,1)}, u32[]{:S(2)}) copy-start(bf16[128,2048]{1,0:T(8,128)(2,1)} %refs_13_.1) | copy-start | bytes 1572868
  16.3 8.2 %collective-permute-start.2 = (bf16[128,1024]{1,0:T(8,128)(2,1)S(1)}, bf16[128,1024]{1,0:T(8,128)(2,1)S(1)}, u32[]{:S(2)}, u32[]{:S(2)}) collective-permute-start(bf16[128,1024]{1,0:T(8,128)(2,1)S(1)} %relay_slot2.1), channel_id=1, source_target_pairs={{0,4},{4,8},{8,12},{1,5},{5,9},{9,13},{2,6},{6,10},{10,14},{3,7},{... | collective-permute-start | bytes 786440 | tf_op jit(solution)/shard_map/ppermute | solution.py:487
  22.8 7.5 %collective-permute-start.4 = (bf16[128,512]{1,0:T(8,128)(2,1)S(1)}, bf16[128,512]{1,0:T(8,128)(2,1)S(1)}, u32[]{:S(2)}, u32[]{:S(2)}) collective-permute-start(bf16[128,512]{1,0:T(8,128)(2,1)S(1)} %get-tuple-element.35), channel_id=1, source_target_pairs={{4,8},{8,12},{5,9},{9,13},{6,10},{10,14},{7,11},{11,15},{20,24},{2... | collective-permute-start | bytes 393224 | tf_op jit(solution)/shard_map/ppermute | solution.py:487
  24.6 5.8 %copy-start.3 = (bf16[128,1024]{1,0:T(8,128)(2,1)S(1)}, bf16[128,1024]{1,0:T(8,128)(2,1)}, u32[]{:S(2)}) copy-start(bf16[128,1024]{1,0:T(8,128)(2,1)} %refs_0_.5) | copy-start | bytes 786436
  24.7 7.4 %copy-start.11 = (f32[2048]{0:T(1024)S(1)}, f32[2048]{0:T(1024)}, u32[]{:S(2)}) copy-start(f32[2048]{0:T(1024)} %refs_3_.7) | copy-start | bytes 24580
  24.7 9.5 %collective-permute-start.3 = (bf16[128,1024]{1,0:T(8,128)(2,1)S(1)}, bf16[128,1024]{1,0:T(8,128)(2,1)S(1)}, u32[]{:S(2)}, u32[]{:S(2)}) collective-permute-start(bf16[128,1024]{1,0:T(8,128)(2,1)S(1)} %relay_slot3.1), channel_id=1, source_target_pairs={{0,4},{4,8},{8,12},{1,5},{5,9},{9,13},{2,6},{6,10},{10,14},{3,7},{... | collective-permute-start | bytes 786440 | tf_op jit(solution)/shard_map/ppermute | solution.py:487

commit v9 on v8

--- a/solution.py
+++ b/solution.py
@@ -1,5 +1,6 @@
 import functools
 import math
+from typing import NamedTuple
 
 import jax
 import jax.numpy as jnp
@@ -310,12 +311,12 @@
 def local_kernel(groups, *refs):
     (
         message_ref, partial_ref, weight_ref, inside_ref, wx_ref, wbc_ref, dt_ref, dt_bias_ref,
-        a_log_ref, wide_skip_ref, begin_ref, kv_ref, entry_ref, z_ref, xc_ref, bcc_ref,
-    ) = refs[:16]
-    state_refs = refs[16 : 16 + groups]
-    out_ref, decay_ref, c_ref, kv_out_ref = refs[16 + groups : 20 + groups]
-    full_refs = refs[20 + groups : 20 + 2 * groups]
-    kv_out_ref[...] = kv_ref[...]
+        a_log_ref, wide_skip_ref, begin_ref, entry_ref, z_ref, xc_ref, bcc_ref,
+    ) = refs[:15]
+    state_refs = refs[15 : 15 + groups]
+    out_ref, decay_ref, c_ref = refs[15 + groups : 18 + groups]
+    full_refs = refs[18 + groups : 18 + 2 * groups]
+
     pad_ref = refs[-1]
     rows, width = xc_ref.shape
     per_group = width // groups
@@ -378,36 +379,70 @@
                 out_ref[:, at + start : at + start + pair_width] = value * gate[:, start : start + pair_width]
 
 
-def attend_kernel(hops, *refs):
-    q_ref = refs[0]
-    kv_refs = refs[1 : 2 + hops]
-    begin_ref, out_hbm_ref, out_ref, sems = refs[2 + hops :]
+def attend(q_ref, kv_refs, begin_ref, blocks, share, head):
     rows = q_ref.shape[0]
     kv_heads = kv_refs[0].shape[1] // (2 * ADIM)
-    share = QHEADS // KVHEADS
-    count = rows * (hops + 1)
+    count = rows * blocks.count
     here = lax.axis_index("seq")
     row = here * rows + lax.broadcasted_iota(jnp.int32, (rows, count), 0)
-    column = (here - hops) * rows + lax.broadcasted_iota(jnp.int32, (rows, count), 1)
-    begin = jnp.concatenate([begin_ref[...]] * (hops + 1), axis=1)
-    allowed = (column <= row) & (column >= begin)
-    scale = ADIM ** (-0.5)
-    ones = jnp.ones((count, ADIM), BF16)
-    allowed = jnp.concatenate([allowed] * share, axis=0)
+    lane = (here - blocks.farthest) * rows + lax.broadcasted_iota(jnp.int32, (rows, count), 1)
+    begin = jnp.concatenate([begin_ref[...]] * blocks.count, axis=1)
+    allowed = jnp.concatenate([(lane <= row) & (lane >= begin)] * share, axis=0)
+    low = head * ADIM
+    keys = jnp.concatenate([ref[:, low : low + ADIM] for ref in kv_refs], axis=0)
+    low = (kv_heads + head) * ADIM
+    values = jnp.concatenate([ref[:, low : low + ADIM] for ref in kv_refs], axis=0)
+    values = jnp.concatenate([values, jnp.ones((count, ADIM), BF16)], axis=1)
+    lows = [(head * share + part) * ADIM for part in range(share)]
+    asking = jnp.concatenate([q_ref[:, low : low + ADIM] for low in lows], axis=0)
+    scores = lax.dot_general(asking, keys, (((1,), (1,)), ((), ())), preferred_element_type=F32)
+    return jnp.where(allowed, scores * ADIM ** (-0.5), BARRED), values
+
+
+class Blocks(NamedTuple):
+    farthest: int
+    count: int
+
+
+def near_kernel(*refs):
+    q_ref, before_ref, own_ref, begin_ref, _, sum_ref, total_ref, peak_ref, kv_ref = refs
+    kv_ref[...] = before_ref[...]
+    rows = q_ref.shape[0]
+    share = QHEADS // KVHEADS
+    for head in range(own_ref.shape[1] // (2 * ADIM)):
+        scores, values = attend(q_ref, (before_ref, own_ref), begin_ref, Blocks(1, 2), share, head)
+        peak = jnp.max(scores, axis=1, keepdims=True)
+        summed = jnp.dot(jnp.exp(scores - peak).astype(BF16), values, preferred_element_type=F32)
+        peak = jnp.broadcast_to(peak, (peak.shape[0], ADIM))
+        for part in range(share):
+            low = (head * share + part) * ADIM
+            these = slice(part * rows, (part + 1) * rows)
+            sum_ref[:, low : low + ADIM] = summed[these, :ADIM]
+            total_ref[:, low : low + ADIM] = summed[these, ADIM:]
+            peak_ref[:, low : low + ADIM] = peak[these]
+
+
+def far_kernel(hops, *refs):
+    q_ref, begin_ref, sum_ref, total_ref, peak_ref = refs[:5]
+    kv_refs = refs[5 : 4 + hops]
+    out_hbm_ref, out_ref, sems = refs[4 + hops :]
+    rows = q_ref.shape[0]
+    share = QHEADS // KVHEADS
     copies = []
-    for head in range(kv_heads):
-        low = head * ADIM
-        keys = jnp.concatenate([ref[:, low : low + ADIM] for ref in kv_refs], axis=0)
-        low = (kv_heads + head) * ADIM
-        values = jnp.concatenate([ref[:, low : low + ADIM] for ref in kv_refs], axis=0)
-        values = jnp.concatenate([values, ones], axis=1)
+    for head in range(kv_refs[0].shape[1] // (2 * ADIM)):
         lows = [(head * share + part) * ADIM for part in range(share)]
-        asking = jnp.concatenate([q_ref[:, low : low + ADIM] for low in lows], axis=0)
-        scores = lax.dot_general(asking, keys, (((1,), (1,)), ((), ())), preferred_element_type=F32)
-        scores = jnp.where(allowed, scores * scale, BARRED)
-        expo = jnp.exp(scores - jnp.max(scores, axis=1, keepdims=True))
+
+        def stacked(ref):
+            return jnp.concatenate([ref[:, low : low + ADIM] for low in lows], axis=0)
+
+        scores, values = attend(q_ref, kv_refs, begin_ref, Blocks(hops, hops - 1), share, head)
+        near = stacked(peak_ref)
+        peak = jnp.maximum(near, jnp.max(scores, axis=1, keepdims=True))
+        expo = jnp.exp(scores - jnp.concatenate([peak] * (scores.shape[1] // ADIM), axis=1))
         summed = jnp.dot(expo.astype(BF16), values, preferred_element_type=F32)
-        result = (summed[:, :ADIM] / summed[:, ADIM:]).astype(BF16)
+        factor = jnp.exp(near - peak)
+        total = stacked(total_ref) * factor + summed[:, ADIM:]
+        result = ((stacked(sum_ref) * factor + summed[:, :ADIM]) / total).astype(BF16)
         for part, low in enumerate(lows):
             out_ref[:, low : low + ADIM] = result[part * rows : (part + 1) * rows]
         columns = pl.ds(head * share * ADIM, share * ADIM)
@@ -513,7 +548,7 @@
     count = lax.axis_size("seq")
     longest = rows * count // 2
     hops = min(count - 1, -(-(longest - 1) // rows))
-    assert hops * rows >= longest and (hops <= 2 or groups == 1)
+    assert hops * rows >= longest and (hops == 2 or hops > 2 and groups == 1)
     shape = jax.ShapeDtypeStruct
     dt = dt_raw.T
     params = [dt, conv_x_weight, conv_x_bias, conv_bc_weight, conv_bc_bias, dt_bias, a_log]
@@ -600,32 +635,38 @@
         )
         slots.append(onward(passed))
         if fulls is None:
-            gated, decay, c_out, kv_on, *fulls = call(
+            gated, decay, c_out, *fulls = call(
                 functools.partial(local_kernel, groups),
                 "local_mix",
                 [
                     shape((rows, width), F32),
                     shape((rows, width), F32),
                     shape((rows, groups * STATE), BF16),
-                    shape(kv.shape, BF16),
                     *(shape((STATE, per_group), BF16) for _ in range(groups)),
                 ],
                 [
                     slots[0], partial, weight, inside, conv_x_weight, conv_bc_weight, dt, dt_bias, a_log,
-                    wide_skip, begin, kvs[1], entry, z_gate, xc, bcc, *states,
+                    wide_skip, begin, entry, z_gate, xc, bcc, *states,
                 ],
-                [WHOLE] * (16 + groups),
+                [WHOLE] * (15 + groups),
                 scratch=[pltpu.VMEM((4, 16, CHUNK), F32)],
             )
+    parts = shape(queries.shape, F32)
+    *near, kv_on = call(
+        near_kernel,
+        "attend_near",
+        [parts, parts, parts, shape(kv.shape, BF16)],
+        [queries, kvs[1], kv, begin, c_out],
+        [WHOLE] * 4 + [UNTOUCHED],
+    )
     for hop in range(1, hops):
         kvs.append(onward(kv_on if hop == 1 else kvs[-1], hop))
-
     (attn_out,) = call(
-        functools.partial(attend_kernel, hops),
-        "attend",
+        functools.partial(far_kernel, hops),
+        "attend_far",
         [shape(queries.shape, BF16)],
-        [queries, *reversed(kvs), begin],
-        [WHOLE] * (hops + 3),
+        [queries, begin, *near, *reversed(kvs[2:])],
+        [WHOLE] * (4 + hops),
         out_specs=[UNTOUCHED],
         scratch=[
             pltpu.VMEM(queries.shape, BF16),

time: 35.5 us -> 35.9 us (1.011)
  starting transfers between devices: 19.2 us -> 19.6 us
    ppermute x5, starting transfers between devices: 19.2 us -> 19.6 us  [onward(): lax.ppermute(value, 'seq', [(source, source + 1) for source in range(firs...]
    pallas_call x8 -> x9, Pallas kernels: 11.6 us -> 11.8 us  [call(): pl.pallas_call(kernel, name=name, grid=(1,), out_shape=outs, in_specs=spe...]
where the time goes in v9:
time: 35.9 us; the launch traced here: 35.6 us
  starting transfers between devices  19.6 us (55%)
  Pallas kernels  11.8 us (33%)
  waiting for transfers between devices  3.26 us (9%)
  between operations  0.97 us (3%)
    ppermute x5, starting transfers between devices, onward(): lax.ppermute(value, 'seq', [(source, source + 1) for source in range(firs...  19.6 us
    pallas_call x9, Pallas kernels, call(): pl.pallas_call(kernel, name=name, grid=(1,), out_shape=outs, in_specs=spe...  11.8 us
    ppermute x5, waiting for transfers between devices, onward(): lax.ppermute(value, 'seq', [(source, source + 1) for source in range(firs...  3.26 us
  transfers between devices with their start and end apart: 5, of which 3 were waited for; matrix products, arithmetic and copies ran while one was open for 0% of the time, Pallas kernels for 22%

profile of v9, /device:TPU:0, one launch (start us, length us, event | category | flops | bytes accessed | tf_op | source)
XLA Modules:
  0.0 35.6 jit_solution(5444877116851755615)
XLA Ops:
  0.8 2.9 %first_state.1.refs_15_.refs_1_ = bf16[144,1024]{1,0:T(8,128)(2,1)} custom-call(bf16[128,2048]{1,0:T(8,128)(2,1)} %refs_0_.5, bf16[128,512]{1,0:T(8,128)(2,1)} %refs_1_.3, f32[32,128]{1,0:T(8,128)} %bitcast.5, f32[4,2048]{1,0:T(4,128)} %refs_7_.5, f32[1,2048]{1,0:T(1,128)} %bitcast.8, f32[4,512]{1,0:T(4,128)} %refs_8_.5, f32[1,512]{1,0:T(1,128)} %bitcast.9, ...), custom_call_target="tpu_custom_call" | custom-call | flops 2000000000 | bytes 1018128 | tf_op jit(solution)/shard_map/first_state/pallas_call | solution.py:506
  3.6 0.0 copy-start.2
  3.7 5.1 %collective-permute-start = (bf16[144,1024]{1,0:T(8,128)(2,1)}, bf16[144,1024]{1,0:T(8,128)(2,1)S(1)}, u32[]{:S(2)}, u32[]{:S(2)}) collective-permute-start(bf16[144,1024]{1,0:T(8,128)(2,1)} %first_state.1.refs_15_.refs_1_), channel_id=1, source_target_pairs={{0,4},{4,8},{8,12},{1,5},{5,9},{9,13},{2,6},{6,10},{10,14},{3,7},{... | collective-permute-start | bytes 884744 | tf_op jit(solution)/shard_map/ppermute | solution.py:522
  8.7 0.0 copy-done
  8.8 0.0 copy-done.4
  8.8 0.0 copy-done.5
  8.8 0.0 copy-done.6
  8.8 0.0 copy-done.7
  8.8 0.0 copy-done.8
  8.8 0.0 copy-done.9
  8.8 0.0 copy-done.10
  8.8 0.0 copy-done.12
  8.8 0.0 copy-done.13
  8.9 2.4 %prepare.1 = (bf16[128,2048]{1,0:T(8,128)(2,1)S(1)}, bf16[128,512]{1,0:T(8,128)(2,1)S(1)}, bf16[128,512]{1,0:T(8,128)(2,1)S(1)}, f32[8,2560]{1,0:T(8,128)S(1)}, ...) custom-call(bf16[128,2048]{1,0:T(8,128)(2,1)S(1)} %copy-done, ...), custom_call_target="tpu_custom_call" | custom-call | flops 2000000000 | bytes 2304400 | tf_op jit(solution)/shard_map/prepare/pallas_call | solution.py:506
  11.3 3.5 %collective-permute-start.3 = (bf16[128,512]{1,0:T(8,128)(2,1)S(1)}, bf16[128,512]{1,0:T(8,128)(2,1)S(1)}, u32[]{:S(2)}, u32[]{:S(2)}) collective-permute-start(bf16[128,512]{1,0:T(8,128)(2,1)S(1)} %get-tuple-element.37.refs_2_), channel_id=1, source_target_pairs={{0,4},{4,8},{8,12},{1,5},{5,9},{9,13},{2,6},{6,10},{10,14},{3,7},{... | collective-permute-start | bytes 393224 | tf_op jit(solution)/shard_map/ppermute | solution.py:522
  14.7 1.3 %collective-permute-done.refs_0_.refs_5_ = bf16[144,1024]{1,0:T(8,128)(2,1)S(1)} collective-permute-done((bf16[144,1024]{1,0:T(8,128)(2,1)}, bf16[144,1024]{1,0:T(8,128)(2,1)S(1)}, u32[]{:S(2)}, u32[]{:S(2)}) %collective-permute-start) | collective-permute-done | bytes 294944 | tf_op jit(solution)/shard_map/ppermute | solution.py:522
  16.0 0.3 relay_slot2.1
  16.3 4.3 %collective-permute-start.1 = (bf16[128,1024]{1,0:T(8,128)(2,1)S(1)}, bf16[128,1024]{1,0:T(8,128)(2,1)S(1)}, u32[]{:S(2)}, u32[]{:S(2)}) collective-permute-start(bf16[128,1024]{1,0:T(8,128)(2,1)S(1)} %relay_slot2.1), channel_id=1, source_target_pairs={{0,4},{4,8},{8,12},{1,5},{5,9},{9,13},{2,6},{6,10},{10,14},{3,7},{... | collective-permute-start | bytes 786440 | tf_op jit(solution)/shard_map/ppermute | solution.py:522
  20.7 0.0 copy-start.3
  20.7 1.9 %local_mix.1 = (f32[128,2048]{1,0:T(8,128)S(1)}, f32[128,2048]{1,0:T(8,128)S(1)}, bf16[128,256]{1,0:T(8,128)(2,1)S(1)}, bf16[128,1024]{1,0:T(8,128)(2,1)}, bf16[128,1024]{1,0:T(8,128)(2,1)S(1)}) custom-call(bf16[144,1024]{1,0:T(8,128)(2,1)S(1)} %collective-permute-done.refs_0_.refs_5_, f32[8,2560]{1,0:T(8,128)S(1)} %get-tuple-element.22.refs_1_.refs_2_, ...), custom_call_target="tpu_custom_call" | custom-call | flops 2000000000 | bytes 5095680 | tf_op jit(solution)/shard_map/local_mix/pallas_call | solution.py:506
  22.6 0.0 collective-permute-done.3.refs_1_
  22.6 0.6 %attend_near.1 = (f32[128,1024]{1,0:T(8,128)S(1)}, f32[128,1024]{1,0:T(8,128)S(1)}, f32[128,1024]{1,0:T(8,128)S(1)}, bf16[128,512]{1,0:T(8,128)(2,1)S(1)}) custom-call(bf16[128,1024]{1,0:T(8,128)(2,1)S(1)} %copy-done.3, bf16[128,512]{1,0:T(8,128)(2,1)S(1)} %collective-permute-done.3.refs_1_, bf16[128,512]{1,0:T(8,128)(2,1)S(1)} %get-tuple-element.37.refs_2_, ...), custom_call_target="tpu_custom_call" | custom-call | flops 2000000000 | bytes 2359296 | tf_op jit(solution)/shard_map/attend_near/pallas_call | solution.py:506
  23.2 0.7 %collective-permute-start.4 = (bf16[128,512]{1,0:T(8,128)(2,1)S(1)}, bf16[128,512]{1,0:T(8,128)(2,1)S(1)}, u32[]{:S(2)}, u32[]{:S(2)}) collective-permute-start(bf16[128,512]{1,0:T(8,128)(2,1)S(1)} %get-tuple-element.41), channel_id=1, source_target_pairs={{4,8},{8,12},{5,9},{9,13},{6,10},{10,14},{7,11},{11,15},{20,24},{2... | collective-permute-start | bytes 393224 | tf_op jit(solution)/shard_map/ppermute | solution.py:522
  23.9 0.7 %collective-permute-done.1.refs_0_.refs_6_ = bf16[128,1024]{1,0:T(8,128)(2,1)S(1)} collective-permute-done((bf16[128,1024]{1,0:T(8,128)(2,1)S(1)}, bf16[128,1024]{1,0:T(8,128)(2,1)S(1)}, u32[]{:S(2)}, u32[]{:S(2)}) %collective-permute-start.1) | collective-permute-done | bytes 262176 | tf_op jit(solution)/shard_map/ppermute | solution.py:522
  24.6 0.1 relay_slot3.1
  24.7 6.1 %collective-permute-start.2 = (bf16[128,1024]{1,0:T(8,128)(2,1)S(1)}, bf16[128,1024]{1,0:T(8,128)(2,1)S(1)}, u32[]{:S(2)}, u32[]{:S(2)}) collective-permute-start(bf16[128,1024]{1,0:T(8,128)(2,1)S(1)} %relay_slot3.1), channel_id=1, source_target_pairs={{0,4},{4,8},{8,12},{1,5},{5,9},{9,13},{2,6},{6,10},{10,14},{3,7},{... | collective-permute-start | bytes 786440 | tf_op jit(solution)/shard_map/ppermute | solution.py:522
  30.7 0.0 collective-permute-done.4.refs_5_
  30.7 0.0 copy-start.11
  30.8 1.4 %attend_far.1 = bf16[128,1024]{1,0:T(8,128)(2,1)} custom-call(bf16[128,1024]{1,0:T(8,128)(2,1)S(1)} %copy-done.3, s32[128,128]{1,0:T(8,128)S(1)} %get-tuple-element.26.refs_10_.refs_3_.refs_1_, f32[128,1024]{1,0:T(8,128)S(1)} %get-tuple-element.38.refs_2_, f32[128,1024]{1,0:T(8,128)S(1)} %get-tuple-element.39.refs_3_, ...), custom_call_target="tpu_custom_call" | custom-call | flops 2000000000 | bytes 2293760 | tf_op jit(solution)/shard_map/attend_far/pallas_call | solution.py:506
  32.2 1.1 %norm_part0.1.refs_6_ = bf16[128,2048]{1,0:T(8,128)(2,1)} custom-call(f32[128,2048]{1,0:T(8,128)S(1)} %get-tuple-element.31.refs_0_, f32[128,2048]{1,0:T(8,128)S(1)} %get-tuple-element.32.refs_1_, bf16[128,256]{1,0:T(8,128)(2,1)S(1)} %get-tuple-element.33.refs_2_.refs_4_, f32[2048]{0:T(1024)S(1)} %copy-done.11, ...), custom_call_target="tpu_custom_call" | custom-call | flops 2000000000 | bytes 3268608 | tf_op jit(solution)/shard_map/norm_part0/pallas_call | solution.py:506
  33.3 1.3 %collective-permute-done.2.refs_5_ = bf16[128,1024]{1,0:T(8,128)(2,1)S(1)} collective-permute-done((bf16[128,1024]{1,0:T(8,128)(2,1)S(1)}, bf16[128,1024]{1,0:T(8,128)(2,1)S(1)}, u32[]{:S(2)}, u32[]{:S(2)}) %collective-permute-start.2) | collective-permute-done | bytes 262176 | tf_op jit(solution)/shard_map/ppermute | solution.py:522
  34.6 1.0 %norm_part1.1 = bf16[128,2048]{1,0:T(8,128)(2,1)} custom-call(f32[128,2048]{1,0:T(8,128)S(1)} %get-tuple-element.31.refs_0_, f32[128,2048]{1,0:T(8,128)S(1)} %get-tuple-element.32.refs_1_, bf16[128,256]{1,0:T(8,128)(2,1)S(1)} %get-tuple-element.33.refs_2_.refs_4_, f32[2048]{0:T(1024)S(1)} %copy-done.11, ...), custom_call_target="tpu_custom_call", output_to_operand_aliasing={{}: (6, {})} | custom-call | flops 2000000000 | bytes 3497984 | tf_op jit(solution)/shard_map/norm_part1/pallas_call | solution.py:506
  (21 shorter events, 0.0 us)
Async XLA Ops:
  0.6 8.1 %copy-start = (bf16[128,2048]{1,0:T(8,128)(2,1)S(1)}, bf16[128,2048]{1,0:T(8,128)(2,1)}, u32[]{:S(2)}) copy-start(bf16[128,2048]{1,0:T(8,128)(2,1)} %refs_0_.5) | copy-start | bytes 1572868
  0.6 8.1 %copy-start.4 = (bf16[128,512]{1,0:T(8,128)(2,1)S(1)}, bf16[128,512]{1,0:T(8,128)(2,1)}, u32[]{:S(2)}) copy-start(bf16[128,512]{1,0:T(8,128)(2,1)} %refs_1_.3) | copy-start | bytes 393220
  0.7 8.1 %copy-start.5 = (bf16[128,256]{1,0:T(8,128)(2,1)S(1)}, bf16[128,256]{1,0:T(8,128)(2,1)}, u32[]{:S(2)}) copy-start(bf16[128,256]{1,0:T(8,128)(2,1)} %refs_11_.1) | copy-start | bytes 196612
  0.7 8.1 %copy-start.6 = (bf16[128,256]{1,0:T(8,128)(2,1)S(1)}, bf16[128,256]{1,0:T(8,128)(2,1)}, u32[]{:S(2)}) copy-start(bf16[128,256]{1,0:T(8,128)(2,1)} %refs_12_.2) | copy-start | bytes 196612
  0.7 8.1 %copy-start.7 = (f32[4,2048]{1,0:T(4,128)S(1)}, f32[4,2048]{1,0:T(4,128)}, u32[]{:S(2)}) copy-start(f32[4,2048]{1,0:T(4,128)} %refs_7_.5) | copy-start | bytes 98308
  0.7 8.1 %copy-start.8 = (f32[128,32]{0,1:T(8,128)S(1)}, f32[128,32]{0,1:T(8,128)}, u32[]{:S(2)}) copy-start(f32[128,32]{0,1:T(8,128)} %param.19) | copy-start | bytes 49156
  0.7 8.1 %copy-start.9 = (f32[2048]{0:T(1024)S(1)}, f32[2048]{0:T(1024)}, u32[]{:S(2)}) copy-start(f32[2048]{0:T(1024)} %refs_4_.2) | copy-start | bytes 24580
  0.7 8.1 %copy-start.10 = (f32[4,512]{1,0:T(4,128)S(1)}, f32[4,512]{1,0:T(4,128)}, u32[]{:S(2)}) copy-start(f32[4,512]{1,0:T(4,128)} %refs_8_.5) | copy-start | bytes 24580
  0.7 8.1 %copy-start.12 = (f32[512]{0:T(512)S(1)}, f32[512]{0:T(512)}, u32[]{:S(2)}) copy-start(f32[512]{0:T(512)} %refs_6_.1) | copy-start | bytes 6148
  0.7 8.1 %copy-start.13 = (s32[4]{0:T(128)S(1)}, s32[4]{0:T(128)}, u32[]{:S(2)}) copy-start(s32[4]{0:T(128)} %refs_10_.1) | copy-start | bytes 52
  0.7 8.1 %copy-start.14 = (f32[32]{0:T(128)S(1)}, f32[32]{0:T(128)}, u32[]{:S(2)}) copy-start(f32[32]{0:T(128)} %refs_9_.3) | copy-start | bytes 388
  0.7 8.1 %copy-start.15 = (f32[32]{0:T(128)S(1)}, f32[32]{0:T(128)}, u32[]{:S(2)}) copy-start(f32[32]{0:T(128)} %refs_7_.4) | copy-start | bytes 388
  0.8 8.1 %copy-start.16 = (f32[32]{0:T(128)S(1)}, f32[32]{0:T(128)}, u32[]{:S(2)}) copy-start(f32[32]{0:T(128)} %refs_8_.4) | copy-start | bytes 388
  3.6 12.4 %copy-start.2 = (bf16[144,1024]{1,0:T(8,128)(2,1)S(1)}, bf16[144,1024]{1,0:T(8,128)(2,1)}, u32[]{:S(2)}) copy-start(bf16[144,1024]{1,0:T(8,128)(2,1)} %first_state.1.refs_15_.refs_1_) | copy-start | bytes 884740
  3.7 12.4 %collective-permute-start = (bf16[144,1024]{1,0:T(8,128)(2,1)}, bf16[144,1024]{1,0:T(8,128)(2,1)S(1)}, u32[]{:S(2)}, u32[]{:S(2)}) collective-permute-start(bf16[144,1024]{1,0:T(8,128)(2,1)} %first_state.1.refs_15_.refs_1_), channel_id=1, source_target_pairs={{0,4},{4,8},{8,12},{1,5},{5,9},{9,13},{2,6},{6,10},{10,14},{3,7},{... | collective-permute-start | bytes 884744 | tf_op jit(solution)/shard_map/ppermute | solution.py:522
  11.3 11.3 %collective-permute-start.3 = (bf16[128,512]{1,0:T(8,128)(2,1)S(1)}, bf16[128,512]{1,0:T(8,128)(2,1)S(1)}, u32[]{:S(2)}, u32[]{:S(2)}) collective-permute-start(bf16[128,512]{1,0:T(8,128)(2,1)S(1)} %get-tuple-element.37.refs_2_), channel_id=1, source_target_pairs={{0,4},{4,8},{8,12},{1,5},{5,9},{9,13},{2,6},{6,10},{10,14},{3,7},{... | collective-permute-start | bytes 393224 | tf_op jit(solution)/shard_map/ppermute | solution.py:522
  16.0 4.6 %copy-start.1 = (bf16[128,2048]{1,0:T(8,128)(2,1)S(1)}, bf16[128,2048]{1,0:T(8,128)(2,1)}, u32[]{:S(2)}) copy-start(bf16[128,2048]{1,0:T(8,128)(2,1)} %refs_12_.3) | copy-start | bytes 1572868
  16.3 8.2 %collective-permute-start.1 = (bf16[128,1024]{1,0:T(8,128)(2,1)S(1)}, bf16[128,1024]{1,0:T(8,128)(2,1)S(1)}, u32[]{:S(2)}, u32[]{:S(2)}) collective-permute-start(bf16[128,1024]{1,0:T(8,128)(2,1)S(1)} %relay_slot2.1), channel_id=1, source_target_pairs={{0,4},{4,8},{8,12},{1,5},{5,9},{9,13},{2,6},{6,10},{10,14},{3,7},{... | collective-permute-start | bytes 786440 | tf_op jit(solution)/shard_map/ppermute | solution.py:522
  20.7 1.9 %copy-start.3 = (bf16[128,1024]{1,0:T(8,128)(2,1)S(1)}, bf16[128,1024]{1,0:T(8,128)(2,1)}, u32[]{:S(2)}) copy-start(bf16[128,1024]{1,0:T(8,128)(2,1)} %refs_0_.7) | copy-start | bytes 786436
  23.2 7.5 %collective-permute-start.4 = (bf16[128,512]{1,0:T(8,128)(2,1)S(1)}, bf16[128,512]{1,0:T(8,128)(2,1)S(1)}, u32[]{:S(2)}, u32[]{:S(2)}) collective-permute-start(bf16[128,512]{1,0:T(8,128)(2,1)S(1)} %get-tuple-element.41), channel_id=1, source_target_pairs={{4,8},{8,12},{5,9},{9,13},{6,10},{10,14},{7,11},{11,15},{20,24},{2... | collective-permute-start | bytes 393224 | tf_op jit(solution)/shard_map/ppermute | solution.py:522
  24.7 9.9 %collective-permute-start.2 = (bf16[128,1024]{1,0:T(8,128)(2,1)S(1)}, bf16[128,1024]{1,0:T(8,128)(2,1)S(1)}, u32[]{:S(2)}, u32[]{:S(2)}) collective-permute-start(bf16[128,1024]{1,0:T(8,128)(2,1)S(1)} %relay_slot3.1), channel_id=1, source_target_pairs={{0,4},{4,8},{8,12},{1,5},{5,9},{9,13},{2,6},{6,10},{10,14},{3,7},{... | collective-permute-start | bytes 786440 | tf_op jit(solution)/shard_map/ppermute | solution.py:522
  30.7 1.5 %copy-start.11 = (f32[2048]{0:T(1024)S(1)}, f32[2048]{0:T(1024)}, u32[]{:S(2)}) copy-start(f32[2048]{0:T(1024)} %refs_3_.7) | copy-start | bytes 24580

commit v10 on v9

--- a/solution.py
+++ b/solution.py
@@ -182,10 +182,10 @@
 
 def prepare_kernel(hops, groups, *refs):
     x_ref, bc_ref, dt_ref, wx_ref, bx_ref, wbc_ref, bbc_ref, dt_bias_ref, a_log_ref, skip_ref, lens_ref = refs[:11]
-    keys_ref, values_ref = refs[11:13]
-    xc_ref, bcc_ref, kv_ref, partial_ref, weight_ref, through_ref, inside_ref, flag_ref, entry_ref = refs[13:22]
-    wide_skip_ref, begin_ref = refs[22:24]
-    state_refs = refs[24:-2]
+    keys_ref, values_ref, z_ref = refs[11:14]
+    xc_ref, bcc_ref, kv_ref, partial_ref, weight_ref, through_ref, inside_ref, flag_ref = refs[14:22]
+    wide_skip_ref, begin_ref, step_ref, running_ref, out_ref, gate_ref, decay_ref = refs[22:29]
+    state_refs = refs[29:-2]
     top_ref, pad_ref = refs[-2:]
     rows, width = x_ref.shape
     per_group = width // groups
@@ -228,7 +228,9 @@
         flag_ref[hop] = jnp.broadcast_to((before == hop).astype(F32), (8, CHUNK))
     begin = doc_start(first + lax.broadcasted_iota(jnp.int32, begin_ref.shape, 0), lens_ref)
     begin_ref[...] = begin
-    entry_ref[...] = jnp.where(begin[:, :heads] < first, jnp.exp(running), 0.0)
+    entry = jnp.where(begin[:, :heads] < first, jnp.exp(running), 0.0)
+    step_ref[...] = step
+    running_ref[...] = running
     row = lax.broadcasted_iota(jnp.int32, (8, heads), 0)
     total = running[rows - 1 : rows]
     weight = step[:8] * jnp.exp(total - running[:8])
@@ -257,6 +259,48 @@
         some(slice(start, start + CHUNK), 0, wx_ref, bx_ref)
     for start in range(0, bc_ref.shape[1], CHUNK):
         some(slice(start, start + CHUNK), width, wbc_ref, bbc_ref)
+
+    row = lax.broadcasted_iota(jnp.int32, (rows, rows), 0)
+    lane = lax.broadcasted_iota(jnp.int32, (rows, rows), 1)
+    linked = (row >= lane) & (first + lane >= begin) & (lane >= 8)
+    turned_running = running.T
+    turned_step = step.T
+    pair_width = 2 * HDIM
+    channel = lax.broadcasted_iota(jnp.int32, (rows, pair_width), 1)
+    below = lax.broadcasted_iota(jnp.int32, (rows, CHUNK), 0) >= 8
+    for group in range(groups):
+        base = group * 2 * STATE
+        meet = lax.dot_general(
+            bcc_ref[:, base + STATE : base + 2 * STATE],
+            bcc_ref[:, base : base + STATE],
+            (((1,), (1,)), ((), ())),
+            preferred_element_type=F32,
+        )
+        meet = jnp.where(linked, meet, 0.0)
+        group_entry = entry[:, group * group_heads : (group + 1) * group_heads]
+        for chunk in range(0, per_group, CHUNK):
+            at = group * per_group + chunk
+            columns = slice(at, at + CHUNK)
+            gate = silu(z_ref[:, columns].astype(F32))
+            gate_ref[:, columns] = gate
+            decay_ref[:, columns] = widen(group_entry, chunk, CHUNK) * gate
+            xc_all = xc_ref[:, columns]
+            skipped = jnp.where(below, xc_all.astype(F32) * wide_skip_ref[0:1, columns], 0.0)
+            for start in range(0, CHUNK, pair_width):
+                parts = []
+                for head in ((at + start) // HDIM, (at + start) // HDIM + 1):
+                    spread = running[:, head : head + 1] - turned_running[head : head + 1]
+                    decay = jnp.exp(jnp.minimum(spread, 0.0))
+                    parts.append((decay * (meet * turned_step[head : head + 1])).astype(BF16))
+                mix = jnp.concatenate(parts, axis=1)
+                here_columns = slice(start, start + pair_width)
+                xc = xc_all[:, here_columns]
+                zero = jnp.zeros_like(xc)
+                stacked = jnp.concatenate(
+                    [jnp.where(channel < HDIM, xc, zero), jnp.where(channel < HDIM, zero, xc)], axis=0
+                )
+                value = jnp.dot(mix, stacked, preferred_element_type=F32) + skipped[:, here_columns]
+                out_ref[:, at + start : at + start + pair_width] = value * gate[:, here_columns]
 
 
 def first_rows(lines, partial_ref, inside_ref, w_ref, pad_ref, slot, at, start):
@@ -308,75 +352,80 @@
         out_ref[:, columns] = full.astype(BF16)
 
 
-def local_kernel(groups, *refs):
+def first_rows_kernel(groups, *refs):
     (
-        message_ref, partial_ref, weight_ref, inside_ref, wx_ref, wbc_ref, dt_ref, dt_bias_ref,
-        a_log_ref, wide_skip_ref, begin_ref, entry_ref, z_ref, xc_ref, bcc_ref,
-    ) = refs[:15]
-    state_refs = refs[15 : 15 + groups]
-    out_ref, decay_ref, c_ref = refs[15 + groups : 18 + groups]
-    full_refs = refs[18 + groups : 18 + 2 * groups]
-
+        message_ref, partial_ref, weight_ref, inside_ref, wx_ref, wbc_ref, step_ref, running_ref,
+        wide_skip_ref, begin_ref, bcc_ref, main_ref, gate_ref,
+    ) = refs[:13]
+    state_refs = refs[13 : 13 + groups]
+    out_ref, c_ref = refs[13 + groups : 15 + groups]
+    full_refs = refs[15 + groups : 15 + 2 * groups]
     pad_ref = refs[-1]
-    rows, width = xc_ref.shape
+    rows, width = main_ref.shape
     per_group = width // groups
     heads = per_group // HDIM
+    lanes = 8 * heads
     first = lax.axis_index("seq") * rows
     lines = tail_lines(message_ref, STATE)
     slots = pad_ref.shape[0]
-
-    def top(w_ref, slot, at, start, below):
-        new = first_rows(lines, partial_ref, inside_ref, w_ref, pad_ref, slot, at, start)
-        old = below[8:EDGE].astype(F32)
-        return jnp.concatenate([jnp.concatenate([new.astype(F32), old], axis=0).astype(BF16), below[EDGE:]], axis=0)
-
-    row = lax.broadcasted_iota(jnp.int32, (rows, rows), 0)
-    lane_row = lax.broadcasted_iota(jnp.int32, (rows, rows), 1)
-    linked = (row >= lane_row) & (first + lane_row >= begin_ref[...])
-    step, running = rates(dt_ref, dt_bias_ref, a_log_ref)
-    turned_running = running.T
-    turned_step = step.T
-    pair_width = 2 * HDIM
-    lane = lax.broadcasted_iota(jnp.int32, (rows, pair_width), 1)
+    top = functools.partial(first_rows, lines, partial_ref, inside_ref)
+    lane = lax.broadcasted_iota(jnp.int32, (rows, lanes), 1)
+    line = lane & 7
+    row = lax.broadcasted_iota(jnp.int32, (rows, lanes), 0)
+    begin = jnp.concatenate([begin_ref[...]] * -(-lanes // rows), axis=1)[:, :lanes]
+    linked = (row >= line) & (first + line >= begin)
+    head = lax.broadcasted_iota(jnp.int32, (3 * heads, lanes), 0)
+    for _ in range(2):
+        head = jnp.where(head >= heads, head - heads, head)
+    spread = (lax.broadcasted_iota(jnp.int32, (3 * heads, lanes), 1) >> 3 == head).astype(F32).astype(BF16)
+    own_line = lax.broadcasted_iota(jnp.int32, (8, lanes), 0) == line[:8]
+
+    def to_lanes(value):
+        high = value.astype(BF16)
+        middle, low = halves(value - high.astype(F32))
+        return jnp.dot(jnp.concatenate([high, middle, low], axis=1), spread, preferred_element_type=F32)
+
+    def by_line(value):
+        return jnp.sum(jnp.where(own_line, value, 0.0), axis=0, keepdims=True)
+
+    channel = lax.broadcasted_iota(jnp.int32, (8, CHUNK), 1)
     for group in range(groups):
         base = group * 2 * STATE
-        pair = top(wbc_ref, group % slots, width, base, bcc_ref[:, base : base + 2 * STATE])
-        inputs = pair[:, :STATE]
-        outputs = pair[:, STATE:]
+        these = slice(group * heads, (group + 1) * heads)
+        new = top(wbc_ref, pad_ref, group % slots, width, base).astype(F32)
+        old = bcc_ref[:, base + STATE : base + 2 * STATE]
+        outputs = jnp.concatenate([new[:, STATE:], old[:EDGE].astype(F32)[8:]], axis=0).astype(BF16)
+        outputs = jnp.concatenate([outputs, old[EDGE:]], axis=0)
         c_ref[:, group * STATE : (group + 1) * STATE] = outputs
-        turned = inputs[:EDGE].astype(F32).T[:, :8].astype(BF16)
+        inputs = jnp.concatenate([new[:, :STATE]] * heads, axis=0).astype(BF16)
         meet = lax.dot_general(
             outputs, inputs, (((1,), (1,)), ((), ())), preferred_element_type=F32
         )
-        meet = jnp.where(linked, meet, 0.0)
+        running = to_lanes(running_ref[:, these])
+        decay = jnp.exp(jnp.minimum(running - by_line(running[:8]), 0.0))
+        mix = decay * (meet * by_line(to_lanes(step_ref[:8, these])))
+        mix = jnp.where(linked, mix, 0.0).astype(BF16)
+        turned = inputs[:EDGE].astype(F32).T[:, :8].astype(BF16)
         for chunk in range(0, per_group, CHUNK):
             at = group * per_group + chunk
-            columns = slice(chunk, chunk + CHUNK)
-            xc_all = top(wx_ref, (chunk // CHUNK) % slots, 0, at, xc_ref[:, at : at + CHUNK])
-            weighted = xc_all[:EDGE].astype(F32)[:8] * weight_ref[:, at : at + CHUNK]
-            full = state_refs[group][:STATE, columns].astype(F32) + jnp.dot(
-                turned, weighted.astype(BF16), preferred_element_type=F32
+            columns = slice(at, at + CHUNK)
+            xc = top(wx_ref, pad_ref, (chunk // CHUNK + 1) % slots, 0, at).astype(F32)
+            full = state_refs[group][:STATE, chunk : chunk + CHUNK].astype(F32) + jnp.dot(
+                turned, (xc * weight_ref[:, columns]).astype(BF16), preferred_element_type=F32
             )
-            full_refs[group][:, columns] = full.astype(BF16)
-            wide_skip = wide_skip_ref[0:1, at : at + CHUNK]
-            gate = silu(z_ref[:, at : at + CHUNK].astype(F32))
-            entry = entry_ref[:, group * heads : (group + 1) * heads]
-            decay_ref[:, at : at + CHUNK] = widen(entry, chunk, CHUNK) * gate
-            for start in range(0, CHUNK, pair_width):
-                parts = []
-                for head in ((at + start) // HDIM, (at + start) // HDIM + 1):
-                    spread = running[:, head : head + 1] - turned_running[head : head + 1]
-                    decay = jnp.exp(jnp.minimum(spread, 0.0))
-                    parts.append((decay * (meet * turned_step[head : head + 1])).astype(BF16))
-                mix = jnp.concatenate(parts, axis=1)
-                xc = xc_all[:, start : start + pair_width]
-                zero = jnp.zeros_like(xc)
-                stacked = jnp.concatenate(
-                    [jnp.where(lane < HDIM, xc, zero), jnp.where(lane < HDIM, zero, xc)], axis=0
-                )
-                value = jnp.dot(mix, stacked, preferred_element_type=F32)
-                value = value + xc.astype(F32) * wide_skip[:, start : start + pair_width]
-                out_ref[:, at + start : at + start + pair_width] = value * gate[:, start : start + pair_width]
+            full_refs[group][:, chunk : chunk + CHUNK] = full.astype(BF16)
+            blocks = []
+            for at_head in range(heads):
+                low = at_head * HDIM - chunk
+                if 0 <= low < CHUNK:
+                    blocks.append(jnp.where((channel >= low) & (channel < low + HDIM), xc, 0.0))
+                else:
+                    blocks.append(jnp.zeros_like(xc))
+            spread_xc = jnp.concatenate(blocks, axis=0).astype(BF16)
+            gate = gate_ref[:, columns]
+            value = main_ref[:, columns] + gate * jnp.dot(mix, spread_xc, preferred_element_type=F32)
+            out_ref[:, columns] = value
+            out_ref[0:8, columns] = value[:8] + gate[:8] * (xc * wide_skip_ref[:, columns])
 
 
 def attend(q_ref, kv_refs, begin_ref, blocks, share, head):
@@ -596,19 +645,24 @@
             shape((8, width), F32),
             shape((conv_x_weight.shape[0] - 1, 8, CHUNK), F32),
             shape((hops, 8, CHUNK), F32),
-            shape((rows, heads), F32),
             shape((8, width), F32),
             shape((rows, rows), jnp.int32),
+            shape((rows, heads), F32),
+            shape((rows, heads), F32),
+            shape((rows, width), F32),
+            shape((rows, width), F32),
+            shape((rows, width), F32),
             *(shape((STATE, per_group), BF16) for _ in range(groups - 1)),
         ],
-        [x_raw, bc_raw, *params, skip_d, doc_lens, keys, values],
-        [WHOLE] * 10 + [SCALARS] + [WHOLE] * 2,
+        [x_raw, bc_raw, *params, skip_d, doc_lens, keys, values, z_gate],
+        [WHOLE] * 10 + [SCALARS] + [WHOLE] * 3,
         scratch=[
             pltpu.VMEM((16, width + bc_width), F32),
             pltpu.VMEM((4, rows + 8, CHUNK), F32),
         ],
     )
-    xc, bcc, kv, partial, weight, through, inside, flags, entry, wide_skip, begin, *states = prepared
+    _, bcc, kv, partial, weight, through, inside, flags, wide_skip, begin, *prepared = prepared
+    step, running, main, gate, decay, *states = prepared
     states = [message, *states]
     kvs = [kv, onward(kv)]
     fulls = None
@@ -635,20 +689,19 @@
         )
         slots.append(onward(passed))
         if fulls is None:
-            gated, decay, c_out, *fulls = call(
-                functools.partial(local_kernel, groups),
-                "local_mix",
+            gated, c_out, *fulls = call(
+                functools.partial(first_rows_kernel, groups),
+                "first_rows",
                 [
-                    shape((rows, width), F32),
                     shape((rows, width), F32),
                     shape((rows, groups * STATE), BF16),
                     *(shape((STATE, per_group), BF16) for _ in range(groups)),
                 ],
                 [
-                    slots[0], partial, weight, inside, conv_x_weight, conv_bc_weight, dt, dt_bias, a_log,
-                    wide_skip, begin, entry, z_gate, xc, bcc, *states,
+                    slots[0], partial, weight, inside, conv_x_weight, conv_bc_weight, step, running,
+                    wide_skip, begin, bcc, main, gate, *states,
                 ],
-                [WHOLE] * (15 + groups),
+                [WHOLE] * (13 + groups),
                 scratch=[pltpu.VMEM((4, 16, CHUNK), F32)],
             )
     parts = shape(queries.shape, F32)

time: 35.9 us -> 35.2 us (0.981)
  the two profiles are of different devices: /device:TPU:0 before, /device:TPU:22 now
where the time goes in v10:
time: 35.2 us; the launch traced here: 34.6 us
  starting transfers between devices  16.1 us (46%)
  Pallas kernels  12.1 us (34%)
  waiting for transfers between devices  5.35 us (15%)
  between operations  0.96 us (3%)
    ppermute x5, starting transfers between devices, onward(): lax.ppermute(value, 'seq', [(source, source + 1) for source in range(firs...  16.1 us
    pallas_call x9, Pallas kernels, call(): pl.pallas_call(kernel, name=name, grid=(1,), out_shape=outs, in_specs=spe...  12.1 us
    ppermute x5, waiting for transfers between devices, onward(): lax.ppermute(value, 'seq', [(source, source + 1) for source in range(firs...  5.35 us
  transfers between devices with their start and end apart: 5, of which 4 were waited for; matrix products, arithmetic and copies ran while one was open for 0% of the time, Pallas kernels for 24%

profile of v10, /device:TPU:22, one launch (start us, length us, event | category | flops | bytes accessed | tf_op | source)
XLA Modules:
  0.0 34.6 jit_solution(372656313171707625)
XLA Ops:
  0.8 2.9 %first_state.1.refs_13_.refs_1_ = bf16[144,1024]{1,0:T(8,128)(2,1)} custom-call(bf16[128,2048]{1,0:T(8,128)(2,1)} %refs_0_.5, bf16[128,512]{1,0:T(8,128)(2,1)} %refs_1_.3, f32[32,128]{1,0:T(8,128)} %bitcast.5, f32[4,2048]{1,0:T(4,128)} %refs_7_.3, f32[1,2048]{1,0:T(1,128)} %bitcast.7, f32[4,512]{1,0:T(4,128)} %refs_8_.3, f32[1,512]{1,0:T(1,128)} %bitcast.8, ...), custom_call_target="tpu_custom_call" | custom-call | flops 2000000000 | bytes 1018128 | tf_op jit(solution)/shard_map/first_state/pallas_call | solution.py:555
  3.7 3.6 %collective-permute-start = (bf16[144,1024]{1,0:T(8,128)(2,1)}, bf16[144,1024]{1,0:T(8,128)(2,1)S(1)}, u32[]{:S(2)}, u32[]{:S(2)}) collective-permute-start(bf16[144,1024]{1,0:T(8,128)(2,1)} %first_state.1.refs_13_.refs_1_), channel_id=1, source_target_pairs={{0,4},{4,8},{8,12},{1,5},{5,9},{9,13},{2,6},{6,10},{10,14},{3,7},{... | collective-permute-start | bytes 884744 | tf_op jit(solution)/shard_map/ppermute | solution.py:571
  7.3 0.0 copy-done
  7.3 0.0 copy-done.1
  7.3 0.0 copy-done.4
  7.3 0.0 copy-done.5
  7.3 0.0 copy-done.6
  7.3 0.0 copy-done.7
  7.4 0.0 copy-done.8
  7.4 0.0 copy-done.9
  7.4 0.0 copy-done.10
  7.4 0.0 copy-done.12
  7.4 0.0 copy-done.13
  7.4 0.0 copy-done.14
  7.4 3.5 %prepare.1 = (bf16[128,2048]{1,0:T(8,128)(2,1)}, bf16[128,512]{1,0:T(8,128)(2,1)S(1)}, bf16[128,512]{1,0:T(8,128)(2,1)S(1)}, f32[8,2560]{1,0:T(8,128)S(1)}, f32[...) custom-call(bf16[128,2048]{1,0:T(8,128)(2,1)S(1)} %copy-done, ...), custom_call_target="tpu_custom_call" | custom-call | flops 2000000000 | bytes 5990800 | tf_op jit(solution)/shard_map/prepare/pallas_call | solution.py:555
  11.0 1.9 %collective-permute-start.3 = (bf16[128,512]{1,0:T(8,128)(2,1)S(1)}, bf16[128,512]{1,0:T(8,128)(2,1)S(1)}, u32[]{:S(2)}, u32[]{:S(2)}) collective-permute-start(bf16[128,512]{1,0:T(8,128)(2,1)S(1)} %get-tuple-element.41.refs_2_), channel_id=1, source_target_pairs={{0,4},{4,8},{8,12},{1,5},{5,9},{9,13},{2,6},{6,10},{10,14},{3,7},{... | collective-permute-start | bytes 393224 | tf_op jit(solution)/shard_map/ppermute | solution.py:571
  12.9 1.8 %collective-permute-done.refs_0_.refs_5_ = bf16[144,1024]{1,0:T(8,128)(2,1)S(1)} collective-permute-done((bf16[144,1024]{1,0:T(8,128)(2,1)}, bf16[144,1024]{1,0:T(8,128)(2,1)S(1)}, u32[]{:S(2)}, u32[]{:S(2)}) %collective-permute-start) | collective-permute-done | bytes 294944 | tf_op jit(solution)/shard_map/ppermute | solution.py:571
  14.7 0.3 relay_slot2.1
  15.1 4.3 %collective-permute-start.1 = (bf16[128,1024]{1,0:T(8,128)(2,1)S(1)}, bf16[128,1024]{1,0:T(8,128)(2,1)S(1)}, u32[]{:S(2)}, u32[]{:S(2)}) collective-permute-start(bf16[128,1024]{1,0:T(8,128)(2,1)S(1)} %relay_slot2.1), channel_id=1, source_target_pairs={{0,4},{4,8},{8,12},{1,5},{5,9},{9,13},{2,6},{6,10},{10,14},{3,7},{... | collective-permute-start | bytes 786440 | tf_op jit(solution)/shard_map/ppermute | solution.py:571
  19.3 0.0 copy-start.3
  19.4 1.1 %first_rows.1 = (f32[128,2048]{1,0:T(8,128)S(1)}, bf16[128,256]{1,0:T(8,128)(2,1)S(1)}, bf16[128,1024]{1,0:T(8,128)(2,1)}, bf16[128,1024]{1,0:T(8,128)(2,1)S(1)}) custom-call(bf16[144,1024]{1,0:T(8,128)(2,1)S(1)} %collective-permute-done.refs_0_.refs_5_, f32[8,2560]{1,0:T(8,128)S(1)} %get-tuple-element.24.refs_1_.refs_2_, ...), custom_call_target="tpu_custom_call" | custom-call | flops 2000000000 | bytes 5095424 | tf_op jit(solution)/shard_map/first_rows/pallas_call | solution.py:555
  20.5 0.0 collective-permute-done.3.refs_1_
  20.5 0.6 %attend_near.1 = (f32[128,1024]{1,0:T(8,128)S(1)}, f32[128,1024]{1,0:T(8,128)S(1)}, f32[128,1024]{1,0:T(8,128)S(1)}, bf16[128,512]{1,0:T(8,128)(2,1)S(1)}) custom-call(bf16[128,1024]{1,0:T(8,128)(2,1)S(1)} %copy-done.3, bf16[128,512]{1,0:T(8,128)(2,1)S(1)} %collective-permute-done.3.refs_1_, bf16[128,512]{1,0:T(8,128)(2,1)S(1)} %get-tuple-element.41.refs_2_, ...), custom_call_target="tpu_custom_call" | custom-call | flops 2000000000 | bytes 2359296 | tf_op jit(solution)/shard_map/attend_near/pallas_call | solution.py:555
  21.1 1.9 %collective-permute-start.4 = (bf16[128,512]{1,0:T(8,128)(2,1)S(1)}, bf16[128,512]{1,0:T(8,128)(2,1)S(1)}, u32[]{:S(2)}, u32[]{:S(2)}) collective-permute-start(bf16[128,512]{1,0:T(8,128)(2,1)S(1)} %get-tuple-element.45), channel_id=1, source_target_pairs={{4,8},{8,12},{5,9},{9,13},{6,10},{10,14},{7,11},{11,15},{20,24},{2... | collective-permute-start | bytes 393224 | tf_op jit(solution)/shard_map/ppermute | solution.py:571
  23.0 1.6 %collective-permute-done.1.refs_0_.refs_6_ = bf16[128,1024]{1,0:T(8,128)(2,1)S(1)} collective-permute-done((bf16[128,1024]{1,0:T(8,128)(2,1)S(1)}, bf16[128,1024]{1,0:T(8,128)(2,1)S(1)}, u32[]{:S(2)}, u32[]{:S(2)}) %collective-permute-start.1) | collective-permute-done | bytes 262176 | tf_op jit(solution)/shard_map/ppermute | solution.py:571
  24.6 0.1 relay_slot3.1
  24.7 4.4 %collective-permute-start.2 = (bf16[128,1024]{1,0:T(8,128)(2,1)S(1)}, bf16[128,1024]{1,0:T(8,128)(2,1)S(1)}, u32[]{:S(2)}, u32[]{:S(2)}) collective-permute-start(bf16[128,1024]{1,0:T(8,128)(2,1)S(1)} %relay_slot3.1), channel_id=1, source_target_pairs={{0,4},{4,8},{8,12},{1,5},{5,9},{9,13},{2,6},{6,10},{10,14},{3,7},{... | collective-permute-start | bytes 786440 | tf_op jit(solution)/shard_map/ppermute | solution.py:571
  29.1 0.2 collective-permute-done.4.refs_5_
  29.3 1.4 %attend_far.1 = bf16[128,1024]{1,0:T(8,128)(2,1)} custom-call(bf16[128,1024]{1,0:T(8,128)(2,1)S(1)} %copy-done.3, s32[128,128]{1,0:T(8,128)S(1)} %get-tuple-element.30.refs_9_.refs_3_.refs_1_, f32[128,1024]{1,0:T(8,128)S(1)} %get-tuple-element.42.refs_2_, f32[128,1024]{1,0:T(8,128)S(1)} %get-tuple-element.43.refs_3_, ...), custom_call_target="tpu_custom_call" | custom-call | flops 2000000000 | bytes 2293760 | tf_op jit(solution)/shard_map/attend_far/pallas_call | solution.py:555
  30.8 1.1 %norm_part0.1.refs_6_ = bf16[128,2048]{1,0:T(8,128)(2,1)} custom-call(f32[128,2048]{1,0:T(8,128)S(1)} %get-tuple-element.35.refs_0_, f32[128,2048]{1,0:T(8,128)S(1)} %get-tuple-element.36.refs_1_, bf16[128,256]{1,0:T(8,128)(2,1)S(1)} %get-tuple-element.37.refs_2_.refs_4_, f32[2048]{0:T(1024)S(1)} %copy-done.11, ...), custom_call_target="tpu_custom_call" | custom-call | flops 2000000000 | bytes 3268608 | tf_op jit(solution)/shard_map/norm_part0/pallas_call | solution.py:555
  31.9 1.7 %collective-permute-done.2.refs_5_ = bf16[128,1024]{1,0:T(8,128)(2,1)S(1)} collective-permute-done((bf16[128,1024]{1,0:T(8,128)(2,1)S(1)}, bf16[128,1024]{1,0:T(8,128)(2,1)S(1)}, u32[]{:S(2)}, u32[]{:S(2)}) %collective-permute-start.2) | collective-permute-done | bytes 262176 | tf_op jit(solution)/shard_map/ppermute | solution.py:571
  33.6 1.1 %norm_part1.1 = bf16[128,2048]{1,0:T(8,128)(2,1)} custom-call(f32[128,2048]{1,0:T(8,128)S(1)} %get-tuple-element.35.refs_0_, f32[128,2048]{1,0:T(8,128)S(1)} %get-tuple-element.36.refs_1_, bf16[128,256]{1,0:T(8,128)(2,1)S(1)} %get-tuple-element.37.refs_2_.refs_4_, f32[2048]{0:T(1024)S(1)} %copy-done.11, ...), custom_call_target="tpu_custom_call", output_to_operand_aliasing={{}: (6, {})} | custom-call | flops 2000000000 | bytes 3497984 | tf_op jit(solution)/shard_map/norm_part1/pallas_call | solution.py:555
  (21 shorter events, 0.0 us)
Async XLA Ops:
  0.6 6.7 %copy-start = (bf16[128,2048]{1,0:T(8,128)(2,1)S(1)}, bf16[128,2048]{1,0:T(8,128)(2,1)}, u32[]{:S(2)}) copy-start(bf16[128,2048]{1,0:T(8,128)(2,1)} %refs_0_.5) | copy-start | bytes 1572868
  0.6 6.7 %copy-start.1 = (bf16[128,2048]{1,0:T(8,128)(2,1)S(1)}, bf16[128,2048]{1,0:T(8,128)(2,1)}, u32[]{:S(2)}) copy-start(bf16[128,2048]{1,0:T(8,128)(2,1)} %refs_13_.1) | copy-start | bytes 1572868
  0.7 6.7 %copy-start.4 = (bf16[128,512]{1,0:T(8,128)(2,1)S(1)}, bf16[128,512]{1,0:T(8,128)(2,1)}, u32[]{:S(2)}) copy-start(bf16[128,512]{1,0:T(8,128)(2,1)} %refs_1_.3) | copy-start | bytes 393220
  0.7 6.7 %copy-start.5 = (bf16[128,256]{1,0:T(8,128)(2,1)S(1)}, bf16[128,256]{1,0:T(8,128)(2,1)}, u32[]{:S(2)}) copy-start(bf16[128,256]{1,0:T(8,128)(2,1)} %refs_11_.1) | copy-start | bytes 196612
  0.7 6.7 %copy-start.6 = (bf16[128,256]{1,0:T(8,128)(2,1)S(1)}, bf16[128,256]{1,0:T(8,128)(2,1)}, u32[]{:S(2)}) copy-start(bf16[128,256]{1,0:T(8,128)(2,1)} %refs_12_.1) | copy-start | bytes 196612
  0.7 6.7 %copy-start.7 = (f32[4,2048]{1,0:T(4,128)S(1)}, f32[4,2048]{1,0:T(4,128)}, u32[]{:S(2)}) copy-start(f32[4,2048]{1,0:T(4,128)} %refs_7_.3) | copy-start | bytes 98308
  0.7 6.7 %copy-start.8 = (f32[128,32]{0,1:T(8,128)S(1)}, f32[128,32]{0,1:T(8,128)}, u32[]{:S(2)}) copy-start(f32[128,32]{0,1:T(8,128)} %param.19) | copy-start | bytes 49156
  0.7 6.7 %copy-start.9 = (f32[2048]{0:T(1024)S(1)}, f32[2048]{0:T(1024)}, u32[]{:S(2)}) copy-start(f32[2048]{0:T(1024)} %refs_4_.2) | copy-start | bytes 24580
  0.7 6.7 %copy-start.10 = (f32[4,512]{1,0:T(4,128)S(1)}, f32[4,512]{1,0:T(4,128)}, u32[]{:S(2)}) copy-start(f32[4,512]{1,0:T(4,128)} %refs_8_.3) | copy-start | bytes 24580
  0.7 6.7 %copy-start.12 = (f32[512]{0:T(512)S(1)}, f32[512]{0:T(512)}, u32[]{:S(2)}) copy-start(f32[512]{0:T(512)} %refs_6_.1) | copy-start | bytes 6148
  0.7 6.7 %copy-start.13 = (f32[32]{0:T(128)S(1)}, f32[32]{0:T(128)}, u32[]{:S(2)}) copy-start(f32[32]{0:T(128)} %refs_7_.2) | copy-start | bytes 388
  0.7 6.7 %copy-start.14 = (f32[32]{0:T(128)S(1)}, f32[32]{0:T(128)}, u32[]{:S(2)}) copy-start(f32[32]{0:T(128)} %refs_8_.2) | copy-start | bytes 388
  0.8 6.7 %copy-start.15 = (s32[4]{0:T(128)S(1)}, s32[4]{0:T(128)}, u32[]{:S(2)}) copy-start(s32[4]{0:T(128)} %refs_10_.1) | copy-start | bytes 52
  0.8 6.7 %copy-start.16 = (f32[32]{0:T(128)S(1)}, f32[32]{0:T(128)}, u32[]{:S(2)}) copy-start(f32[32]{0:T(128)} %refs_9_.3) | copy-start | bytes 388
  3.7 11.1 %copy-start.2 = (bf16[144,1024]{1,0:T(8,128)(2,1)S(1)}, bf16[144,1024]{1,0:T(8,128)(2,1)}, u32[]{:S(2)}) copy-start(bf16[144,1024]{1,0:T(8,128)(2,1)} %first_state.1.refs_13_.refs_1_) | copy-start | bytes 884740
  3.7 11.0 %collective-permute-start = (bf16[144,1024]{1,0:T(8,128)(2,1)}, bf16[144,1024]{1,0:T(8,128)(2,1)S(1)}, u32[]{:S(2)}, u32[]{:S(2)}) collective-permute-start(bf16[144,1024]{1,0:T(8,128)(2,1)} %first_state.1.refs_13_.refs_1_), channel_id=1, source_target_pairs={{0,4},{4,8},{8,12},{1,5},{5,9},{9,13},{2,6},{6,10},{10,14},{3,7},{... | collective-permute-start | bytes 884744 | tf_op jit(solution)/shard_map/ppermute | solution.py:571
  11.0 9.5 %collective-permute-start.3 = (bf16[128,512]{1,0:T(8,128)(2,1)S(1)}, bf16[128,512]{1,0:T(8,128)(2,1)S(1)}, u32[]{:S(2)}, u32[]{:S(2)}) collective-permute-start(bf16[128,512]{1,0:T(8,128)(2,1)S(1)} %get-tuple-element.41.refs_2_), channel_id=1, source_target_pairs={{0,4},{4,8},{8,12},{1,5},{5,9},{9,13},{2,6},{6,10},{10,14},{3,7},{... | collective-permute-start | bytes 393224 | tf_op jit(solution)/shard_map/ppermute | solution.py:571
  15.1 9.6 %collective-permute-start.1 = (bf16[128,1024]{1,0:T(8,128)(2,1)S(1)}, bf16[128,1024]{1,0:T(8,128)(2,1)S(1)}, u32[]{:S(2)}, u32[]{:S(2)}) collective-permute-start(bf16[128,1024]{1,0:T(8,128)(2,1)S(1)} %relay_slot2.1), channel_id=1, source_target_pairs={{0,4},{4,8},{8,12},{1,5},{5,9},{9,13},{2,6},{6,10},{10,14},{3,7},{... | collective-permute-start | bytes 786440 | tf_op jit(solution)/shard_map/ppermute | solution.py:571
  19.3 1.1 %copy-start.3 = (bf16[128,1024]{1,0:T(8,128)(2,1)S(1)}, bf16[128,1024]{1,0:T(8,128)(2,1)}, u32[]{:S(2)}) copy-start(bf16[128,1024]{1,0:T(8,128)(2,1)} %refs_0_.7) | copy-start | bytes 786436
  21.1 8.2 %collective-permute-start.4 = (bf16[128,512]{1,0:T(8,128)(2,1)S(1)}, bf16[128,512]{1,0:T(8,128)(2,1)S(1)}, u32[]{:S(2)}, u32[]{:S(2)}) collective-permute-start(bf16[128,512]{1,0:T(8,128)(2,1)S(1)} %get-tuple-element.45), channel_id=1, source_target_pairs={{4,8},{8,12},{5,9},{9,13},{6,10},{10,14},{7,11},{11,15},{20,24},{2... | collective-permute-start | bytes 393224 | tf_op jit(solution)/shard_map/ppermute | solution.py:571
  24.7 8.9 %collective-permute-start.2 = (bf16[128,1024]{1,0:T(8,128)(2,1)S(1)}, bf16[128,1024]{1,0:T(8,128)(2,1)S(1)}, u32[]{:S(2)}, u32[]{:S(2)}) collective-permute-start(bf16[128,1024]{1,0:T(8,128)(2,1)S(1)} %relay_slot3.1), channel_id=1, source_target_pairs={{0,4},{4,8},{8,12},{1,5},{5,9},{9,13},{2,6},{6,10},{10,14},{3,7},{... | collective-permute-start | bytes 786440 | tf_op jit(solution)/shard_map/ppermute | solution.py:571
  29.3 1.4 %copy-start.11 = (f32[2048]{0:T(1024)S(1)}, f32[2048]{0:T(1024)}, u32[]{:S(2)}) copy-start(f32[2048]{0:T(1024)} %refs_3_.7) | copy-start | bytes 24580

commit v11 on v10

--- a/solution.py
+++ b/solution.py
@@ -182,10 +182,10 @@
 
 def prepare_kernel(hops, groups, *refs):
     x_ref, bc_ref, dt_ref, wx_ref, bx_ref, wbc_ref, bbc_ref, dt_bias_ref, a_log_ref, skip_ref, lens_ref = refs[:11]
-    keys_ref, values_ref, z_ref = refs[11:14]
-    xc_ref, bcc_ref, kv_ref, partial_ref, weight_ref, through_ref, inside_ref, flag_ref = refs[14:22]
-    wide_skip_ref, begin_ref, step_ref, running_ref, out_ref, gate_ref, decay_ref = refs[22:29]
-    state_refs = refs[29:-2]
+    z_ref = refs[11]
+    xc_ref, bcc_ref, partial_ref, weight_ref, through_ref, inside_ref, flag_ref = refs[12:19]
+    wide_skip_ref, begin_ref, step_ref, running_ref, out_ref, gate_ref, decay_ref = refs[19:26]
+    state_refs = refs[26:-2]
     top_ref, pad_ref = refs[-2:]
     rows, width = x_ref.shape
     per_group = width // groups
@@ -193,9 +193,6 @@
     slots = pad_ref.shape[0]
     here = lax.axis_index("seq")
     first = here * rows
-    kv_width = keys_ref.shape[1]
-    kv_ref[:, :kv_width] = keys_ref[...]
-    kv_ref[:, kv_width:] = values_ref[...]
     inside = insides(first, (rows, CHUNK), taps, lens_ref)
     step, running = rates(dt_ref, dt_bias_ref, a_log_ref)
     heads = step.shape[1]
@@ -453,45 +450,61 @@
     count: int
 
 
-def near_kernel(*refs):
-    q_ref, before_ref, own_ref, begin_ref, _, sum_ref, total_ref, peak_ref, kv_ref = refs
-    kv_ref[...] = before_ref[...]
+def fold(q_ref, kv_refs, begin_ref, blocks, share, head, carry):
+    lows = [(head * share + part) * ADIM for part in range(share)]
+    scores, values = attend(q_ref, kv_refs, begin_ref, blocks, share, head)
+    peak = jnp.max(scores, axis=1, keepdims=True)
+    peak = jnp.broadcast_to(peak, (peak.shape[0], ADIM))
+    if carry is not None:
+        sums, totals, before = (
+            jnp.concatenate([ref[:, low : low + ADIM] for low in lows], axis=0) for ref in carry
+        )
+        peak = jnp.maximum(peak, before)
+    expo = jnp.exp(scores - jnp.concatenate([peak] * (scores.shape[1] // ADIM), axis=1))
+    summed = jnp.dot(expo.astype(BF16), values, preferred_element_type=F32)
+    if carry is None:
+        return lows, summed[:, :ADIM], summed[:, ADIM:], peak
+    factor = jnp.exp(before - peak)
+    return lows, sums * factor + summed[:, :ADIM], totals * factor + summed[:, ADIM:], peak
+
+
+def own_kernel(q_ref, keys_ref, values_ref, begin_ref, *outs):
+    kv_ref = outs[3]
+    kv_width = keys_ref.shape[1]
+    kv_ref[:, :kv_width] = keys_ref[...]
+    kv_ref[:, kv_width:] = values_ref[...]
     rows = q_ref.shape[0]
     share = QHEADS // KVHEADS
-    for head in range(own_ref.shape[1] // (2 * ADIM)):
-        scores, values = attend(q_ref, (before_ref, own_ref), begin_ref, Blocks(1, 2), share, head)
-        peak = jnp.max(scores, axis=1, keepdims=True)
-        summed = jnp.dot(jnp.exp(scores - peak).astype(BF16), values, preferred_element_type=F32)
-        peak = jnp.broadcast_to(peak, (peak.shape[0], ADIM))
-        for part in range(share):
-            low = (head * share + part) * ADIM
-            these = slice(part * rows, (part + 1) * rows)
-            sum_ref[:, low : low + ADIM] = summed[these, :ADIM]
-            total_ref[:, low : low + ADIM] = summed[these, ADIM:]
-            peak_ref[:, low : low + ADIM] = peak[these]
+    for head in range(kv_width // ADIM):
+        lows, *results = fold(q_ref, (kv_ref,), begin_ref, Blocks(0, 1), share, head, None)
+        for ref, result in zip(outs, results):
+            for part, low in enumerate(lows):
+                ref[:, low : low + ADIM] = result[part * rows : (part + 1) * rows]
+
+
+def near_kernel(q_ref, before_ref, begin_ref, *refs):
+    carry, outs = refs[:3], refs[4:]
+    outs[3][...] = before_ref[...]
+    rows = q_ref.shape[0]
+    share = QHEADS // KVHEADS
+    for head in range(before_ref.shape[1] // (2 * ADIM)):
+        lows, *results = fold(q_ref, (before_ref,), begin_ref, Blocks(1, 1), share, head, carry)
+        for ref, result in zip(outs, results):
+            for part, low in enumerate(lows):
+                ref[:, low : low + ADIM] = result[part * rows : (part + 1) * rows]
 
 
 def far_kernel(hops, *refs):
-    q_ref, begin_ref, sum_ref, total_ref, peak_ref = refs[:5]
+    q_ref, begin_ref = refs[:2]
     kv_refs = refs[5 : 4 + hops]
     out_hbm_ref, out_ref, sems = refs[4 + hops :]
     rows = q_ref.shape[0]
     share = QHEADS // KVHEADS
     copies = []
     for head in range(kv_refs[0].shape[1] // (2 * ADIM)):
-        lows = [(head * share + part) * ADIM for part in range(share)]
-
-        def stacked(ref):
-            return jnp.concatenate([ref[:, low : low + ADIM] for low in lows], axis=0)
-
-        scores, values = attend(q_ref, kv_refs, begin_ref, Blocks(hops, hops - 1), share, head)
-        near = stacked(peak_ref)
-        peak = jnp.maximum(near, jnp.max(scores, axis=1, keepdims=True))
-        expo = jnp.exp(scores - jnp.concatenate([peak] * (scores.shape[1] // ADIM), axis=1))
-        summed = jnp.dot(expo.astype(BF16), values, preferred_element_type=F32)
-        factor = jnp.exp(near - peak)
-        total = stacked(total_ref) * factor + summed[:, ADIM:]
-        result = ((stacked(sum_ref) * factor + summed[:, :ADIM]) / total).astype(BF16)
+        blocks = Blocks(hops, hops - 1)
+        lows, sums, totals, _ = fold(q_ref, kv_refs, begin_ref, blocks, share, head, refs[2:5])
+        result = (sums / totals).astype(BF16)
         for part, low in enumerate(lows):
             out_ref[:, low : low + ADIM] = result[part * rows : (part + 1) * rows]
         columns = pl.ds(head * share * ADIM, share * ADIM)
@@ -503,42 +516,52 @@
         copy.wait()
 
 
-def norm_kernel(part, hops, *refs):
+def norm_kernel(part, hops, first, given, *refs):
     local_ref, decay_ref, c_ref, gain_ref, flag_ref = refs[:5]
     got_refs = refs[5 : 5 + hops]
-    out_hbm_ref, gated_ref, out_ref, sems = refs[-4:]
-    rows, width = gated_ref.shape
-    outputs = c_ref[:, part * STATE : (part + 1) * STATE]
-    squares = jnp.zeros((rows, 128), F32)
-    for start in range(0, width, CHUNK):
-        columns = slice(start, start + CHUNK)
-        placed = slice(part * width + start, part * width + start + CHUNK)
-        state = got_refs[0][:STATE, columns]
-        for hop in range(1, hops):
-            there = flag_ref[hop, 0:1] > 0.5
-            state = jnp.where(there, got_refs[hop][:STATE, columns].astype(F32), state.astype(F32))
-        carried = jnp.dot(outputs, state.astype(BF16), preferred_element_type=F32)
-        gated = local_ref[:, placed] + carried * decay_ref[:, placed]
-        gated_ref[:, columns] = gated
-        for lane in range(0, CHUNK, 128):
-            squares = squares + gated[:, lane : lane + 128] * gated[:, lane : lane + 128]
-    squares = jnp.sum(squares, axis=1, keepdims=True)
-    multiplier = lax.rsqrt(squares * (1.0 / width) + EPSILON)
-    copies = []
-    for start in range(0, width, CHUNK):
-        columns = slice(start, start + CHUNK)
-        gain = gain_ref[part * width + start : part * width + start + CHUNK]
-        out_ref[:, columns] = (gated_ref[:, columns] * multiplier * gain.reshape(1, -1)).astype(BF16)
-        copies.append(
-            pltpu.make_async_copy(
-                out_ref.at[:, pl.ds(start, CHUNK)],
-                out_hbm_ref.at[:, pl.ds(part * width + start, CHUNK)],
-                sems.at[start // CHUNK],
+    out_hbm_ref, *token_refs = refs[5 + hops + given : -3]
+    gated_ref, out_ref, sems = refs[-3:]
+    for ref in token_refs:
+        ref[...] = jnp.zeros_like(ref)
+
+    def work():
+        rows, width = gated_ref.shape
+        outputs = c_ref[:, part * STATE : (part + 1) * STATE]
+        squares = jnp.zeros((rows, 128), F32)
+        for start in range(0, width, CHUNK):
+            columns = slice(start, start + CHUNK)
+            placed = slice(part * width + start, part * width + start + CHUNK)
+            state = got_refs[0][:STATE, columns]
+            for hop in range(1, hops):
+                there = flag_ref[first + hop, 0:1] > 0.5
+                state = jnp.where(there, got_refs[hop][:STATE, columns].astype(F32), state.astype(F32))
+            carried = jnp.dot(outputs, state.astype(BF16), preferred_element_type=F32)
+            gated = local_ref[:, placed] + carried * decay_ref[:, placed]
+            gated_ref[:, columns] = gated
+            for lane in range(0, CHUNK, 128):
+                squares = squares + gated[:, lane : lane + 128] * gated[:, lane : lane + 128]
+        squares = jnp.sum(squares, axis=1, keepdims=True)
+        multiplier = lax.rsqrt(squares * (1.0 / width) + EPSILON)
+        copies = []
+        for start in range(0, width, CHUNK):
+            columns = slice(start, start + CHUNK)
+            gain = gain_ref[part * width + start : part * width + start + CHUNK]
+            out_ref[:, columns] = (gated_ref[:, columns] * multiplier * gain.reshape(1, -1)).astype(BF16)
+            copies.append(
+                pltpu.make_async_copy(
+                    out_ref.at[:, pl.ds(start, CHUNK)],
+                    out_hbm_ref.at[:, pl.ds(part * width + start, CHUNK)],
+                    sems.at[start // CHUNK],
+                )
             )
-        )
-        copies[-1].start()
-    for copy in copies:
-        copy.wait()
+            copies[-1].start()
+        for copy in copies:
+            copy.wait()
+
+    if first:
+        pl.when(jnp.max(flag_ref[first:]) > 0.5)(work)
+    else:
+        work()
 
 
 WHOLE = pl.BlockSpec(memory_space=pltpu.VMEM)
@@ -639,7 +662,6 @@
         [
             shape((rows, width), BF16),
             shape((rows, bc_width), BF16),
-            shape((rows, 2 * keys.shape[1]), BF16),
             shape((8, width + bc_width), F32),
             shape((8, width), F32),
             shape((8, width), F32),
@@ -654,16 +676,18 @@
             shape((rows, width), F32),
             *(shape((STATE, per_group), BF16) for _ in range(groups - 1)),
         ],
-        [x_raw, bc_raw, *params, skip_d, doc_lens, keys, values, z_gate],
-        [WHOLE] * 10 + [SCALARS] + [WHOLE] * 3,
+        [x_raw, bc_raw, *params, skip_d, doc_lens, z_gate],
+        [WHOLE] * 10 + [SCALARS] + [WHOLE],
         scratch=[
             pltpu.VMEM((16, width + bc_width), F32),
             pltpu.VMEM((4, rows + 8, CHUNK), F32),
         ],
     )
-    _, bcc, kv, partial, weight, through, inside, flags, wide_skip, begin, *prepared = prepared
+    _, bcc, partial, weight, through, inside, flags, wide_skip, begin, *prepared = prepared
     step, running, main, gate, decay, *states = prepared
     states = [message, *states]
+    carried = [shape(queries.shape, F32)] * 3 + [shape((rows, 2 * keys.shape[1]), BF16)]
+    *carry, kv = call(own_kernel, "attend_own", carried, [queries, keys, values, begin], [WHOLE] * 4)
     kvs = [kv, onward(kv)]
     fulls = None
     for slot in range(2, hops + groups):
@@ -704,13 +728,39 @@
                 [WHOLE] * (13 + groups),
                 scratch=[pltpu.VMEM((4, 16, CHUNK), F32)],
             )
-    parts = shape(queries.shape, F32)
-    *near, kv_on = call(
+    def norm(part, first, got, out=None, token=False):
+        operands = [gated, decay, c_out, norm_gain, flags, *got]
+        specs = [WHOLE] * len(operands)
+        outs = [shape((rows, width), BF16)] + [shape((8, 128), F32)] * token
+        aliases = {}
+        if out is not None:
+            aliases = {len(operands): 0}
+            operands.append(out)
+            specs.append(UNTOUCHED)
+        return call(
+            functools.partial(norm_kernel, part, len(got), first, out is not None),
+            f"norm_part{part}_{first}",
+            outs,
+            operands,
+            specs,
+            out_specs=[UNTOUCHED] + [WHOLE] * token,
+            scratch=[
+                pltpu.VMEM((rows, per_group), F32),
+                pltpu.VMEM((rows, per_group), BF16),
+                pltpu.SemaphoreType.DMA((per_group // CHUNK,)),
+            ],
+            aliases=aliases,
+        )
+
+    mamba_out, token = None, c_out
+    for part in range(groups - 1):
+        mamba_out, token = norm(part, 0, slots[part : part + 1], mamba_out, True)
+    *carry, kv_on = call(
         near_kernel,
         "attend_near",
-        [parts, parts, parts, shape(kv.shape, BF16)],
-        [queries, kvs[1], kv, begin, c_out],
-        [WHOLE] * 4 + [UNTOUCHED],
+        carried,
+        [queries, kvs[1], begin, *carry, token],
+        [WHOLE] * 6 + [UNTOUCHED],
     )
     for hop in range(1, hops):
         kvs.append(onward(kv_on if hop == 1 else kvs[-1], hop))
@@ -718,7 +768,7 @@
         functools.partial(far_kernel, hops),
         "attend_far",
         [shape(queries.shape, BF16)],
-        [queries, begin, *near, *reversed(kvs[2:])],
+        [queries, begin, *carry, *reversed(kvs[2:])],
         [WHOLE] * (4 + hops),
         out_specs=[UNTOUCHED],
         scratch=[
@@ -726,30 +776,9 @@
             pltpu.SemaphoreType.DMA((keys.shape[1] // ADIM,)),
         ],
     )
-    mamba_out = None
-    for part in range(groups):
-        got = slots[-1:] if part == groups - 1 else slots[part : part + hops]
-        operands = [gated, decay, c_out, norm_gain, flags, *got]
-        specs = [WHOLE] * (5 + len(got))
-        aliases = {}
-        if mamba_out is not None:
-            operands.append(mamba_out)
-            specs.append(UNTOUCHED)
-            aliases = {len(operands) - 1: 0}
-        (mamba_out,) = call(
-            functools.partial(norm_kernel, part, len(got)),
-            f"norm_part{part}",
-            [shape((rows, width), BF16)],
-            operands,
-            specs,
-            out_specs=[UNTOUCHED],
-            scratch=[
-                pltpu.VMEM((rows, per_group), F32),
-                pltpu.VMEM((rows, per_group), BF16),
-                pltpu.SemaphoreType.DMA((per_group // CHUNK,)),
-            ],
-            aliases=aliases,
-        )
+    for part in range(groups - 1):
+        (mamba_out,) = norm(part, 1, slots[part + 1 : part + hops], mamba_out)
+    (mamba_out,) = norm(groups - 1, 0, slots[-1:], mamba_out)
     return (mamba_out, attn_out)
 
 

time: 35.2 us -> 35.4 us (level)
  Pallas kernels: 12.1 us -> 14.3 us
  starting transfers between devices: 16.1 us -> 14.9 us
  waiting for transfers between devices: 5.35 us -> 4.83 us
    pallas_call x9 -> x11, Pallas kernels: 12.1 us -> 14.3 us  [call(): pl.pallas_call(kernel, name=name, grid=(1,), out_shape=outs, in_specs=spe...]
    ppermute x5, starting transfers between devices: 16.1 us -> 14.9 us  [onward(): lax.ppermute(value, 'seq', [(source, source + 1) for source in range(firs...]
    ppermute x5, waiting for transfers between devices: 5.35 us -> 4.83 us  [onward(): lax.ppermute(value, 'seq', [(source, source + 1) for source in range(firs...]
  transfers between devices with their start and end apart: 5 -> 5, of which waited for: 4 -> 4; matrix products, arithmetic and copies ran while one was open for 0% -> 0% of each run, Pallas kernels for 24% -> 30%
where the time goes in v11:
time: 35.4 us; the launch traced here: 35 us
  starting transfers between devices  14.9 us (42%)
  Pallas kernels  14.3 us (40%)
  waiting for transfers between devices  4.83 us (14%)
  between operations  0.97 us (3%)
    ppermute x5, starting transfers between devices, onward(): lax.ppermute(value, 'seq', [(source, source + 1) for source in range(firs...  14.9 us
    pallas_call x11, Pallas kernels, call(): pl.pallas_call(kernel, name=name, grid=(1,), out_shape=outs, in_specs=spe...  14.3 us
    ppermute x5, waiting for transfers between devices, onward(): lax.ppermute(value, 'seq', [(source, source + 1) for source in range(firs...  4.83 us
  transfers between devices with their start and end apart: 5, of which 4 were waited for; matrix products, arithmetic and copies ran while one was open for 0% of the time, Pallas kernels for 30%

profile of v11, /device:TPU:22, one launch (start us, length us, event | category | flops | bytes accessed | tf_op | source)
XLA Modules:
  0.0 35.0 jit_solution(7601280728240677348)
XLA Ops:
  0.6 0.0 copy-start
  0.6 0.0 copy-start.1
  0.7 0.0 copy-start.4
  0.7 0.0 copy-start.7
  0.7 0.0 copy-start.8
  0.7 0.0 copy-start.9
  0.8 2.9 %first_state.1.refs_13_.refs_1_ = bf16[144,1024]{1,0:T(8,128)(2,1)} custom-call(bf16[128,2048]{1,0:T(8,128)(2,1)} %refs_0_.4, bf16[128,512]{1,0:T(8,128)(2,1)} %refs_1_.3, f32[32,128]{1,0:T(8,128)} %bitcast.5, f32[4,2048]{1,0:T(4,128)} %refs_7_.3, f32[1,2048]{1,0:T(1,128)} %bitcast.7, f32[4,512]{1,0:T(4,128)} %refs_8_.3, f32[1,512]{1,0:T(1,128)} %bitcast.8, ...), custom_call_target="tpu_custom_call" | custom-call | flops 2000000000 | bytes 1018128 | tf_op jit(solution)/shard_map/first_state/pallas_call | solution.py:578
  3.7 0.0 copy-start.3
  3.7 0.0 copy-start.5
  3.7 0.0 copy-start.6
  3.7 3.6 %collective-permute-start = (bf16[144,1024]{1,0:T(8,128)(2,1)}, bf16[144,1024]{1,0:T(8,128)(2,1)S(1)}, u32[]{:S(2)}, u32[]{:S(2)}) collective-permute-start(bf16[144,1024]{1,0:T(8,128)(2,1)} %first_state.1.refs_13_.refs_1_), channel_id=1, source_target_pairs={{0,4},{4,8},{8,12},{1,5},{5,9},{9,13},{2,6},{6,10},{10,14},{3,7},{... | collective-permute-start | bytes 884744 | tf_op jit(solution)/shard_map/ppermute | solution.py:594
  7.4 3.6 %prepare.1 = (bf16[128,2048]{1,0:T(8,128)(2,1)}, bf16[128,512]{1,0:T(8,128)(2,1)S(1)}, f32[8,2560]{1,0:T(8,128)S(1)}, f32[8,2048]{1,0:T(8,128)S(1)}, f32[8,2048]...) custom-call(bf16[128,2048]{1,0:T(8,128)(2,1)S(1)} %copy-done, ...), custom_call_target="tpu_custom_call" | custom-call | flops 2000000000 | bytes 5728656 | tf_op jit(solution)/shard_map/prepare/pallas_call | solution.py:578
  11.1 0.8 %attend_own.1 = (f32[128,1024]{1,0:T(8,128)S(1)}, f32[128,1024]{1,0:T(8,128)S(1)}, f32[128,1024]{1,0:T(8,128)S(1)}, bf16[128,512]{1,0:T(8,128)(2,1)S(1)}) custom-call(bf16[128,1024]{1,0:T(8,128)(2,1)S(1)} %copy-done.3, bf16[128,256]{1,0:T(8,128)(2,1)S(1)} %copy-done.5, bf16[128,256]{1,0:T(8,128)(2,1)S(1)} %copy-done.6, ...), custom_call_target="tpu_custom_call" | custom-call | flops 2000000000 | bytes 2162688 | tf_op jit(solution)/shard_map/attend_own/pallas_call | solution.py:578
  11.8 1.9 %collective-permute-start.3 = (bf16[128,512]{1,0:T(8,128)(2,1)S(1)}, bf16[128,512]{1,0:T(8,128)(2,1)S(1)}, u32[]{:S(2)}, u32[]{:S(2)}) collective-permute-start(bf16[128,512]{1,0:T(8,128)(2,1)S(1)} %get-tuple-element.47), channel_id=1, source_target_pairs={{0,4},{4,8},{8,12},{1,5},{5,9},{9,13},{2,6},{6,10},{10,14},{3,7},{... | collective-permute-start | bytes 393224 | tf_op jit(solution)/shard_map/ppermute | solution.py:594
  13.8 0.9 %collective-permute-done.refs_0_.refs_5_ = bf16[144,1024]{1,0:T(8,128)(2,1)S(1)} collective-permute-done((bf16[144,1024]{1,0:T(8,128)(2,1)}, bf16[144,1024]{1,0:T(8,128)(2,1)S(1)}, u32[]{:S(2)}, u32[]{:S(2)}) %collective-permute-start) | collective-permute-done | bytes 294944 | tf_op jit(solution)/shard_map/ppermute | solution.py:594
  14.7 0.0 copy-done.2
  14.7 0.3 relay_slot2.1
  15.0 3.5 %collective-permute-start.1 = (bf16[128,1024]{1,0:T(8,128)(2,1)S(1)}, bf16[128,1024]{1,0:T(8,128)(2,1)S(1)}, u32[]{:S(2)}, u32[]{:S(2)}) collective-permute-start(bf16[128,1024]{1,0:T(8,128)(2,1)S(1)} %relay_slot2.1), channel_id=1, source_target_pairs={{0,4},{4,8},{8,12},{1,5},{5,9},{9,13},{2,6},{6,10},{10,14},{3,7},{... | collective-permute-start | bytes 786440 | tf_op jit(solution)/shard_map/ppermute | solution.py:594
  18.5 0.0 copy-start.11
  18.5 1.1 %first_rows.1 = (f32[128,2048]{1,0:T(8,128)S(1)}, bf16[128,256]{1,0:T(8,128)(2,1)S(1)}, bf16[128,1024]{1,0:T(8,128)(2,1)}, bf16[128,1024]{1,0:T(8,128)(2,1)S(1)}) custom-call(bf16[144,1024]{1,0:T(8,128)(2,1)S(1)} %collective-permute-done.refs_0_.refs_5_, f32[8,2560]{1,0:T(8,128)S(1)} %get-tuple-element.29.refs_1_.refs_2_, ...), custom_call_target="tpu_custom_call" | custom-call | flops 2000000000 | bytes 5095424 | tf_op jit(solution)/shard_map/first_rows/pallas_call | solution.py:578
  19.6 1.0 %norm_part0_0.1 = (bf16[128,2048]{1,0:T(8,128)(2,1)}, f32[8,128]{1,0:T(8,128)S(1)}) custom-call(f32[128,2048]{1,0:T(8,128)S(1)} %get-tuple-element.40.refs_0_, f32[128,2048]{1,0:T(8,128)S(1)} %get-tuple-element.41.refs_1_, bf16[128,256]{1,0:T(8,128)(2,1)S(1)} %get-tuple-element.42.refs_2_, f32[2048]{0:T(1024)S(1)} %copy-done.11, ...), custom_call_target="tpu_custom_call" | custom-call | flops 2000000000 | bytes 3010560 | tf_op jit(solution)/shard_map/norm_part0_0/pallas_call | solution.py:578
  20.7 0.0 collective-permute-done.3.before_ref
  20.7 0.8 %attend_near.1 = (f32[128,1024]{1,0:T(8,128)S(1)}, f32[128,1024]{1,0:T(8,128)S(1)}, f32[128,1024]{1,0:T(8,128)S(1)}, bf16[128,512]{1,0:T(8,128)(2,1)S(1)}) custom-call(bf16[128,1024]{1,0:T(8,128)(2,1)S(1)} %copy-done.3, bf16[128,512]{1,0:T(8,128)(2,1)S(1)} %collective-permute-done.3.before_ref, s32[128,128]{1,0:T(8,128)S(1)} %get-tuple-element.35.refs_9_.begin_ref.refs_1_, ...), custom_call_target="tpu_custom_call" | custom-call | flops 2000000000 | bytes 3739648 | tf_op jit(solution)/shard_map/attend_near/pallas_call | solution.py:578
  21.5 1.9 %collective-permute-start.4 = (bf16[128,512]{1,0:T(8,128)(2,1)S(1)}, bf16[128,512]{1,0:T(8,128)(2,1)S(1)}, u32[]{:S(2)}, u32[]{:S(2)}) collective-permute-start(bf16[128,512]{1,0:T(8,128)(2,1)S(1)} %get-tuple-element.55), channel_id=1, source_target_pairs={{4,8},{8,12},{5,9},{9,13},{6,10},{10,14},{7,11},{11,15},{20,24},{2... | collective-permute-start | bytes 393224 | tf_op jit(solution)/shard_map/ppermute | solution.py:594
  23.4 0.9 %collective-permute-done.1.refs_0_.refs_5_ = bf16[128,1024]{1,0:T(8,128)(2,1)S(1)} collective-permute-done((bf16[128,1024]{1,0:T(8,128)(2,1)S(1)}, bf16[128,1024]{1,0:T(8,128)(2,1)S(1)}, u32[]{:S(2)}, u32[]{:S(2)}) %collective-permute-start.1) | collective-permute-done | bytes 262176 | tf_op jit(solution)/shard_map/ppermute | solution.py:594
  24.3 0.1 relay_slot3.1
  24.4 3.9 %collective-permute-start.2 = (bf16[128,1024]{1,0:T(8,128)(2,1)S(1)}, bf16[128,1024]{1,0:T(8,128)(2,1)S(1)}, u32[]{:S(2)}, u32[]{:S(2)}) collective-permute-start(bf16[128,1024]{1,0:T(8,128)(2,1)S(1)} %relay_slot3.1), channel_id=1, source_target_pairs={{0,4},{4,8},{8,12},{1,5},{5,9},{9,13},{2,6},{6,10},{10,14},{3,7},{... | collective-permute-start | bytes 786440 | tf_op jit(solution)/shard_map/ppermute | solution.py:594
  28.3 1.2 %collective-permute-done.4.refs_5_ = bf16[128,512]{1,0:T(8,128)(2,1)S(1)} collective-permute-done((bf16[128,512]{1,0:T(8,128)(2,1)S(1)}, bf16[128,512]{1,0:T(8,128)(2,1)S(1)}, u32[]{:S(2)}, u32[]{:S(2)}) %collective-permute-start.4) | collective-permute-done | bytes 131104 | tf_op jit(solution)/shard_map/ppermute | solution.py:594
  29.5 1.5 %attend_far.1 = bf16[128,1024]{1,0:T(8,128)(2,1)} custom-call(bf16[128,1024]{1,0:T(8,128)(2,1)S(1)} %copy-done.3, s32[128,128]{1,0:T(8,128)S(1)} %get-tuple-element.35.refs_9_.begin_ref.refs_1_, f32[128,1024]{1,0:T(8,128)S(1)} %get-tuple-element.52.refs_2_, f32[128,1024]{1,0:T(8,128)S(1)} %get-tuple-element.53.refs_3_, ...), custom_call_target="tpu_custom_call" | custom-call | flops 2000000000 | bytes 2293760 | tf_op jit(solution)/shard_map/attend_far/pallas_call | solution.py:578
  31.0 1.2 %norm_part0_1.1.refs_6_ = bf16[128,2048]{1,0:T(8,128)(2,1)} custom-call(f32[128,2048]{1,0:T(8,128)S(1)} %get-tuple-element.40.refs_0_, f32[128,2048]{1,0:T(8,128)S(1)} %get-tuple-element.41.refs_1_, bf16[128,256]{1,0:T(8,128)(2,1)S(1)} %get-tuple-element.42.refs_2_, f32[2048]{0:T(1024)S(1)} %copy-done.11, ...), custom_call_target="tpu_custom_call", output_to_operand_aliasing={{}: (6, {})} | custom-call | flops 2000000000 | bytes 3497984 | tf_op jit(solution)/shard_map/norm_part0_1/pallas_call | solution.py:578
  32.2 1.8 %collective-permute-done.2.refs_5_ = bf16[128,1024]{1,0:T(8,128)(2,1)S(1)} collective-permute-done((bf16[128,1024]{1,0:T(8,128)(2,1)S(1)}, bf16[128,1024]{1,0:T(8,128)(2,1)S(1)}, u32[]{:S(2)}, u32[]{:S(2)}) %collective-permute-start.2) | collective-permute-done | bytes 262176 | tf_op jit(solution)/shard_map/ppermute | solution.py:594
  34.0 1.0 %norm_part1_0.1 = bf16[128,2048]{1,0:T(8,128)(2,1)} custom-call(f32[128,2048]{1,0:T(8,128)S(1)} %get-tuple-element.40.refs_0_, f32[128,2048]{1,0:T(8,128)S(1)} %get-tuple-element.41.refs_1_, bf16[128,256]{1,0:T(8,128)(2,1)S(1)} %get-tuple-element.42.refs_2_, f32[2048]{0:T(1024)S(1)} %copy-done.11, ...), custom_call_target="tpu_custom_call", output_to_operand_aliasing={{}: (6, {})} | custom-call | flops 2000000000 | bytes 3497984 | tf_op jit(solution)/shard_map/norm_part1_0/pallas_call | solution.py:578
  (23 shorter events, 0.0 us)
Async XLA Ops:
  0.6 6.7 %copy-start = (bf16[128,2048]{1,0:T(8,128)(2,1)S(1)}, bf16[128,2048]{1,0:T(8,128)(2,1)}, u32[]{:S(2)}) copy-start(bf16[128,2048]{1,0:T(8,128)(2,1)} %refs_0_.4) | copy-start | bytes 1572868
  0.6 6.7 %copy-start.1 = (bf16[128,2048]{1,0:T(8,128)(2,1)S(1)}, bf16[128,2048]{1,0:T(8,128)(2,1)}, u32[]{:S(2)}) copy-start(bf16[128,2048]{1,0:T(8,128)(2,1)} %refs_11_.1) | copy-start | bytes 1572868
  0.7 6.7 %copy-start.4 = (bf16[128,512]{1,0:T(8,128)(2,1)S(1)}, bf16[128,512]{1,0:T(8,128)(2,1)}, u32[]{:S(2)}) copy-start(bf16[128,512]{1,0:T(8,128)(2,1)} %refs_1_.3) | copy-start | bytes 393220
  0.7 6.7 %copy-start.7 = (f32[4,2048]{1,0:T(4,128)S(1)}, f32[4,2048]{1,0:T(4,128)}, u32[]{:S(2)}) copy-start(f32[4,2048]{1,0:T(4,128)} %refs_7_.3) | copy-start | bytes 98308
  0.7 6.7 %copy-start.8 = (f32[128,32]{0,1:T(8,128)S(1)}, f32[128,32]{0,1:T(8,128)}, u32[]{:S(2)}) copy-start(f32[128,32]{0,1:T(8,128)} %param.19) | copy-start | bytes 49156
  0.7 6.7 %copy-start.9 = (f32[2048]{0:T(1024)S(1)}, f32[2048]{0:T(1024)}, u32[]{:S(2)}) copy-start(f32[2048]{0:T(1024)} %refs_4_.2) | copy-start | bytes 24580
  0.7 6.7 %copy-start.10 = (f32[4,512]{1,0:T(4,128)S(1)}, f32[4,512]{1,0:T(4,128)}, u32[]{:S(2)}) copy-start(f32[4,512]{1,0:T(4,128)} %refs_8_.3) | copy-start | bytes 24580
  0.7 6.7 %copy-start.12 = (f32[512]{0:T(512)S(1)}, f32[512]{0:T(512)}, u32[]{:S(2)}) copy-start(f32[512]{0:T(512)} %refs_6_.1) | copy-start | bytes 6148
  0.7 6.7 %copy-start.13 = (f32[32]{0:T(128)S(1)}, f32[32]{0:T(128)}, u32[]{:S(2)}) copy-start(f32[32]{0:T(128)} %refs_7_.2) | copy-start | bytes 388
  0.7 6.7 %copy-start.14 = (f32[32]{0:T(128)S(1)}, f32[32]{0:T(128)}, u32[]{:S(2)}) copy-start(f32[32]{0:T(128)} %refs_8_.2) | copy-start | bytes 388
  0.7 6.7 %copy-start.15 = (s32[4]{0:T(128)S(1)}, s32[4]{0:T(128)}, u32[]{:S(2)}) copy-start(s32[4]{0:T(128)} %refs_10_.1) | copy-start | bytes 52
  0.7 6.7 %copy-start.16 = (f32[32]{0:T(128)S(1)}, f32[32]{0:T(128)}, u32[]{:S(2)}) copy-start(f32[32]{0:T(128)} %refs_9_.3) | copy-start | bytes 388
  3.7 7.4 %copy-start.3 = (bf16[128,1024]{1,0:T(8,128)(2,1)S(1)}, bf16[128,1024]{1,0:T(8,128)(2,1)}, u32[]{:S(2)}) copy-start(bf16[128,1024]{1,0:T(8,128)(2,1)} %refs_0_.5) | copy-start | bytes 786436
  3.7 7.4 %copy-start.5 = (bf16[128,256]{1,0:T(8,128)(2,1)S(1)}, bf16[128,256]{1,0:T(8,128)(2,1)}, u32[]{:S(2)}) copy-start(bf16[128,256]{1,0:T(8,128)(2,1)} %keys_ref.1) | copy-start | bytes 196612
  3.7 7.4 %copy-start.6 = (bf16[128,256]{1,0:T(8,128)(2,1)S(1)}, bf16[128,256]{1,0:T(8,128)(2,1)}, u32[]{:S(2)}) copy-start(bf16[128,256]{1,0:T(8,128)(2,1)} %values_ref.1) | copy-start | bytes 196612
  3.7 11.0 %collective-permute-start = (bf16[144,1024]{1,0:T(8,128)(2,1)}, bf16[144,1024]{1,0:T(8,128)(2,1)S(1)}, u32[]{:S(2)}, u32[]{:S(2)}) collective-permute-start(bf16[144,1024]{1,0:T(8,128)(2,1)} %first_state.1.refs_13_.refs_1_), channel_id=1, source_target_pairs={{0,4},{4,8},{8,12},{1,5},{5,9},{9,13},{2,6},{6,10},{10,14},{3,7},{... | collective-permute-start | bytes 884744 | tf_op jit(solution)/shard_map/ppermute | solution.py:594
  11.0 3.6 %copy-start.2 = (bf16[144,1024]{1,0:T(8,128)(2,1)S(1)}, bf16[144,1024]{1,0:T(8,128)(2,1)}, u32[]{:S(2)}) copy-start(bf16[144,1024]{1,0:T(8,128)(2,1)} %first_state.1.refs_13_.refs_1_) | copy-start | bytes 884740
  11.8 8.9 %collective-permute-start.3 = (bf16[128,512]{1,0:T(8,128)(2,1)S(1)}, bf16[128,512]{1,0:T(8,128)(2,1)S(1)}, u32[]{:S(2)}, u32[]{:S(2)}) collective-permute-start(bf16[128,512]{1,0:T(8,128)(2,1)S(1)} %get-tuple-element.47), channel_id=1, source_target_pairs={{0,4},{4,8},{8,12},{1,5},{5,9},{9,13},{2,6},{6,10},{10,14},{3,7},{... | collective-permute-start | bytes 393224 | tf_op jit(solution)/shard_map/ppermute | solution.py:594
  15.0 9.3 %collective-permute-start.1 = (bf16[128,1024]{1,0:T(8,128)(2,1)S(1)}, bf16[128,1024]{1,0:T(8,128)(2,1)S(1)}, u32[]{:S(2)}, u32[]{:S(2)}) collective-permute-start(bf16[128,1024]{1,0:T(8,128)(2,1)S(1)} %relay_slot2.1), channel_id=1, source_target_pairs={{0,4},{4,8},{8,12},{1,5},{5,9},{9,13},{2,6},{6,10},{10,14},{3,7},{... | collective-permute-start | bytes 786440 | tf_op jit(solution)/shard_map/ppermute | solution.py:594
  18.5 1.1 %copy-start.11 = (f32[2048]{0:T(1024)S(1)}, f32[2048]{0:T(1024)}, u32[]{:S(2)}) copy-start(f32[2048]{0:T(1024)} %refs_3_.9) | copy-start | bytes 24580
  21.5 8.1 %collective-permute-start.4 = (bf16[128,512]{1,0:T(8,128)(2,1)S(1)}, bf16[128,512]{1,0:T(8,128)(2,1)S(1)}, u32[]{:S(2)}, u32[]{:S(2)}) collective-permute-start(bf16[128,512]{1,0:T(8,128)(2,1)S(1)} %get-tuple-element.55), channel_id=1, source_target_pairs={{4,8},{8,12},{5,9},{9,13},{6,10},{10,14},{7,11},{11,15},{20,24},{2... | collective-permute-start | bytes 393224 | tf_op jit(solution)/shard_map/ppermute | solution.py:594
  24.4 9.6 %collective-permute-start.2 = (bf16[128,1024]{1,0:T(8,128)(2,1)S(1)}, bf16[128,1024]{1,0:T(8,128)(2,1)S(1)}, u32[]{:S(2)}, u32[]{:S(2)}) collective-permute-start(bf16[128,1024]{1,0:T(8,128)(2,1)S(1)} %relay_slot3.1), channel_id=1, source_target_pairs={{0,4},{4,8},{8,12},{1,5},{5,9},{9,13},{2,6},{6,10},{10,14},{3,7},{... | collective-permute-start | bytes 786440 | tf_op jit(solution)/shard_map/ppermute | solution.py:594

commit v12 on v10

--- a/solution.py
+++ b/solution.py
@@ -85,7 +85,7 @@
     for lag in range(1, taps):
         term = pad[8 - lag : 8 - lag + rows] * weight[taps - 1 - lag : taps - lag]
         total = total + jnp.where(inside[lag], term, 0.0)
-    return silu(total).astype(BF16)
+    return silu(total)
 
 
 def tail_lines(message, rows):
@@ -146,7 +146,7 @@
     for at in (1, 5, 6):
         copies[at].wait()
     inputs = conv_rows(b_pad_ref, b_ref[...], wbc_ref[...], bbc_ref[...], narrow)
-    turned = inputs.astype(F32).T.astype(BF16)
+    turned = inputs.T.astype(BF16)
     for at in (0, 3, 4):
         copies[at].wait()
     slots = pad_ref.shape[0]
@@ -161,7 +161,7 @@
         columns = slice(start, start + CHUNK)
         pad = pad_ref.at[(at + 1) % slots]
         xc = conv_rows(pad, x_ref[:, columns], wx_ref[:, columns], bx_ref[:, columns], inside)
-        weighted = (xc.astype(F32) * widen(weight, start, CHUNK)).astype(BF16)
+        weighted = (xc * widen(weight, start, CHUNK)).astype(BF16)
         out_ref[:STATE, columns] = jnp.dot(turned, weighted, preferred_element_type=F32).astype(BF16)
         if at % 2:
             send(at // 2, (pl.ds(0, STATE), pl.ds(start - CHUNK, 2 * CHUNK)))
@@ -182,10 +182,10 @@
 
 def prepare_kernel(hops, groups, *refs):
     x_ref, bc_ref, dt_ref, wx_ref, bx_ref, wbc_ref, bbc_ref, dt_bias_ref, a_log_ref, skip_ref, lens_ref = refs[:11]
-    keys_ref, values_ref, z_ref = refs[11:14]
-    xc_ref, bcc_ref, kv_ref, partial_ref, weight_ref, through_ref, inside_ref, flag_ref = refs[14:22]
-    wide_skip_ref, begin_ref, step_ref, running_ref, out_ref, gate_ref, decay_ref = refs[22:29]
-    state_refs = refs[29:-2]
+    z_ref = refs[11]
+    xc_ref, bcc_ref, partial_ref, weight_ref, through_ref, inside_ref, flag_ref = refs[12:19]
+    wide_skip_ref, begin_ref, step_ref, running_ref, out_ref, gate_ref, decay_ref = refs[19:26]
+    state_refs = refs[26:-2]
     top_ref, pad_ref = refs[-2:]
     rows, width = x_ref.shape
     per_group = width // groups
@@ -193,9 +193,6 @@
     slots = pad_ref.shape[0]
     here = lax.axis_index("seq")
     first = here * rows
-    kv_width = keys_ref.shape[1]
-    kv_ref[:, :kv_width] = keys_ref[...]
-    kv_ref[:, kv_width:] = values_ref[...]
     inside = insides(first, (rows, CHUNK), taps, lens_ref)
     step, running = rates(dt_ref, dt_bias_ref, a_log_ref)
     heads = step.shape[1]
@@ -204,16 +201,16 @@
     for group in range(groups):
         base = slice(group * 2 * STATE, (group + 1) * 2 * STATE)
         pair = conv_rows(pad_ref.at[0], bc_ref[:, base], wbc_ref[:, base], bbc_ref[base], inside)
-        bcc_ref[:, base] = pair
-        turned = pair[:, :STATE].astype(F32).T.astype(BF16)
+        bcc_ref[:, base] = pair.astype(BF16)
+        turned = pair[:, :STATE].T.astype(BF16)
         part_weight = kept[:, group * group_heads : (group + 1) * group_heads]
         for chunk in range(0, per_group, CHUNK):
             columns = slice(group * per_group + chunk, group * per_group + chunk + CHUNK)
             pad = pad_ref.at[(chunk // CHUNK + 1) % slots]
             xc = conv_rows(pad, x_ref[:, columns], wx_ref[:, columns], bx_ref[columns], inside)
-            xc_ref[:, columns] = xc
+            xc_ref[:, columns] = xc.astype(BF16)
             if group:
-                weighted = (xc.astype(F32) * widen(part_weight, chunk, CHUNK)).astype(BF16)
+                weighted = (xc * widen(part_weight, chunk, CHUNK)).astype(BF16)
                 state_refs[group - 1][:, chunk : chunk + CHUNK] = jnp.dot(
                     turned, weighted, preferred_element_type=F32
                 ).astype(BF16)
@@ -453,45 +450,61 @@
     count: int
 
 
-def near_kernel(*refs):
-    q_ref, before_ref, own_ref, begin_ref, _, sum_ref, total_ref, peak_ref, kv_ref = refs
-    kv_ref[...] = before_ref[...]
+def fold(q_ref, kv_refs, begin_ref, blocks, share, head, carry):
+    lows = [(head * share + part) * ADIM for part in range(share)]
+    scores, values = attend(q_ref, kv_refs, begin_ref, blocks, share, head)
+    peak = jnp.max(scores, axis=1, keepdims=True)
+    peak = jnp.broadcast_to(peak, (peak.shape[0], ADIM))
+    if carry is not None:
+        sums, totals, before = (
+            jnp.concatenate([ref[:, low : low + ADIM] for low in lows], axis=0) for ref in carry
+        )
+        peak = jnp.maximum(peak, before)
+    expo = jnp.exp(scores - jnp.concatenate([peak] * (scores.shape[1] // ADIM), axis=1))
+    summed = jnp.dot(expo.astype(BF16), values, preferred_element_type=F32)
+    if carry is None:
+        return lows, summed[:, :ADIM], summed[:, ADIM:], peak
+    factor = jnp.exp(before - peak)
+    return lows, sums * factor + summed[:, :ADIM], totals * factor + summed[:, ADIM:], peak
+
+
+def own_kernel(q_ref, keys_ref, values_ref, begin_ref, *outs):
+    kv_ref = outs[3]
+    kv_width = keys_ref.shape[1]
+    kv_ref[:, :kv_width] = keys_ref[...]
+    kv_ref[:, kv_width:] = values_ref[...]
     rows = q_ref.shape[0]
     share = QHEADS // KVHEADS
-    for head in range(own_ref.shape[1] // (2 * ADIM)):
-        scores, values = attend(q_ref, (before_ref, own_ref), begin_ref, Blocks(1, 2), share, head)
-        peak = jnp.max(scores, axis=1, keepdims=True)
-        summed = jnp.dot(jnp.exp(scores - peak).astype(BF16), values, preferred_element_type=F32)
-        peak = jnp.broadcast_to(peak, (peak.shape[0], ADIM))
-        for part in range(share):
-            low = (head * share + part) * ADIM
-            these = slice(part * rows, (part + 1) * rows)
-            sum_ref[:, low : low + ADIM] = summed[these, :ADIM]
-            total_ref[:, low : low + ADIM] = summed[these, ADIM:]
-            peak_ref[:, low : low + ADIM] = peak[these]
+    for head in range(kv_width // ADIM):
+        lows, *results = fold(q_ref, (kv_ref,), begin_ref, Blocks(0, 1), share, head, None)
+        for ref, result in zip(outs, results):
+            for part, low in enumerate(lows):
+                ref[:, low : low + ADIM] = result[part * rows : (part + 1) * rows]
+
+
+def near_kernel(q_ref, before_ref, begin_ref, *refs):
+    carry, outs = refs[:3], refs[4:]
+    outs[3][...] = before_ref[...]
+    rows = q_ref.shape[0]
+    share = QHEADS // KVHEADS
+    for head in range(before_ref.shape[1] // (2 * ADIM)):
+        lows, *results = fold(q_ref, (before_ref,), begin_ref, Blocks(1, 1), share, head, carry)
+        for ref, result in zip(outs, results):
+            for part, low in enumerate(lows):
+                ref[:, low : low + ADIM] = result[part * rows : (part + 1) * rows]
 
 
 def far_kernel(hops, *refs):
-    q_ref, begin_ref, sum_ref, total_ref, peak_ref = refs[:5]
+    q_ref, begin_ref = refs[:2]
     kv_refs = refs[5 : 4 + hops]
     out_hbm_ref, out_ref, sems = refs[4 + hops :]
     rows = q_ref.shape[0]
     share = QHEADS // KVHEADS
     copies = []
     for head in range(kv_refs[0].shape[1] // (2 * ADIM)):
-        lows = [(head * share + part) * ADIM for part in range(share)]
-
-        def stacked(ref):
-            return jnp.concatenate([ref[:, low : low + ADIM] for low in lows], axis=0)
-
-        scores, values = attend(q_ref, kv_refs, begin_ref, Blocks(hops, hops - 1), share, head)
-        near = stacked(peak_ref)
-        peak = jnp.maximum(near, jnp.max(scores, axis=1, keepdims=True))
-        expo = jnp.exp(scores - jnp.concatenate([peak] * (scores.shape[1] // ADIM), axis=1))
-        summed = jnp.dot(expo.astype(BF16), values, preferred_element_type=F32)
-        factor = jnp.exp(near - peak)
-        total = stacked(total_ref) * factor + summed[:, ADIM:]
-        result = ((stacked(sum_ref) * factor + summed[:, :ADIM]) / total).astype(BF16)
+        blocks = Blocks(hops, hops - 1)
+        lows, sums, totals, _ = fold(q_ref, kv_refs, begin_ref, blocks, share, head, refs[2:5])
+        result = (sums / totals).astype(BF16)
         for part, low in enumerate(lows):
             out_ref[:, low : low + ADIM] = result[part * rows : (part + 1) * rows]
         columns = pl.ds(head * share * ADIM, share * ADIM)
@@ -639,7 +652,6 @@
         [
             shape((rows, width), BF16),
             shape((rows, bc_width), BF16),
-            shape((rows, 2 * keys.shape[1]), BF16),
             shape((8, width + bc_width), F32),
             shape((8, width), F32),
             shape((8, width), F32),
@@ -654,16 +666,18 @@
             shape((rows, width), F32),
             *(shape((STATE, per_group), BF16) for _ in range(groups - 1)),
         ],
-        [x_raw, bc_raw, *params, skip_d, doc_lens, keys, values, z_gate],
-        [WHOLE] * 10 + [SCALARS] + [WHOLE] * 3,
+        [x_raw, bc_raw, *params, skip_d, doc_lens, z_gate],
+        [WHOLE] * 10 + [SCALARS] + [WHOLE],
         scratch=[
             pltpu.VMEM((16, width + bc_width), F32),
             pltpu.VMEM((4, rows + 8, CHUNK), F32),
         ],
     )
-    _, bcc, kv, partial, weight, through, inside, flags, wide_skip, begin, *prepared = prepared
+    _, bcc, partial, weight, through, inside, flags, wide_skip, begin, *prepared = prepared
     step, running, main, gate, decay, *states = prepared
     states = [message, *states]
+    carried = [shape(queries.shape, F32)] * 3 + [shape((rows, 2 * keys.shape[1]), BF16)]
+    *carry, kv = call(own_kernel, "attend_own", carried, [queries, keys, values, begin], [WHOLE] * 4)
     kvs = [kv, onward(kv)]
     fulls = None
     for slot in range(2, hops + groups):
@@ -704,13 +718,12 @@
                 [WHOLE] * (13 + groups),
                 scratch=[pltpu.VMEM((4, 16, CHUNK), F32)],
             )
-    parts = shape(queries.shape, F32)
-    *near, kv_on = call(
+    *carry, kv_on = call(
         near_kernel,
         "attend_near",
-        [parts, parts, parts, shape(kv.shape, BF16)],
-        [queries, kvs[1], kv, begin, c_out],
-        [WHOLE] * 4 + [UNTOUCHED],
+        carried,
+        [queries, kvs[1], begin, *carry, c_out],
+        [WHOLE] * 6 + [UNTOUCHED],
     )
     for hop in range(1, hops):
         kvs.append(onward(kv_on if hop == 1 else kvs[-1], hop))
@@ -718,7 +731,7 @@
         functools.partial(far_kernel, hops),
         "attend_far",
         [shape(queries.shape, BF16)],
-        [queries, begin, *near, *reversed(kvs[2:])],
+        [queries, begin, *carry, *reversed(kvs[2:])],
         [WHOLE] * (4 + hops),
         out_specs=[UNTOUCHED],
         scratch=[

time: 35.2 us -> 35.3 us (level)
  the two profiles are of different devices: /device:TPU:22 before, /device:TPU:0 now
where the time goes in v12:
time: 35.3 us; the launch traced here: 35.1 us
  starting transfers between devices  17.1 us (48%)
  Pallas kernels  13 us (37%)
  waiting for transfers between devices  3.91 us (11%)
  between operations  0.99 us (3%)
    ppermute x5, starting transfers between devices, onward(): lax.ppermute(value, 'seq', [(source, source + 1) for source in range(firs...  17.1 us
    pallas_call x10, Pallas kernels, call(): pl.pallas_call(kernel, name=name, grid=(1,), out_shape=outs, in_specs=spe...  13 us
    ppermute x5, waiting for transfers between devices, onward(): lax.ppermute(value, 'seq', [(source, source + 1) for source in range(firs...  3.91 us
  transfers between devices with their start and end apart: 5, of which 2 were waited for; matrix products, arithmetic and copies ran while one was open for 0% of the time, Pallas kernels for 26%

profile of v12, /device:TPU:0, one launch (start us, length us, event | category | flops | bytes accessed | tf_op | source)
XLA Modules:
  0.0 35.1 jit_solution(16587136043369520522)
XLA Ops:
  0.6 0.0 copy-start
  0.6 0.0 copy-start.1
  0.7 0.0 copy-start.4
  0.7 0.0 copy-start.7
  0.7 0.0 copy-start.8
  0.8 2.8 %first_state.1.refs_13_.refs_1_ = bf16[144,1024]{1,0:T(8,128)(2,1)} custom-call(bf16[128,2048]{1,0:T(8,128)(2,1)} %refs_0_.4, bf16[128,512]{1,0:T(8,128)(2,1)} %refs_1_.3, f32[32,128]{1,0:T(8,128)} %bitcast.5, f32[4,2048]{1,0:T(4,128)} %refs_7_.3, f32[1,2048]{1,0:T(1,128)} %bitcast.7, f32[4,512]{1,0:T(4,128)} %refs_8_.3, f32[1,512]{1,0:T(1,128)} %bitcast.8, ...), custom_call_target="tpu_custom_call" | custom-call | flops 2000000000 | bytes 1018128 | tf_op jit(solution)/shard_map/first_state/pallas_call | solution.py:568
  3.6 0.0 copy-start.3
  3.6 0.0 copy-start.5
  3.6 0.0 copy-start.6
  3.6 5.1 %collective-permute-start = (bf16[144,1024]{1,0:T(8,128)(2,1)}, bf16[144,1024]{1,0:T(8,128)(2,1)S(1)}, u32[]{:S(2)}, u32[]{:S(2)}) collective-permute-start(bf16[144,1024]{1,0:T(8,128)(2,1)} %first_state.1.refs_13_.refs_1_), channel_id=1, source_target_pairs={{0,4},{4,8},{8,12},{1,5},{5,9},{9,13},{2,6},{6,10},{10,14},{3,7},{... | collective-permute-start | bytes 884744 | tf_op jit(solution)/shard_map/ppermute | solution.py:584
  8.8 3.6 %prepare.1 = (bf16[128,2048]{1,0:T(8,128)(2,1)}, bf16[128,512]{1,0:T(8,128)(2,1)S(1)}, f32[8,2560]{1,0:T(8,128)S(1)}, f32[8,2048]{1,0:T(8,128)S(1)}, f32[8,2048]...) custom-call(bf16[128,2048]{1,0:T(8,128)(2,1)S(1)} %copy-done, ...), custom_call_target="tpu_custom_call" | custom-call | flops 2000000000 | bytes 5728656 | tf_op jit(solution)/shard_map/prepare/pallas_call | solution.py:568
  12.4 0.0 copy-done.6
  12.4 0.0 copy-start.2
  12.4 0.8 %attend_own.1 = (f32[128,1024]{1,0:T(8,128)S(1)}, f32[128,1024]{1,0:T(8,128)S(1)}, f32[128,1024]{1,0:T(8,128)S(1)}, bf16[128,512]{1,0:T(8,128)(2,1)S(1)}) custom-call(bf16[128,1024]{1,0:T(8,128)(2,1)S(1)} %copy-done.3, bf16[128,256]{1,0:T(8,128)(2,1)S(1)} %copy-done.5, bf16[128,256]{1,0:T(8,128)(2,1)S(1)} %copy-done.6, ...), custom_call_target="tpu_custom_call" | custom-call | flops 2000000000 | bytes 2162688 | tf_op jit(solution)/shard_map/attend_own/pallas_call | solution.py:568
  13.2 3.5 %collective-permute-start.3 = (bf16[128,512]{1,0:T(8,128)(2,1)S(1)}, bf16[128,512]{1,0:T(8,128)(2,1)S(1)}, u32[]{:S(2)}, u32[]{:S(2)}) collective-permute-start(bf16[128,512]{1,0:T(8,128)(2,1)S(1)} %get-tuple-element.44), channel_id=1, source_target_pairs={{0,4},{4,8},{8,12},{1,5},{5,9},{9,13},{2,6},{6,10},{10,14},{3,7},{... | collective-permute-start | bytes 393224 | tf_op jit(solution)/shard_map/ppermute | solution.py:584
  16.7 0.0 collective-permute-done.refs_0_.refs_5_
  16.7 0.3 relay_slot2.1
  17.0 3.5 %collective-permute-start.1 = (bf16[128,1024]{1,0:T(8,128)(2,1)S(1)}, bf16[128,1024]{1,0:T(8,128)(2,1)S(1)}, u32[]{:S(2)}, u32[]{:S(2)}) collective-permute-start(bf16[128,1024]{1,0:T(8,128)(2,1)S(1)} %relay_slot2.1), channel_id=1, source_target_pairs={{0,4},{4,8},{8,12},{1,5},{5,9},{9,13},{2,6},{6,10},{10,14},{3,7},{... | collective-permute-start | bytes 786440 | tf_op jit(solution)/shard_map/ppermute | solution.py:584
  20.5 1.1 %first_rows.1 = (f32[128,2048]{1,0:T(8,128)S(1)}, bf16[128,256]{1,0:T(8,128)(2,1)S(1)}, bf16[128,1024]{1,0:T(8,128)(2,1)}, bf16[128,1024]{1,0:T(8,128)(2,1)S(1)}) custom-call(bf16[144,1024]{1,0:T(8,128)(2,1)S(1)} %collective-permute-done.refs_0_.refs_5_, f32[8,2560]{1,0:T(8,128)S(1)} %get-tuple-element.27.refs_1_.refs_2_, ...), custom_call_target="tpu_custom_call" | custom-call | flops 2000000000 | bytes 5095424 | tf_op jit(solution)/shard_map/first_rows/pallas_call | solution.py:568
  21.6 0.0 collective-permute-done.3.before_ref
  21.6 0.8 %attend_near.1 = (f32[128,1024]{1,0:T(8,128)S(1)}, f32[128,1024]{1,0:T(8,128)S(1)}, f32[128,1024]{1,0:T(8,128)S(1)}, bf16[128,512]{1,0:T(8,128)(2,1)S(1)}) custom-call(bf16[128,1024]{1,0:T(8,128)(2,1)S(1)} %copy-done.3, bf16[128,512]{1,0:T(8,128)(2,1)S(1)} %collective-permute-done.3.before_ref, s32[128,128]{1,0:T(8,128)S(1)} %get-tuple-element.33.refs_9_.begin_ref.refs_1_, ...), custom_call_target="tpu_custom_call" | custom-call | flops 2000000000 | bytes 3801088 | tf_op jit(solution)/shard_map/attend_near/pallas_call | solution.py:568
  22.4 0.7 %collective-permute-start.4 = (bf16[128,512]{1,0:T(8,128)(2,1)S(1)}, bf16[128,512]{1,0:T(8,128)(2,1)S(1)}, u32[]{:S(2)}, u32[]{:S(2)}) collective-permute-start(bf16[128,512]{1,0:T(8,128)(2,1)S(1)} %get-tuple-element.51), channel_id=1, source_target_pairs={{4,8},{8,12},{5,9},{9,13},{6,10},{10,14},{7,11},{11,15},{20,24},{2... | collective-permute-start | bytes 393224 | tf_op jit(solution)/shard_map/ppermute | solution.py:584
  23.1 2.4 %collective-permute-done.1.refs_0_.refs_6_ = bf16[128,1024]{1,0:T(8,128)(2,1)S(1)} collective-permute-done((bf16[128,1024]{1,0:T(8,128)(2,1)S(1)}, bf16[128,1024]{1,0:T(8,128)(2,1)S(1)}, u32[]{:S(2)}, u32[]{:S(2)}) %collective-permute-start.1) | collective-permute-done | bytes 262176 | tf_op jit(solution)/shard_map/ppermute | solution.py:584
  25.5 0.1 relay_slot3.1
  25.6 4.4 %collective-permute-start.2 = (bf16[128,1024]{1,0:T(8,128)(2,1)S(1)}, bf16[128,1024]{1,0:T(8,128)(2,1)S(1)}, u32[]{:S(2)}, u32[]{:S(2)}) collective-permute-start(bf16[128,1024]{1,0:T(8,128)(2,1)S(1)} %relay_slot3.1), channel_id=1, source_target_pairs={{0,4},{4,8},{8,12},{1,5},{5,9},{9,13},{2,6},{6,10},{10,14},{3,7},{... | collective-permute-start | bytes 786440 | tf_op jit(solution)/shard_map/ppermute | solution.py:584
  30.0 0.0 collective-permute-done.4.refs_5_
  30.0 0.0 copy-start.11
  30.0 1.4 %attend_far.1 = bf16[128,1024]{1,0:T(8,128)(2,1)} custom-call(bf16[128,1024]{1,0:T(8,128)(2,1)S(1)} %copy-done.3, s32[128,128]{1,0:T(8,128)S(1)} %get-tuple-element.33.refs_9_.begin_ref.refs_1_, f32[128,1024]{1,0:T(8,128)S(1)} %get-tuple-element.48.refs_2_, f32[128,1024]{1,0:T(8,128)S(1)} %get-tuple-element.49.refs_3_, ...), custom_call_target="tpu_custom_call" | custom-call | flops 2000000000 | bytes 2293760 | tf_op jit(solution)/shard_map/attend_far/pallas_call | solution.py:568
  31.5 0.0 copy-done.11
  31.5 1.1 %norm_part0.1.refs_6_ = bf16[128,2048]{1,0:T(8,128)(2,1)} custom-call(f32[128,2048]{1,0:T(8,128)S(1)} %get-tuple-element.38.refs_0_, f32[128,2048]{1,0:T(8,128)S(1)} %get-tuple-element.39.refs_1_, bf16[128,256]{1,0:T(8,128)(2,1)S(1)} %get-tuple-element.40.refs_2_.refs_3_, f32[2048]{0:T(1024)S(1)} %copy-done.11, ...), custom_call_target="tpu_custom_call" | custom-call | flops 2000000000 | bytes 3268608 | tf_op jit(solution)/shard_map/norm_part0/pallas_call | solution.py:568
  32.5 1.5 %collective-permute-done.2.refs_5_ = bf16[128,1024]{1,0:T(8,128)(2,1)S(1)} collective-permute-done((bf16[128,1024]{1,0:T(8,128)(2,1)S(1)}, bf16[128,1024]{1,0:T(8,128)(2,1)S(1)}, u32[]{:S(2)}, u32[]{:S(2)}) %collective-permute-start.2) | collective-permute-done | bytes 262176 | tf_op jit(solution)/shard_map/ppermute | solution.py:584
  34.0 1.0 %norm_part1.1 = bf16[128,2048]{1,0:T(8,128)(2,1)} custom-call(f32[128,2048]{1,0:T(8,128)S(1)} %get-tuple-element.38.refs_0_, f32[128,2048]{1,0:T(8,128)S(1)} %get-tuple-element.39.refs_1_, bf16[128,256]{1,0:T(8,128)(2,1)S(1)} %get-tuple-element.40.refs_2_.refs_3_, f32[2048]{0:T(1024)S(1)} %copy-done.11, ...), custom_call_target="tpu_custom_call", output_to_operand_aliasing={{}: (6, {})} | custom-call | flops 2000000000 | bytes 3497984 | tf_op jit(solution)/shard_map/norm_part1/pallas_call | solution.py:568
  (22 shorter events, 0.0 us)
Async XLA Ops:
  0.6 8.1 %copy-start = (bf16[128,2048]{1,0:T(8,128)(2,1)S(1)}, bf16[128,2048]{1,0:T(8,128)(2,1)}, u32[]{:S(2)}) copy-start(bf16[128,2048]{1,0:T(8,128)(2,1)} %refs_0_.4) | copy-start | bytes 1572868
  0.6 8.1 %copy-start.1 = (bf16[128,2048]{1,0:T(8,128)(2,1)S(1)}, bf16[128,2048]{1,0:T(8,128)(2,1)}, u32[]{:S(2)}) copy-start(bf16[128,2048]{1,0:T(8,128)(2,1)} %refs_11_.1) | copy-start | bytes 1572868
  0.7 8.1 %copy-start.4 = (bf16[128,512]{1,0:T(8,128)(2,1)S(1)}, bf16[128,512]{1,0:T(8,128)(2,1)}, u32[]{:S(2)}) copy-start(bf16[128,512]{1,0:T(8,128)(2,1)} %refs_1_.3) | copy-start | bytes 393220
  0.7 8.1 %copy-start.7 = (f32[4,2048]{1,0:T(4,128)S(1)}, f32[4,2048]{1,0:T(4,128)}, u32[]{:S(2)}) copy-start(f32[4,2048]{1,0:T(4,128)} %refs_7_.3) | copy-start | bytes 98308
  0.7 8.1 %copy-start.8 = (f32[128,32]{0,1:T(8,128)S(1)}, f32[128,32]{0,1:T(8,128)}, u32[]{:S(2)}) copy-start(f32[128,32]{0,1:T(8,128)} %param.19) | copy-start | bytes 49156
  0.7 8.1 %copy-start.9 = (f32[2048]{0:T(1024)S(1)}, f32[2048]{0:T(1024)}, u32[]{:S(2)}) copy-start(f32[2048]{0:T(1024)} %refs_4_.2) | copy-start | bytes 24580
  0.7 8.1 %copy-start.10 = (f32[4,512]{1,0:T(4,128)S(1)}, f32[4,512]{1,0:T(4,128)}, u32[]{:S(2)}) copy-start(f32[4,512]{1,0:T(4,128)} %refs_8_.3) | copy-start | bytes 24580
  0.7 8.1 %copy-start.12 = (f32[512]{0:T(512)S(1)}, f32[512]{0:T(512)}, u32[]{:S(2)}) copy-start(f32[512]{0:T(512)} %refs_6_.1) | copy-start | bytes 6148
  0.7 8.1 %copy-start.13 = (f32[32]{0:T(128)S(1)}, f32[32]{0:T(128)}, u32[]{:S(2)}) copy-start(f32[32]{0:T(128)} %refs_7_.2) | copy-start | bytes 388
  0.7 8.1 %copy-start.14 = (f32[32]{0:T(128)S(1)}, f32[32]{0:T(128)}, u32[]{:S(2)}) copy-start(f32[32]{0:T(128)} %refs_8_.2) | copy-start | bytes 388
  0.7 8.1 %copy-start.15 = (s32[4]{0:T(128)S(1)}, s32[4]{0:T(128)}, u32[]{:S(2)}) copy-start(s32[4]{0:T(128)} %refs_10_.1) | copy-start | bytes 52
  0.7 8.1 %copy-start.16 = (f32[32]{0:T(128)S(1)}, f32[32]{0:T(128)}, u32[]{:S(2)}) copy-start(f32[32]{0:T(128)} %refs_9_.3) | copy-start | bytes 388
  3.6 8.8 %copy-start.3 = (bf16[128,1024]{1,0:T(8,128)(2,1)S(1)}, bf16[128,1024]{1,0:T(8,128)(2,1)}, u32[]{:S(2)}) copy-start(bf16[128,1024]{1,0:T(8,128)(2,1)} %refs_0_.5) | copy-start | bytes 786436
  3.6 8.8 %copy-start.5 = (bf16[128,256]{1,0:T(8,128)(2,1)S(1)}, bf16[128,256]{1,0:T(8,128)(2,1)}, u32[]{:S(2)}) copy-start(bf16[128,256]{1,0:T(8,128)(2,1)} %keys_ref.1) | copy-start | bytes 196612
  3.6 8.8 %copy-start.6 = (bf16[128,256]{1,0:T(8,128)(2,1)S(1)}, bf16[128,256]{1,0:T(8,128)(2,1)}, u32[]{:S(2)}) copy-start(bf16[128,256]{1,0:T(8,128)(2,1)} %values_ref.1) | copy-start | bytes 196612
  3.6 13.0 %collective-permute-start = (bf16[144,1024]{1,0:T(8,128)(2,1)}, bf16[144,1024]{1,0:T(8,128)(2,1)S(1)}, u32[]{:S(2)}, u32[]{:S(2)}) collective-permute-start(bf16[144,1024]{1,0:T(8,128)(2,1)} %first_state.1.refs_13_.refs_1_), channel_id=1, source_target_pairs={{0,4},{4,8},{8,12},{1,5},{5,9},{9,13},{2,6},{6,10},{10,14},{3,7},{... | collective-permute-start | bytes 884744 | tf_op jit(solution)/shard_map/ppermute | solution.py:584
  12.4 4.3 %copy-start.2 = (bf16[144,1024]{1,0:T(8,128)(2,1)S(1)}, bf16[144,1024]{1,0:T(8,128)(2,1)}, u32[]{:S(2)}) copy-start(bf16[144,1024]{1,0:T(8,128)(2,1)} %first_state.1.refs_13_.refs_1_) | copy-start | bytes 884740
  13.2 8.4 %collective-permute-start.3 = (bf16[128,512]{1,0:T(8,128)(2,1)S(1)}, bf16[128,512]{1,0:T(8,128)(2,1)S(1)}, u32[]{:S(2)}, u32[]{:S(2)}) collective-permute-start(bf16[128,512]{1,0:T(8,128)(2,1)S(1)} %get-tuple-element.44), channel_id=1, source_target_pairs={{0,4},{4,8},{8,12},{1,5},{5,9},{9,13},{2,6},{6,10},{10,14},{3,7},{... | collective-permute-start | bytes 393224 | tf_op jit(solution)/shard_map/ppermute | solution.py:584
  17.0 8.5 %collective-permute-start.1 = (bf16[128,1024]{1,0:T(8,128)(2,1)S(1)}, bf16[128,1024]{1,0:T(8,128)(2,1)S(1)}, u32[]{:S(2)}, u32[]{:S(2)}) collective-permute-start(bf16[128,1024]{1,0:T(8,128)(2,1)S(1)} %relay_slot2.1), channel_id=1, source_target_pairs={{0,4},{4,8},{8,12},{1,5},{5,9},{9,13},{2,6},{6,10},{10,14},{3,7},{... | collective-permute-start | bytes 786440 | tf_op jit(solution)/shard_map/ppermute | solution.py:584
  22.4 7.6 %collective-permute-start.4 = (bf16[128,512]{1,0:T(8,128)(2,1)S(1)}, bf16[128,512]{1,0:T(8,128)(2,1)S(1)}, u32[]{:S(2)}, u32[]{:S(2)}) collective-permute-start(bf16[128,512]{1,0:T(8,128)(2,1)S(1)} %get-tuple-element.51), channel_id=1, source_target_pairs={{4,8},{8,12},{5,9},{9,13},{6,10},{10,14},{7,11},{11,15},{20,24},{2... | collective-permute-start | bytes 393224 | tf_op jit(solution)/shard_map/ppermute | solution.py:584
  25.6 8.4 %collective-permute-start.2 = (bf16[128,1024]{1,0:T(8,128)(2,1)S(1)}, bf16[128,1024]{1,0:T(8,128)(2,1)S(1)}, u32[]{:S(2)}, u32[]{:S(2)}) collective-permute-start(bf16[128,1024]{1,0:T(8,128)(2,1)S(1)} %relay_slot3.1), channel_id=1, source_target_pairs={{0,4},{4,8},{8,12},{1,5},{5,9},{9,13},{2,6},{6,10},{10,14},{3,7},{... | collective-permute-start | bytes 786440 | tf_op jit(solution)/shard_map/ppermute | solution.py:584
  30.0 1.5 %copy-start.11 = (f32[2048]{0:T(1024)S(1)}, f32[2048]{0:T(1024)}, u32[]{:S(2)}) copy-start(f32[2048]{0:T(1024)} %refs_3_.7) | copy-start | bytes 24580

commit v13 on v11

--- a/solution.py
+++ b/solution.py
@@ -85,7 +85,7 @@
     for lag in range(1, taps):
         term = pad[8 - lag : 8 - lag + rows] * weight[taps - 1 - lag : taps - lag]
         total = total + jnp.where(inside[lag], term, 0.0)
-    return silu(total).astype(BF16)
+    return silu(total)
 
 
 def tail_lines(message, rows):
@@ -146,7 +146,7 @@
     for at in (1, 5, 6):
         copies[at].wait()
     inputs = conv_rows(b_pad_ref, b_ref[...], wbc_ref[...], bbc_ref[...], narrow)
-    turned = inputs.astype(F32).T.astype(BF16)
+    turned = inputs.T.astype(BF16)
     for at in (0, 3, 4):
         copies[at].wait()
     slots = pad_ref.shape[0]
@@ -161,7 +161,7 @@
         columns = slice(start, start + CHUNK)
         pad = pad_ref.at[(at + 1) % slots]
         xc = conv_rows(pad, x_ref[:, columns], wx_ref[:, columns], bx_ref[:, columns], inside)
-        weighted = (xc.astype(F32) * widen(weight, start, CHUNK)).astype(BF16)
+        weighted = (xc * widen(weight, start, CHUNK)).astype(BF16)
         out_ref[:STATE, columns] = jnp.dot(turned, weighted, preferred_element_type=F32).astype(BF16)
         if at % 2:
             send(at // 2, (pl.ds(0, STATE), pl.ds(start - CHUNK, 2 * CHUNK)))
@@ -201,16 +201,16 @@
     for group in range(groups):
         base = slice(group * 2 * STATE, (group + 1) * 2 * STATE)
         pair = conv_rows(pad_ref.at[0], bc_ref[:, base], wbc_ref[:, base], bbc_ref[base], inside)
-        bcc_ref[:, base] = pair
-        turned = pair[:, :STATE].astype(F32).T.astype(BF16)
+        bcc_ref[:, base] = pair.astype(BF16)
+        turned = pair[:, :STATE].T.astype(BF16)
         part_weight = kept[:, group * group_heads : (group + 1) * group_heads]
         for chunk in range(0, per_group, CHUNK):
             columns = slice(group * per_group + chunk, group * per_group + chunk + CHUNK)
             pad = pad_ref.at[(chunk // CHUNK + 1) % slots]
             xc = conv_rows(pad, x_ref[:, columns], wx_ref[:, columns], bx_ref[columns], inside)
-            xc_ref[:, columns] = xc
+            xc_ref[:, columns] = xc.astype(BF16)
             if group:
-                weighted = (xc.astype(F32) * widen(part_weight, chunk, CHUNK)).astype(BF16)
+                weighted = (xc * widen(part_weight, chunk, CHUNK)).astype(BF16)
                 state_refs[group - 1][:, chunk : chunk + CHUNK] = jnp.dot(
                     turned, weighted, preferred_element_type=F32
                 ).astype(BF16)
@@ -516,7 +516,7 @@
         copy.wait()
 
 
-def norm_kernel(part, hops, first, given, *refs):
+def norm_kernel(part, hops, turn, given, *refs):
     local_ref, decay_ref, c_ref, gain_ref, flag_ref = refs[:5]
     got_refs = refs[5 : 5 + hops]
     out_hbm_ref, *token_refs = refs[5 + hops + given : -3]
@@ -533,7 +533,7 @@
             placed = slice(part * width + start, part * width + start + CHUNK)
             state = got_refs[0][:STATE, columns]
             for hop in range(1, hops):
-                there = flag_ref[first + hop, 0:1] > 0.5
+                there = flag_ref[hop, 0:1] > 0.5
                 state = jnp.where(there, got_refs[hop][:STATE, columns].astype(F32), state.astype(F32))
             carried = jnp.dot(outputs, state.astype(BF16), preferred_element_type=F32)
             gated = local_ref[:, placed] + carried * decay_ref[:, placed]
@@ -558,8 +558,11 @@
         for copy in copies:
             copy.wait()
 
-    if first:
-        pl.when(jnp.max(flag_ref[first:]) > 0.5)(work)
+    odd = lax.axis_index("dp") % 2 == 1
+    if turn == 0:
+        pl.when(odd)(work)
+    elif turn == 1:
+        pl.when(jnp.logical_not(odd) | (jnp.max(flag_ref[1:]) > 0.5))(work)
     else:
         work()
 
@@ -711,7 +714,7 @@
             [WHOLE] * len(operands),
             scratch=scratch,
         )
-        slots.append(onward(passed))
+        slots.append(onward(passed, max(0, slot - groups)))
         if fulls is None:
             gated, c_out, *fulls = call(
                 functools.partial(first_rows_kernel, groups),
@@ -728,7 +731,7 @@
                 [WHOLE] * (13 + groups),
                 scratch=[pltpu.VMEM((4, 16, CHUNK), F32)],
             )
-    def norm(part, first, got, out=None, token=False):
+    def norm(part, turn, got, out=None, token=False):
         operands = [gated, decay, c_out, norm_gain, flags, *got]
         specs = [WHOLE] * len(operands)
         outs = [shape((rows, width), BF16)] + [shape((8, 128), F32)] * token
@@ -738,8 +741,8 @@
             operands.append(out)
             specs.append(UNTOUCHED)
         return call(
-            functools.partial(norm_kernel, part, len(got), first, out is not None),
-            f"norm_part{part}_{first}",
+            functools.partial(norm_kernel, part, len(got), turn, out is not None),
+            f"norm_part{part}_{turn}",
             outs,
             operands,
             specs,
@@ -776,9 +779,9 @@
             pltpu.SemaphoreType.DMA((keys.shape[1] // ADIM,)),
         ],
     )
-    for part in range(groups - 1):
-        (mamba_out,) = norm(part, 1, slots[part + 1 : part + hops], mamba_out)
-    (mamba_out,) = norm(groups - 1, 0, slots[-1:], mamba_out)
+    for part in range(groups):
+        last = part == groups - 1
+        (mamba_out,) = norm(part, 1 + last, slots[part : part + hops], mamba_out)
     return (mamba_out, attn_out)
 
 

time: 35.4 us -> 34.3 us (0.969)
  Pallas kernels: 14.3 us -> 13.2 us
    pallas_call x11, Pallas kernels: 14.3 us -> 13.2 us  [call(): pl.pallas_call(kernel, name=name, grid=(1,), out_shape=outs, in_specs=spe...]
  transfers between devices with their start and end apart: 5 -> 5, of which waited for: 4 -> 3; matrix products, arithmetic and copies ran while one was open for 0% -> 0% of each run, Pallas kernels for 30% -> 27%
where the time goes in v13:
time: 34.3 us; the launch traced here: 34.1 us
  starting transfers between devices  15 us (44%)
  Pallas kernels  13.2 us (38%)
  waiting for transfers between devices  4.86 us (14%)
  between operations  0.98 us (3%)
    ppermute x5, starting transfers between devices, onward(): lax.ppermute(value, 'seq', [(source, source + 1) for source in range(firs...  15 us
    pallas_call x11, Pallas kernels, call(): pl.pallas_call(kernel, name=name, grid=(1,), out_shape=outs, in_specs=spe...  13.2 us
    ppermute x5, waiting for transfers between devices, onward(): lax.ppermute(value, 'seq', [(source, source + 1) for source in range(firs...  4.86 us
  transfers between devices with their start and end apart: 5, of which 3 were waited for; matrix products, arithmetic and copies ran while one was open for 0% of the time, Pallas kernels for 27%

profile of v13, /device:TPU:22, one launch (start us, length us, event | category | flops | bytes accessed | tf_op | source)
XLA Modules:
  0.0 34.1 jit_solution(14134185747445759115)
XLA Ops:
  0.6 0.0 copy-start
  0.6 0.0 copy-start.1
  0.7 0.0 copy-start.4
  0.7 0.0 copy-start.7
  0.7 0.0 copy-start.8
  0.7 0.0 copy-start.9
  0.8 2.8 %first_state.1.refs_13_.refs_1_ = bf16[144,1024]{1,0:T(8,128)(2,1)} custom-call(bf16[128,2048]{1,0:T(8,128)(2,1)} %refs_0_.4, bf16[128,512]{1,0:T(8,128)(2,1)} %refs_1_.3, f32[32,128]{1,0:T(8,128)} %bitcast.5, f32[4,2048]{1,0:T(4,128)} %refs_7_.3, f32[1,2048]{1,0:T(1,128)} %bitcast.7, f32[4,512]{1,0:T(4,128)} %refs_8_.3, f32[1,512]{1,0:T(1,128)} %bitcast.8, ...), custom_call_target="tpu_custom_call" | custom-call | flops 2000000000 | bytes 1018128 | tf_op jit(solution)/shard_map/first_state/pallas_call | solution.py:581
  3.6 0.0 copy-start.3
  3.6 0.0 copy-start.5
  3.6 0.0 copy-start.6
  3.6 3.6 %collective-permute-start = (bf16[144,1024]{1,0:T(8,128)(2,1)}, bf16[144,1024]{1,0:T(8,128)(2,1)S(1)}, u32[]{:S(2)}, u32[]{:S(2)}) collective-permute-start(bf16[144,1024]{1,0:T(8,128)(2,1)} %first_state.1.refs_13_.refs_1_), channel_id=1, source_target_pairs={{0,4},{4,8},{8,12},{1,5},{5,9},{9,13},{2,6},{6,10},{10,14},{3,7},{... | collective-permute-start | bytes 884744 | tf_op jit(solution)/shard_map/ppermute | solution.py:597
  7.4 3.6 %prepare.1 = (bf16[128,2048]{1,0:T(8,128)(2,1)}, bf16[128,512]{1,0:T(8,128)(2,1)S(1)}, f32[8,2560]{1,0:T(8,128)S(1)}, f32[8,2048]{1,0:T(8,128)S(1)}, f32[8,2048]...) custom-call(bf16[128,2048]{1,0:T(8,128)(2,1)S(1)} %copy-done, ...), custom_call_target="tpu_custom_call" | custom-call | flops 2000000000 | bytes 5728656 | tf_op jit(solution)/shard_map/prepare/pallas_call | solution.py:581
  11.0 0.0 copy-start.2
  11.0 0.8 %attend_own.1 = (f32[128,1024]{1,0:T(8,128)S(1)}, f32[128,1024]{1,0:T(8,128)S(1)}, f32[128,1024]{1,0:T(8,128)S(1)}, bf16[128,512]{1,0:T(8,128)(2,1)S(1)}) custom-call(bf16[128,1024]{1,0:T(8,128)(2,1)S(1)} %copy-done.3, bf16[128,256]{1,0:T(8,128)(2,1)S(1)} %copy-done.5, bf16[128,256]{1,0:T(8,128)(2,1)S(1)} %copy-done.6, ...), custom_call_target="tpu_custom_call" | custom-call | flops 2000000000 | bytes 2162688 | tf_op jit(solution)/shard_map/attend_own/pallas_call | solution.py:581
  11.7 1.9 %collective-permute-start.3 = (bf16[128,512]{1,0:T(8,128)(2,1)S(1)}, bf16[128,512]{1,0:T(8,128)(2,1)S(1)}, u32[]{:S(2)}, u32[]{:S(2)}) collective-permute-start(bf16[128,512]{1,0:T(8,128)(2,1)S(1)} %get-tuple-element.47), channel_id=1, source_target_pairs={{0,4},{4,8},{8,12},{1,5},{5,9},{9,13},{2,6},{6,10},{10,14},{3,7},{... | collective-permute-start | bytes 393224 | tf_op jit(solution)/shard_map/ppermute | solution.py:597
  13.7 1.0 %collective-permute-done.refs_0_.refs_5_ = bf16[144,1024]{1,0:T(8,128)(2,1)S(1)} collective-permute-done((bf16[144,1024]{1,0:T(8,128)(2,1)}, bf16[144,1024]{1,0:T(8,128)(2,1)S(1)}, u32[]{:S(2)}, u32[]{:S(2)}) %collective-permute-start) | collective-permute-done | bytes 294944 | tf_op jit(solution)/shard_map/ppermute | solution.py:597
  14.6 0.3 relay_slot2.1
  15.0 3.5 %collective-permute-start.1 = (bf16[128,1024]{1,0:T(8,128)(2,1)S(1)}, bf16[128,1024]{1,0:T(8,128)(2,1)S(1)}, u32[]{:S(2)}, u32[]{:S(2)}) collective-permute-start(bf16[128,1024]{1,0:T(8,128)(2,1)S(1)} %relay_slot2.1), channel_id=1, source_target_pairs={{0,4},{4,8},{8,12},{1,5},{5,9},{9,13},{2,6},{6,10},{10,14},{3,7},{... | collective-permute-start | bytes 786440 | tf_op jit(solution)/shard_map/ppermute | solution.py:597
  18.5 0.0 copy-start.11
  18.5 1.1 %first_rows.1 = (f32[128,2048]{1,0:T(8,128)S(1)}, bf16[128,256]{1,0:T(8,128)(2,1)S(1)}, bf16[128,1024]{1,0:T(8,128)(2,1)}, bf16[128,1024]{1,0:T(8,128)(2,1)S(1)}) custom-call(bf16[144,1024]{1,0:T(8,128)(2,1)S(1)} %collective-permute-done.refs_0_.refs_5_, f32[8,2560]{1,0:T(8,128)S(1)} %get-tuple-element.29.refs_1_.refs_2_, ...), custom_call_target="tpu_custom_call" | custom-call | flops 2000000000 | bytes 5095424 | tf_op jit(solution)/shard_map/first_rows/pallas_call | solution.py:581
  19.6 0.0 copy-done.11
  19.7 0.0 collective-permute-done.3.before_ref
  19.7 0.8 %attend_near.1 = (f32[128,1024]{1,0:T(8,128)S(1)}, f32[128,1024]{1,0:T(8,128)S(1)}, f32[128,1024]{1,0:T(8,128)S(1)}, bf16[128,512]{1,0:T(8,128)(2,1)S(1)}) custom-call(bf16[128,1024]{1,0:T(8,128)(2,1)S(1)} %copy-done.3, bf16[128,512]{1,0:T(8,128)(2,1)S(1)} %collective-permute-done.3.before_ref, s32[128,128]{1,0:T(8,128)S(1)} %get-tuple-element.35.refs_9_.begin_ref.refs_1_, ...), custom_call_target="tpu_custom_call" | custom-call | flops 2000000000 | bytes 3739648 | tf_op jit(solution)/shard_map/attend_near/pallas_call | solution.py:581
  20.5 1.9 %collective-permute-start.4 = (bf16[128,512]{1,0:T(8,128)(2,1)S(1)}, bf16[128,512]{1,0:T(8,128)(2,1)S(1)}, u32[]{:S(2)}, u32[]{:S(2)}) collective-permute-start(bf16[128,512]{1,0:T(8,128)(2,1)S(1)} %get-tuple-element.55), channel_id=1, source_target_pairs={{4,8},{8,12},{5,9},{9,13},{6,10},{10,14},{7,11},{11,15},{20,24},{2... | collective-permute-start | bytes 393224 | tf_op jit(solution)/shard_map/ppermute | solution.py:597
  22.4 1.8 %collective-permute-done.1.refs_0_.refs_6_.refs_5_ = bf16[128,1024]{1,0:T(8,128)(2,1)S(1)} collective-permute-done((bf16[128,1024]{1,0:T(8,128)(2,1)S(1)}, bf16[128,1024]{1,0:T(8,128)(2,1)S(1)}, u32[]{:S(2)}, u32[]{:S(2)}) %collective-permute-start.1) | collective-permute-done | bytes 262176 | tf_op jit(solution)/shard_map/ppermute | solution.py:597
  24.2 0.1 relay_slot3.1
  24.3 4.0 %collective-permute-start.2 = (bf16[128,1024]{1,0:T(8,128)(2,1)S(1)}, bf16[128,1024]{1,0:T(8,128)(2,1)S(1)}, u32[]{:S(2)}, u32[]{:S(2)}) collective-permute-start(bf16[128,1024]{1,0:T(8,128)(2,1)S(1)} %relay_slot3.1), channel_id=1, source_target_pairs={{4,8},{8,12},{5,9},{9,13},{6,10},{10,14},{7,11},{11,15},{20,24},{2... | collective-permute-start | bytes 786440 | tf_op jit(solution)/shard_map/ppermute | solution.py:597
  28.3 0.0 collective-permute-done.4.refs_5_
  28.3 1.5 %attend_far.1 = bf16[128,1024]{1,0:T(8,128)(2,1)} custom-call(bf16[128,1024]{1,0:T(8,128)(2,1)S(1)} %copy-done.3, s32[128,128]{1,0:T(8,128)S(1)} %get-tuple-element.35.refs_9_.begin_ref.refs_1_, f32[128,1024]{1,0:T(8,128)S(1)} %get-tuple-element.52.refs_2_, f32[128,1024]{1,0:T(8,128)S(1)} %get-tuple-element.53.refs_3_, ...), custom_call_target="tpu_custom_call" | custom-call | flops 2000000000 | bytes 2293760 | tf_op jit(solution)/shard_map/attend_far/pallas_call | solution.py:581
  29.7 1.2 %norm_part0_1.1.refs_7_ = bf16[128,2048]{1,0:T(8,128)(2,1)} custom-call(f32[128,2048]{1,0:T(8,128)S(1)} %get-tuple-element.40.refs_0_, f32[128,2048]{1,0:T(8,128)S(1)} %get-tuple-element.41.refs_1_, bf16[128,256]{1,0:T(8,128)(2,1)S(1)} %get-tuple-element.42.refs_2_, f32[2048]{0:T(1024)S(1)} %copy-done.11, ...), custom_call_target="tpu_custom_call", output_to_operand_aliasing={{}: (7, {})} | custom-call | flops 2000000000 | bytes 3792896 | tf_op jit(solution)/shard_map/norm_part0_1/pallas_call | solution.py:581
  30.9 2.1 %collective-permute-done.2.refs_6_ = bf16[128,1024]{1,0:T(8,128)(2,1)S(1)} collective-permute-done((bf16[128,1024]{1,0:T(8,128)(2,1)S(1)}, bf16[128,1024]{1,0:T(8,128)(2,1)S(1)}, u32[]{:S(2)}, u32[]{:S(2)}) %collective-permute-start.2) | collective-permute-done | bytes 262176 | tf_op jit(solution)/shard_map/ppermute | solution.py:597
  33.0 1.1 %norm_part1_2.1 = bf16[128,2048]{1,0:T(8,128)(2,1)} custom-call(f32[128,2048]{1,0:T(8,128)S(1)} %get-tuple-element.40.refs_0_, f32[128,2048]{1,0:T(8,128)S(1)} %get-tuple-element.41.refs_1_, bf16[128,256]{1,0:T(8,128)(2,1)S(1)} %get-tuple-element.42.refs_2_, f32[2048]{0:T(1024)S(1)} %copy-done.11, ...), custom_call_target="tpu_custom_call", output_to_operand_aliasing={{}: (7, {})} | custom-call | flops 2000000000 | bytes 3760128 | tf_op jit(solution)/shard_map/norm_part1_2/pallas_call | solution.py:581
  (23 shorter events, 0.1 us)
Async XLA Ops:
  0.6 6.6 %copy-start = (bf16[128,2048]{1,0:T(8,128)(2,1)S(1)}, bf16[128,2048]{1,0:T(8,128)(2,1)}, u32[]{:S(2)}) copy-start(bf16[128,2048]{1,0:T(8,128)(2,1)} %refs_0_.4) | copy-start | bytes 1572868
  0.6 6.6 %copy-start.1 = (bf16[128,2048]{1,0:T(8,128)(2,1)S(1)}, bf16[128,2048]{1,0:T(8,128)(2,1)}, u32[]{:S(2)}) copy-start(bf16[128,2048]{1,0:T(8,128)(2,1)} %refs_11_.1) | copy-start | bytes 1572868
  0.7 6.6 %copy-start.4 = (bf16[128,512]{1,0:T(8,128)(2,1)S(1)}, bf16[128,512]{1,0:T(8,128)(2,1)}, u32[]{:S(2)}) copy-start(bf16[128,512]{1,0:T(8,128)(2,1)} %refs_1_.3) | copy-start | bytes 393220
  0.7 6.6 %copy-start.7 = (f32[4,2048]{1,0:T(4,128)S(1)}, f32[4,2048]{1,0:T(4,128)}, u32[]{:S(2)}) copy-start(f32[4,2048]{1,0:T(4,128)} %refs_7_.3) | copy-start | bytes 98308
  0.7 6.6 %copy-start.8 = (f32[128,32]{0,1:T(8,128)S(1)}, f32[128,32]{0,1:T(8,128)}, u32[]{:S(2)}) copy-start(f32[128,32]{0,1:T(8,128)} %param.19) | copy-start | bytes 49156
  0.7 6.6 %copy-start.9 = (f32[2048]{0:T(1024)S(1)}, f32[2048]{0:T(1024)}, u32[]{:S(2)}) copy-start(f32[2048]{0:T(1024)} %refs_4_.2) | copy-start | bytes 24580
  0.7 6.6 %copy-start.10 = (f32[4,512]{1,0:T(4,128)S(1)}, f32[4,512]{1,0:T(4,128)}, u32[]{:S(2)}) copy-start(f32[4,512]{1,0:T(4,128)} %refs_8_.3) | copy-start | bytes 24580
  0.7 6.6 %copy-start.12 = (f32[512]{0:T(512)S(1)}, f32[512]{0:T(512)}, u32[]{:S(2)}) copy-start(f32[512]{0:T(512)} %refs_6_.1) | copy-start | bytes 6148
  0.7 6.6 %copy-start.13 = (f32[32]{0:T(128)S(1)}, f32[32]{0:T(128)}, u32[]{:S(2)}) copy-start(f32[32]{0:T(128)} %refs_7_.2) | copy-start | bytes 388
  0.7 6.6 %copy-start.14 = (f32[32]{0:T(128)S(1)}, f32[32]{0:T(128)}, u32[]{:S(2)}) copy-start(f32[32]{0:T(128)} %refs_8_.2) | copy-start | bytes 388
  0.7 6.6 %copy-start.15 = (s32[4]{0:T(128)S(1)}, s32[4]{0:T(128)}, u32[]{:S(2)}) copy-start(s32[4]{0:T(128)} %refs_10_.1) | copy-start | bytes 52
  0.7 6.6 %copy-start.16 = (f32[32]{0:T(128)S(1)}, f32[32]{0:T(128)}, u32[]{:S(2)}) copy-start(f32[32]{0:T(128)} %refs_9_.3) | copy-start | bytes 388
  3.6 7.3 %copy-start.3 = (bf16[128,1024]{1,0:T(8,128)(2,1)S(1)}, bf16[128,1024]{1,0:T(8,128)(2,1)}, u32[]{:S(2)}) copy-start(bf16[128,1024]{1,0:T(8,128)(2,1)} %refs_0_.5) | copy-start | bytes 786436
  3.6 7.3 %copy-start.5 = (bf16[128,256]{1,0:T(8,128)(2,1)S(1)}, bf16[128,256]{1,0:T(8,128)(2,1)}, u32[]{:S(2)}) copy-start(bf16[128,256]{1,0:T(8,128)(2,1)} %keys_ref.1) | copy-start | bytes 196612
  3.6 7.3 %copy-start.6 = (bf16[128,256]{1,0:T(8,128)(2,1)S(1)}, bf16[128,256]{1,0:T(8,128)(2,1)}, u32[]{:S(2)}) copy-start(bf16[128,256]{1,0:T(8,128)(2,1)} %values_ref.1) | copy-start | bytes 196612
  3.6 11.0 %collective-permute-start = (bf16[144,1024]{1,0:T(8,128)(2,1)}, bf16[144,1024]{1,0:T(8,128)(2,1)S(1)}, u32[]{:S(2)}, u32[]{:S(2)}) collective-permute-start(bf16[144,1024]{1,0:T(8,128)(2,1)} %first_state.1.refs_13_.refs_1_), channel_id=1, source_target_pairs={{0,4},{4,8},{8,12},{1,5},{5,9},{9,13},{2,6},{6,10},{10,14},{3,7},{... | collective-permute-start | bytes 884744 | tf_op jit(solution)/shard_map/ppermute | solution.py:597
  11.0 3.7 %copy-start.2 = (bf16[144,1024]{1,0:T(8,128)(2,1)S(1)}, bf16[144,1024]{1,0:T(8,128)(2,1)}, u32[]{:S(2)}) copy-start(bf16[144,1024]{1,0:T(8,128)(2,1)} %first_state.1.refs_13_.refs_1_) | copy-start | bytes 884740
  11.7 7.9 %collective-permute-start.3 = (bf16[128,512]{1,0:T(8,128)(2,1)S(1)}, bf16[128,512]{1,0:T(8,128)(2,1)S(1)}, u32[]{:S(2)}, u32[]{:S(2)}) collective-permute-start(bf16[128,512]{1,0:T(8,128)(2,1)S(1)} %get-tuple-element.47), channel_id=1, source_target_pairs={{0,4},{4,8},{8,12},{1,5},{5,9},{9,13},{2,6},{6,10},{10,14},{3,7},{... | collective-permute-start | bytes 393224 | tf_op jit(solution)/shard_map/ppermute | solution.py:597
  15.0 9.2 %collective-permute-start.1 = (bf16[128,1024]{1,0:T(8,128)(2,1)S(1)}, bf16[128,1024]{1,0:T(8,128)(2,1)S(1)}, u32[]{:S(2)}, u32[]{:S(2)}) collective-permute-start(bf16[128,1024]{1,0:T(8,128)(2,1)S(1)} %relay_slot2.1), channel_id=1, source_target_pairs={{0,4},{4,8},{8,12},{1,5},{5,9},{9,13},{2,6},{6,10},{10,14},{3,7},{... | collective-permute-start | bytes 786440 | tf_op jit(solution)/shard_map/ppermute | solution.py:597
  18.5 1.1 %copy-start.11 = (f32[2048]{0:T(1024)S(1)}, f32[2048]{0:T(1024)}, u32[]{:S(2)}) copy-start(f32[2048]{0:T(1024)} %refs_3_.9) | copy-start | bytes 24580
  20.5 7.8 %collective-permute-start.4 = (bf16[128,512]{1,0:T(8,128)(2,1)S(1)}, bf16[128,512]{1,0:T(8,128)(2,1)S(1)}, u32[]{:S(2)}, u32[]{:S(2)}) collective-permute-start(bf16[128,512]{1,0:T(8,128)(2,1)S(1)} %get-tuple-element.55), channel_id=1, source_target_pairs={{4,8},{8,12},{5,9},{9,13},{6,10},{10,14},{7,11},{11,15},{20,24},{2... | collective-permute-start | bytes 393224 | tf_op jit(solution)/shard_map/ppermute | solution.py:597
  24.3 8.7 %collective-permute-start.2 = (bf16[128,1024]{1,0:T(8,128)(2,1)S(1)}, bf16[128,1024]{1,0:T(8,128)(2,1)S(1)}, u32[]{:S(2)}, u32[]{:S(2)}) collective-permute-start(bf16[128,1024]{1,0:T(8,128)(2,1)S(1)} %relay_slot3.1), channel_id=1, source_target_pairs={{4,8},{8,12},{5,9},{9,13},{6,10},{10,14},{7,11},{11,15},{20,24},{2... | collective-permute-start | bytes 786440 | tf_op jit(solution)/shard_map/ppermute | solution.py:597
